TPU v7x, 32 devices: a whole 2x2x4 slice. The times are simulated.
32 devices in a mesh: shard: 32 (over z, y, x, core).
Axes of the slice: x: 2, y: 2, z: 4, core: 2. Of those that a mesh axis runs over, the one named last changes fastest.
Arguments:
- features: bfloat16 [32768, 128], P('shard'), may hold values from -6 to 6
- conv_weight: bfloat16 [27, 128, 128], replicated, may hold values from -0.125 to 0.125
- down_weight: bfloat16 [8, 128, 256], replicated, may hold values from -0.25 to 0.25
- neighbour_map: int32 [27, 32768], P(None, 'shard'), may hold values from 0 to 1280, as said below
- halo_rows: int32 [4, 2048], P(None, 'shard'), may hold values from 0 to 1024, as said below
- child_map: int32 [8, 8192], P(None, 'shard'), may hold values from 0 to 1152, as said below
- child_rows: int32 [4, 1024], P(None, 'shard'), may hold values from 0 to 1024, as said below
- out_grad: bfloat16 [8192, 256], P('shard'), may hold values from -6 to 6
Outputs:
- coarse: bfloat16 [8192, 256], P('shard')
- input_grad: float32 [32768, 128], P('shard')
- conv_grad: float32 [27, 128, 128], replicated
- down_grad: float32 [8, 128, 256], replicated
Inputs may be any that keep to these rules, and one draw needn't show every extreme that they name: `neighbour_map`: indices into the device's extended fine table: below 1024 a local voxel, 1024 + s*64 + c row c received in slot s, the largest value a missing neighbour. Offset 13 maps every voxel to itself. Rows received in slot s that a map reads are live entries of the sender's list. `halo_rows`: live entries come first in a slot, the rest are 1024; every slot toward a missing device is empty; the slot of offset +1 is full on every device that has a next device. `child_map`: as neighbour_map, for the extended hidden table with 32 rows per slot. `child_rows`: as halo_rows, with 32 rows per slot.
All inputs are finite; a program needn't handle non-finite values.
Results may differ from a plain program's by a relative error of at most 0.006.
Values may be sent and summed in bfloat16 or wider, within the bound.
No kernel may reach another device: no remote copies, remote signals or barrier semaphores. Data moves between devices by JAX's collectives and lax.ppermute only.
A program may use at most 64 MiB of HBM per device.

v0:
```python
import functools
import math

import jax
import jax.numpy as jnp
from jax import lax
from jax.experimental import pallas as pl
from jax.experimental.pallas import tpu as pltpu
from jax.sharding import PartitionSpec as P

BF16 = jnp.bfloat16
F32 = jnp.float32
LANES = 128
RIGHT = 4096


def offsets_list(slot_count):
    half_count = slot_count // 2
    return [number - half_count for number in range(half_count)] + [
        number + 1 for number in range(half_count)
    ]


def shift(value, axis, by):
    count = lax.axis_size(axis)
    pairs = [(i, i + by) for i in range(count) if 0 <= i + by < count]
    return lax.ppermute(value, axis, pairs)


def matmul(left, right):
    return jnp.dot(left, right, preferred_element_type=F32)


def matmul_rt(left, right):
    return lax.dot_general(left, right, (((1,), (1,)), ((), ())), preferred_element_type=F32)


def column(row):
    pieces = []
    for start in range(0, row.shape[1], LANES):
        piece = jnp.broadcast_to(row[:, start : start + LANES], (LANES, LANES))
        pieces.append(jnp.transpose(piece))
    return pieces[0] if len(pieces) == 1 else jnp.concatenate(pieces, axis=0)


def one_hot_rows(col, width):
    blocks = []
    lane = lax.broadcasted_iota(jnp.int32, col.shape, 1)
    for start in range(0, width, LANES):
        blocks.append(jnp.where(col == lane + start, 1.0, 0.0).astype(BF16))
    return jnp.concatenate(blocks, axis=1)


def one_hot_columns(row, height):
    place = lax.broadcasted_iota(jnp.int32, (height, row.shape[1]), 0)
    return jnp.where(place == row, 1.0, 0.0).astype(BF16)


def list_row(lists, first, per_row):
    pieces = [lists[first + n : first + n + 1, :] for n in range(per_row)]
    return pieces[0] if per_row == 1 else jnp.concatenate(pieces, axis=1)


def gather_lists(lists_ref, table):
    slots, cap = lists_ref.shape
    lists = lists_ref[...]
    per_row = max(1, min(slots, LANES // cap))
    parts = []
    for first in range(0, slots, per_row):
        chooser = one_hot_rows(column(list_row(lists, first, per_row)), table.shape[0])
        parts.append(matmul(chooser, table))
    return parts[0] if len(parts) == 1 else jnp.concatenate(parts, axis=0)


def head_kernel(features_ref, halo_ref, child_map_ref, out_grad_ref, down_ref, *outs):
    sends, back_ref = outs[:-1], outs[-1]
    slots, cap = halo_ref.shape
    voxels = features_ref.shape[0]
    octants = child_map_ref.shape[0]
    table_rows = back_ref.shape[0]
    cap2 = (table_rows - voxels) // slots
    listed = gather_lists(halo_ref, features_ref[...]).astype(BF16)
    for s in range(slots):
        sends[s][0:cap, :] = listed[s * cap : (s + 1) * cap, :]
    upstream = out_grad_ref[...]
    total = jnp.zeros((table_rows, LANES), F32)
    child_map = child_map_ref[...]
    for o in range(octants):
        part = matmul_rt(upstream, down_ref[o]).astype(BF16)
        total = total + matmul(one_hot_columns(child_map[o : o + 1, :], table_rows), part)
    back_ref[...] = total
    for s in range(slots):
        slot = slots - 1 - s
        first = voxels + slot * cap2
        sends[s][cap : cap + cap2, :] = total[first : first + cap2, :].astype(BF16)


def forward_kernel(slots, *refs):
    received = refs[:slots]
    (features_ref, map_ref, weight_ref, back_ref, child_ref) = refs[slots : slots + 5]
    (hidden_ref, leaving_ref, hgrad_ref, pgrad_ref, cgrad_ref) = refs[slots + 5 : slots + 10]
    (table_ref, stacked_ref, acc_ref) = refs[slots + 10 :]
    voxels = features_ref.shape[0]
    kernel_count = map_ref.shape[0]
    middle = kernel_count // 2
    cap2 = child_ref.shape[1]
    cap = received[0].shape[0] - cap2
    half, half_halo = voxels // 2, slots * cap // 2
    features = features_ref[...]
    table_ref[0:half, 0:LANES] = features[0:half]
    table_ref[0:half, LANES : 2 * LANES] = features[half:voxels]
    for s in range(slots):
        place = half + (s % (slots // 2)) * cap
        side = (s // (slots // 2)) * LANES
        table_ref[place : place + cap, side : side + LANES] = received[s][0:cap, :]
    table_rows = half + half_halo

    def gather(k):
        row = map_ref[pl.ds(k, 1), :]
        outside = row >= voxels
        beyond = row - voxels
        near_code = row + jnp.where(row >= half, RIGHT - half, 0)
        far_code = half + beyond + jnp.where(beyond >= half_halo, RIGHT - half_halo, 0)
        code = jnp.where(outside, far_code, near_code)
        col = column(code)
        chooser = one_hot_rows(col & (RIGHT - 1), table_rows)
        both = matmul(chooser, table_ref[...])
        picked = jnp.where(col >= RIGHT, both[:, LANES:], both[:, :LANES]).astype(BF16)
        stacked_ref[k] = picked
        return picked

    acc_ref[...] = matmul(features, weight_ref[middle])

    def step(j, carry):
        near, far = gather(j), gather(j + middle + 1)
        pair = jnp.concatenate([near, far], axis=1)
        kernel = jnp.concatenate([weight_ref[j], weight_ref[j + middle + 1]], axis=0)
        acc_ref[...] += matmul(pair, kernel)
        return carry

    lax.fori_loop(0, middle, step, 0)
    pre = acc_ref[...]
    sig = jax.nn.sigmoid(pre)
    hidden = (features.astype(F32) + pre * sig).astype(BF16)
    hidden_ref[...] = hidden
    leaving_ref[...] = gather_lists(child_ref, hidden).astype(BF16)
    hgrad = back_ref[...]
    lists = child_ref[...]
    for s in range(slots):
        returned = received[slots - 1 - s][cap : cap + cap2, :]
        hgrad = hgrad + matmul(one_hot_columns(lists[s : s + 1, :], voxels), returned)
    hgrad_ref[...] = hgrad
    pgrad = hgrad * (sig * (1.0 + pre * (1.0 - sig)))
    pgrad_ref[...] = pgrad.astype(BF16)
    pgrad_t = jnp.transpose(pgrad).astype(BF16)
    rows = kernel_count * LANES
    cgrad_ref[rows:, :] = jnp.zeros((cgrad_ref.shape[0] - rows, LANES), BF16)

    def put(k, value):
        cgrad_ref[pl.ds(pl.multiple_of(k * LANES, LANES), LANES), :] = jnp.transpose(value).astype(BF16)

    put(middle, matmul(pgrad_t, features))

    def weight_step(j, carry):
        pair = jnp.concatenate([stacked_ref[j], stacked_ref[j + middle + 1]], axis=1)
        both = matmul(pgrad_t, pair)
        put(j, both[:, :LANES])
        put(j + middle + 1, both[:, LANES:])
        return carry

    lax.fori_loop(0, middle, weight_step, 0)


def spread_kernel(slots, pgrad_ref, map_ref, weight_ref, back_ref, *sends):
    acc_ref = sends[-1]
    sends = sends[:-1]
    voxels = pgrad_ref.shape[0]
    kernel_count = map_ref.shape[0]
    middle = kernel_count // 2
    cap = sends[0].shape[0]
    table_rows = voxels + slots * cap
    pgrad = pgrad_ref[...]
    acc_ref[0:voxels, :] = matmul_rt(pgrad, weight_ref[middle])
    acc_ref[voxels:, :] = jnp.zeros((table_rows - voxels, LANES), F32)

    def step(j, carry):
        for k in (j, j + middle + 1):
            part = matmul_rt(pgrad, weight_ref[k]).astype(BF16)
            acc_ref[...] += matmul(one_hot_columns(map_ref[pl.ds(k, 1), :], table_rows), part)
        return carry

    lax.fori_loop(0, middle, step, 0)
    back_ref[...] = acc_ref[0:voxels, :]
    for s in range(slots):
        slot = slots - 1 - s
        first = voxels + slot * cap
        sends[s][...] = acc_ref[first : first + cap, :].astype(BF16)


def down_kernel(slots, *refs):
    received = refs[:slots]
    hidden_ref, map_ref, down_ref, out_grad_ref, coarse_ref, dgrad_ref = refs[slots:]
    table = jnp.concatenate([hidden_ref[...]] + [r[...] for r in received], axis=0)
    upstream = out_grad_ref[...]
    parents = upstream.shape[0]
    channels = down_ref.shape[1]
    upstream_t = jnp.transpose(upstream.astype(F32)).astype(BF16)
    total = jnp.zeros((parents, down_ref.shape[2]), F32)
    child_map = map_ref[...]
    for o in range(map_ref.shape[0]):
        chooser = one_hot_rows(column(child_map[o : o + 1, :]), table.shape[0])
        picked = matmul(chooser, table).astype(BF16)
        total = total + matmul(picked, down_ref[o])
        terms = matmul(upstream_t, picked)
        dgrad_ref[o * channels : (o + 1) * channels, :] = jnp.transpose(terms).astype(BF16)
    coarse_ref[...] = total.astype(BF16)


def tail_kernel(slots, *refs):
    received = refs[:slots]
    hgrad_ref, back_ref, halo_ref, out_ref = refs[slots:]
    voxels = hgrad_ref.shape[0]
    total = hgrad_ref[...] + back_ref[...]
    lists = halo_ref[...]
    for s in range(slots):
        chooser = one_hot_columns(lists[s : s + 1, :], voxels)
        total = total + matmul(chooser, received[slots - 1 - s][...])
    out_ref[...] = total


def vmem():
    return pl.BlockSpec(memory_space=pltpu.VMEM)


def call(kernel, operands, outs, scratch=(), limit=32, flops=0):
    return pl.pallas_call(
        kernel,
        out_shape=[jax.ShapeDtypeStruct(s, d) for s, d in outs],
        in_specs=[vmem() for _ in operands],
        out_specs=[vmem() for _ in outs],
        scratch_shapes=list(scratch),
        compiler_params=pltpu.CompilerParams(vmem_limit_bytes=limit * 2**20),
        cost_estimate=pl.CostEstimate(flops=flops, bytes_accessed=4 * 2**20, transcendentals=0),
    )(*operands)


def reduce_all(terms, scale, devices):
    rows, width = terms.shape
    parts = lax.all_to_all(terms, "shard", 0, 0, tiled=True)
    mine = jnp.sum(parts.reshape(devices, rows // devices, width).astype(F32), axis=0) * scale
    return lax.all_gather(mine.astype(BF16), "shard", axis=0, tiled=True)


def local(
    features, conv_weight, down_weight, neighbour_map, halo_rows, child_map, child_rows, out_grad
):
    voxels, channels = features.shape
    parents, coarse_channels = out_grad.shape
    kernel_count = conv_weight.shape[0]
    octants = down_weight.shape[0]
    slots, cap = halo_rows.shape
    cap2 = child_rows.shape[1]
    offsets = offsets_list(slots)
    devices = lax.axis_size("shard")
    scale = 1.0 / math.sqrt(voxels * devices)
    giga = 10**9

    first = call(
        head_kernel,
        (features, halo_rows, child_map, out_grad, down_weight),
        [((cap + cap2, channels), BF16)] * slots + [((voxels + slots * cap2, channels), F32)],
        flops=giga,
    )
    back_h = first[-1][:voxels]
    received = [shift(first[s], "shard", offsets[s]) for s in range(slots)]
    grain = 16 * devices
    grad_rows = -(-kernel_count * channels // grain) * grain
    hidden, leaving, hidden_grad, pre_grad, conv_terms = call(
        functools.partial(forward_kernel, slots),
        (*received, features, neighbour_map, conv_weight, back_h, child_rows),
        [
            ((voxels, channels), BF16),
            ((slots * cap2, channels), BF16),
            ((voxels, channels), F32),
            ((voxels, channels), BF16),
            ((grad_rows, channels), BF16),
        ],
        scratch=[
            pltpu.VMEM((voxels // 2 + slots * cap // 2, 2 * channels), BF16),
            pltpu.VMEM((kernel_count, voxels, channels), BF16),
            pltpu.VMEM((voxels, channels), F32),
        ],
        limit=48,
        flops=12 * giga,
    )
    received_h = [
        shift(leaving[s * cap2 : (s + 1) * cap2], "shard", offsets[s]) for s in range(slots)
    ]
    coarse, down_terms = call(
        functools.partial(down_kernel, slots),
        (*received_h, hidden, child_map, down_weight, out_grad),
        [
            ((parents, coarse_channels), BF16),
            ((octants * channels, coarse_channels), BF16),
        ],
        flops=2 * giga,
    )
    spread = call(
        functools.partial(spread_kernel, slots),
        (pre_grad, neighbour_map, conv_weight),
        [((voxels, channels), F32)] + [((cap, channels), BF16)] * slots,
        scratch=[pltpu.VMEM((voxels + slots * cap, channels), F32)],
        flops=20 * giga,
    )
    returned = [shift(spread[1 + s], "shard", offsets[s]) for s in range(slots)]
    (input_grad,) = call(
        functools.partial(tail_kernel, slots),
        (*returned, hidden_grad, spread[0], halo_rows),
        [((voxels, channels), F32)],
        flops=giga,
    )
    conv_sum = reduce_all(conv_terms, scale, devices)
    down_sum = reduce_all(down_terms, scale, devices)
    conv_grad = conv_sum[: kernel_count * channels].astype(F32).reshape(conv_weight.shape)
    down_grad = down_sum.astype(F32).reshape(down_weight.shape)
    return (coarse, input_grad, conv_grad, down_grad)


def solution(mesh):
    return jax.shard_map(
        local,
        mesh=mesh,
        in_specs=(
            P("shard", None),
            P(),
            P(),
            P(None, "shard"),
            P(None, "shard"),
            P(None, "shard"),
            P(None, "shard"),
            P("shard", None),
        ),
        out_specs=(P("shard", None), P("shard", None), P(), P()),
        check_vma=False,
    )
```

profile of v0, /device:TPU:1, one launch (start us, length us, event | category | flops | bytes accessed | tf_op | source)
XLA Modules:
  0.0 228.8 jit_solution(12263354432482144815)
XLA Ops:
  0.6 0.0 copy-start
  0.6 0.0 copy-start.1
  0.7 1.1 copy-done.1
  1.8 0.0 copy-start.3
  1.8 0.9 copy-done.3
  2.7 0.0 copy-start.5
  2.7 0.9 copy-done.5
  3.6 0.0 copy-start.8
  3.6 0.7 copy-done.8
  4.3 0.0 copy-start.11
  4.3 0.7 copy-done.11
  5.0 0.0 copy-start.4
  5.0 0.0 copy-start.7
  5.0 3.4 %shard_map.111 = (bf16[96,128]{1,0:T(8,128)(2,1)S(1)}, bf16[96,128]{1,0:T(8,128)(2,1)S(1)}, bf16[96,128]{1,0:T(8,128)(2,1)S(1)}, bf16[96,128]{1,0:T(8,128)(2,1)S(1)}, f32[1152,128]{1,0:T(8,128)S(1)}) custom-call(bf16[1024,128]{1,0:T(8,128)(2,1)S(1)} %copy-done.3, s32[4,64]{1,0:T(4,128)S(1)} %copy-done.11, s32[8,256]{1,0:T(8,128)S(1)} %copy-done.8, ...), custom_call_target="tpu_custom_call" | custom-call | flops 1000000000 | bytes 4194304 | tf_op jit(solution)/shard_map/pallas_call | solution.py:236
  8.5 1.3 collective-permute-start
  9.8 2.0 collective-permute-start.1
  11.7 5.1 %collective-permute-start.2 = (bf16[96,128]{1,0:T(8,128)(2,1)S(1)}, bf16[96,128]{1,0:T(8,128)(2,1)S(1)}, u32[]{:S(2)}, u32[]{:S(2)}) collective-permute-start(bf16[96,128]{1,0:T(8,128)(2,1)S(1)} %get-tuple-element.23), channel_id=1, source_target_pairs={{0,1},{1,2},{2,3},{3,4},{4,5},{5,6},{6,7},{7,8},{8,9},{9,10},{10,1... | collective-permute-start | bytes 73736 | tf_op jit(solution)/shard_map/ppermute | solution.py:27
  16.8 4.5 %collective-permute-start.3 = (bf16[96,128]{1,0:T(8,128)(2,1)S(1)}, bf16[96,128]{1,0:T(8,128)(2,1)S(1)}, u32[]{:S(2)}, u32[]{:S(2)}) collective-permute-start(bf16[96,128]{1,0:T(8,128)(2,1)S(1)} %get-tuple-element.24), channel_id=1, source_target_pairs={{0,2},{1,3},{2,4},{3,5},{4,6},{5,7},{6,8},{7,9},{8,10},{9,11},{10,... | collective-permute-start | bytes 73736 | tf_op jit(solution)/shard_map/ppermute | solution.py:27
  21.4 0.0 copy-start.2
  21.4 0.0 copy-start.6
  21.4 0.0 copy-start.9
  21.5 0.0 collective-permute-done.refs_0_
  21.5 0.0 collective-permute-done.1.refs_1_
  21.5 0.0 collective-permute-done.2.refs_2_
  21.5 0.8 collective-permute-done.3.refs_3_
  22.3 0.0 copy-done
  22.3 0.0 copy-done.4
  22.3 0.0 copy-done.7
  22.3 0.0 copy-done.10
  22.3 23.4 %shard_map.112 = (bf16[1024,128]{1,0:T(8,128)(2,1)S(1)}, bf16[128,128]{1,0:T(8,128)(2,1)S(1)}, f32[1024,128]{1,0:T(8,128)S(1)}, bf16[1024,128]{1,0:T(8,128)(2,1)S(1)}, bf16[3584,128]{1,0:T(8,128)(2,1)}) custom-call(bf16[96,128]{1,0:T(8,128)(2,1)S(1)} %collective-permute-done.refs_0_, bf16[96,128]{1,0:T(8,128)(2,1)S(1)} %collective-permute-done.1.refs_1_, ...), custom_call_target="tpu_custom_call" | custom-call | flops 12000000000 | bytes 4194304 | tf_op jit(solution)/shard_map/pallas_call | solution.py:236
  45.7 1.3 collective-permute-start.4
  47.0 1.9 collective-permute-start.5
  49.0 3.9 %collective-permute-start.6 = (bf16[32,128]{1,0:T(8,128)(2,1)S(1)}, bf16[32,128]{1,0:T(8,128)(2,1)S(1)}, u32[]{:S(2)}, u32[]{:S(2)}) collective-permute-start(bf16[32,128]{1,0:T(8,128)(2,1)S(1)} %get-tuple-element.39), channel_id=1, source_target_pairs={{0,1},{1,2},{2,3},{3,4},{4,5},{5,6},{6,7},{7,8},{8,9},{9,10},{10,1... | collective-permute-start | bytes 24584 | tf_op jit(solution)/shard_map/ppermute | solution.py:27
  52.9 4.9 %collective-permute-start.7 = (bf16[32,128]{1,0:T(8,128)(2,1)S(1)}, bf16[32,128]{1,0:T(8,128)(2,1)S(1)}, u32[]{:S(2)}, u32[]{:S(2)}) collective-permute-start(bf16[32,128]{1,0:T(8,128)(2,1)S(1)} %get-tuple-element.38), channel_id=1, source_target_pairs={{0,2},{1,3},{2,4},{3,5},{4,6},{5,7},{6,8},{7,9},{8,10},{9,11},{10,... | collective-permute-start | bytes 24584 | tf_op jit(solution)/shard_map/ppermute | solution.py:27
  57.8 0.0 collective-permute-done.4.refs_0_
  57.8 0.0 collective-permute-done.5.refs_1_
  57.8 0.0 collective-permute-done.6.refs_2_
  57.8 0.7 collective-permute-done.7.refs_3_
  58.6 0.0 copy-done.2
  58.6 0.0 copy-done.6
  58.6 0.0 copy-done.9
  58.6 3.7 %shard_map.113 = (bf16[256,256]{1,0:T(8,128)(2,1)}, bf16[1024,256]{1,0:T(8,128)(2,1)S(1)}) custom-call(bf16[32,128]{1,0:T(8,128)(2,1)S(1)} %collective-permute-done.4.refs_0_, bf16[32,128]{1,0:T(8,128)(2,1)S(1)} %collective-permute-done.5.refs_1_, bf16[32,128]{1,0:T(8,128)(2,1)S(1)} %collective-permute-done.6.refs_2_, ...), custom_call_target="tpu_custom_call" | custom-call | flops 2000000000 | bytes 4194304 | tf_op jit(solution)/shard_map/pallas_call | solution.py:236
  62.3 24.1 %all_to_all.18 = bf16[32,32,256]{2,1,0:T(8,128)(2,1)S(1)} all-to-all(bf16[32,32,256]{2,1,0:T(8,128)(2,1)S(1)} %bitcast.6), channel_id=1, replica_groups=mesh['shard'=32] {'shard'}, dimensions={0} | all-to-all | bytes 1048576 | tf_op jit(solution)/shard_map/all_to_all | solution.py:249
  86.4 3.4 %all-to-all-start = ((bf16[32,112,128]{2,1,0:T(8,128)(2,1)}), bf16[32,112,128]{2,1,0:T(8,128)(2,1)S(1)}, u32[]{:S(2)}, u32[]{:S(2)}) async-start(bf16[32,112,128]{2,1,0:T(8,128)(2,1)} %bitcast), calls=%async_computation | async-start | bytes 1835008 | tf_op jit(solution)/shard_map/all_to_all | solution.py:249
  89.9 0.0 copy-start.12
  89.9 39.6 %shard_map.114 = (f32[1024,128]{1,0:T(8,128)S(1)}, bf16[64,128]{1,0:T(8,128)(2,1)S(1)}, bf16[64,128]{1,0:T(8,128)(2,1)S(1)}, bf16[64,128]{1,0:T(8,128)(2,1)S(1)}, bf16[64,128]{1,0:T(8,128)(2,1)S(1)}) custom-call(bf16[1024,128]{1,0:T(8,128)(2,1)S(1)} %get-tuple-element.29.pgrad_ref, s32[27,1024]{1,0:T(8,128)S(1)} %copy-done.7, bf16[27,128,128]{2,1,0:T(8,128)(2,1)S(1)} %copy-done), custom_call_target="tpu_custom_call" | custom-call | flops 20000000000 | bytes 4194304 | tf_op jit(solution)/shard_map/pallas_call | solution.py:236
  129.5 1.3 collective-permute-start.8
  130.8 2.2 collective-permute-start.9
  133.0 4.2 %collective-permute-start.10 = (bf16[64,128]{1,0:T(8,128)(2,1)S(1)}, bf16[64,128]{1,0:T(8,128)(2,1)S(1)}, u32[]{:S(2)}, u32[]{:S(2)}) collective-permute-start(bf16[64,128]{1,0:T(8,128)(2,1)S(1)} %get-tuple-element.32), channel_id=1, source_target_pairs={{0,1},{1,2},{2,3},{3,4},{4,5},{5,6},{6,7},{7,8},{8,9},{9,10},{10,1... | collective-permute-start | bytes 49160 | tf_op jit(solution)/shard_map/ppermute | solution.py:27
  137.1 4.3 %collective-permute-start.11 = (bf16[64,128]{1,0:T(8,128)(2,1)S(1)}, bf16[64,128]{1,0:T(8,128)(2,1)S(1)}, u32[]{:S(2)}, u32[]{:S(2)}) collective-permute-start(bf16[64,128]{1,0:T(8,128)(2,1)S(1)} %get-tuple-element.33), channel_id=1, source_target_pairs={{0,2},{1,3},{2,4},{3,5},{4,6},{5,7},{6,8},{7,9},{8,10},{9,11},{10,... | collective-permute-start | bytes 49160 | tf_op jit(solution)/shard_map/ppermute | solution.py:27
  141.4 0.0 collective-permute-done.8.refs_0_
  141.5 0.0 collective-permute-done.9.refs_1_
  141.5 0.0 collective-permute-done.10.refs_2_
  141.5 0.8 collective-permute-done.11.refs_3_
  142.3 0.0 copy-done.12
  142.3 1.2 shard_map.115
  143.5 0.1 convert_reduce_fusion.1
  143.6 43.4 %all_gather.7 = bf16[1024,256]{1,0:T(8,128)(2,1)S(1)} all-gather(bf16[32,256]{1,0:T(8,128)(2,1)S(1)} %multiply_convert_fusion.1), channel_id=1, replica_groups=mesh['shard'=32] {'shard'}, dimensions={0}, use_global_device_ids=true | all-gather | bytes 540672 | tf_op jit(solution)/shard_map/all_gather | solution.py:251
  187.0 1.1 convert.3
  188.0 0.0 all-to-all-done
  188.0 0.1 convert_reduce_fusion
  188.2 39.2 %all_gather.6 = bf16[3584,128]{1,0:T(8,128)(2,1)S(1)} all-gather(bf16[112,128]{1,0:T(8,128)(2,1)S(1)} %multiply_convert_fusion), channel_id=1, replica_groups=mesh['shard'=32] {'shard'}, dimensions={0}, use_global_device_ids=true | all-gather | bytes 946176 | tf_op jit(solution)/shard_map/all_gather | solution.py:251
  227.3 0.1 slice.24
  227.4 1.4 convert.2
  (5 shorter events, 0.1 us)
Async XLA Ops:
  0.6 21.7 %copy-start = (bf16[27,128,128]{2,1,0:T(8,128)(2,1)S(1)}, bf16[27,128,128]{2,1,0:T(8,128)(2,1)}, u32[]{:S(2)}) copy-start(bf16[27,128,128]{2,1,0:T(8,128)(2,1)} %weight_ref.1) | copy-start | bytes 2654212
  0.6 1.1 copy-start.1
  1.8 0.9 copy-start.3
  2.7 0.9 copy-start.5
  3.6 0.7 copy-start.8
  4.3 0.7 copy-start.11
  5.0 17.3 %copy-start.4 = (bf16[1024,128]{1,0:T(8,128)(2,1)S(1)}, bf16[1024,128]{1,0:T(8,128)(2,1)}, u32[]{:S(2)}) copy-start(bf16[1024,128]{1,0:T(8,128)(2,1)} %refs_4_.1) | copy-start | bytes 786436
  5.0 17.3 %copy-start.7 = (s32[27,1024]{1,0:T(8,128)S(1)}, s32[27,1024]{1,0:T(8,128)}, u32[]{:S(2)}) copy-start(s32[27,1024]{1,0:T(8,128)} %map_ref.1) | copy-start | bytes 331780
  5.0 17.3 %copy-start.10 = (s32[4,32]{1,0:T(4,128)S(1)}, s32[4,32]{1,0:T(4,128)}, u32[]{:S(2)}) copy-start(s32[4,32]{1,0:T(4,128)} %refs_8_.1) | copy-start | bytes 1540
  8.5 13.0 %collective-permute-start = (bf16[96,128]{1,0:T(8,128)(2,1)S(1)}, bf16[96,128]{1,0:T(8,128)(2,1)S(1)}, u32[]{:S(2)}, u32[]{:S(2)}) collective-permute-start(bf16[96,128]{1,0:T(8,128)(2,1)S(1)} %get-tuple-element.21), channel_id=1, source_target_pairs={{2,0},{3,1},{4,2},{5,3},{6,4},{7,5},{8,6},{9,7},{10,8},{11,9},{12,... | collective-permute-start | bytes 73736 | tf_op jit(solution)/shard_map/ppermute | solution.py:27
  9.8 11.7 %collective-permute-start.1 = (bf16[96,128]{1,0:T(8,128)(2,1)S(1)}, bf16[96,128]{1,0:T(8,128)(2,1)S(1)}, u32[]{:S(2)}, u32[]{:S(2)}) collective-permute-start(bf16[96,128]{1,0:T(8,128)(2,1)S(1)} %get-tuple-element.22), channel_id=1, source_target_pairs={{1,0},{2,1},{3,2},{4,3},{5,4},{6,5},{7,6},{8,7},{9,8},{10,9},{11,1... | collective-permute-start | bytes 73736 | tf_op jit(solution)/shard_map/ppermute | solution.py:27
  11.7 9.7 %collective-permute-start.2 = (bf16[96,128]{1,0:T(8,128)(2,1)S(1)}, bf16[96,128]{1,0:T(8,128)(2,1)S(1)}, u32[]{:S(2)}, u32[]{:S(2)}) collective-permute-start(bf16[96,128]{1,0:T(8,128)(2,1)S(1)} %get-tuple-element.23), channel_id=1, source_target_pairs={{0,1},{1,2},{2,3},{3,4},{4,5},{5,6},{6,7},{7,8},{8,9},{9,10},{10,1... | collective-permute-start | bytes 73736 | tf_op jit(solution)/shard_map/ppermute | solution.py:27
  16.8 5.5 %collective-permute-start.3 = (bf16[96,128]{1,0:T(8,128)(2,1)S(1)}, bf16[96,128]{1,0:T(8,128)(2,1)S(1)}, u32[]{:S(2)}, u32[]{:S(2)}) collective-permute-start(bf16[96,128]{1,0:T(8,128)(2,1)S(1)} %get-tuple-element.24), channel_id=1, source_target_pairs={{0,2},{1,3},{2,4},{3,5},{4,6},{5,7},{6,8},{7,9},{8,10},{9,11},{10,... | collective-permute-start | bytes 73736 | tf_op jit(solution)/shard_map/ppermute | solution.py:27
  21.4 37.2 %copy-start.2 = (bf16[8,128,256]{2,1,0:T(8,128)(2,1)S(1)}, bf16[8,128,256]{2,1,0:T(8,128)(2,1)}, u32[]{:S(2)}) copy-start(bf16[8,128,256]{2,1,0:T(8,128)(2,1)} %refs_6_.4) | copy-start | bytes 1572868
  21.4 37.1 %copy-start.6 = (bf16[256,256]{1,0:T(8,128)(2,1)S(1)}, bf16[256,256]{1,0:T(8,128)(2,1)}, u32[]{:S(2)}) copy-start(bf16[256,256]{1,0:T(8,128)(2,1)} %refs_7_.1) | copy-start | bytes 393220
  21.4 37.1 %copy-start.9 = (s32[8,256]{1,0:T(8,128)S(1)}, s32[8,256]{1,0:T(8,128)}, u32[]{:S(2)}) copy-start(s32[8,256]{1,0:T(8,128)} %refs_5_.3) | copy-start | bytes 24580
  45.7 12.1 %collective-permute-start.4 = (bf16[32,128]{1,0:T(8,128)(2,1)S(1)}, bf16[32,128]{1,0:T(8,128)(2,1)S(1)}, u32[]{:S(2)}, u32[]{:S(2)}) collective-permute-start(bf16[32,128]{1,0:T(8,128)(2,1)S(1)} %get-tuple-element.41), channel_id=1, source_target_pairs={{2,0},{3,1},{4,2},{5,3},{6,4},{7,5},{8,6},{9,7},{10,8},{11,9},{12,... | collective-permute-start | bytes 24584 | tf_op jit(solution)/shard_map/ppermute | solution.py:27
  47.0 10.8 %collective-permute-start.5 = (bf16[32,128]{1,0:T(8,128)(2,1)S(1)}, bf16[32,128]{1,0:T(8,128)(2,1)S(1)}, u32[]{:S(2)}, u32[]{:S(2)}) collective-permute-start(bf16[32,128]{1,0:T(8,128)(2,1)S(1)} %get-tuple-element.40), channel_id=1, source_target_pairs={{1,0},{2,1},{3,2},{4,3},{5,4},{6,5},{7,6},{8,7},{9,8},{10,9},{11,1... | collective-permute-start | bytes 24584 | tf_op jit(solution)/shard_map/ppermute | solution.py:27
  49.0 8.9 %collective-permute-start.6 = (bf16[32,128]{1,0:T(8,128)(2,1)S(1)}, bf16[32,128]{1,0:T(8,128)(2,1)S(1)}, u32[]{:S(2)}, u32[]{:S(2)}) collective-permute-start(bf16[32,128]{1,0:T(8,128)(2,1)S(1)} %get-tuple-element.39), channel_id=1, source_target_pairs={{0,1},{1,2},{2,3},{3,4},{4,5},{5,6},{6,7},{7,8},{8,9},{9,10},{10,1... | collective-permute-start | bytes 24584 | tf_op jit(solution)/shard_map/ppermute | solution.py:27
  52.9 5.7 %collective-permute-start.7 = (bf16[32,128]{1,0:T(8,128)(2,1)S(1)}, bf16[32,128]{1,0:T(8,128)(2,1)S(1)}, u32[]{:S(2)}, u32[]{:S(2)}) collective-permute-start(bf16[32,128]{1,0:T(8,128)(2,1)S(1)} %get-tuple-element.38), channel_id=1, source_target_pairs={{0,2},{1,3},{2,4},{3,5},{4,6},{5,7},{6,8},{7,9},{8,10},{9,11},{10,... | collective-permute-start | bytes 24584 | tf_op jit(solution)/shard_map/ppermute | solution.py:27
  86.4 101.6 %all-to-all-start = ((bf16[32,112,128]{2,1,0:T(8,128)(2,1)}), bf16[32,112,128]{2,1,0:T(8,128)(2,1)S(1)}, u32[]{:S(2)}, u32[]{:S(2)}) async-start(bf16[32,112,128]{2,1,0:T(8,128)(2,1)} %bitcast), calls=%async_computation | async-start | bytes 1835008 | tf_op jit(solution)/shard_map/all_to_all | solution.py:249
  89.9 52.4 %copy-start.12 = (s32[4,64]{1,0:T(4,128)S(1)}, s32[4,64]{1,0:T(4,128)}, u32[]{:S(2)}) copy-start(s32[4,64]{1,0:T(4,128)} %refs_6_.5) | copy-start | bytes 3076
  129.5 11.9 %collective-permute-start.8 = (bf16[64,128]{1,0:T(8,128)(2,1)S(1)}, bf16[64,128]{1,0:T(8,128)(2,1)S(1)}, u32[]{:S(2)}, u32[]{:S(2)}) collective-permute-start(bf16[64,128]{1,0:T(8,128)(2,1)S(1)} %get-tuple-element.30), channel_id=1, source_target_pairs={{2,0},{3,1},{4,2},{5,3},{6,4},{7,5},{8,6},{9,7},{10,8},{11,9},{12,... | collective-permute-start | bytes 49160 | tf_op jit(solution)/shard_map/ppermute | solution.py:27
  130.8 10.7 %collective-permute-start.9 = (bf16[64,128]{1,0:T(8,128)(2,1)S(1)}, bf16[64,128]{1,0:T(8,128)(2,1)S(1)}, u32[]{:S(2)}, u32[]{:S(2)}) collective-permute-start(bf16[64,128]{1,0:T(8,128)(2,1)S(1)} %get-tuple-element.31), channel_id=1, source_target_pairs={{1,0},{2,1},{3,2},{4,3},{5,4},{6,5},{7,6},{8,7},{9,8},{10,9},{11,1... | collective-permute-start | bytes 49160 | tf_op jit(solution)/shard_map/ppermute | solution.py:27
  133.0 8.5 %collective-permute-start.10 = (bf16[64,128]{1,0:T(8,128)(2,1)S(1)}, bf16[64,128]{1,0:T(8,128)(2,1)S(1)}, u32[]{:S(2)}, u32[]{:S(2)}) collective-permute-start(bf16[64,128]{1,0:T(8,128)(2,1)S(1)} %get-tuple-element.32), channel_id=1, source_target_pairs={{0,1},{1,2},{2,3},{3,4},{4,5},{5,6},{6,7},{7,8},{8,9},{9,10},{10,1... | collective-permute-start | bytes 49160 | tf_op jit(solution)/shard_map/ppermute | solution.py:27
  137.1 5.2 %collective-permute-start.11 = (bf16[64,128]{1,0:T(8,128)(2,1)S(1)}, bf16[64,128]{1,0:T(8,128)(2,1)S(1)}, u32[]{:S(2)}, u32[]{:S(2)}) collective-permute-start(bf16[64,128]{1,0:T(8,128)(2,1)S(1)} %get-tuple-element.33), channel_id=1, source_target_pairs={{0,2},{1,3},{2,4},{3,5},{4,6},{5,7},{6,8},{7,9},{8,10},{9,11},{10,... | collective-permute-start | bytes 49160 | tf_op jit(solution)/shard_map/ppermute | solution.py:27
where the time goes:
time: 230 us; the launch traced here: 229 us
  blocking collectives  107 us (47%)
  Pallas kernels  71.4 us (31%)
  starting transfers between devices  40.2 us (17%)
  local copies, waits for them, and re-layouts  4.48 us (2%)
  other arithmetic  2.7 us (1%)
  waiting for transfers between devices  2.41 us (1%)
    all_gather x2, blocking collectives, reduce_all(): return lax.all_gather(mine.astype(BF16), 'shard', axis=0, tiled=True)  82.5 us
    pallas_call x5, Pallas kernels, call(): pl.pallas_call(kernel, out_shape=[jax.ShapeDtypeStruct(s, d) for s, d in...  71.4 us
    ppermute x12, starting transfers between devices, shift(): return lax.ppermute(value, axis, pairs)  36.8 us
    all_to_all x1, blocking collectives, reduce_all(): parts = lax.all_to_all(terms, 'shard', 0, 0, tiled=True)  24.1 us
  transfers between devices with their start and end apart: 13, of which 3 were waited for; matrix products, arithmetic and copies ran while one was open for 1% of the time, Pallas kernels for 18%

commit v1 on v0

--- a/solution.py
+++ b/solution.py
@@ -11,7 +11,6 @@
 BF16 = jnp.bfloat16
 F32 = jnp.float32
 LANES = 128
-RIGHT = 4096
 
 
 def offsets_list(slot_count):
@@ -35,25 +34,35 @@
     return lax.dot_general(left, right, (((1,), (1,)), ((), ())), preferred_element_type=F32)
 
 
-def column(row):
+def pick_one(mask):
+    return jnp.where(mask, jnp.ones(mask.shape, BF16), jnp.zeros(mask.shape, BF16))
+
+
+def encode(row):
+    return jnp.left_shift((row & (LANES - 1)) + LANES, row >> 7).astype(F32)
+
+
+def column(codes):
     pieces = []
-    for start in range(0, row.shape[1], LANES):
-        piece = jnp.broadcast_to(row[:, start : start + LANES], (LANES, LANES))
+    for start in range(0, codes.shape[1], LANES):
+        piece = jnp.broadcast_to(codes[:, start : start + LANES], (LANES, LANES))
         pieces.append(jnp.transpose(piece))
     return pieces[0] if len(pieces) == 1 else jnp.concatenate(pieces, axis=0)
 
 
 def one_hot_rows(col, width):
+    lane = lax.broadcasted_iota(jnp.int32, (16, LANES), 1)
     blocks = []
-    lane = lax.broadcasted_iota(jnp.int32, col.shape, 1)
     for start in range(0, width, LANES):
-        blocks.append(jnp.where(col == lane + start, 1.0, 0.0).astype(BF16))
+        pattern = jnp.broadcast_to(encode(lane + start).astype(BF16)[0:1], col.shape)
+        blocks.append(pick_one(col == pattern))
     return jnp.concatenate(blocks, axis=1)
 
 
-def one_hot_columns(row, height):
-    place = lax.broadcasted_iota(jnp.int32, (height, row.shape[1]), 0)
-    return jnp.where(place == row, 1.0, 0.0).astype(BF16)
+def one_hot_columns(codes, height):
+    place = lax.broadcasted_iota(jnp.int32, (height, codes.shape[1]), 0)
+    pattern = encode(place).astype(BF16)
+    return pick_one(jnp.broadcast_to(codes, pattern.shape) == pattern)
 
 
 def list_row(lists, first, per_row):
@@ -67,7 +76,8 @@
     per_row = max(1, min(slots, LANES // cap))
     parts = []
     for first in range(0, slots, per_row):
-        chooser = one_hot_rows(column(list_row(lists, first, per_row)), table.shape[0])
+        codes = encode(list_row(lists, first, per_row))
+        chooser = one_hot_rows(column(codes).astype(BF16), table.shape[0])
         parts.append(matmul(chooser, table))
     return parts[0] if len(parts) == 1 else jnp.concatenate(parts, axis=0)
 
@@ -84,15 +94,27 @@
         sends[s][0:cap, :] = listed[s * cap : (s + 1) * cap, :]
     upstream = out_grad_ref[...]
     total = jnp.zeros((table_rows, LANES), F32)
-    child_map = child_map_ref[...]
+    codes = encode(child_map_ref[...]).astype(BF16)
     for o in range(octants):
         part = matmul_rt(upstream, down_ref[o]).astype(BF16)
-        total = total + matmul(one_hot_columns(child_map[o : o + 1, :], table_rows), part)
+        total = total + matmul(one_hot_columns(codes[o : o + 1, :], table_rows), part)
     back_ref[...] = total
     for s in range(slots):
         slot = slots - 1 - s
         first = voxels + slot * cap2
         sends[s][cap : cap + cap2, :] = total[first : first + cap2, :].astype(BF16)
+
+
+def half_codes(row, voxels, received):
+    half, half_received = voxels // 2, received // 2
+    beyond = row - voxels
+    outside = beyond >= 0
+    near = row - jnp.where(row >= half, half, 0)
+    far = half + beyond - jnp.where(beyond >= half_received, half_received, 0)
+    code = encode(jnp.where(outside, far, near))
+    near_sign = jnp.where(row >= half, -1.0, 1.0)
+    far_sign = jnp.where(beyond >= half_received, -1.0, 1.0)
+    return code * jnp.where(outside, far_sign, near_sign)
 
 
 def forward_kernel(slots, *refs):
@@ -116,16 +138,10 @@
     table_rows = half + half_halo
 
     def gather(k):
-        row = map_ref[pl.ds(k, 1), :]
-        outside = row >= voxels
-        beyond = row - voxels
-        near_code = row + jnp.where(row >= half, RIGHT - half, 0)
-        far_code = half + beyond + jnp.where(beyond >= half_halo, RIGHT - half_halo, 0)
-        code = jnp.where(outside, far_code, near_code)
-        col = column(code)
-        chooser = one_hot_rows(col & (RIGHT - 1), table_rows)
+        col = column(half_codes(map_ref[pl.ds(k, 1), :], voxels, slots * cap))
+        chooser = one_hot_rows(jnp.abs(col).astype(BF16), table_rows)
         both = matmul(chooser, table_ref[...])
-        picked = jnp.where(col >= RIGHT, both[:, LANES:], both[:, :LANES]).astype(BF16)
+        picked = jnp.where(col < 0.0, both[:, LANES:], both[:, :LANES]).astype(BF16)
         stacked_ref[k] = picked
         return picked
 
@@ -145,7 +161,7 @@
     hidden_ref[...] = hidden
     leaving_ref[...] = gather_lists(child_ref, hidden).astype(BF16)
     hgrad = back_ref[...]
-    lists = child_ref[...]
+    lists = encode(child_ref[...]).astype(BF16)
     for s in range(slots):
         returned = received[slots - 1 - s][cap : cap + cap2, :]
         hgrad = hgrad + matmul(one_hot_columns(lists[s : s + 1, :], voxels), returned)
@@ -178,23 +194,36 @@
     kernel_count = map_ref.shape[0]
     middle = kernel_count // 2
     cap = sends[0].shape[0]
-    table_rows = voxels + slots * cap
+    half = voxels // 2
+    table_rows = half + slots * cap // 2
     pgrad = pgrad_ref[...]
-    acc_ref[0:voxels, :] = matmul_rt(pgrad, weight_ref[middle])
-    acc_ref[voxels:, :] = jnp.zeros((table_rows - voxels, LANES), F32)
+    own = matmul_rt(pgrad, weight_ref[middle])
+    acc_ref[0:half, 0:LANES] = own[0:half]
+    acc_ref[0:half, LANES:] = own[half:]
+    acc_ref[half:, :] = jnp.zeros((table_rows - half, 2 * LANES), F32)
+
+    def parts(k):
+        codes = half_codes(map_ref[pl.ds(k, 1), :], voxels, slots * cap)
+        terms = matmul_rt(pgrad, weight_ref[k])
+        right = column(codes) < 0.0
+        sides = [jnp.where(right, 0.0, terms), jnp.where(right, terms, 0.0)]
+        chooser = one_hot_columns(jnp.abs(codes).astype(BF16), table_rows)
+        return chooser, jnp.concatenate(sides, axis=1).astype(BF16)
 
     def step(j, carry):
-        for k in (j, j + middle + 1):
-            part = matmul_rt(pgrad, weight_ref[k]).astype(BF16)
-            acc_ref[...] += matmul(one_hot_columns(map_ref[pl.ds(k, 1), :], table_rows), part)
+        near_chooser, near_terms = parts(j)
+        far_chooser, far_terms = parts(j + middle + 1)
+        acc_ref[...] += matmul(near_chooser, near_terms) + matmul(far_chooser, far_terms)
         return carry
 
     lax.fori_loop(0, middle, step, 0)
-    back_ref[...] = acc_ref[0:voxels, :]
+    back_ref[0:half, :] = acc_ref[0:half, 0:LANES]
+    back_ref[half:, :] = acc_ref[0:half, LANES:]
     for s in range(slots):
         slot = slots - 1 - s
-        first = voxels + slot * cap
-        sends[s][...] = acc_ref[first : first + cap, :].astype(BF16)
+        first = half + (slot % (slots // 2)) * cap
+        side = (slot // (slots // 2)) * LANES
+        sends[s][...] = acc_ref[first : first + cap, side : side + LANES].astype(BF16)
 
 
 def down_kernel(slots, *refs):
@@ -206,9 +235,9 @@
     channels = down_ref.shape[1]
     upstream_t = jnp.transpose(upstream.astype(F32)).astype(BF16)
     total = jnp.zeros((parents, down_ref.shape[2]), F32)
-    child_map = map_ref[...]
+    codes = encode(map_ref[...])
     for o in range(map_ref.shape[0]):
-        chooser = one_hot_rows(column(child_map[o : o + 1, :]), table.shape[0])
+        chooser = one_hot_rows(column(codes[o : o + 1, :]).astype(BF16), table.shape[0])
         picked = matmul(chooser, table).astype(BF16)
         total = total + matmul(picked, down_ref[o])
         terms = matmul(upstream_t, picked)
@@ -221,7 +250,7 @@
     hgrad_ref, back_ref, halo_ref, out_ref = refs[slots:]
     voxels = hgrad_ref.shape[0]
     total = hgrad_ref[...] + back_ref[...]
-    lists = halo_ref[...]
+    lists = encode(halo_ref[...]).astype(BF16)
     for s in range(slots):
         chooser = one_hot_columns(lists[s : s + 1, :], voxels)
         total = total + matmul(chooser, received[slots - 1 - s][...])
@@ -244,11 +273,22 @@
     )(*operands)
 
 
+def sum_kernel(devices, scale, parts_ref, out_ref):
+    rows = parts_ref.shape[0] // devices
+    total = parts_ref[0:rows, :].astype(F32)
+    for d in range(1, devices):
+        total = total + parts_ref[d * rows : (d + 1) * rows, :].astype(F32)
+    total = (total * scale).astype(BF16)
+    for d in range(devices):
+        out_ref[d * rows : (d + 1) * rows, :] = total
+
+
 def reduce_all(terms, scale, devices):
-    rows, width = terms.shape
     parts = lax.all_to_all(terms, "shard", 0, 0, tiled=True)
-    mine = jnp.sum(parts.reshape(devices, rows // devices, width).astype(F32), axis=0) * scale
-    return lax.all_gather(mine.astype(BF16), "shard", axis=0, tiled=True)
+    (mine,) = call(
+        functools.partial(sum_kernel, devices, scale), (parts,), [(terms.shape, BF16)], flops=10**6
+    )
+    return lax.all_to_all(mine, "shard", 0, 0, tiled=True)
 
 
 def local(
@@ -309,7 +349,7 @@
         functools.partial(spread_kernel, slots),
         (pre_grad, neighbour_map, conv_weight),
         [((voxels, channels), F32)] + [((cap, channels), BF16)] * slots,
-        scratch=[pltpu.VMEM((voxels + slots * cap, channels), F32)],
+        scratch=[pltpu.VMEM((voxels // 2 + slots * cap // 2, 2 * channels), F32)],
         flops=20 * giga,
     )
     returned = [shift(spread[1 + s], "shard", offsets[s]) for s in range(slots)]

time: 230 us -> 170 us (0.74)
  blocking collectives: 107 us -> 24.1 us
  waiting for transfers between devices: 2.41 us -> 38.2 us
  Pallas kernels: 71.4 us -> 48.5 us
  starting transfers between devices: 40.2 us -> 48.2 us
    all_gather x2 -> x0, blocking collectives: 82.5 us -> none  [reduce_all(): return lax.all_gather(mine.astype(BF16), 'shard', axis=0, tiled=True)]
    pallas_call x5 -> x7, Pallas kernels: 71.4 us -> 48.5 us  [call(): pl.pallas_call(kernel, out_shape=[jax.ShapeDtypeStruct(s, d) for s, d in...]
    all_to_all x1, waiting for transfers between devices: 0.01 us -> 21.6 us  [reduce_all(): parts = lax.all_to_all(terms, 'shard', 0, 0, tiled=True)]
    all_to_all x0 -> x2, waiting for transfers between devices: none -> 14.1 us  [reduce_all(): return lax.all_to_all(mine, 'shard', 0, 0, tiled=True)]
    all_to_all x0 -> x2, starting transfers between devices: none -> 7.93 us  [reduce_all(): return lax.all_to_all(mine, 'shard', 0, 0, tiled=True)]
  transfers between devices with their start and end apart: 13 -> 15, of which waited for: 3 -> 5; matrix products, arithmetic and copies ran while one was open for 1% -> 1% of each run, Pallas kernels for 18% -> 11%
where the time goes in v1:
time: 170 us; the launch traced here: 167 us
  Pallas kernels  48.5 us (29%)
  starting transfers between devices  48.2 us (28%)
  waiting for transfers between devices  38.2 us (22%)
  blocking collectives  24.1 us (14%)
  local copies, waits for them, and re-layouts  4.48 us (3%)
  other arithmetic  2.47 us (1%)
    pallas_call x7, Pallas kernels, call(): pl.pallas_call(kernel, out_shape=[jax.ShapeDtypeStruct(s, d) for s, d in...  48.5 us
    ppermute x12, starting transfers between devices, shift(): return lax.ppermute(value, axis, pairs)  36.8 us
    all_to_all x1, blocking collectives, reduce_all(): parts = lax.all_to_all(terms, 'shard', 0, 0, tiled=True)  24.1 us
    all_to_all x1, waiting for transfers between devices, reduce_all(): parts = lax.all_to_all(terms, 'shard', 0, 0, tiled=True)  21.6 us
    all_to_all x2, waiting for transfers between devices, reduce_all(): return lax.all_to_all(mine, 'shard', 0, 0, tiled=True)  14.1 us
    all_to_all x2, starting transfers between devices, reduce_all(): return lax.all_to_all(mine, 'shard', 0, 0, tiled=True)  7.93 us
    unnamed x26, local copies, waits for them, and re-layouts  4.39 us
    all_to_all x1, starting transfers between devices, reduce_all(): parts = lax.all_to_all(terms, 'shard', 0, 0, tiled=True)  3.42 us
  transfers between devices with their start and end apart: 15, of which 5 were waited for; matrix products, arithmetic and copies ran while one was open for 1% of the time, Pallas kernels for 11%

profile of v1, /device:TPU:1, one launch (start us, length us, event | category | flops | bytes accessed | tf_op | source)
XLA Modules:
  0.0 166.9 jit_solution(6354206779968014167)
XLA Ops:
  0.6 0.0 copy-start
  0.6 0.0 copy-start.1
  0.7 1.1 copy-done.1
  1.8 0.0 copy-start.3
  1.8 0.9 copy-done.3
  2.7 0.0 copy-start.5
  2.7 0.9 copy-done.5
  3.6 0.0 copy-start.8
  3.6 0.7 copy-done.8
  4.3 0.0 copy-start.11
  4.3 0.7 copy-done.11
  5.0 3.4 %shard_map.111 = (bf16[96,128]{1,0:T(8,128)(2,1)S(1)}, bf16[96,128]{1,0:T(8,128)(2,1)S(1)}, bf16[96,128]{1,0:T(8,128)(2,1)S(1)}, bf16[96,128]{1,0:T(8,128)(2,1)S(1)}, f32[1152,128]{1,0:T(8,128)S(1)}) custom-call(bf16[1024,128]{1,0:T(8,128)(2,1)S(1)} %copy-done.3, s32[4,64]{1,0:T(4,128)S(1)} %copy-done.11, s32[8,256]{1,0:T(8,128)S(1)} %copy-done.8, ...), custom_call_target="tpu_custom_call" | custom-call | flops 1000000000 | bytes 4194304 | tf_op jit(solution)/shard_map/pallas_call | solution.py:265
  8.4 1.3 collective-permute-start
  9.7 2.0 %collective-permute-start.1 = (bf16[96,128]{1,0:T(8,128)(2,1)S(1)}, bf16[96,128]{1,0:T(8,128)(2,1)S(1)}, u32[]{:S(2)}, u32[]{:S(2)}) collective-permute-start(bf16[96,128]{1,0:T(8,128)(2,1)S(1)} %get-tuple-element.22), channel_id=1, source_target_pairs={{1,0},{2,1},{3,2},{4,3},{5,4},{6,5},{7,6},{8,7},{9,8},{10,9},{11,1... | collective-permute-start | bytes 73736 | tf_op jit(solution)/shard_map/ppermute | solution.py:26
  11.7 5.1 %collective-permute-start.2 = (bf16[96,128]{1,0:T(8,128)(2,1)S(1)}, bf16[96,128]{1,0:T(8,128)(2,1)S(1)}, u32[]{:S(2)}, u32[]{:S(2)}) collective-permute-start(bf16[96,128]{1,0:T(8,128)(2,1)S(1)} %get-tuple-element.23), channel_id=1, source_target_pairs={{0,1},{1,2},{2,3},{3,4},{4,5},{5,6},{6,7},{7,8},{8,9},{9,10},{10,1... | collective-permute-start | bytes 73736 | tf_op jit(solution)/shard_map/ppermute | solution.py:26
  16.8 4.5 %collective-permute-start.3 = (bf16[96,128]{1,0:T(8,128)(2,1)S(1)}, bf16[96,128]{1,0:T(8,128)(2,1)S(1)}, u32[]{:S(2)}, u32[]{:S(2)}) collective-permute-start(bf16[96,128]{1,0:T(8,128)(2,1)S(1)} %get-tuple-element.24), channel_id=1, source_target_pairs={{0,2},{1,3},{2,4},{3,5},{4,6},{5,7},{6,8},{7,9},{8,10},{9,11},{10,... | collective-permute-start | bytes 73736 | tf_op jit(solution)/shard_map/ppermute | solution.py:26
  21.4 0.0 copy-start.2
  21.4 0.0 copy-start.6
  21.4 0.0 copy-start.9
  21.4 0.0 collective-permute-done.refs_0_
  21.4 0.0 collective-permute-done.1.refs_1_
  21.4 0.0 collective-permute-done.2.refs_2_
  21.5 0.8 collective-permute-done.3.refs_3_
  22.3 0.0 copy-done
  22.3 0.0 copy-done.4
  22.3 0.0 copy-done.7
  22.3 0.0 copy-done.10
  22.3 23.3 %shard_map.112 = (bf16[1024,128]{1,0:T(8,128)(2,1)S(1)}, bf16[128,128]{1,0:T(8,128)(2,1)S(1)}, f32[1024,128]{1,0:T(8,128)S(1)}, bf16[1024,128]{1,0:T(8,128)(2,1)S(1)}, bf16[3584,128]{1,0:T(8,128)(2,1)}) custom-call(bf16[96,128]{1,0:T(8,128)(2,1)S(1)} %collective-permute-done.refs_0_, bf16[96,128]{1,0:T(8,128)(2,1)S(1)} %collective-permute-done.1.refs_1_, ...), custom_call_target="tpu_custom_call" | custom-call | flops 12000000000 | bytes 4194304 | tf_op jit(solution)/shard_map/pallas_call | solution.py:265
  45.6 1.3 collective-permute-start.4
  46.9 1.9 %collective-permute-start.5 = (bf16[32,128]{1,0:T(8,128)(2,1)S(1)}, bf16[32,128]{1,0:T(8,128)(2,1)S(1)}, u32[]{:S(2)}, u32[]{:S(2)}) collective-permute-start(bf16[32,128]{1,0:T(8,128)(2,1)S(1)} %get-tuple-element.40), channel_id=1, source_target_pairs={{1,0},{2,1},{3,2},{4,3},{5,4},{6,5},{7,6},{8,7},{9,8},{10,9},{11,1... | collective-permute-start | bytes 24584 | tf_op jit(solution)/shard_map/ppermute | solution.py:26
  48.8 3.9 %collective-permute-start.6 = (bf16[32,128]{1,0:T(8,128)(2,1)S(1)}, bf16[32,128]{1,0:T(8,128)(2,1)S(1)}, u32[]{:S(2)}, u32[]{:S(2)}) collective-permute-start(bf16[32,128]{1,0:T(8,128)(2,1)S(1)} %get-tuple-element.39), channel_id=1, source_target_pairs={{0,1},{1,2},{2,3},{3,4},{4,5},{5,6},{6,7},{7,8},{8,9},{9,10},{10,1... | collective-permute-start | bytes 24584 | tf_op jit(solution)/shard_map/ppermute | solution.py:26
  52.7 4.9 %collective-permute-start.7 = (bf16[32,128]{1,0:T(8,128)(2,1)S(1)}, bf16[32,128]{1,0:T(8,128)(2,1)S(1)}, u32[]{:S(2)}, u32[]{:S(2)}) collective-permute-start(bf16[32,128]{1,0:T(8,128)(2,1)S(1)} %get-tuple-element.38), channel_id=1, source_target_pairs={{0,2},{1,3},{2,4},{3,5},{4,6},{5,7},{6,8},{7,9},{8,10},{9,11},{10,... | collective-permute-start | bytes 24584 | tf_op jit(solution)/shard_map/ppermute | solution.py:26
  57.6 0.0 collective-permute-done.4.refs_0_
  57.6 0.0 collective-permute-done.5.refs_1_
  57.6 0.0 collective-permute-done.6.refs_2_
  57.7 0.7 collective-permute-done.7.refs_3_
  58.4 0.0 copy-done.2
  58.4 0.0 copy-done.6
  58.4 0.0 copy-done.9
  58.4 3.7 %shard_map.113 = (bf16[256,256]{1,0:T(8,128)(2,1)}, bf16[1024,256]{1,0:T(8,128)(2,1)S(1)}) custom-call(bf16[32,128]{1,0:T(8,128)(2,1)S(1)} %collective-permute-done.4.refs_0_, bf16[32,128]{1,0:T(8,128)(2,1)S(1)} %collective-permute-done.5.refs_1_, bf16[32,128]{1,0:T(8,128)(2,1)S(1)} %collective-permute-done.6.refs_2_, ...), custom_call_target="tpu_custom_call" | custom-call | flops 2000000000 | bytes 4194304 | tf_op jit(solution)/shard_map/pallas_call | solution.py:265
  62.1 24.1 %all_to_all.43 = bf16[32,32,256]{2,1,0:T(8,128)(2,1)S(1)} all-to-all(bf16[32,32,256]{2,1,0:T(8,128)(2,1)S(1)} %bitcast.15), channel_id=1, replica_groups=mesh['shard'=32] {'shard'}, dimensions={0} | all-to-all | bytes 1048576 | tf_op jit(solution)/shard_map/all_to_all | solution.py:287
  86.2 3.4 %all-to-all-start = ((bf16[32,112,128]{2,1,0:T(8,128)(2,1)}), bf16[32,112,128]{2,1,0:T(8,128)(2,1)S(1)}, u32[]{:S(2)}, u32[]{:S(2)}) async-start(bf16[32,112,128]{2,1,0:T(8,128)(2,1)} %bitcast), calls=%async_computation | async-start | bytes 1835008 | tf_op jit(solution)/shard_map/all_to_all | solution.py:287
  89.7 0.9 shard_map.117
  90.6 21.6 %all-to-all-done = bf16[32,112,128]{2,1,0:T(8,128)(2,1)S(1)} async-done(((bf16[32,112,128]{2,1,0:T(8,128)(2,1)}), bf16[32,112,128]{2,1,0:T(8,128)(2,1)S(1)}, u32[]{:S(2)}, u32[]{:S(2)}) %all-to-all-start) | async-done | bytes 917536 | tf_op jit(solution)/shard_map/all_to_all | solution.py:287
  112.2 4.5 %all-to-all-start.3 = ((bf16[32,32,256]{2,1,0:T(8,128)(2,1)}), bf16[32,32,256]{2,1,0:T(8,128)(2,1)S(1)}, u32[]{:S(2)}, u32[]{:S(2)}) async-start(bf16[32,32,256]{2,1,0:T(8,128)(2,1)} %bitcast.7), calls=%async_computation.3 | async-start | bytes 1048576 | tf_op jit(solution)/shard_map/all_to_all | solution.py:291
  116.7 1.1 shard_map.116
  117.8 14.1 %all-to-all-done.3 = bf16[32,32,256]{2,1,0:T(8,128)(2,1)S(1)} async-done(((bf16[32,32,256]{2,1,0:T(8,128)(2,1)}), bf16[32,32,256]{2,1,0:T(8,128)(2,1)S(1)}, u32[]{:S(2)}, u32[]{:S(2)}) %all-to-all-start.3) | async-done | bytes 524320 | tf_op jit(solution)/shard_map/all_to_all | solution.py:291
  131.9 3.4 %all-to-all-start.1 = ((bf16[32,112,128]{2,1,0:T(8,128)(2,1)}), bf16[32,112,128]{2,1,0:T(8,128)(2,1)S(1)}, u32[]{:S(2)}, u32[]{:S(2)}) async-start(bf16[32,112,128]{2,1,0:T(8,128)(2,1)} %bitcast.2), calls=%async_computation.1 | async-start | bytes 1835008 | tf_op jit(solution)/shard_map/all_to_all | solution.py:291
  135.3 0.0 copy-start.12
  135.4 14.9 %shard_map.114 = (f32[1024,128]{1,0:T(8,128)S(1)}, bf16[64,128]{1,0:T(8,128)(2,1)S(1)}, bf16[64,128]{1,0:T(8,128)(2,1)S(1)}, bf16[64,128]{1,0:T(8,128)(2,1)S(1)}, bf16[64,128]{1,0:T(8,128)(2,1)S(1)}) custom-call(bf16[1024,128]{1,0:T(8,128)(2,1)S(1)} %get-tuple-element.29.pgrad_ref, s32[27,1024]{1,0:T(8,128)S(1)} %copy-done.7, bf16[27,128,128]{2,1,0:T(8,128)(2,1)S(1)} %copy-done), custom_call_target="tpu_custom_call" | custom-call | flops 20000000000 | bytes 4194304 | tf_op jit(solution)/shard_map/pallas_call | solution.py:265
  150.3 1.3 collective-permute-start.8
  151.6 2.2 %collective-permute-start.9 = (bf16[64,128]{1,0:T(8,128)(2,1)S(1)}, bf16[64,128]{1,0:T(8,128)(2,1)S(1)}, u32[]{:S(2)}, u32[]{:S(2)}) collective-permute-start(bf16[64,128]{1,0:T(8,128)(2,1)S(1)} %get-tuple-element.31), channel_id=1, source_target_pairs={{1,0},{2,1},{3,2},{4,3},{5,4},{6,5},{7,6},{8,7},{9,8},{10,9},{11,1... | collective-permute-start | bytes 49160 | tf_op jit(solution)/shard_map/ppermute | solution.py:26
  153.8 4.2 %collective-permute-start.10 = (bf16[64,128]{1,0:T(8,128)(2,1)S(1)}, bf16[64,128]{1,0:T(8,128)(2,1)S(1)}, u32[]{:S(2)}, u32[]{:S(2)}) collective-permute-start(bf16[64,128]{1,0:T(8,128)(2,1)S(1)} %get-tuple-element.32), channel_id=1, source_target_pairs={{0,1},{1,2},{2,3},{3,4},{4,5},{5,6},{6,7},{7,8},{8,9},{9,10},{10,1... | collective-permute-start | bytes 49160 | tf_op jit(solution)/shard_map/ppermute | solution.py:26
  158.0 4.3 %collective-permute-start.11 = (bf16[64,128]{1,0:T(8,128)(2,1)S(1)}, bf16[64,128]{1,0:T(8,128)(2,1)S(1)}, u32[]{:S(2)}, u32[]{:S(2)}) collective-permute-start(bf16[64,128]{1,0:T(8,128)(2,1)S(1)} %get-tuple-element.33), channel_id=1, source_target_pairs={{0,2},{1,3},{2,4},{3,5},{4,6},{5,7},{6,8},{7,9},{8,10},{9,11},{10,... | collective-permute-start | bytes 49160 | tf_op jit(solution)/shard_map/ppermute | solution.py:26
  162.2 0.0 collective-permute-done.8.refs_0_
  162.3 0.0 collective-permute-done.9.refs_1_
  162.3 0.0 collective-permute-done.10.refs_2_
  162.3 0.8 collective-permute-done.11.refs_3_
  163.1 0.0 copy-done.12
  163.1 1.2 shard_map.115
  164.3 1.1 bitcast_convert_fusion
  165.4 0.0 all-to-all-done.1
  165.4 0.1 slice.24
  165.5 1.4 convert.2
  (5 shorter events, 0.0 us)
Async XLA Ops:
  0.6 21.6 %copy-start = (bf16[27,128,128]{2,1,0:T(8,128)(2,1)S(1)}, bf16[27,128,128]{2,1,0:T(8,128)(2,1)}, u32[]{:S(2)}) copy-start(bf16[27,128,128]{2,1,0:T(8,128)(2,1)} %weight_ref.1) | copy-start | bytes 2654212
  0.6 1.1 copy-start.1
  1.8 0.9 copy-start.3
  2.7 0.9 copy-start.5
  3.6 0.7 copy-start.8
  4.3 0.7 copy-start.11
  5.0 17.3 %copy-start.4 = (bf16[1024,128]{1,0:T(8,128)(2,1)S(1)}, bf16[1024,128]{1,0:T(8,128)(2,1)}, u32[]{:S(2)}) copy-start(bf16[1024,128]{1,0:T(8,128)(2,1)} %refs_4_.1) | copy-start | bytes 786436
  5.0 17.3 %copy-start.7 = (s32[27,1024]{1,0:T(8,128)S(1)}, s32[27,1024]{1,0:T(8,128)}, u32[]{:S(2)}) copy-start(s32[27,1024]{1,0:T(8,128)} %map_ref.1) | copy-start | bytes 331780
  5.0 17.3 %copy-start.10 = (s32[4,32]{1,0:T(4,128)S(1)}, s32[4,32]{1,0:T(4,128)}, u32[]{:S(2)}) copy-start(s32[4,32]{1,0:T(4,128)} %refs_8_.1) | copy-start | bytes 1540
  8.4 13.0 %collective-permute-start = (bf16[96,128]{1,0:T(8,128)(2,1)S(1)}, bf16[96,128]{1,0:T(8,128)(2,1)S(1)}, u32[]{:S(2)}, u32[]{:S(2)}) collective-permute-start(bf16[96,128]{1,0:T(8,128)(2,1)S(1)} %get-tuple-element.21), channel_id=1, source_target_pairs={{2,0},{3,1},{4,2},{5,3},{6,4},{7,5},{8,6},{9,7},{10,8},{11,9},{12,... | collective-permute-start | bytes 73736 | tf_op jit(solution)/shard_map/ppermute | solution.py:26
  9.7 11.7 %collective-permute-start.1 = (bf16[96,128]{1,0:T(8,128)(2,1)S(1)}, bf16[96,128]{1,0:T(8,128)(2,1)S(1)}, u32[]{:S(2)}, u32[]{:S(2)}) collective-permute-start(bf16[96,128]{1,0:T(8,128)(2,1)S(1)} %get-tuple-element.22), channel_id=1, source_target_pairs={{1,0},{2,1},{3,2},{4,3},{5,4},{6,5},{7,6},{8,7},{9,8},{10,9},{11,1... | collective-permute-start | bytes 73736 | tf_op jit(solution)/shard_map/ppermute | solution.py:26
  11.7 9.7 %collective-permute-start.2 = (bf16[96,128]{1,0:T(8,128)(2,1)S(1)}, bf16[96,128]{1,0:T(8,128)(2,1)S(1)}, u32[]{:S(2)}, u32[]{:S(2)}) collective-permute-start(bf16[96,128]{1,0:T(8,128)(2,1)S(1)} %get-tuple-element.23), channel_id=1, source_target_pairs={{0,1},{1,2},{2,3},{3,4},{4,5},{5,6},{6,7},{7,8},{8,9},{9,10},{10,1... | collective-permute-start | bytes 73736 | tf_op jit(solution)/shard_map/ppermute | solution.py:26
  16.8 5.5 %collective-permute-start.3 = (bf16[96,128]{1,0:T(8,128)(2,1)S(1)}, bf16[96,128]{1,0:T(8,128)(2,1)S(1)}, u32[]{:S(2)}, u32[]{:S(2)}) collective-permute-start(bf16[96,128]{1,0:T(8,128)(2,1)S(1)} %get-tuple-element.24), channel_id=1, source_target_pairs={{0,2},{1,3},{2,4},{3,5},{4,6},{5,7},{6,8},{7,9},{8,10},{9,11},{10,... | collective-permute-start | bytes 73736 | tf_op jit(solution)/shard_map/ppermute | solution.py:26
  21.4 37.0 %copy-start.2 = (bf16[8,128,256]{2,1,0:T(8,128)(2,1)S(1)}, bf16[8,128,256]{2,1,0:T(8,128)(2,1)}, u32[]{:S(2)}) copy-start(bf16[8,128,256]{2,1,0:T(8,128)(2,1)} %refs_6_.4) | copy-start | bytes 1572868
  21.4 37.0 %copy-start.6 = (bf16[256,256]{1,0:T(8,128)(2,1)S(1)}, bf16[256,256]{1,0:T(8,128)(2,1)}, u32[]{:S(2)}) copy-start(bf16[256,256]{1,0:T(8,128)(2,1)} %refs_7_.1) | copy-start | bytes 393220
  21.4 37.0 %copy-start.9 = (s32[8,256]{1,0:T(8,128)S(1)}, s32[8,256]{1,0:T(8,128)}, u32[]{:S(2)}) copy-start(s32[8,256]{1,0:T(8,128)} %refs_5_.3) | copy-start | bytes 24580
  45.6 12.0 %collective-permute-start.4 = (bf16[32,128]{1,0:T(8,128)(2,1)S(1)}, bf16[32,128]{1,0:T(8,128)(2,1)S(1)}, u32[]{:S(2)}, u32[]{:S(2)}) collective-permute-start(bf16[32,128]{1,0:T(8,128)(2,1)S(1)} %get-tuple-element.41), channel_id=1, source_target_pairs={{2,0},{3,1},{4,2},{5,3},{6,4},{7,5},{8,6},{9,7},{10,8},{11,9},{12,... | collective-permute-start | bytes 24584 | tf_op jit(solution)/shard_map/ppermute | solution.py:26
  46.9 10.8 %collective-permute-start.5 = (bf16[32,128]{1,0:T(8,128)(2,1)S(1)}, bf16[32,128]{1,0:T(8,128)(2,1)S(1)}, u32[]{:S(2)}, u32[]{:S(2)}) collective-permute-start(bf16[32,128]{1,0:T(8,128)(2,1)S(1)} %get-tuple-element.40), channel_id=1, source_target_pairs={{1,0},{2,1},{3,2},{4,3},{5,4},{6,5},{7,6},{8,7},{9,8},{10,9},{11,1... | collective-permute-start | bytes 24584 | tf_op jit(solution)/shard_map/ppermute | solution.py:26
  48.8 8.9 %collective-permute-start.6 = (bf16[32,128]{1,0:T(8,128)(2,1)S(1)}, bf16[32,128]{1,0:T(8,128)(2,1)S(1)}, u32[]{:S(2)}, u32[]{:S(2)}) collective-permute-start(bf16[32,128]{1,0:T(8,128)(2,1)S(1)} %get-tuple-element.39), channel_id=1, source_target_pairs={{0,1},{1,2},{2,3},{3,4},{4,5},{5,6},{6,7},{7,8},{8,9},{9,10},{10,1... | collective-permute-start | bytes 24584 | tf_op jit(solution)/shard_map/ppermute | solution.py:26
  52.7 5.7 %collective-permute-start.7 = (bf16[32,128]{1,0:T(8,128)(2,1)S(1)}, bf16[32,128]{1,0:T(8,128)(2,1)S(1)}, u32[]{:S(2)}, u32[]{:S(2)}) collective-permute-start(bf16[32,128]{1,0:T(8,128)(2,1)S(1)} %get-tuple-element.38), channel_id=1, source_target_pairs={{0,2},{1,3},{2,4},{3,5},{4,6},{5,7},{6,8},{7,9},{8,10},{9,11},{10,... | collective-permute-start | bytes 24584 | tf_op jit(solution)/shard_map/ppermute | solution.py:26
  86.2 26.0 %all-to-all-start = ((bf16[32,112,128]{2,1,0:T(8,128)(2,1)}), bf16[32,112,128]{2,1,0:T(8,128)(2,1)S(1)}, u32[]{:S(2)}, u32[]{:S(2)}) async-start(bf16[32,112,128]{2,1,0:T(8,128)(2,1)} %bitcast), calls=%async_computation | async-start | bytes 1835008 | tf_op jit(solution)/shard_map/all_to_all | solution.py:287
  112.2 19.7 %all-to-all-start.3 = ((bf16[32,32,256]{2,1,0:T(8,128)(2,1)}), bf16[32,32,256]{2,1,0:T(8,128)(2,1)S(1)}, u32[]{:S(2)}, u32[]{:S(2)}) async-start(bf16[32,32,256]{2,1,0:T(8,128)(2,1)} %bitcast.7), calls=%async_computation.3 | async-start | bytes 1048576 | tf_op jit(solution)/shard_map/all_to_all | solution.py:291
  131.9 33.5 %all-to-all-start.1 = ((bf16[32,112,128]{2,1,0:T(8,128)(2,1)}), bf16[32,112,128]{2,1,0:T(8,128)(2,1)S(1)}, u32[]{:S(2)}, u32[]{:S(2)}) async-start(bf16[32,112,128]{2,1,0:T(8,128)(2,1)} %bitcast.2), calls=%async_computation.1 | async-start | bytes 1835008 | tf_op jit(solution)/shard_map/all_to_all | solution.py:291
  135.3 27.8 %copy-start.12 = (s32[4,64]{1,0:T(4,128)S(1)}, s32[4,64]{1,0:T(4,128)}, u32[]{:S(2)}) copy-start(s32[4,64]{1,0:T(4,128)} %refs_6_.5) | copy-start | bytes 3076
  150.3 12.0 %collective-permute-start.8 = (bf16[64,128]{1,0:T(8,128)(2,1)S(1)}, bf16[64,128]{1,0:T(8,128)(2,1)S(1)}, u32[]{:S(2)}, u32[]{:S(2)}) collective-permute-start(bf16[64,128]{1,0:T(8,128)(2,1)S(1)} %get-tuple-element.30), channel_id=1, source_target_pairs={{2,0},{3,1},{4,2},{5,3},{6,4},{7,5},{8,6},{9,7},{10,8},{11,9},{12,... | collective-permute-start | bytes 49160 | tf_op jit(solution)/shard_map/ppermute | solution.py:26
  151.6 10.7 %collective-permute-start.9 = (bf16[64,128]{1,0:T(8,128)(2,1)S(1)}, bf16[64,128]{1,0:T(8,128)(2,1)S(1)}, u32[]{:S(2)}, u32[]{:S(2)}) collective-permute-start(bf16[64,128]{1,0:T(8,128)(2,1)S(1)} %get-tuple-element.31), channel_id=1, source_target_pairs={{1,0},{2,1},{3,2},{4,3},{5,4},{6,5},{7,6},{8,7},{9,8},{10,9},{11,1... | collective-permute-start | bytes 49160 | tf_op jit(solution)/shard_map/ppermute | solution.py:26
  153.8 8.5 %collective-permute-start.10 = (bf16[64,128]{1,0:T(8,128)(2,1)S(1)}, bf16[64,128]{1,0:T(8,128)(2,1)S(1)}, u32[]{:S(2)}, u32[]{:S(2)}) collective-permute-start(bf16[64,128]{1,0:T(8,128)(2,1)S(1)} %get-tuple-element.32), channel_id=1, source_target_pairs={{0,1},{1,2},{2,3},{3,4},{4,5},{5,6},{6,7},{7,8},{8,9},{9,10},{10,1... | collective-permute-start | bytes 49160 | tf_op jit(solution)/shard_map/ppermute | solution.py:26
  158.0 5.1 %collective-permute-start.11 = (bf16[64,128]{1,0:T(8,128)(2,1)S(1)}, bf16[64,128]{1,0:T(8,128)(2,1)S(1)}, u32[]{:S(2)}, u32[]{:S(2)}) collective-permute-start(bf16[64,128]{1,0:T(8,128)(2,1)S(1)} %get-tuple-element.33), channel_id=1, source_target_pairs={{0,2},{1,3},{2,4},{3,5},{4,6},{5,7},{6,8},{7,9},{8,10},{9,11},{10,... | collective-permute-start | bytes 49160 | tf_op jit(solution)/shard_map/ppermute | solution.py:26

commit v2 on v1

--- a/solution.py
+++ b/solution.py
@@ -82,23 +82,41 @@
     return parts[0] if len(parts) == 1 else jnp.concatenate(parts, axis=0)
 
 
-def head_kernel(features_ref, halo_ref, child_map_ref, out_grad_ref, down_ref, *outs):
+def head_kernel(features_hbm, halo_hbm, child_map_hbm, out_grad_hbm, down_hbm, *refs):
+    sources = (features_hbm, halo_hbm, child_map_hbm, out_grad_hbm, down_hbm)
+    buffers, sems = refs[-len(sources) - 1 : -1], refs[-1]
+    features_ref, halo_ref, child_map_ref, out_grad_ref, down_ref = buffers
+    copies = [
+        pltpu.make_async_copy(source, buffer, sems.at[n])
+        for n, (source, buffer) in enumerate(zip(sources, buffers))
+    ]
+    for copy in copies:
+        copy.start()
+    outs = refs[: -len(sources) - 1]
     sends, back_ref = outs[:-1], outs[-1]
     slots, cap = halo_ref.shape
     voxels = features_ref.shape[0]
     octants = child_map_ref.shape[0]
-    table_rows = back_ref.shape[0]
+    table_rows = voxels + slots * (sends[0].shape[0] - cap)
     cap2 = (table_rows - voxels) // slots
+    copies[0].wait()
+    copies[1].wait()
     listed = gather_lists(halo_ref, features_ref[...]).astype(BF16)
     for s in range(slots):
         sends[s][0:cap, :] = listed[s * cap : (s + 1) * cap, :]
+    for copy in copies[2:]:
+        copy.wait()
     upstream = out_grad_ref[...]
-    total = jnp.zeros((table_rows, LANES), F32)
+    both = jnp.zeros((table_rows, 2 * LANES), F32)
     codes = encode(child_map_ref[...]).astype(BF16)
     for o in range(octants):
-        part = matmul_rt(upstream, down_ref[o]).astype(BF16)
-        total = total + matmul(one_hot_columns(codes[o : o + 1, :], table_rows), part)
-    back_ref[...] = total
+        part = matmul_rt(upstream, down_ref[o])
+        high = part.astype(BF16)
+        low = (part - high.astype(F32)).astype(BF16)
+        chooser = one_hot_columns(codes[o : o + 1, :], table_rows)
+        both = both + matmul(chooser, jnp.concatenate([high, low], axis=1))
+    total = both[:, :LANES] + both[:, LANES:]
+    back_ref[...] = total[:voxels]
     for s in range(slots):
         slot = slots - 1 - s
         first = voxels + slot * cap2
@@ -169,8 +187,6 @@
     pgrad = hgrad * (sig * (1.0 + pre * (1.0 - sig)))
     pgrad_ref[...] = pgrad.astype(BF16)
     pgrad_t = jnp.transpose(pgrad).astype(BF16)
-    rows = kernel_count * LANES
-    cgrad_ref[rows:, :] = jnp.zeros((cgrad_ref.shape[0] - rows, LANES), BF16)
 
     def put(k, value):
         cgrad_ref[pl.ds(pl.multiple_of(k * LANES, LANES), LANES), :] = jnp.transpose(value).astype(BF16)
@@ -226,23 +242,65 @@
         sends[s][...] = acc_ref[first : first + cap, side : side + LANES].astype(BF16)
 
 
+def my_half(rows):
+    core = lax.rem(lax.axis_index("shard"), 2)
+    return pl.multiple_of(core * rows, 16), pl.multiple_of((1 - core) * rows, 16)
+
+
 def down_kernel(slots, *refs):
     received = refs[:slots]
-    hidden_ref, map_ref, down_ref, out_grad_ref, coarse_ref, dgrad_ref = refs[slots:]
+    (hidden_ref, map_ref, down_ref, out_grad_ref, cgrad_ref) = refs[slots : slots + 5]
+    coarse_ref, terms_ref, send_ref = refs[slots + 5 :]
     table = jnp.concatenate([hidden_ref[...]] + [r[...] for r in received], axis=0)
     upstream = out_grad_ref[...]
     parents = upstream.shape[0]
-    channels = down_ref.shape[1]
     upstream_t = jnp.transpose(upstream.astype(F32)).astype(BF16)
     total = jnp.zeros((parents, down_ref.shape[2]), F32)
     codes = encode(map_ref[...])
+    row = cgrad_ref.shape[0]
+    terms_ref[0:row, :] = cgrad_ref[...]
     for o in range(map_ref.shape[0]):
         chooser = one_hot_rows(column(codes[o : o + 1, :]).astype(BF16), table.shape[0])
         picked = matmul(chooser, table).astype(BF16)
         total = total + matmul(picked, down_ref[o])
         terms = matmul(upstream_t, picked)
-        dgrad_ref[o * channels : (o + 1) * channels, :] = jnp.transpose(terms).astype(BF16)
+        for start in range(0, terms.shape[0], LANES):
+            block = jnp.transpose(terms[start : start + LANES, :]).astype(BF16)
+            terms_ref[row : row + LANES, :] = block
+            row += LANES
+    terms_ref[row:, :] = jnp.zeros((terms_ref.shape[0] - row, LANES), BF16)
     coarse_ref[...] = total.astype(BF16)
+    send_ref[...] = terms_ref[pl.ds(my_half(send_ref.shape[0])[1], send_ref.shape[0]), :]
+
+
+def pair_kernel(terms_ref, other_ref, out_ref):
+    rows = other_ref.shape[0]
+    mine = terms_ref[pl.ds(my_half(rows)[0], rows), :].astype(F32)
+    out_ref[...] = (mine + other_ref[...].astype(F32)).astype(BF16)
+
+
+def sum_kernel(groups, scale, parts_ref, after_ref, out_ref):
+    rows = parts_ref.shape[0] // groups
+    total = parts_ref[0:rows, :].astype(F32)
+    for d in range(1, groups):
+        total = total + parts_ref[d * rows : (d + 1) * rows, :].astype(F32)
+    total = (total * scale).astype(BF16)
+    for d in range(groups):
+        out_ref[d * rows : (d + 1) * rows, :] = total
+
+
+def final_kernel(mine_ref, other_ref, conv_ref, down_ref, whole_ref):
+    rows = mine_ref.shape[0]
+    mine, other = my_half(rows)
+    whole_ref[pl.ds(mine, rows), :] = mine_ref[...]
+    whole_ref[pl.ds(other, rows), :] = other_ref[...]
+    row = conv_ref.shape[0]
+    conv_ref[...] = whole_ref[0:row, :].astype(F32)
+    for first in range(0, down_ref.shape[0], LANES):
+        for start in range(0, down_ref.shape[1], LANES):
+            block = whole_ref[row : row + LANES, :].astype(F32)
+            down_ref[first : first + LANES, start : start + LANES] = block
+            row += LANES
 
 
 def tail_kernel(slots, *refs):
@@ -257,38 +315,26 @@
     out_ref[...] = total
 
 
-def vmem():
-    return pl.BlockSpec(memory_space=pltpu.VMEM)
-
-
-def call(kernel, operands, outs, scratch=(), limit=32, flops=0):
+def call(kernel, operands, outs, scratch=(), limit=32, flops=0, in_hbm=()):
+    spaces = [pl.ANY if n in in_hbm else pltpu.VMEM for n in range(len(operands))]
     return pl.pallas_call(
         kernel,
         out_shape=[jax.ShapeDtypeStruct(s, d) for s, d in outs],
-        in_specs=[vmem() for _ in operands],
-        out_specs=[vmem() for _ in outs],
+        in_specs=[pl.BlockSpec(memory_space=space) for space in spaces],
+        out_specs=[pl.BlockSpec(memory_space=pltpu.VMEM) for _ in outs],
         scratch_shapes=list(scratch),
         compiler_params=pltpu.CompilerParams(vmem_limit_bytes=limit * 2**20),
         cost_estimate=pl.CostEstimate(flops=flops, bytes_accessed=4 * 2**20, transcendentals=0),
     )(*operands)
 
 
-def sum_kernel(devices, scale, parts_ref, out_ref):
-    rows = parts_ref.shape[0] // devices
-    total = parts_ref[0:rows, :].astype(F32)
-    for d in range(1, devices):
-        total = total + parts_ref[d * rows : (d + 1) * rows, :].astype(F32)
-    total = (total * scale).astype(BF16)
-    for d in range(devices):
-        out_ref[d * rows : (d + 1) * rows, :] = total
-
-
-def reduce_all(terms, scale, devices):
-    parts = lax.all_to_all(terms, "shard", 0, 0, tiled=True)
-    (mine,) = call(
-        functools.partial(sum_kernel, devices, scale), (parts,), [(terms.shape, BF16)], flops=10**6
-    )
-    return lax.all_to_all(mine, "shard", 0, 0, tiled=True)
+def swap_cores(value, devices):
+    return lax.ppermute(value, "shard", [(i, i + 1 - 2 * (i % 2)) for i in range(devices)])
+
+
+def exchange(value, devices):
+    groups = [list(range(core, devices, 2)) for core in range(2)]
+    return lax.all_to_all(value, "shard", 0, 0, axis_index_groups=groups, tiled=True)
 
 
 def local(
@@ -308,13 +354,22 @@
     first = call(
         head_kernel,
         (features, halo_rows, child_map, out_grad, down_weight),
-        [((cap + cap2, channels), BF16)] * slots + [((voxels + slots * cap2, channels), F32)],
+        [((cap + cap2, channels), BF16)] * slots + [((voxels, channels), F32)],
+        scratch=[
+            pltpu.VMEM(value.shape, value.dtype)
+            for value in (features, halo_rows, child_map, out_grad, down_weight)
+        ]
+        + [pltpu.SemaphoreType.DMA((5,))],
+        limit=60,
         flops=giga,
-    )
-    back_h = first[-1][:voxels]
+        in_hbm=range(5),
+    )
+    back_h = first[-1]
     received = [shift(first[s], "shard", offsets[s]) for s in range(slots)]
+    conv_rows = kernel_count * channels
+    down_rows = octants * channels * coarse_channels // LANES
     grain = 16 * devices
-    grad_rows = -(-kernel_count * channels // grain) * grain
+    half_rows = -(-(conv_rows + down_rows) // grain) * grain // 2
     hidden, leaving, hidden_grad, pre_grad, conv_terms = call(
         functools.partial(forward_kernel, slots),
         (*received, features, neighbour_map, conv_weight, back_h, child_rows),
@@ -323,7 +378,7 @@
             ((slots * cap2, channels), BF16),
             ((voxels, channels), F32),
             ((voxels, channels), BF16),
-            ((grad_rows, channels), BF16),
+            ((conv_rows, channels), BF16),
         ],
         scratch=[
             pltpu.VMEM((voxels // 2 + slots * cap // 2, 2 * channels), BF16),
@@ -336,15 +391,23 @@
     received_h = [
         shift(leaving[s * cap2 : (s + 1) * cap2], "shard", offsets[s]) for s in range(slots)
     ]
-    coarse, down_terms = call(
+    coarse, terms, leaving_terms = call(
         functools.partial(down_kernel, slots),
-        (*received_h, hidden, child_map, down_weight, out_grad),
+        (*received_h, hidden, child_map, down_weight, out_grad, conv_terms),
         [
             ((parents, coarse_channels), BF16),
-            ((octants * channels, coarse_channels), BF16),
+            ((2 * half_rows, LANES), BF16),
+            ((half_rows, LANES), BF16),
         ],
         flops=2 * giga,
     )
+    (pair_terms,) = call(
+        pair_kernel,
+        (terms, swap_cores(leaving_terms, devices)),
+        [((half_rows, LANES), BF16)],
+        flops=10**6,
+    )
+    parts = exchange(pair_terms, devices)
     spread = call(
         functools.partial(spread_kernel, slots),
         (pre_grad, neighbour_map, conv_weight),
@@ -359,11 +422,23 @@
         [((voxels, channels), F32)],
         flops=giga,
     )
-    conv_sum = reduce_all(conv_terms, scale, devices)
-    down_sum = reduce_all(down_terms, scale, devices)
-    conv_grad = conv_sum[: kernel_count * channels].astype(F32).reshape(conv_weight.shape)
-    down_grad = down_sum.astype(F32).reshape(down_weight.shape)
-    return (coarse, input_grad, conv_grad, down_grad)
+    (summed,) = call(
+        functools.partial(sum_kernel, devices // 2, scale),
+        (parts, spread[1]),
+        [((half_rows, LANES), BF16)],
+        flops=10**6,
+        in_hbm=(1,),
+    )
+    mine = exchange(summed, devices)
+    conv_grad, down_grad = call(
+        final_kernel,
+        (mine, swap_cores(mine, devices)),
+        [((conv_rows, LANES), F32), ((octants * channels, coarse_channels), F32)],
+        scratch=[pltpu.VMEM((2 * half_rows, LANES), BF16)],
+        flops=10**6,
+    )
+    conv_grad = conv_grad.reshape(conv_weight.shape)
+    return (coarse, input_grad, conv_grad, down_grad.reshape(down_weight.shape))
 
 
 def solution(mesh):

time: 170 us -> 137 us (0.81)
  waiting for transfers between devices: 38.2 us -> 10.1 us
  local copies, waits for them, and re-layouts: 4.48 us -> 1.08 us
  other arithmetic: 2.47 us -> 0 us
  Pallas kernels: 48.5 us -> 50.6 us
    all_to_all x3 -> x1, waiting for transfers between devices: 35.8 us -> 0.93 us  [exchange(): lax.all_to_all(value, 'shard', 0, 0, axis_index_groups=groups, tiled=True)]
    ppermute x12, waiting for transfers between devices: 2.4 us -> 7.35 us  [shift(): return lax.ppermute(value, axis, pairs)]
    ppermute x0 -> x2, starting transfers between devices: none -> 3.8 us  [swap_cores(): lax.ppermute(value, 'shard', [(i, i + 1 - 2 * (i % 2)) for i in range(dev...]
    unnamed x26 -> x18, local copies, waits for them, and re-layouts: 4.39 us -> 1.07 us
    ppermute x12, starting transfers between devices: 36.8 us -> 34.5 us  [shift(): return lax.ppermute(value, axis, pairs)]
    pallas_call x7 -> x8, Pallas kernels: 48.5 us -> 50.6 us  [call(): pl.pallas_call(kernel, out_shape=[jax.ShapeDtypeStruct(s, d) for s, d in...]
    ppermute x0 -> x2, waiting for transfers between devices: none -> 1.82 us  [swap_cores(): lax.ppermute(value, 'shard', [(i, i + 1 - 2 * (i % 2)) for i in range(dev...]
    all_to_all x3 -> x1, starting transfers between devices: 11.4 us -> 9.7 us  [exchange(): lax.all_to_all(value, 'shard', 0, 0, axis_index_groups=groups, tiled=True)]
  transfers between devices with their start and end apart: 15 -> 15, of which waited for: 5 -> 6; matrix products, arithmetic and copies ran while one was open for 1% -> 0% of each run, Pallas kernels for 11% -> 12%
where the time goes in v2:
time: 137 us; the launch traced here: 135 us
  Pallas kernels  50.6 us (37%)
  starting transfers between devices  48 us (35%)
  blocking collectives  24.6 us (18%)
  waiting for transfers between devices  10.1 us (7%)
    pallas_call x8, Pallas kernels, call(): pl.pallas_call(kernel, out_shape=[jax.ShapeDtypeStruct(s, d) for s, d in...  50.6 us
    ppermute x12, starting transfers between devices, shift(): return lax.ppermute(value, axis, pairs)  34.5 us
    all_to_all x1, blocking collectives, exchange(): lax.all_to_all(value, 'shard', 0, 0, axis_index_groups=groups, tiled=True)  24.6 us
    all_to_all x1, starting transfers between devices, exchange(): lax.all_to_all(value, 'shard', 0, 0, axis_index_groups=groups, tiled=True)  9.7 us
    ppermute x12, waiting for transfers between devices, shift(): return lax.ppermute(value, axis, pairs)  7.35 us
    ppermute x2, starting transfers between devices, swap_cores(): lax.ppermute(value, 'shard', [(i, i + 1 - 2 * (i % 2)) for i in range(dev...  3.8 us
  transfers between devices with their start and end apart: 15, of which 6 were waited for; matrix products, arithmetic and copies ran while one was open for 0% of the time, Pallas kernels for 12%

profile of v2, /device:TPU:1, one launch (start us, length us, event | category | flops | bytes accessed | tf_op | source)
XLA Modules:
  0.0 135.3 jit_solution(10850570670278468088)
XLA Ops:
  0.6 0.0 copy-start.2
  0.6 0.0 copy-start.4
  0.7 0.0 copy-start
  0.7 0.0 copy-start.6
  0.7 5.5 %shard_map.111 = (bf16[96,128]{1,0:T(8,128)(2,1)}, bf16[96,128]{1,0:T(8,128)(2,1)}, bf16[96,128]{1,0:T(8,128)(2,1)}, bf16[96,128]{1,0:T(8,128)(2,1)}, f32[1024,128]{1,0:T(8,128)}) custom-call(bf16[1024,128]{1,0:T(8,128)(2,1)} %refs_4_.1, s32[4,64]{1,0:T(4,128)} %refs_6_.5, s32[8,256]{1,0:T(8,128)} %refs_5_.3, bf16[256,256]{1,0:T(8,128)(2,1)} %refs_7_.1, ...), custom_call_target="tpu_custom_call" | custom-call | flops 1000000000 | bytes 4194304 | tf_op jit(solution)/shard_map/pallas_call | solution.py:320
  6.1 1.3 collective-permute-start
  7.4 2.0 %collective-permute-start.1 = (bf16[96,128]{1,0:T(8,128)(2,1)}, bf16[96,128]{1,0:T(8,128)(2,1)S(1)}, u32[]{:S(2)}, u32[]{:S(2)}) collective-permute-start(bf16[96,128]{1,0:T(8,128)(2,1)} %get-tuple-element.25), channel_id=1, source_target_pairs={{1,0},{2,1},{3,2},{4,3},{5,4},{6,5},{7,6},{8,7},{9,8},{10,9},{11,1... | collective-permute-start | bytes 73736 | tf_op jit(solution)/shard_map/ppermute | solution.py:26
  9.4 5.1 %collective-permute-start.2 = (bf16[96,128]{1,0:T(8,128)(2,1)}, bf16[96,128]{1,0:T(8,128)(2,1)S(1)}, u32[]{:S(2)}, u32[]{:S(2)}) collective-permute-start(bf16[96,128]{1,0:T(8,128)(2,1)} %get-tuple-element.26), channel_id=1, source_target_pairs={{0,1},{1,2},{2,3},{3,4},{4,5},{5,6},{6,7},{7,8},{8,9},{9,10},{10,1... | collective-permute-start | bytes 73736 | tf_op jit(solution)/shard_map/ppermute | solution.py:26
  14.5 4.5 %collective-permute-start.3 = (bf16[96,128]{1,0:T(8,128)(2,1)}, bf16[96,128]{1,0:T(8,128)(2,1)S(1)}, u32[]{:S(2)}, u32[]{:S(2)}) collective-permute-start(bf16[96,128]{1,0:T(8,128)(2,1)} %get-tuple-element.27), channel_id=1, source_target_pairs={{0,2},{1,3},{2,4},{3,5},{4,6},{5,7},{6,8},{7,9},{8,10},{9,11},{10,... | collective-permute-start | bytes 73736 | tf_op jit(solution)/shard_map/ppermute | solution.py:26
  19.1 0.0 collective-permute-done.refs_0_
  19.1 0.0 collective-permute-done.1.refs_1_
  19.1 0.0 collective-permute-done.2.refs_2_
  19.1 1.1 collective-permute-done.3.refs_3_
  20.2 0.0 copy-done.2
  20.2 0.0 copy-done.4
  20.2 0.0 copy-done
  20.2 0.0 copy-done.6
  20.2 0.0 copy-start.8
  20.2 1.0 copy-done.8
  21.2 0.0 copy-start.1
  21.3 0.0 copy-start.3
  21.3 0.0 copy-start.5
  21.3 22.4 %shard_map.112 = (bf16[1024,128]{1,0:T(8,128)(2,1)S(1)}, bf16[128,128]{1,0:T(8,128)(2,1)S(1)}, f32[1024,128]{1,0:T(8,128)S(1)}, bf16[1024,128]{1,0:T(8,128)(2,1)S(1)}, bf16[3456,128]{1,0:T(8,128)(2,1)S(1)}) custom-call(bf16[96,128]{1,0:T(8,128)(2,1)S(1)} %collective-permute-done.refs_0_, bf16[96,128]{1,0:T(8,128)(2,1)S(1)} %collective-permute-done.1.refs_1_, ...), custom_call_target="tpu_custom_call" | custom-call | flops 12000000000 | bytes 4194304 | tf_op jit(solution)/shard_map/pallas_call | solution.py:320
  43.6 3.6 %collective-permute-start.7 = (bf16[32,128]{1,0:T(8,128)(2,1)S(1)}, bf16[32,128]{1,0:T(8,128)(2,1)S(1)}, u32[]{:S(2)}, u32[]{:S(2)}) collective-permute-start(bf16[32,128]{1,0:T(8,128)(2,1)S(1)} %get-tuple-element.44), channel_id=1, source_target_pairs={{0,2},{1,3},{2,4},{3,5},{4,6},{5,7},{6,8},{7,9},{8,10},{9,11},{10,... | collective-permute-start | bytes 24584 | tf_op jit(solution)/shard_map/ppermute | solution.py:26
  47.3 4.8 %collective-permute-start.6 = (bf16[32,128]{1,0:T(8,128)(2,1)S(1)}, bf16[32,128]{1,0:T(8,128)(2,1)S(1)}, u32[]{:S(2)}, u32[]{:S(2)}) collective-permute-start(bf16[32,128]{1,0:T(8,128)(2,1)S(1)} %get-tuple-element.45), channel_id=1, source_target_pairs={{0,1},{1,2},{2,3},{3,4},{4,5},{5,6},{6,7},{7,8},{8,9},{9,10},{10,1... | collective-permute-start | bytes 24584 | tf_op jit(solution)/shard_map/ppermute | solution.py:26
  52.1 1.9 %collective-permute-start.5 = (bf16[32,128]{1,0:T(8,128)(2,1)S(1)}, bf16[32,128]{1,0:T(8,128)(2,1)S(1)}, u32[]{:S(2)}, u32[]{:S(2)}) collective-permute-start(bf16[32,128]{1,0:T(8,128)(2,1)S(1)} %get-tuple-element.46), channel_id=1, source_target_pairs={{1,0},{2,1},{3,2},{4,3},{5,4},{6,5},{7,6},{8,7},{9,8},{10,9},{11,1... | collective-permute-start | bytes 24584 | tf_op jit(solution)/shard_map/ppermute | solution.py:26
  54.1 1.3 collective-permute-start.4
  55.4 0.0 collective-permute-done.7.refs_3_
  55.4 0.0 collective-permute-done.6.refs_2_
  55.4 1.7 %collective-permute-done.5.refs_1_ = bf16[32,128]{1,0:T(8,128)(2,1)S(1)} collective-permute-done((bf16[32,128]{1,0:T(8,128)(2,1)S(1)}, bf16[32,128]{1,0:T(8,128)(2,1)S(1)}, u32[]{:S(2)}, u32[]{:S(2)}) %collective-permute-start.5) | collective-permute-done | bytes 8224 | tf_op jit(solution)/shard_map/ppermute | solution.py:26
  57.1 1.4 %collective-permute-done.4.refs_0_ = bf16[32,128]{1,0:T(8,128)(2,1)S(1)} collective-permute-done((bf16[32,128]{1,0:T(8,128)(2,1)S(1)}, bf16[32,128]{1,0:T(8,128)(2,1)S(1)}, u32[]{:S(2)}, u32[]{:S(2)}) %collective-permute-start.4) | collective-permute-done | bytes 8224 | tf_op jit(solution)/shard_map/ppermute | solution.py:26
  58.4 0.0 copy-done.1
  58.5 0.0 copy-done.3
  58.5 0.0 copy-done.5
  58.5 3.7 %shard_map.113 = (bf16[256,256]{1,0:T(8,128)(2,1)}, bf16[5632,128]{1,0:T(8,128)(2,1)S(1)}, bf16[2816,128]{1,0:T(8,128)(2,1)S(1)}) custom-call(bf16[32,128]{1,0:T(8,128)(2,1)S(1)} %collective-permute-done.4.refs_0_, bf16[32,128]{1,0:T(8,128)(2,1)S(1)} %collective-permute-done.5.refs_1_, bf16[32,128]{1,0:T(8,128)(2,1)S(1)} %collective-permute-done.6.refs_2_, ...), custom_call_target="tpu_custom_call" | custom-call | flops 2000000000 | bytes 4194304 | tf_op jit(solution)/shard_map/pallas_call | solution.py:320
  62.2 1.3 collective-permute-start.12
  63.4 1.8 %collective-permute-done.12.other_ref = bf16[2816,128]{1,0:T(8,128)(2,1)S(1)} collective-permute-done((bf16[2816,128]{1,0:T(8,128)(2,1)S(1)}, bf16[2816,128]{1,0:T(8,128)(2,1)S(1)}, u32[]{:S(2)}, u32[]{:S(2)}) %collective-permute-start.12) | collective-permute-done | bytes 720928 | tf_op jit(solution)/shard_map/ppermute | solution.py:332
  65.3 1.0 shard_map.116
  66.3 9.7 %all-to-all-start = ((bf16[16,176,128]{2,1,0:T(8,128)(2,1)}), bf16[16,176,128]{2,1,0:T(8,128)(2,1)S(1)}, u32[]{:S(2)}, u32[]{:S(2)}) async-start(bf16[16,176,128]{2,1,0:T(8,128)(2,1)} %bitcast), calls=%async_computation | async-start | bytes 1441792 | tf_op jit(solution)/shard_map/all_to_all | solution.py:337
  76.0 14.9 %shard_map.114 = (f32[1024,128]{1,0:T(8,128)S(1)}, bf16[64,128]{1,0:T(8,128)(2,1)S(1)}, bf16[64,128]{1,0:T(8,128)(2,1)S(1)}, bf16[64,128]{1,0:T(8,128)(2,1)S(1)}, bf16[64,128]{1,0:T(8,128)(2,1)S(1)}) custom-call(bf16[1024,128]{1,0:T(8,128)(2,1)S(1)} %get-tuple-element.33.pgrad_ref, s32[27,1024]{1,0:T(8,128)S(1)} %copy-done.4, bf16[27,128,128]{2,1,0:T(8,128)(2,1)S(1)} %copy-done), custom_call_target="tpu_custom_call" | custom-call | flops 20000000000 | bytes 4194304 | tf_op jit(solution)/shard_map/pallas_call | solution.py:320
  90.9 0.0 copy-start.7
  90.9 0.9 all-to-all-done
  91.9 0.1 shard_map.117
  92.0 24.6 %all_to_all.22 = bf16[16,176,128]{2,1,0:T(8,128)(2,1)S(1)} all-to-all(bf16[16,176,128]{2,1,0:T(8,128)(2,1)S(1)} %bitcast.9), channel_id=1, replica_groups={{0,2,4,6,8,10,12,14,16,18,20,22,24,26,28,30},{1,3,5,7,9,11,13,15,17,19,..., dimensions={0} | all-to-all | bytes 1441792 | tf_op jit(solution)/shard_map/all_to_all | solution.py:337
  116.6 2.5 %collective-permute-start.13 = (bf16[2816,128]{1,0:T(8,128)(2,1)S(1)}, bf16[2816,128]{1,0:T(8,128)(2,1)S(1)}, u32[]{:S(2)}, u32[]{:S(2)}) collective-permute-start(bf16[2816,128]{1,0:T(8,128)(2,1)S(1)} %bitcast.6), channel_id=1, source_target_pairs={{0,1},{1,0},{2,3},{3,2},{4,5},{5,4},{6,7},{7,6},{8,9},{9,8},{10,11... | collective-permute-start | bytes 2162696 | tf_op jit(solution)/shard_map/ppermute | solution.py:332
  119.1 1.9 %collective-permute-start.9 = (bf16[64,128]{1,0:T(8,128)(2,1)S(1)}, bf16[64,128]{1,0:T(8,128)(2,1)S(1)}, u32[]{:S(2)}, u32[]{:S(2)}) collective-permute-start(bf16[64,128]{1,0:T(8,128)(2,1)S(1)} %get-tuple-element.35), channel_id=1, source_target_pairs={{1,0},{2,1},{3,2},{4,3},{5,4},{6,5},{7,6},{8,7},{9,8},{10,9},{11,1... | collective-permute-start | bytes 49160 | tf_op jit(solution)/shard_map/ppermute | solution.py:26
  121.1 3.6 %collective-permute-start.10 = (bf16[64,128]{1,0:T(8,128)(2,1)S(1)}, bf16[64,128]{1,0:T(8,128)(2,1)S(1)}, u32[]{:S(2)}, u32[]{:S(2)}) collective-permute-start(bf16[64,128]{1,0:T(8,128)(2,1)S(1)} %get-tuple-element.36), channel_id=1, source_target_pairs={{0,1},{1,2},{2,3},{3,4},{4,5},{5,6},{6,7},{7,8},{8,9},{9,10},{10,1... | collective-permute-start | bytes 49160 | tf_op jit(solution)/shard_map/ppermute | solution.py:26
  124.7 3.1 %collective-permute-start.11 = (bf16[64,128]{1,0:T(8,128)(2,1)S(1)}, bf16[64,128]{1,0:T(8,128)(2,1)S(1)}, u32[]{:S(2)}, u32[]{:S(2)}) collective-permute-start(bf16[64,128]{1,0:T(8,128)(2,1)S(1)} %get-tuple-element.37), channel_id=1, source_target_pairs={{0,2},{1,3},{2,4},{3,5},{4,6},{5,7},{6,8},{7,9},{8,10},{9,11},{10,... | collective-permute-start | bytes 49160 | tf_op jit(solution)/shard_map/ppermute | solution.py:26
  127.8 1.3 collective-permute-start.8
  129.1 0.0 collective-permute-done.9.refs_1_
  129.1 0.0 collective-permute-done.10.refs_2_
  129.1 0.0 collective-permute-done.11.refs_3_
  129.1 3.2 %collective-permute-done.8.refs_0_ = bf16[64,128]{1,0:T(8,128)(2,1)S(1)} collective-permute-done((bf16[64,128]{1,0:T(8,128)(2,1)S(1)}, bf16[64,128]{1,0:T(8,128)(2,1)S(1)}, u32[]{:S(2)}, u32[]{:S(2)}) %collective-permute-start.8) | collective-permute-done | bytes 16416 | tf_op jit(solution)/shard_map/ppermute | solution.py:26
  132.3 0.0 copy-done.7
  132.3 1.2 shard_map.115
  133.5 0.0 collective-permute-done.13.other_ref
  133.5 1.8 %shard_map.118 = (f32[3456,128]{1,0:T(8,128)}, f32[1024,256]{1,0:T(8,128)}) custom-call(bf16[2816,128]{1,0:T(8,128)(2,1)S(1)} %bitcast.7, bf16[2816,128]{1,0:T(8,128)(2,1)S(1)} %collective-permute-done.13.other_ref), custom_call_target="tpu_custom_call" | custom-call | flops 1000000 | bytes 4194304 | tf_op jit(solution)/shard_map/pallas_call | solution.py:320
  (1 shorter events, 0.0 us)
Async XLA Ops:
  0.6 19.6 %copy-start.2 = (bf16[1024,128]{1,0:T(8,128)(2,1)S(1)}, bf16[1024,128]{1,0:T(8,128)(2,1)}, u32[]{:S(2)}) copy-start(bf16[1024,128]{1,0:T(8,128)(2,1)} %refs_4_.1) | copy-start | bytes 786436
  0.6 19.6 %copy-start.4 = (s32[27,1024]{1,0:T(8,128)S(1)}, s32[27,1024]{1,0:T(8,128)}, u32[]{:S(2)}) copy-start(s32[27,1024]{1,0:T(8,128)} %map_ref.1) | copy-start | bytes 331780
  0.7 19.5 %copy-start = (bf16[27,128,128]{2,1,0:T(8,128)(2,1)S(1)}, bf16[27,128,128]{2,1,0:T(8,128)(2,1)}, u32[]{:S(2)}) copy-start(bf16[27,128,128]{2,1,0:T(8,128)(2,1)} %weight_ref.1) | copy-start | bytes 2654212
  0.7 19.5 %copy-start.6 = (s32[4,32]{1,0:T(4,128)S(1)}, s32[4,32]{1,0:T(4,128)}, u32[]{:S(2)}) copy-start(s32[4,32]{1,0:T(4,128)} %refs_8_.1) | copy-start | bytes 1540
  6.1 12.9 %collective-permute-start = (bf16[96,128]{1,0:T(8,128)(2,1)}, bf16[96,128]{1,0:T(8,128)(2,1)S(1)}, u32[]{:S(2)}, u32[]{:S(2)}) collective-permute-start(bf16[96,128]{1,0:T(8,128)(2,1)} %get-tuple-element.24), channel_id=1, source_target_pairs={{2,0},{3,1},{4,2},{5,3},{6,4},{7,5},{8,6},{9,7},{10,8},{11,9},{12,... | collective-permute-start | bytes 73736 | tf_op jit(solution)/shard_map/ppermute | solution.py:26
  7.4 11.6 %collective-permute-start.1 = (bf16[96,128]{1,0:T(8,128)(2,1)}, bf16[96,128]{1,0:T(8,128)(2,1)S(1)}, u32[]{:S(2)}, u32[]{:S(2)}) collective-permute-start(bf16[96,128]{1,0:T(8,128)(2,1)} %get-tuple-element.25), channel_id=1, source_target_pairs={{1,0},{2,1},{3,2},{4,3},{5,4},{6,5},{7,6},{8,7},{9,8},{10,9},{11,1... | collective-permute-start | bytes 73736 | tf_op jit(solution)/shard_map/ppermute | solution.py:26
  9.4 9.7 %collective-permute-start.2 = (bf16[96,128]{1,0:T(8,128)(2,1)}, bf16[96,128]{1,0:T(8,128)(2,1)S(1)}, u32[]{:S(2)}, u32[]{:S(2)}) collective-permute-start(bf16[96,128]{1,0:T(8,128)(2,1)} %get-tuple-element.26), channel_id=1, source_target_pairs={{0,1},{1,2},{2,3},{3,4},{4,5},{5,6},{6,7},{7,8},{8,9},{9,10},{10,1... | collective-permute-start | bytes 73736 | tf_op jit(solution)/shard_map/ppermute | solution.py:26
  14.5 5.7 %collective-permute-start.3 = (bf16[96,128]{1,0:T(8,128)(2,1)}, bf16[96,128]{1,0:T(8,128)(2,1)S(1)}, u32[]{:S(2)}, u32[]{:S(2)}) collective-permute-start(bf16[96,128]{1,0:T(8,128)(2,1)} %get-tuple-element.27), channel_id=1, source_target_pairs={{0,2},{1,3},{2,4},{3,5},{4,6},{5,7},{6,8},{7,9},{8,10},{9,11},{10,... | collective-permute-start | bytes 73736 | tf_op jit(solution)/shard_map/ppermute | solution.py:26
  20.2 1.0 copy-start.8
  21.2 37.2 %copy-start.1 = (bf16[8,128,256]{2,1,0:T(8,128)(2,1)S(1)}, bf16[8,128,256]{2,1,0:T(8,128)(2,1)}, u32[]{:S(2)}) copy-start(bf16[8,128,256]{2,1,0:T(8,128)(2,1)} %refs_6_.4) | copy-start | bytes 1572868
  21.3 37.2 %copy-start.3 = (bf16[256,256]{1,0:T(8,128)(2,1)S(1)}, bf16[256,256]{1,0:T(8,128)(2,1)}, u32[]{:S(2)}) copy-start(bf16[256,256]{1,0:T(8,128)(2,1)} %refs_7_.1) | copy-start | bytes 393220
  21.3 37.2 %copy-start.5 = (s32[8,256]{1,0:T(8,128)S(1)}, s32[8,256]{1,0:T(8,128)}, u32[]{:S(2)}) copy-start(s32[8,256]{1,0:T(8,128)} %refs_5_.3) | copy-start | bytes 24580
  43.6 11.7 %collective-permute-start.7 = (bf16[32,128]{1,0:T(8,128)(2,1)S(1)}, bf16[32,128]{1,0:T(8,128)(2,1)S(1)}, u32[]{:S(2)}, u32[]{:S(2)}) collective-permute-start(bf16[32,128]{1,0:T(8,128)(2,1)S(1)} %get-tuple-element.44), channel_id=1, source_target_pairs={{0,2},{1,3},{2,4},{3,5},{4,6},{5,7},{6,8},{7,9},{8,10},{9,11},{10,... | collective-permute-start | bytes 24584 | tf_op jit(solution)/shard_map/ppermute | solution.py:26
  47.3 8.1 %collective-permute-start.6 = (bf16[32,128]{1,0:T(8,128)(2,1)S(1)}, bf16[32,128]{1,0:T(8,128)(2,1)S(1)}, u32[]{:S(2)}, u32[]{:S(2)}) collective-permute-start(bf16[32,128]{1,0:T(8,128)(2,1)S(1)} %get-tuple-element.45), channel_id=1, source_target_pairs={{0,1},{1,2},{2,3},{3,4},{4,5},{5,6},{6,7},{7,8},{8,9},{9,10},{10,1... | collective-permute-start | bytes 24584 | tf_op jit(solution)/shard_map/ppermute | solution.py:26
  52.1 5.0 %collective-permute-start.5 = (bf16[32,128]{1,0:T(8,128)(2,1)S(1)}, bf16[32,128]{1,0:T(8,128)(2,1)S(1)}, u32[]{:S(2)}, u32[]{:S(2)}) collective-permute-start(bf16[32,128]{1,0:T(8,128)(2,1)S(1)} %get-tuple-element.46), channel_id=1, source_target_pairs={{1,0},{2,1},{3,2},{4,3},{5,4},{6,5},{7,6},{8,7},{9,8},{10,9},{11,1... | collective-permute-start | bytes 24584 | tf_op jit(solution)/shard_map/ppermute | solution.py:26
  54.1 4.4 %collective-permute-start.4 = (bf16[32,128]{1,0:T(8,128)(2,1)S(1)}, bf16[32,128]{1,0:T(8,128)(2,1)S(1)}, u32[]{:S(2)}, u32[]{:S(2)}) collective-permute-start(bf16[32,128]{1,0:T(8,128)(2,1)S(1)} %get-tuple-element.47), channel_id=1, source_target_pairs={{2,0},{3,1},{4,2},{5,3},{6,4},{7,5},{8,6},{9,7},{10,8},{11,9},{12,... | collective-permute-start | bytes 24584 | tf_op jit(solution)/shard_map/ppermute | solution.py:26
  62.2 3.1 %collective-permute-start.12 = (bf16[2816,128]{1,0:T(8,128)(2,1)S(1)}, bf16[2816,128]{1,0:T(8,128)(2,1)S(1)}, u32[]{:S(2)}, u32[]{:S(2)}) collective-permute-start(bf16[2816,128]{1,0:T(8,128)(2,1)S(1)} %get-tuple-element.41), channel_id=1, source_target_pairs={{0,1},{1,0},{2,3},{3,2},{4,5},{5,4},{6,7},{7,6},{8,9},{9,8},{10,11... | collective-permute-start | bytes 2162696 | tf_op jit(solution)/shard_map/ppermute | solution.py:332
  66.3 25.6 %all-to-all-start = ((bf16[16,176,128]{2,1,0:T(8,128)(2,1)}), bf16[16,176,128]{2,1,0:T(8,128)(2,1)S(1)}, u32[]{:S(2)}, u32[]{:S(2)}) async-start(bf16[16,176,128]{2,1,0:T(8,128)(2,1)} %bitcast), calls=%async_computation | async-start | bytes 1441792 | tf_op jit(solution)/shard_map/all_to_all | solution.py:337
  90.9 41.4 %copy-start.7 = (s32[4,64]{1,0:T(4,128)S(1)}, s32[4,64]{1,0:T(4,128)}, u32[]{:S(2)}) copy-start(s32[4,64]{1,0:T(4,128)} %refs_6_.5) | copy-start | bytes 3076
  116.6 16.9 %collective-permute-start.13 = (bf16[2816,128]{1,0:T(8,128)(2,1)S(1)}, bf16[2816,128]{1,0:T(8,128)(2,1)S(1)}, u32[]{:S(2)}, u32[]{:S(2)}) collective-permute-start(bf16[2816,128]{1,0:T(8,128)(2,1)S(1)} %bitcast.6), channel_id=1, source_target_pairs={{0,1},{1,0},{2,3},{3,2},{4,5},{5,4},{6,7},{7,6},{8,9},{9,8},{10,11... | collective-permute-start | bytes 2162696 | tf_op jit(solution)/shard_map/ppermute | solution.py:332
  119.1 10.0 %collective-permute-start.9 = (bf16[64,128]{1,0:T(8,128)(2,1)S(1)}, bf16[64,128]{1,0:T(8,128)(2,1)S(1)}, u32[]{:S(2)}, u32[]{:S(2)}) collective-permute-start(bf16[64,128]{1,0:T(8,128)(2,1)S(1)} %get-tuple-element.35), channel_id=1, source_target_pairs={{1,0},{2,1},{3,2},{4,3},{5,4},{6,5},{7,6},{8,7},{9,8},{10,9},{11,1... | collective-permute-start | bytes 49160 | tf_op jit(solution)/shard_map/ppermute | solution.py:26
  121.1 8.1 %collective-permute-start.10 = (bf16[64,128]{1,0:T(8,128)(2,1)S(1)}, bf16[64,128]{1,0:T(8,128)(2,1)S(1)}, u32[]{:S(2)}, u32[]{:S(2)}) collective-permute-start(bf16[64,128]{1,0:T(8,128)(2,1)S(1)} %get-tuple-element.36), channel_id=1, source_target_pairs={{0,1},{1,2},{2,3},{3,4},{4,5},{5,6},{6,7},{7,8},{8,9},{9,10},{10,1... | collective-permute-start | bytes 49160 | tf_op jit(solution)/shard_map/ppermute | solution.py:26
  124.7 4.4 %collective-permute-start.11 = (bf16[64,128]{1,0:T(8,128)(2,1)S(1)}, bf16[64,128]{1,0:T(8,128)(2,1)S(1)}, u32[]{:S(2)}, u32[]{:S(2)}) collective-permute-start(bf16[64,128]{1,0:T(8,128)(2,1)S(1)} %get-tuple-element.37), channel_id=1, source_target_pairs={{0,2},{1,3},{2,4},{3,5},{4,6},{5,7},{6,8},{7,9},{8,10},{9,11},{10,... | collective-permute-start | bytes 49160 | tf_op jit(solution)/shard_map/ppermute | solution.py:26
  127.8 4.5 %collective-permute-start.8 = (bf16[64,128]{1,0:T(8,128)(2,1)S(1)}, bf16[64,128]{1,0:T(8,128)(2,1)S(1)}, u32[]{:S(2)}, u32[]{:S(2)}) collective-permute-start(bf16[64,128]{1,0:T(8,128)(2,1)S(1)} %get-tuple-element.34.after_ref), channel_id=1, source_target_pairs={{2,0},{3,1},{4,2},{5,3},{6,4},{7,5},{8,6},{9,7},{10,8},{11,9},{12,... | collective-permute-start | bytes 49160 | tf_op jit(solution)/shard_map/ppermute | solution.py:26

commit v3 on v2

--- a/solution.py
+++ b/solution.py
@@ -13,17 +13,43 @@
 LANES = 128
 
 
-def offsets_list(slot_count):
-    half_count = slot_count // 2
-    return [number - half_count for number in range(half_count)] + [
-        number + 1 for number in range(half_count)
-    ]
-
-
-def shift(value, axis, by):
-    count = lax.axis_size(axis)
-    pairs = [(i, i + by) for i in range(count) if 0 <= i + by < count]
-    return lax.ppermute(value, axis, pairs)
+def swaps(by_step, reach):
+    devices = lax.axis_size("shard")
+    moved = []
+    for m in range(1, reach + 1):
+        for phase in range(2):
+            sign = [1 if (i // m) % 2 == phase else -1 for i in range(devices)]
+            pairs = [(i, i + m * sign[i]) for i in range(devices) if 0 <= i + m * sign[i] < devices]
+            moved.append(lax.ppermute(by_step[len(moved)], "shard", pairs))
+    return moved
+
+
+def is_even(m):
+    return lax.rem(lax.div(lax.axis_index("shard"), m), 2) == 0
+
+
+def to_steps(slots, back):
+    reach = len(slots) // 2
+    steps = []
+    for m in range(1, reach + 1):
+        first, second = slots[reach + m - 1], slots[reach - m]
+        if back:
+            first, second = second, first
+        steps.append(lax.select(is_even(m), first, second))
+        steps.append(lax.select(is_even(m), second, first))
+    return steps
+
+
+def to_slots(steps, back):
+    reach = len(steps) // 2
+    slots = [None] * len(steps)
+    for m in range(1, reach + 1):
+        first = lax.select(is_even(m), steps[2 * m - 2], steps[2 * m - 1])
+        second = lax.select(is_even(m), steps[2 * m - 1], steps[2 * m - 2])
+        if back:
+            first, second = second, first
+        slots[reach - m], slots[reach + m - 1] = first, second
+    return slots
 
 
 def matmul(left, right):
@@ -102,8 +128,8 @@
     copies[0].wait()
     copies[1].wait()
     listed = gather_lists(halo_ref, features_ref[...]).astype(BF16)
-    for s in range(slots):
-        sends[s][0:cap, :] = listed[s * cap : (s + 1) * cap, :]
+    for send, block in zip(sends, to_steps(jnp.split(listed, slots), False)):
+        send[0:cap, :] = block
     for copy in copies[2:]:
         copy.wait()
     upstream = out_grad_ref[...]
@@ -117,10 +143,8 @@
         both = both + matmul(chooser, jnp.concatenate([high, low], axis=1))
     total = both[:, :LANES] + both[:, LANES:]
     back_ref[...] = total[:voxels]
-    for s in range(slots):
-        slot = slots - 1 - s
-        first = voxels + slot * cap2
-        sends[s][cap : cap + cap2, :] = total[first : first + cap2, :].astype(BF16)
+    for send, block in zip(sends, to_steps(jnp.split(total[voxels:].astype(BF16), slots), True)):
+        send[cap : cap + cap2, :] = block
 
 
 def half_codes(row, voxels, received):
@@ -137,9 +161,12 @@
 
 def forward_kernel(slots, *refs):
     received = refs[:slots]
-    (features_ref, map_ref, weight_ref, back_ref, child_ref) = refs[slots : slots + 5]
-    (hidden_ref, leaving_ref, hgrad_ref, pgrad_ref, cgrad_ref) = refs[slots + 5 : slots + 10]
-    (table_ref, stacked_ref, acc_ref) = refs[slots + 10 :]
+    (features_ref, map_ref, weight_ref, child_ref, back_hbm) = refs[slots : slots + 5]
+    (hidden_ref, hgrad_ref, pgrad_ref, cgrad_ref) = refs[slots + 5 : slots + 9]
+    sends = refs[slots + 9 : 2 * slots + 9]
+    (table_ref, stacked_ref, acc_ref, back_ref, sem) = refs[2 * slots + 9 :]
+    back_copy = pltpu.make_async_copy(back_hbm, back_ref, sem)
+    back_copy.start()
     voxels = features_ref.shape[0]
     kernel_count = map_ref.shape[0]
     middle = kernel_count // 2
@@ -149,10 +176,10 @@
     features = features_ref[...]
     table_ref[0:half, 0:LANES] = features[0:half]
     table_ref[0:half, LANES : 2 * LANES] = features[half:voxels]
-    for s in range(slots):
+    for s, block in enumerate(to_slots([r[0:cap, :] for r in received], False)):
         place = half + (s % (slots // 2)) * cap
         side = (s // (slots // 2)) * LANES
-        table_ref[place : place + cap, side : side + LANES] = received[s][0:cap, :]
+        table_ref[place : place + cap, side : side + LANES] = block
     table_rows = half + half_halo
 
     def gather(k):
@@ -177,12 +204,14 @@
     sig = jax.nn.sigmoid(pre)
     hidden = (features.astype(F32) + pre * sig).astype(BF16)
     hidden_ref[...] = hidden
-    leaving_ref[...] = gather_lists(child_ref, hidden).astype(BF16)
+    leaving = gather_lists(child_ref, hidden).astype(BF16)
+    for send, block in zip(sends, to_steps(jnp.split(leaving, slots), False)):
+        send[...] = block
+    back_copy.wait()
     hgrad = back_ref[...]
     lists = encode(child_ref[...]).astype(BF16)
-    for s in range(slots):
-        returned = received[slots - 1 - s][cap : cap + cap2, :]
-        hgrad = hgrad + matmul(one_hot_columns(lists[s : s + 1, :], voxels), returned)
+    for s, block in enumerate(to_slots([r[cap : cap + cap2, :] for r in received], True)):
+        hgrad = hgrad + matmul(one_hot_columns(lists[s : s + 1, :], voxels), block)
     hgrad_ref[...] = hgrad
     pgrad = hgrad * (sig * (1.0 + pre * (1.0 - sig)))
     pgrad_ref[...] = pgrad.astype(BF16)
@@ -203,7 +232,7 @@
     lax.fori_loop(0, middle, weight_step, 0)
 
 
-def spread_kernel(slots, pgrad_ref, map_ref, weight_ref, back_ref, *sends):
+def spread_kernel(slots, pgrad_ref, map_ref, weight_ref, after_ref, back_ref, *sends):
     acc_ref = sends[-1]
     sends = sends[:-1]
     voxels = pgrad_ref.shape[0]
@@ -235,11 +264,13 @@
     lax.fori_loop(0, middle, step, 0)
     back_ref[0:half, :] = acc_ref[0:half, 0:LANES]
     back_ref[half:, :] = acc_ref[0:half, LANES:]
+    blocks = []
     for s in range(slots):
-        slot = slots - 1 - s
-        first = half + (slot % (slots // 2)) * cap
-        side = (slot // (slots // 2)) * LANES
-        sends[s][...] = acc_ref[first : first + cap, side : side + LANES].astype(BF16)
+        first = half + (s % (slots // 2)) * cap
+        side = (s // (slots // 2)) * LANES
+        blocks.append(acc_ref[first : first + cap, side : side + LANES].astype(BF16))
+    for send, block in zip(sends, to_steps(blocks, True)):
+        send[...] = block
 
 
 def my_half(rows):
@@ -251,7 +282,7 @@
     received = refs[:slots]
     (hidden_ref, map_ref, down_ref, out_grad_ref, cgrad_ref) = refs[slots : slots + 5]
     coarse_ref, terms_ref, send_ref = refs[slots + 5 :]
-    table = jnp.concatenate([hidden_ref[...]] + [r[...] for r in received], axis=0)
+    table = jnp.concatenate([hidden_ref[...]] + to_slots([r[...] for r in received], False), axis=0)
     upstream = out_grad_ref[...]
     parents = upstream.shape[0]
     upstream_t = jnp.transpose(upstream.astype(F32)).astype(BF16)
@@ -279,14 +310,16 @@
     out_ref[...] = (mine + other_ref[...].astype(F32)).astype(BF16)
 
 
-def sum_kernel(groups, scale, parts_ref, after_ref, out_ref):
-    rows = parts_ref.shape[0] // groups
-    total = parts_ref[0:rows, :].astype(F32)
-    for d in range(1, groups):
-        total = total + parts_ref[d * rows : (d + 1) * rows, :].astype(F32)
-    total = (total * scale).astype(BF16)
-    for d in range(groups):
-        out_ref[d * rows : (d + 1) * rows, :] = total
+def sum_kernel(devices, scale, parts_ref, after_ref, out_ref):
+    rows = parts_ref.shape[0] // devices
+    for core in range(2):
+        mine = range(core, devices, 2)
+        total = jnp.zeros((rows, LANES), F32)
+        for d in mine:
+            total = total + parts_ref[d * rows : (d + 1) * rows, :].astype(F32)
+        total = (total * scale).astype(BF16)
+        for d in mine:
+            out_ref[d * rows : (d + 1) * rows, :] = total
 
 
 def final_kernel(mine_ref, other_ref, conv_ref, down_ref, whole_ref):
@@ -309,9 +342,8 @@
     voxels = hgrad_ref.shape[0]
     total = hgrad_ref[...] + back_ref[...]
     lists = encode(halo_ref[...]).astype(BF16)
-    for s in range(slots):
-        chooser = one_hot_columns(lists[s : s + 1, :], voxels)
-        total = total + matmul(chooser, received[slots - 1 - s][...])
+    for s, block in enumerate(to_slots([r[...] for r in received], True)):
+        total = total + matmul(one_hot_columns(lists[s : s + 1, :], voxels), block)
     out_ref[...] = total
 
 
@@ -332,9 +364,8 @@
     return lax.ppermute(value, "shard", [(i, i + 1 - 2 * (i % 2)) for i in range(devices)])
 
 
-def exchange(value, devices):
-    groups = [list(range(core, devices, 2)) for core in range(2)]
-    return lax.all_to_all(value, "shard", 0, 0, axis_index_groups=groups, tiled=True)
+def exchange(value):
+    return lax.all_to_all(value, "shard", 0, 0, tiled=True)
 
 
 def local(
@@ -346,7 +377,7 @@
     octants = down_weight.shape[0]
     slots, cap = halo_rows.shape
     cap2 = child_rows.shape[1]
-    offsets = offsets_list(slots)
+    reach = slots // 2
     devices = lax.axis_size("shard")
     scale = 1.0 / math.sqrt(voxels * devices)
     giga = 10**9
@@ -365,32 +396,33 @@
         in_hbm=range(5),
     )
     back_h = first[-1]
-    received = [shift(first[s], "shard", offsets[s]) for s in range(slots)]
+    received = swaps(first[:-1], reach)
     conv_rows = kernel_count * channels
     down_rows = octants * channels * coarse_channels // LANES
-    grain = 16 * devices
-    half_rows = -(-(conv_rows + down_rows) // grain) * grain // 2
-    hidden, leaving, hidden_grad, pre_grad, conv_terms = call(
+    grain = 8 * devices
+    half_rows = -(-(conv_rows + down_rows) // (2 * grain)) * grain
+    hidden, hidden_grad, pre_grad, conv_terms, *leaving = call(
         functools.partial(forward_kernel, slots),
-        (*received, features, neighbour_map, conv_weight, back_h, child_rows),
+        (*received, features, neighbour_map, conv_weight, child_rows, back_h),
         [
             ((voxels, channels), BF16),
-            ((slots * cap2, channels), BF16),
             ((voxels, channels), F32),
             ((voxels, channels), BF16),
             ((conv_rows, channels), BF16),
-        ],
+        ]
+        + [((cap2, channels), BF16)] * slots,
         scratch=[
             pltpu.VMEM((voxels // 2 + slots * cap // 2, 2 * channels), BF16),
             pltpu.VMEM((kernel_count, voxels, channels), BF16),
             pltpu.VMEM((voxels, channels), F32),
+            pltpu.VMEM((voxels, channels), F32),
+            pltpu.SemaphoreType.DMA(()),
         ],
         limit=48,
         flops=12 * giga,
-    )
-    received_h = [
-        shift(leaving[s * cap2 : (s + 1) * cap2], "shard", offsets[s]) for s in range(slots)
-    ]
+        in_hbm=(slots + 4,),
+    )
+    received_h = swaps(leaving, reach)
     coarse, terms, leaving_terms = call(
         functools.partial(down_kernel, slots),
         (*received_h, hidden, child_map, down_weight, out_grad, conv_terms),
@@ -407,29 +439,30 @@
         [((half_rows, LANES), BF16)],
         flops=10**6,
     )
-    parts = exchange(pair_terms, devices)
+    parts = exchange(pair_terms)
     spread = call(
         functools.partial(spread_kernel, slots),
-        (pre_grad, neighbour_map, conv_weight),
+        (pre_grad, neighbour_map, conv_weight, pair_terms),
         [((voxels, channels), F32)] + [((cap, channels), BF16)] * slots,
         scratch=[pltpu.VMEM((voxels // 2 + slots * cap // 2, 2 * channels), F32)],
         flops=20 * giga,
-    )
-    returned = [shift(spread[1 + s], "shard", offsets[s]) for s in range(slots)]
+        in_hbm=(3,),
+    )
+    (summed,) = call(
+        functools.partial(sum_kernel, devices, scale),
+        (parts, spread[1]),
+        [((half_rows, LANES), BF16)],
+        flops=10**6,
+        in_hbm=(1,),
+    )
+    summed, *returning = lax.optimization_barrier((summed, *spread[1:]))
+    mine, *returned = lax.optimization_barrier((exchange(summed), *swaps(returning, reach)))
     (input_grad,) = call(
         functools.partial(tail_kernel, slots),
         (*returned, hidden_grad, spread[0], halo_rows),
         [((voxels, channels), F32)],
         flops=giga,
     )
-    (summed,) = call(
-        functools.partial(sum_kernel, devices // 2, scale),
-        (parts, spread[1]),
-        [((half_rows, LANES), BF16)],
-        flops=10**6,
-        in_hbm=(1,),
-    )
-    mine = exchange(summed, devices)
     conv_grad, down_grad = call(
         final_kernel,
         (mine, swap_cores(mine, devices)),

time: 137 us -> 114 us (0.83)
  blocking collectives: 24.6 us -> 0 us
  waiting for transfers between devices: 10.1 us -> 21.4 us
  starting transfers between devices: 48 us -> 38.2 us
    all_to_all x1 -> x0, blocking collectives: 24.6 us -> none  [exchange(): lax.all_to_all(value, 'shard', 0, 0, axis_index_groups=groups, tiled=True)]
    all_to_all x1 -> x2, waiting for transfers between devices: 0.93 us -> 15.6 us  [exchange(): return lax.all_to_all(value, 'shard', 0, 0, tiled=True)]
    ppermute x12, starting transfers between devices: 34.5 us -> 22.1 us  [swaps(): moved.append(lax.ppermute(by_step[len(moved)], 'shard', pairs))]
    all_to_all x1 -> x2, starting transfers between devices: 9.7 us -> 15.4 us  [exchange(): return lax.all_to_all(value, 'shard', 0, 0, tiled=True)]
    ppermute x12, waiting for transfers between devices: 7.35 us -> 3.06 us  [swaps(): moved.append(lax.ppermute(by_step[len(moved)], 'shard', pairs))]
    ppermute x2, starting transfers between devices: 3.8 us -> 0.69 us  [swap_cores(): lax.ppermute(value, 'shard', [(i, i + 1 - 2 * (i % 2)) for i in range(dev...]
  transfers between devices with their start and end apart: 15 -> 16, of which waited for: 6 -> 8; matrix products, arithmetic and copies ran while one was open for 0% -> 0% of each run, Pallas kernels for 12% -> 14%
where the time goes in v3:
time: 114 us; the launch traced here: 113 us
  Pallas kernels  51.7 us (45%)
  starting transfers between devices  38.2 us (34%)
  waiting for transfers between devices  21.4 us (19%)
    pallas_call x8, Pallas kernels, call(): pl.pallas_call(kernel, out_shape=[jax.ShapeDtypeStruct(s, d) for s, d in...  51.7 us
    ppermute x12, starting transfers between devices, swaps(): moved.append(lax.ppermute(by_step[len(moved)], 'shard', pairs))  22.1 us
    all_to_all x2, waiting for transfers between devices, exchange(): return lax.all_to_all(value, 'shard', 0, 0, tiled=True)  15.6 us
    all_to_all x2, starting transfers between devices, exchange(): return lax.all_to_all(value, 'shard', 0, 0, tiled=True)  15.4 us
    ppermute x12, waiting for transfers between devices, swaps(): moved.append(lax.ppermute(by_step[len(moved)], 'shard', pairs))  3.06 us
    ppermute x2, waiting for transfers between devices, swap_cores(): lax.ppermute(value, 'shard', [(i, i + 1 - 2 * (i % 2)) for i in range(dev...  2.77 us
  transfers between devices with their start and end apart: 16, of which 8 were waited for; matrix products, arithmetic and copies ran while one was open for 0% of the time, Pallas kernels for 14%

profile of v3, /device:TPU:1, one launch (start us, length us, event | category | flops | bytes accessed | tf_op | source)
XLA Modules:
  0.0 113.2 jit_solution(7526298724316267224)
XLA Ops:
  0.6 0.0 copy-start.2
  0.6 0.0 copy-start.4
  0.7 0.0 copy-start
  0.7 0.0 copy-start.6
  0.7 5.5 %shard_map.111 = (bf16[96,128]{1,0:T(8,128)(2,1)}, bf16[96,128]{1,0:T(8,128)(2,1)}, bf16[96,128]{1,0:T(8,128)(2,1)}, bf16[96,128]{1,0:T(8,128)(2,1)}, f32[1024,128]{1,0:T(8,128)}) custom-call(bf16[1024,128]{1,0:T(8,128)(2,1)} %refs_4_.1, s32[4,64]{1,0:T(4,128)} %refs_6_.5, s32[8,256]{1,0:T(8,128)} %refs_5_.3, bf16[256,256]{1,0:T(8,128)(2,1)} %refs_7_.3, ...), custom_call_target="tpu_custom_call" | custom-call | flops 1000000000 | bytes 4194304 | tf_op jit(solution)/shard_map/pallas_call | solution.py:352
  6.2 0.1 collective-permute-start
  6.3 4.5 %collective-permute-start.1 = (bf16[96,128]{1,0:T(8,128)(2,1)}, bf16[96,128]{1,0:T(8,128)(2,1)S(1)}, u32[]{:S(2)}, u32[]{:S(2)}) collective-permute-start(bf16[96,128]{1,0:T(8,128)(2,1)} %get-tuple-element.38), channel_id=1, source_target_pairs={{1,2},{2,1},{3,4},{4,3},{5,6},{6,5},{7,8},{8,7},{9,10},{10,9},{11,... | collective-permute-start | bytes 73736 | tf_op jit(solution)/shard_map/ppermute | solution.py:23
  10.8 1.3 %collective-permute-start.2 = (bf16[96,128]{1,0:T(8,128)(2,1)}, bf16[96,128]{1,0:T(8,128)(2,1)S(1)}, u32[]{:S(2)}, u32[]{:S(2)}) collective-permute-start(bf16[96,128]{1,0:T(8,128)(2,1)} %get-tuple-element.39), channel_id=1, source_target_pairs={{0,2},{1,3},{2,0},{3,1},{4,6},{5,7},{6,4},{7,5},{8,10},{9,11},{10,... | collective-permute-start | bytes 73736 | tf_op jit(solution)/shard_map/ppermute | solution.py:23
  12.1 0.7 collective-permute-start.3
  12.7 0.0 collective-permute-done.refs_0_
  12.7 0.0 collective-permute-done.1.refs_1_
  12.7 1.0 collective-permute-done.2.refs_2_
  13.7 0.0 collective-permute-done.3.refs_3_
  13.7 0.0 copy-done.2
  13.7 0.0 copy-done.4
  13.7 0.0 copy-done
  13.7 0.0 copy-done.6
  13.8 0.0 copy-start.8
  13.8 1.0 copy-done.8
  14.8 0.0 copy-start.1
  14.8 0.0 copy-start.3
  14.8 0.0 copy-start.5
  14.8 22.6 %shard_map.112 = (bf16[1024,128]{1,0:T(8,128)(2,1)S(1)}, f32[1024,128]{1,0:T(8,128)S(1)}, bf16[1024,128]{1,0:T(8,128)(2,1)S(1)}, bf16[3456,128]{1,0:T(8,128)(2,1...) custom-call(bf16[96,128]{1,0:T(8,128)(2,1)S(1)} %collective-permute-, ...), custom_call_target="tpu_custom_call" | custom-call | flops 12000000000 | bytes 4194304 | tf_op jit(solution)/shard_map/pallas_call | solution.py:352
  37.4 0.1 collective-permute-start.4
  37.4 6.7 %collective-permute-start.5 = (bf16[32,128]{1,0:T(8,128)(2,1)S(1)}, bf16[32,128]{1,0:T(8,128)(2,1)S(1)}, u32[]{:S(2)}, u32[]{:S(2)}) collective-permute-start(bf16[32,128]{1,0:T(8,128)(2,1)S(1)} %get-tuple-element.43), channel_id=1, source_target_pairs={{1,2},{2,1},{3,4},{4,3},{5,6},{6,5},{7,8},{8,7},{9,10},{10,9},{11,... | collective-permute-start | bytes 24584 | tf_op jit(solution)/shard_map/ppermute | solution.py:23
  44.1 2.5 %collective-permute-start.6 = (bf16[32,128]{1,0:T(8,128)(2,1)S(1)}, bf16[32,128]{1,0:T(8,128)(2,1)S(1)}, u32[]{:S(2)}, u32[]{:S(2)}) collective-permute-start(bf16[32,128]{1,0:T(8,128)(2,1)S(1)} %get-tuple-element.44), channel_id=1, source_target_pairs={{0,2},{1,3},{2,0},{3,1},{4,6},{5,7},{6,4},{7,5},{8,10},{9,11},{10,... | collective-permute-start | bytes 24584 | tf_op jit(solution)/shard_map/ppermute | solution.py:23
  46.7 0.6 collective-permute-start.7
  47.3 0.0 collective-permute-done.4.refs_0_
  47.4 0.0 collective-permute-done.5.refs_1_
  47.4 0.4 collective-permute-done.6.refs_2_
  47.7 0.0 collective-permute-done.7.refs_3_
  47.7 0.0 copy-done.1
  47.7 0.0 copy-done.3
  47.7 0.0 copy-done.5
  47.7 3.7 %shard_map.113 = (bf16[256,256]{1,0:T(8,128)(2,1)}, bf16[5632,128]{1,0:T(8,128)(2,1)S(1)}, bf16[2816,128]{1,0:T(8,128)(2,1)S(1)}) custom-call(bf16[32,128]{1,0:T(8,128)(2,1)S(1)} %collective-permute-done.4.refs_0_, bf16[32,128]{1,0:T(8,128)(2,1)S(1)} %collective-permute-done.5.refs_1_, bf16[32,128]{1,0:T(8,128)(2,1)S(1)} %collective-permute-done.6.refs_2_, ...), custom_call_target="tpu_custom_call" | custom-call | flops 2000000000 | bytes 4194304 | tf_op jit(solution)/shard_map/pallas_call | solution.py:352
  51.4 0.0 collective-permute-start.8
  51.5 2.2 %collective-permute-done.8.other_ref = bf16[2816,128]{1,0:T(8,128)(2,1)S(1)} collective-permute-done((bf16[2816,128]{1,0:T(8,128)(2,1)S(1)}, bf16[2816,128]{1,0:T(8,128)(2,1)S(1)}, u32[]{:S(2)}, u32[]{:S(2)}) %collective-permute-start.8) | collective-permute-done | bytes 720928 | tf_op jit(solution)/shard_map/ppermute | solution.py:364
  53.6 1.0 shard_map.114.after_ref
  54.7 11.5 %all-to-all-start = ((bf16[32,88,128]{2,1,0:T(8,128)(2,1)}), bf16[32,88,128]{2,1,0:T(8,128)(2,1)S(1)}, u32[]{:S(2)}, u32[]{:S(2)}) async-start(bf16[32,88,128]{2,1,0:T(8,128)(2,1)} %bitcast), calls=%async_computation | async-start | bytes 1441792 | tf_op jit(solution)/shard_map/all_to_all | solution.py:368
  66.2 14.9 %shard_map.115 = (f32[1024,128]{1,0:T(8,128)S(1)}, bf16[64,128]{1,0:T(8,128)(2,1)S(1)}, bf16[64,128]{1,0:T(8,128)(2,1)S(1)}, bf16[64,128]{1,0:T(8,128)(2,1)S(1)}, bf16[64,128]{1,0:T(8,128)(2,1)S(1)}) custom-call(bf16[1024,128]{1,0:T(8,128)(2,1)S(1)} %get-tuple-element.51.pgrad_ref, s32[27,1024]{1,0:T(8,128)S(1)} %copy-done.4, ...), custom_call_target="tpu_custom_call" | custom-call | flops 20000000000 | bytes 4194304 | tf_op jit(solution)/shard_map/pallas_call | solution.py:352
  81.1 0.0 copy-start.7
  81.1 4.0 %all-to-all-done = bf16[32,88,128]{2,1,0:T(8,128)(2,1)S(1)} async-done(((bf16[32,88,128]{2,1,0:T(8,128)(2,1)}), bf16[32,88,128]{2,1,0:T(8,128)(2,1)S(1)}, u32[]{:S(2)}, u32[]{:S(2)}) %all-to-all-start) | async-done | bytes 720928 | tf_op jit(solution)/shard_map/all_to_all | solution.py:368
  85.2 1.0 shard_map.116
  86.1 3.9 %all-to-all-start.1 = ((bf16[32,88,128]{2,1,0:T(8,128)(2,1)}), bf16[32,88,128]{2,1,0:T(8,128)(2,1)S(1)}, u32[]{:S(2)}, u32[]{:S(2)}) async-start(bf16[32,88,128]{2,1,0:T(8,128)(2,1)} %bitcast.2), calls=%async_computation.1 | async-start | bytes 1441792 | tf_op jit(solution)/shard_map/all_to_all | solution.py:368
  90.0 0.3 collective-permute-start.9
  90.3 3.4 %collective-permute-start.10 = (bf16[64,128]{1,0:T(8,128)(2,1)S(1)}, bf16[64,128]{1,0:T(8,128)(2,1)S(1)}, u32[]{:S(2)}, u32[]{:S(2)}) collective-permute-start(bf16[64,128]{1,0:T(8,128)(2,1)S(1)} %get-tuple-element.58), channel_id=1, source_target_pairs={{1,2},{2,1},{3,4},{4,3},{5,6},{6,5},{7,8},{8,7},{9,10},{10,9},{11,... | collective-permute-start | bytes 49160 | tf_op jit(solution)/shard_map/ppermute | solution.py:23
  93.7 1.2 %collective-permute-start.11 = (bf16[64,128]{1,0:T(8,128)(2,1)S(1)}, bf16[64,128]{1,0:T(8,128)(2,1)S(1)}, u32[]{:S(2)}, u32[]{:S(2)}) collective-permute-start(bf16[64,128]{1,0:T(8,128)(2,1)S(1)} %get-tuple-element.59), channel_id=1, source_target_pairs={{0,2},{1,3},{2,0},{3,1},{4,6},{5,7},{6,4},{7,5},{8,10},{9,11},{10,... | collective-permute-start | bytes 49160 | tf_op jit(solution)/shard_map/ppermute | solution.py:23
  95.0 0.7 collective-permute-start.12
  95.7 0.0 collective-permute-done.9.refs_0_
  95.7 0.1 collective-permute-done.10.refs_1_
  95.7 1.6 %collective-permute-done.11.refs_2_ = bf16[64,128]{1,0:T(8,128)(2,1)S(1)} collective-permute-done((bf16[64,128]{1,0:T(8,128)(2,1)S(1)}, bf16[64,128]{1,0:T(8,128)(2,1)S(1)}, u32[]{:S(2)}, u32[]{:S(2)}) %collective-permute-start.11) | collective-permute-done | bytes 16416 | tf_op jit(solution)/shard_map/ppermute | solution.py:23
  97.4 0.0 collective-permute-done.12.refs_3_
  97.4 11.6 %all-to-all-done.1 = bf16[32,88,128]{2,1,0:T(8,128)(2,1)S(1)} async-done(((bf16[32,88,128]{2,1,0:T(8,128)(2,1)}), bf16[32,88,128]{2,1,0:T(8,128)(2,1)S(1)}, u32[]{:S(2)}, u32[]{:S(2)}) %all-to-all-start.1) | async-done | bytes 720928 | tf_op jit(solution)/shard_map/all_to_all | solution.py:368
  109.0 0.7 collective-permute-start.13
  109.6 0.0 copy-done.7
  109.6 1.2 %shard_map.117 = f32[1024,128]{1,0:T(8,128)} custom-call(bf16[64,128]{1,0:T(8,128)(2,1)S(1)} %collective-permute-done.9.refs_0_, bf16[64,128]{1,0:T(8,128)(2,1)S(1)} %collective-permute-done.10.refs_1_, bf16[64,128]{1,0:T(8,128)(2,1)S(1)} %collective-permute-done.11.refs_2_, bf16[64,128]{1,0:T(8,128)(2,1)S(1)} %collective-permute-done.12.refs_3_, ...), custom_call_target="tpu_custom_call" | custom-call | flops 1000000000 | bytes 4194304 | tf_op jit(solution)/shard_map/pallas_call | solution.py:352
  110.9 0.6 collective-permute-done.13.other_ref
  111.5 1.8 %shard_map.118 = (f32[3456,128]{1,0:T(8,128)}, f32[1024,256]{1,0:T(8,128)}) custom-call(bf16[2816,128]{1,0:T(8,128)(2,1)S(1)} %bitcast.7, bf16[2816,128]{1,0:T(8,128)(2,1)S(1)} %collective-permute-done.13.other_ref), custom_call_target="tpu_custom_call" | custom-call | flops 1000000 | bytes 4194304 | tf_op jit(solution)/shard_map/pallas_call | solution.py:352
Async XLA Ops:
  0.6 13.1 %copy-start.2 = (bf16[1024,128]{1,0:T(8,128)(2,1)S(1)}, bf16[1024,128]{1,0:T(8,128)(2,1)}, u32[]{:S(2)}) copy-start(bf16[1024,128]{1,0:T(8,128)(2,1)} %refs_4_.1) | copy-start | bytes 786436
  0.6 13.1 %copy-start.4 = (s32[27,1024]{1,0:T(8,128)S(1)}, s32[27,1024]{1,0:T(8,128)}, u32[]{:S(2)}) copy-start(s32[27,1024]{1,0:T(8,128)} %map_ref.1) | copy-start | bytes 331780
  0.7 13.1 %copy-start = (bf16[27,128,128]{2,1,0:T(8,128)(2,1)S(1)}, bf16[27,128,128]{2,1,0:T(8,128)(2,1)}, u32[]{:S(2)}) copy-start(bf16[27,128,128]{2,1,0:T(8,128)(2,1)} %weight_ref.1) | copy-start | bytes 2654212
  0.7 13.1 %copy-start.6 = (s32[4,32]{1,0:T(4,128)S(1)}, s32[4,32]{1,0:T(4,128)}, u32[]{:S(2)}) copy-start(s32[4,32]{1,0:T(4,128)} %refs_7_.2) | copy-start | bytes 1540
  6.2 6.5 %collective-permute-start = (bf16[96,128]{1,0:T(8,128)(2,1)}, bf16[96,128]{1,0:T(8,128)(2,1)S(1)}, u32[]{:S(2)}, u32[]{:S(2)}) collective-permute-start(bf16[96,128]{1,0:T(8,128)(2,1)} %get-tuple-element.37), channel_id=1, source_target_pairs={{0,1},{1,0},{2,3},{3,2},{4,5},{5,4},{6,7},{7,6},{8,9},{9,8},{10,11... | collective-permute-start | bytes 73736 | tf_op jit(solution)/shard_map/ppermute | solution.py:23
  6.3 6.4 %collective-permute-start.1 = (bf16[96,128]{1,0:T(8,128)(2,1)}, bf16[96,128]{1,0:T(8,128)(2,1)S(1)}, u32[]{:S(2)}, u32[]{:S(2)}) collective-permute-start(bf16[96,128]{1,0:T(8,128)(2,1)} %get-tuple-element.38), channel_id=1, source_target_pairs={{1,2},{2,1},{3,4},{4,3},{5,6},{6,5},{7,8},{8,7},{9,10},{10,9},{11,... | collective-permute-start | bytes 73736 | tf_op jit(solution)/shard_map/ppermute | solution.py:23
  10.8 3.0 %collective-permute-start.2 = (bf16[96,128]{1,0:T(8,128)(2,1)}, bf16[96,128]{1,0:T(8,128)(2,1)S(1)}, u32[]{:S(2)}, u32[]{:S(2)}) collective-permute-start(bf16[96,128]{1,0:T(8,128)(2,1)} %get-tuple-element.39), channel_id=1, source_target_pairs={{0,2},{1,3},{2,0},{3,1},{4,6},{5,7},{6,4},{7,5},{8,10},{9,11},{10,... | collective-permute-start | bytes 73736 | tf_op jit(solution)/shard_map/ppermute | solution.py:23
  12.1 1.7 %collective-permute-start.3 = (bf16[96,128]{1,0:T(8,128)(2,1)}, bf16[96,128]{1,0:T(8,128)(2,1)S(1)}, u32[]{:S(2)}, u32[]{:S(2)}) collective-permute-start(bf16[96,128]{1,0:T(8,128)(2,1)} %get-tuple-element.40), channel_id=1, source_target_pairs={{2,4},{3,5},{4,2},{5,3},{6,8},{7,9},{8,6},{9,7},{10,12},{11,13},{1... | collective-permute-start | bytes 73736 | tf_op jit(solution)/shard_map/ppermute | solution.py:23
  13.8 1.0 copy-start.8
  14.8 32.9 %copy-start.1 = (bf16[8,128,256]{2,1,0:T(8,128)(2,1)S(1)}, bf16[8,128,256]{2,1,0:T(8,128)(2,1)}, u32[]{:S(2)}) copy-start(bf16[8,128,256]{2,1,0:T(8,128)(2,1)} %refs_6_.4) | copy-start | bytes 1572868
  14.8 32.9 %copy-start.3 = (bf16[256,256]{1,0:T(8,128)(2,1)S(1)}, bf16[256,256]{1,0:T(8,128)(2,1)}, u32[]{:S(2)}) copy-start(bf16[256,256]{1,0:T(8,128)(2,1)} %refs_7_.3) | copy-start | bytes 393220
  14.8 32.9 %copy-start.5 = (s32[8,256]{1,0:T(8,128)S(1)}, s32[8,256]{1,0:T(8,128)}, u32[]{:S(2)}) copy-start(s32[8,256]{1,0:T(8,128)} %refs_5_.3) | copy-start | bytes 24580
  37.4 10.0 %collective-permute-start.4 = (bf16[32,128]{1,0:T(8,128)(2,1)S(1)}, bf16[32,128]{1,0:T(8,128)(2,1)S(1)}, u32[]{:S(2)}, u32[]{:S(2)}) collective-permute-start(bf16[32,128]{1,0:T(8,128)(2,1)S(1)} %get-tuple-element.42), channel_id=1, source_target_pairs={{0,1},{1,0},{2,3},{3,2},{4,5},{5,4},{6,7},{7,6},{8,9},{9,8},{10,11... | collective-permute-start | bytes 24584 | tf_op jit(solution)/shard_map/ppermute | solution.py:23
  37.4 9.9 %collective-permute-start.5 = (bf16[32,128]{1,0:T(8,128)(2,1)S(1)}, bf16[32,128]{1,0:T(8,128)(2,1)S(1)}, u32[]{:S(2)}, u32[]{:S(2)}) collective-permute-start(bf16[32,128]{1,0:T(8,128)(2,1)S(1)} %get-tuple-element.43), channel_id=1, source_target_pairs={{1,2},{2,1},{3,4},{4,3},{5,6},{6,5},{7,8},{8,7},{9,10},{10,9},{11,... | collective-permute-start | bytes 24584 | tf_op jit(solution)/shard_map/ppermute | solution.py:23
  44.1 3.6 %collective-permute-start.6 = (bf16[32,128]{1,0:T(8,128)(2,1)S(1)}, bf16[32,128]{1,0:T(8,128)(2,1)S(1)}, u32[]{:S(2)}, u32[]{:S(2)}) collective-permute-start(bf16[32,128]{1,0:T(8,128)(2,1)S(1)} %get-tuple-element.44), channel_id=1, source_target_pairs={{0,2},{1,3},{2,0},{3,1},{4,6},{5,7},{6,4},{7,5},{8,10},{9,11},{10,... | collective-permute-start | bytes 24584 | tf_op jit(solution)/shard_map/ppermute | solution.py:23
  46.7 1.0 collective-permute-start.7
  51.4 2.2 %collective-permute-start.8 = (bf16[2816,128]{1,0:T(8,128)(2,1)S(1)}, bf16[2816,128]{1,0:T(8,128)(2,1)S(1)}, u32[]{:S(2)}, u32[]{:S(2)}) collective-permute-start(bf16[2816,128]{1,0:T(8,128)(2,1)S(1)} %get-tuple-element.50), channel_id=1, source_target_pairs={{0,1},{1,0},{2,3},{3,2},{4,5},{5,4},{6,7},{7,6},{8,9},{9,8},{10,11... | collective-permute-start | bytes 2162696 | tf_op jit(solution)/shard_map/ppermute | solution.py:364
  54.7 30.5 %all-to-all-start = ((bf16[32,88,128]{2,1,0:T(8,128)(2,1)}), bf16[32,88,128]{2,1,0:T(8,128)(2,1)S(1)}, u32[]{:S(2)}, u32[]{:S(2)}) async-start(bf16[32,88,128]{2,1,0:T(8,128)(2,1)} %bitcast), calls=%async_computation | async-start | bytes 1441792 | tf_op jit(solution)/shard_map/all_to_all | solution.py:368
  81.1 28.5 %copy-start.7 = (s32[4,64]{1,0:T(4,128)S(1)}, s32[4,64]{1,0:T(4,128)}, u32[]{:S(2)}) copy-start(s32[4,64]{1,0:T(4,128)} %refs_6_.5) | copy-start | bytes 3076
  86.1 22.8 %all-to-all-start.1 = ((bf16[32,88,128]{2,1,0:T(8,128)(2,1)}), bf16[32,88,128]{2,1,0:T(8,128)(2,1)S(1)}, u32[]{:S(2)}, u32[]{:S(2)}) async-start(bf16[32,88,128]{2,1,0:T(8,128)(2,1)} %bitcast.2), calls=%async_computation.1 | async-start | bytes 1441792 | tf_op jit(solution)/shard_map/all_to_all | solution.py:368
  90.0 5.7 %collective-permute-start.9 = (bf16[64,128]{1,0:T(8,128)(2,1)S(1)}, bf16[64,128]{1,0:T(8,128)(2,1)S(1)}, u32[]{:S(2)}, u32[]{:S(2)}) collective-permute-start(bf16[64,128]{1,0:T(8,128)(2,1)S(1)} %get-tuple-element.57.after_ref), channel_id=1, source_target_pairs={{0,1},{1,0},{2,3},{3,2},{4,5},{5,4},{6,7},{7,6},{8,9},{9,8},{10,11... | collective-permute-start | bytes 49160 | tf_op jit(solution)/shard_map/ppermute | solution.py:23
  90.3 5.4 %collective-permute-start.10 = (bf16[64,128]{1,0:T(8,128)(2,1)S(1)}, bf16[64,128]{1,0:T(8,128)(2,1)S(1)}, u32[]{:S(2)}, u32[]{:S(2)}) collective-permute-start(bf16[64,128]{1,0:T(8,128)(2,1)S(1)} %get-tuple-element.58), channel_id=1, source_target_pairs={{1,2},{2,1},{3,4},{4,3},{5,6},{6,5},{7,8},{8,7},{9,10},{10,9},{11,... | collective-permute-start | bytes 49160 | tf_op jit(solution)/shard_map/ppermute | solution.py:23
  93.7 3.6 %collective-permute-start.11 = (bf16[64,128]{1,0:T(8,128)(2,1)S(1)}, bf16[64,128]{1,0:T(8,128)(2,1)S(1)}, u32[]{:S(2)}, u32[]{:S(2)}) collective-permute-start(bf16[64,128]{1,0:T(8,128)(2,1)S(1)} %get-tuple-element.59), channel_id=1, source_target_pairs={{0,2},{1,3},{2,0},{3,1},{4,6},{5,7},{6,4},{7,5},{8,10},{9,11},{10,... | collective-permute-start | bytes 49160 | tf_op jit(solution)/shard_map/ppermute | solution.py:23
  95.0 2.4 %collective-permute-start.12 = (bf16[64,128]{1,0:T(8,128)(2,1)S(1)}, bf16[64,128]{1,0:T(8,128)(2,1)S(1)}, u32[]{:S(2)}, u32[]{:S(2)}) collective-permute-start(bf16[64,128]{1,0:T(8,128)(2,1)S(1)} %get-tuple-element.60), channel_id=1, source_target_pairs={{2,4},{3,5},{4,2},{5,3},{6,8},{7,9},{8,6},{9,7},{10,12},{11,13},{1... | collective-permute-start | bytes 49160 | tf_op jit(solution)/shard_map/ppermute | solution.py:23
  109.0 2.5 %collective-permute-start.13 = (bf16[2816,128]{1,0:T(8,128)(2,1)S(1)}, bf16[2816,128]{1,0:T(8,128)(2,1)S(1)}, u32[]{:S(2)}, u32[]{:S(2)}) collective-permute-start(bf16[2816,128]{1,0:T(8,128)(2,1)S(1)} %bitcast.6), channel_id=1, source_target_pairs={{0,1},{1,0},{2,3},{3,2},{4,5},{5,4},{6,7},{7,6},{8,9},{9,8},{10,11... | collective-permute-start | bytes 2162696 | tf_op jit(solution)/shard_map/ppermute | solution.py:364

commit v4 on v3

--- a/solution.py
+++ b/solution.py
@@ -89,6 +89,11 @@
     place = lax.broadcasted_iota(jnp.int32, (height, codes.shape[1]), 0)
     pattern = encode(place).astype(BF16)
     return pick_one(jnp.broadcast_to(codes, pattern.shape) == pattern)
+
+
+def pick_rows(col, table):
+    both = matmul(one_hot_rows(jnp.abs(col), table.shape[0]), table).astype(BF16)
+    return jnp.where(col < jnp.zeros(col.shape, BF16), both[:, LANES:], both[:, :LANES])
 
 
 def list_row(lists, first, per_row):
@@ -183,10 +188,8 @@
     table_rows = half + half_halo
 
     def gather(k):
-        col = column(half_codes(map_ref[pl.ds(k, 1), :], voxels, slots * cap))
-        chooser = one_hot_rows(jnp.abs(col).astype(BF16), table_rows)
-        both = matmul(chooser, table_ref[...])
-        picked = jnp.where(col < 0.0, both[:, LANES:], both[:, :LANES]).astype(BF16)
+        codes = half_codes(map_ref[pl.ds(k, 1), :], voxels, slots * cap).astype(BF16)
+        picked = pick_rows(column(codes), table_ref[...])
         stacked_ref[k] = picked
         return picked
 
@@ -233,8 +236,8 @@
 
 
 def spread_kernel(slots, pgrad_ref, map_ref, weight_ref, after_ref, back_ref, *sends):
-    acc_ref = sends[-1]
-    sends = sends[:-1]
+    acc_ref, codes_ref = sends[-2:]
+    sends = sends[:-2]
     voxels = pgrad_ref.shape[0]
     kernel_count = map_ref.shape[0]
     middle = kernel_count // 2
@@ -247,17 +250,29 @@
     acc_ref[0:half, LANES:] = own[half:]
     acc_ref[half:, :] = jnp.zeros((table_rows - half, 2 * LANES), F32)
 
-    def parts(k):
-        codes = half_codes(map_ref[pl.ds(k, 1), :], voxels, slots * cap)
+    codes_ref[...] = jnp.zeros(codes_ref.shape, F32)
+    codes_ref[0:kernel_count, :] = half_codes(map_ref[...], voxels, slots * cap)
+    turned = jnp.concatenate(
+        [
+            jnp.transpose(codes_ref[:, first : first + LANES]).astype(BF16)
+            for first in range(0, voxels, LANES)
+        ],
+        axis=0,
+    )
+    number = lax.broadcasted_iota(jnp.int32, (LANES, LANES), 0)
+
+    def parts(k, spread_codes):
         terms = matmul_rt(pgrad, weight_ref[k])
-        right = column(codes) < 0.0
+        right = spread_codes < 0.0
         sides = [jnp.where(right, 0.0, terms), jnp.where(right, terms, 0.0)]
-        chooser = one_hot_columns(jnp.abs(codes).astype(BF16), table_rows)
-        return chooser, jnp.concatenate(sides, axis=1).astype(BF16)
+        codes = jnp.abs(codes_ref[pl.ds(k, 1), :]).astype(BF16)
+        return one_hot_columns(codes, table_rows), jnp.concatenate(sides, axis=1).astype(BF16)
 
     def step(j, carry):
-        near_chooser, near_terms = parts(j)
-        far_chooser, far_terms = parts(j + middle + 1)
+        chosen = [pick_one(number == k) for k in (j, j + middle + 1)]
+        both = matmul(turned, jnp.concatenate(chosen, axis=1))
+        near_chooser, near_terms = parts(j, both[:, :LANES])
+        far_chooser, far_terms = parts(j + middle + 1, both[:, LANES:])
         acc_ref[...] += matmul(near_chooser, near_terms) + matmul(far_chooser, far_terms)
         return carry
 
@@ -281,24 +296,36 @@
 def down_kernel(slots, *refs):
     received = refs[:slots]
     (hidden_ref, map_ref, down_ref, out_grad_ref, cgrad_ref) = refs[slots : slots + 5]
-    coarse_ref, terms_ref, send_ref = refs[slots + 5 :]
-    table = jnp.concatenate([hidden_ref[...]] + to_slots([r[...] for r in received], False), axis=0)
+    coarse_ref, terms_ref, send_ref, table_ref = refs[slots + 5 :]
+    voxels = hidden_ref.shape[0]
+    cap2 = received[0].shape[0]
+    half, half_halo = voxels // 2, slots * cap2 // 2
+    blocks = to_slots([r[...] for r in received], False)
+    table_ref[0:half, 0:LANES] = hidden_ref[0:half, :]
+    table_ref[0:half, LANES:] = hidden_ref[half:, :]
+    for s, block in enumerate(blocks):
+        place = half + (s % (slots // 2)) * cap2
+        side = (s // (slots // 2)) * LANES
+        table_ref[place : place + cap2, side : side + LANES] = block
+    padding = table_ref.shape[0] - half - half_halo
+    table_ref[half + half_halo :, :] = jnp.zeros((padding, 2 * LANES), BF16)
     upstream = out_grad_ref[...]
     parents = upstream.shape[0]
+    octants = map_ref.shape[0]
     upstream_t = jnp.transpose(upstream.astype(F32)).astype(BF16)
-    total = jnp.zeros((parents, down_ref.shape[2]), F32)
-    codes = encode(map_ref[...])
+    codes = half_codes(map_ref[...], voxels, slots * cap2)
+    col = jnp.concatenate([column(codes[o : o + 1, :]) for o in range(octants)], axis=0)
+    picked = pick_rows(col.astype(BF16), table_ref[...])
+    picked = jnp.concatenate(jnp.split(picked, octants), axis=1)
     row = cgrad_ref.shape[0]
     terms_ref[0:row, :] = cgrad_ref[...]
-    for o in range(map_ref.shape[0]):
-        chooser = one_hot_rows(column(codes[o : o + 1, :]).astype(BF16), table.shape[0])
-        picked = matmul(chooser, table).astype(BF16)
-        total = total + matmul(picked, down_ref[o])
-        terms = matmul(upstream_t, picked)
+    terms = matmul(upstream_t, picked)
+    for o in range(octants):
         for start in range(0, terms.shape[0], LANES):
-            block = jnp.transpose(terms[start : start + LANES, :]).astype(BF16)
-            terms_ref[row : row + LANES, :] = block
+            block = terms[start : start + LANES, o * LANES : (o + 1) * LANES]
+            terms_ref[row : row + LANES, :] = jnp.transpose(block).astype(BF16)
             row += LANES
+    total = matmul(picked, down_ref[...].reshape(octants * LANES, down_ref.shape[2]))
     terms_ref[row:, :] = jnp.zeros((terms_ref.shape[0] - row, LANES), BF16)
     coarse_ref[...] = total.astype(BF16)
     send_ref[...] = terms_ref[pl.ds(my_half(send_ref.shape[0])[1], send_ref.shape[0]), :]
@@ -431,6 +458,7 @@
             ((2 * half_rows, LANES), BF16),
             ((half_rows, LANES), BF16),
         ],
+        scratch=[pltpu.VMEM((-(-(voxels + slots * cap2) // 256) * 128, 2 * channels), BF16)],
         flops=2 * giga,
     )
     (pair_terms,) = call(
@@ -444,7 +472,10 @@
         functools.partial(spread_kernel, slots),
         (pre_grad, neighbour_map, conv_weight, pair_terms),
         [((voxels, channels), F32)] + [((cap, channels), BF16)] * slots,
-        scratch=[pltpu.VMEM((voxels // 2 + slots * cap // 2, 2 * channels), F32)],
+        scratch=[
+            pltpu.VMEM((voxels // 2 + slots * cap // 2, 2 * channels), F32),
+            pltpu.VMEM((LANES, voxels), F32),
+        ],
         flops=20 * giga,
         in_hbm=(3,),
     )
@@ -456,13 +487,14 @@
         in_hbm=(1,),
     )
     summed, *returning = lax.optimization_barrier((summed, *spread[1:]))
-    mine, *returned = lax.optimization_barrier((exchange(summed), *swaps(returning, reach)))
+    returned = swaps(returning, reach)
     (input_grad,) = call(
         functools.partial(tail_kernel, slots),
         (*returned, hidden_grad, spread[0], halo_rows),
         [((voxels, channels), F32)],
         flops=giga,
     )
+    mine, input_grad = lax.optimization_barrier((exchange(summed), input_grad))
     conv_grad, down_grad = call(
         final_kernel,
         (mine, swap_cores(mine, devices)),

time: 114 us -> 118 us (1.035)
  Pallas kernels: 51.7 us -> 57.8 us
  waiting for transfers between devices: 21.4 us -> 17.4 us
  starting transfers between devices: 38.2 us -> 40.2 us
    pallas_call x8, Pallas kernels: 51.7 us -> 57.8 us  [call(): pl.pallas_call(kernel, out_shape=[jax.ShapeDtypeStruct(s, d) for s, d in...]
    all_to_all x2, waiting for transfers between devices: 15.6 us -> 10.4 us  [exchange(): return lax.all_to_all(value, 'shard', 0, 0, tiled=True)]
    all_to_all x2, starting transfers between devices: 15.4 us -> 17.4 us  [exchange(): return lax.all_to_all(value, 'shard', 0, 0, tiled=True)]
    ppermute x2, waiting for transfers between devices: 2.77 us -> 4.01 us  [swap_cores(): lax.ppermute(value, 'shard', [(i, i + 1 - 2 * (i % 2)) for i in range(dev...]
  transfers between devices with their start and end apart: 16 -> 16, of which waited for: 8 -> 7; matrix products, arithmetic and copies ran while one was open for 0% -> 0% of each run, Pallas kernels for 14% -> 20%
where the time goes in v4:
time: 118 us; the launch traced here: 117 us
  Pallas kernels  57.8 us (49%)
  starting transfers between devices  40.2 us (34%)
  waiting for transfers between devices  17.4 us (15%)
    pallas_call x8, Pallas kernels, call(): pl.pallas_call(kernel, out_shape=[jax.ShapeDtypeStruct(s, d) for s, d in...  57.8 us
    ppermute x12, starting transfers between devices, swaps(): moved.append(lax.ppermute(by_step[len(moved)], 'shard', pairs))  22.1 us
    all_to_all x2, starting transfers between devices, exchange(): return lax.all_to_all(value, 'shard', 0, 0, tiled=True)  17.4 us
    all_to_all x2, waiting for transfers between devices, exchange(): return lax.all_to_all(value, 'shard', 0, 0, tiled=True)  10.4 us
    ppermute x2, waiting for transfers between devices, swap_cores(): lax.ppermute(value, 'shard', [(i, i + 1 - 2 * (i % 2)) for i in range(dev...  4.01 us
    ppermute x12, waiting for transfers between devices, swaps(): moved.append(lax.ppermute(by_step[len(moved)], 'shard', pairs))  3.06 us
  transfers between devices with their start and end apart: 16, of which 7 were waited for; matrix products, arithmetic and copies ran while one was open for 0% of the time, Pallas kernels for 20%

profile of v4, /device:TPU:1, one launch (start us, length us, event | category | flops | bytes accessed | tf_op | source)
XLA Modules:
  0.0 117.4 jit_solution(1984189911647316521)
XLA Ops:
  0.6 0.0 copy-start.2
  0.6 0.0 copy-start.4
  0.7 0.0 copy-start
  0.7 0.0 copy-start.6
  0.7 5.5 %shard_map.111 = (bf16[96,128]{1,0:T(8,128)(2,1)}, bf16[96,128]{1,0:T(8,128)(2,1)}, bf16[96,128]{1,0:T(8,128)(2,1)}, bf16[96,128]{1,0:T(8,128)(2,1)}, f32[1024,128]{1,0:T(8,128)}) custom-call(bf16[1024,128]{1,0:T(8,128)(2,1)} %refs_4_.1, s32[4,64]{1,0:T(4,128)} %refs_6_.5, s32[8,256]{1,0:T(8,128)} %refs_5_.3, bf16[256,256]{1,0:T(8,128)(2,1)} %refs_7_.3, ...), custom_call_target="tpu_custom_call" | custom-call | flops 1000000000 | bytes 4194304 | tf_op jit(solution)/shard_map/pallas_call | solution.py:379
  6.2 0.1 collective-permute-start
  6.3 4.5 %collective-permute-start.1 = (bf16[96,128]{1,0:T(8,128)(2,1)}, bf16[96,128]{1,0:T(8,128)(2,1)S(1)}, u32[]{:S(2)}, u32[]{:S(2)}) collective-permute-start(bf16[96,128]{1,0:T(8,128)(2,1)} %get-tuple-element.35), channel_id=1, source_target_pairs={{1,2},{2,1},{3,4},{4,3},{5,6},{6,5},{7,8},{8,7},{9,10},{10,9},{11,... | collective-permute-start | bytes 73736 | tf_op jit(solution)/shard_map/ppermute | solution.py:23
  10.8 1.3 %collective-permute-start.2 = (bf16[96,128]{1,0:T(8,128)(2,1)}, bf16[96,128]{1,0:T(8,128)(2,1)S(1)}, u32[]{:S(2)}, u32[]{:S(2)}) collective-permute-start(bf16[96,128]{1,0:T(8,128)(2,1)} %get-tuple-element.36), channel_id=1, source_target_pairs={{0,2},{1,3},{2,0},{3,1},{4,6},{5,7},{6,4},{7,5},{8,10},{9,11},{10,... | collective-permute-start | bytes 73736 | tf_op jit(solution)/shard_map/ppermute | solution.py:23
  12.1 0.7 collective-permute-start.3
  12.7 0.0 collective-permute-done.refs_0_
  12.7 0.0 collective-permute-done.1.refs_1_
  12.7 1.0 collective-permute-done.2.refs_2_
  13.7 0.0 collective-permute-done.3.refs_3_
  13.7 0.0 copy-done.2
  13.7 0.0 copy-done.4
  13.7 0.0 copy-done
  13.7 0.0 copy-done.6
  13.8 0.0 copy-start.8
  13.8 1.0 copy-done.8
  14.8 0.0 copy-start.1
  14.8 0.0 copy-start.3
  14.8 0.0 copy-start.5
  14.8 22.3 %shard_map.112 = (bf16[1024,128]{1,0:T(8,128)(2,1)S(1)}, f32[1024,128]{1,0:T(8,128)S(1)}, bf16[1024,128]{1,0:T(8,128)(2,1)S(1)}, bf16[3456,128]{1,0:T(8,128)(2,1...) custom-call(bf16[96,128]{1,0:T(8,128)(2,1)S(1)} %collective-permute-, ...), custom_call_target="tpu_custom_call" | custom-call | flops 12000000000 | bytes 4194304 | tf_op jit(solution)/shard_map/pallas_call | solution.py:379
  37.1 0.1 collective-permute-start.4
  37.2 6.7 %collective-permute-start.5 = (bf16[32,128]{1,0:T(8,128)(2,1)S(1)}, bf16[32,128]{1,0:T(8,128)(2,1)S(1)}, u32[]{:S(2)}, u32[]{:S(2)}) collective-permute-start(bf16[32,128]{1,0:T(8,128)(2,1)S(1)} %get-tuple-element.40), channel_id=1, source_target_pairs={{1,2},{2,1},{3,4},{4,3},{5,6},{6,5},{7,8},{8,7},{9,10},{10,9},{11,... | collective-permute-start | bytes 24584 | tf_op jit(solution)/shard_map/ppermute | solution.py:23
  43.9 2.5 %collective-permute-start.6 = (bf16[32,128]{1,0:T(8,128)(2,1)S(1)}, bf16[32,128]{1,0:T(8,128)(2,1)S(1)}, u32[]{:S(2)}, u32[]{:S(2)}) collective-permute-start(bf16[32,128]{1,0:T(8,128)(2,1)S(1)} %get-tuple-element.41), channel_id=1, source_target_pairs={{0,2},{1,3},{2,0},{3,1},{4,6},{5,7},{6,4},{7,5},{8,10},{9,11},{10,... | collective-permute-start | bytes 24584 | tf_op jit(solution)/shard_map/ppermute | solution.py:23
  46.4 0.6 collective-permute-start.7
  47.1 0.0 collective-permute-done.4.refs_0_
  47.1 0.0 collective-permute-done.5.refs_1_
  47.1 0.4 collective-permute-done.6.refs_2_
  47.5 0.0 collective-permute-done.7.refs_3_
  47.5 0.0 copy-done.1
  47.5 0.0 copy-done.3
  47.5 0.0 copy-done.5
  47.5 2.5 %shard_map.113 = (bf16[256,256]{1,0:T(8,128)(2,1)}, bf16[5632,128]{1,0:T(8,128)(2,1)S(1)}, bf16[2816,128]{1,0:T(8,128)(2,1)S(1)}) custom-call(bf16[32,128]{1,0:T(8,128)(2,1)S(1)} %collective-permute-done.4.refs_0_, bf16[32,128]{1,0:T(8,128)(2,1)S(1)} %collective-permute-done.5.refs_1_, bf16[32,128]{1,0:T(8,128)(2,1)S(1)} %collective-permute-done.6.refs_2_, ...), custom_call_target="tpu_custom_call" | custom-call | flops 2000000000 | bytes 4194304 | tf_op jit(solution)/shard_map/pallas_call | solution.py:379
  50.0 0.0 collective-permute-start.8
  50.0 2.2 %collective-permute-done.8.other_ref = bf16[2816,128]{1,0:T(8,128)(2,1)S(1)} collective-permute-done((bf16[2816,128]{1,0:T(8,128)(2,1)S(1)}, bf16[2816,128]{1,0:T(8,128)(2,1)S(1)}, u32[]{:S(2)}, u32[]{:S(2)}) %collective-permute-start.8) | collective-permute-done | bytes 720928 | tf_op jit(solution)/shard_map/ppermute | solution.py:391
  52.2 1.0 shard_map.114.after_ref
  53.3 11.5 %all-to-all-start = ((bf16[32,88,128]{2,1,0:T(8,128)(2,1)}), bf16[32,88,128]{2,1,0:T(8,128)(2,1)S(1)}, u32[]{:S(2)}, u32[]{:S(2)}) async-start(bf16[32,88,128]{2,1,0:T(8,128)(2,1)} %bitcast), calls=%async_computation | async-start | bytes 1441792 | tf_op jit(solution)/shard_map/all_to_all | solution.py:395
  64.8 22.5 %shard_map.115 = (f32[1024,128]{1,0:T(8,128)S(1)}, bf16[64,128]{1,0:T(8,128)(2,1)S(1)}, bf16[64,128]{1,0:T(8,128)(2,1)S(1)}, bf16[64,128]{1,0:T(8,128)(2,1)S(1)}, bf16[64,128]{1,0:T(8,128)(2,1)S(1)}) custom-call(bf16[1024,128]{1,0:T(8,128)(2,1)S(1)} %get-tuple-element.48.pgrad_ref, s32[27,1024]{1,0:T(8,128)S(1)} %copy-done.4, ...), custom_call_target="tpu_custom_call" | custom-call | flops 20000000000 | bytes 4194304 | tf_op jit(solution)/shard_map/pallas_call | solution.py:379
  87.3 0.0 copy-start.7
  87.3 0.0 all-to-all-done
  87.3 1.0 shard_map.116
  88.3 5.8 %all-to-all-start.1 = ((bf16[32,88,128]{2,1,0:T(8,128)(2,1)}), bf16[32,88,128]{2,1,0:T(8,128)(2,1)S(1)}, u32[]{:S(2)}, u32[]{:S(2)}) async-start(bf16[32,88,128]{2,1,0:T(8,128)(2,1)} %bitcast.2), calls=%async_computation.1 | async-start | bytes 1441792 | tf_op jit(solution)/shard_map/all_to_all | solution.py:395
  94.1 0.3 collective-permute-start.9
  94.4 3.4 %collective-permute-start.10 = (bf16[64,128]{1,0:T(8,128)(2,1)S(1)}, bf16[64,128]{1,0:T(8,128)(2,1)S(1)}, u32[]{:S(2)}, u32[]{:S(2)}) collective-permute-start(bf16[64,128]{1,0:T(8,128)(2,1)S(1)} %get-tuple-element.55), channel_id=1, source_target_pairs={{1,2},{2,1},{3,4},{4,3},{5,6},{6,5},{7,8},{8,7},{9,10},{10,9},{11,... | collective-permute-start | bytes 49160 | tf_op jit(solution)/shard_map/ppermute | solution.py:23
  97.9 1.2 %collective-permute-start.11 = (bf16[64,128]{1,0:T(8,128)(2,1)S(1)}, bf16[64,128]{1,0:T(8,128)(2,1)S(1)}, u32[]{:S(2)}, u32[]{:S(2)}) collective-permute-start(bf16[64,128]{1,0:T(8,128)(2,1)S(1)} %get-tuple-element.56), channel_id=1, source_target_pairs={{0,2},{1,3},{2,0},{3,1},{4,6},{5,7},{6,4},{7,5},{8,10},{9,11},{10,... | collective-permute-start | bytes 49160 | tf_op jit(solution)/shard_map/ppermute | solution.py:23
  99.1 0.7 collective-permute-start.12
  99.8 0.0 collective-permute-done.9.refs_0_
  99.8 0.1 collective-permute-done.10.refs_1_
  99.8 1.6 %collective-permute-done.11.refs_2_ = bf16[64,128]{1,0:T(8,128)(2,1)S(1)} collective-permute-done((bf16[64,128]{1,0:T(8,128)(2,1)S(1)}, bf16[64,128]{1,0:T(8,128)(2,1)S(1)}, u32[]{:S(2)}, u32[]{:S(2)}) %collective-permute-start.11) | collective-permute-done | bytes 16416 | tf_op jit(solution)/shard_map/ppermute | solution.py:23
  101.5 0.0 collective-permute-done.12.refs_3_
  101.5 0.0 copy-done.7
  101.5 1.2 %shard_map.117 = f32[1024,128]{1,0:T(8,128)} custom-call(bf16[64,128]{1,0:T(8,128)(2,1)S(1)} %collective-permute-done.9.refs_0_, bf16[64,128]{1,0:T(8,128)(2,1)S(1)} %collective-permute-done.10.refs_1_, bf16[64,128]{1,0:T(8,128)(2,1)S(1)} %collective-permute-done.11.refs_2_, bf16[64,128]{1,0:T(8,128)(2,1)S(1)} %collective-permute-done.12.refs_3_, ...), custom_call_target="tpu_custom_call" | custom-call | flops 1000000000 | bytes 4194304 | tf_op jit(solution)/shard_map/pallas_call | solution.py:379
  102.7 10.4 %all-to-all-done.1 = bf16[32,88,128]{2,1,0:T(8,128)(2,1)S(1)} async-done(((bf16[32,88,128]{2,1,0:T(8,128)(2,1)}), bf16[32,88,128]{2,1,0:T(8,128)(2,1)S(1)}, u32[]{:S(2)}, u32[]{:S(2)}) %all-to-all-start.1) | async-done | bytes 720928 | tf_op jit(solution)/shard_map/all_to_all | solution.py:395
  113.1 0.7 collective-permute-start.13
  113.8 1.8 %collective-permute-done.13.other_ref = bf16[2816,128]{1,0:T(8,128)(2,1)S(1)} collective-permute-done((bf16[2816,128]{1,0:T(8,128)(2,1)S(1)}, bf16[2816,128]{1,0:T(8,128)(2,1)S(1)}, u32[]{:S(2)}, u32[]{:S(2)}) %collective-permute-start.13) | collective-permute-done | bytes 720928 | tf_op jit(solution)/shard_map/ppermute | solution.py:391
  115.6 1.8 %shard_map.118 = (f32[3456,128]{1,0:T(8,128)}, f32[1024,256]{1,0:T(8,128)}) custom-call(bf16[2816,128]{1,0:T(8,128)(2,1)S(1)} %bitcast.7, bf16[2816,128]{1,0:T(8,128)(2,1)S(1)} %collective-permute-done.13.other_ref), custom_call_target="tpu_custom_call" | custom-call | flops 1000000 | bytes 4194304 | tf_op jit(solution)/shard_map/pallas_call | solution.py:379
Async XLA Ops:
  0.6 13.1 %copy-start.2 = (bf16[1024,128]{1,0:T(8,128)(2,1)S(1)}, bf16[1024,128]{1,0:T(8,128)(2,1)}, u32[]{:S(2)}) copy-start(bf16[1024,128]{1,0:T(8,128)(2,1)} %refs_4_.1) | copy-start | bytes 786436
  0.6 13.1 %copy-start.4 = (s32[27,1024]{1,0:T(8,128)S(1)}, s32[27,1024]{1,0:T(8,128)}, u32[]{:S(2)}) copy-start(s32[27,1024]{1,0:T(8,128)} %map_ref.1) | copy-start | bytes 331780
  0.7 13.1 %copy-start = (bf16[27,128,128]{2,1,0:T(8,128)(2,1)S(1)}, bf16[27,128,128]{2,1,0:T(8,128)(2,1)}, u32[]{:S(2)}) copy-start(bf16[27,128,128]{2,1,0:T(8,128)(2,1)} %weight_ref.1) | copy-start | bytes 2654212
  0.7 13.1 %copy-start.6 = (s32[4,32]{1,0:T(4,128)S(1)}, s32[4,32]{1,0:T(4,128)}, u32[]{:S(2)}) copy-start(s32[4,32]{1,0:T(4,128)} %refs_7_.2) | copy-start | bytes 1540
  6.2 6.5 %collective-permute-start = (bf16[96,128]{1,0:T(8,128)(2,1)}, bf16[96,128]{1,0:T(8,128)(2,1)S(1)}, u32[]{:S(2)}, u32[]{:S(2)}) collective-permute-start(bf16[96,128]{1,0:T(8,128)(2,1)} %get-tuple-element.34), channel_id=1, source_target_pairs={{0,1},{1,0},{2,3},{3,2},{4,5},{5,4},{6,7},{7,6},{8,9},{9,8},{10,11... | collective-permute-start | bytes 73736 | tf_op jit(solution)/shard_map/ppermute | solution.py:23
  6.3 6.4 %collective-permute-start.1 = (bf16[96,128]{1,0:T(8,128)(2,1)}, bf16[96,128]{1,0:T(8,128)(2,1)S(1)}, u32[]{:S(2)}, u32[]{:S(2)}) collective-permute-start(bf16[96,128]{1,0:T(8,128)(2,1)} %get-tuple-element.35), channel_id=1, source_target_pairs={{1,2},{2,1},{3,4},{4,3},{5,6},{6,5},{7,8},{8,7},{9,10},{10,9},{11,... | collective-permute-start | bytes 73736 | tf_op jit(solution)/shard_map/ppermute | solution.py:23
  10.8 3.0 %collective-permute-start.2 = (bf16[96,128]{1,0:T(8,128)(2,1)}, bf16[96,128]{1,0:T(8,128)(2,1)S(1)}, u32[]{:S(2)}, u32[]{:S(2)}) collective-permute-start(bf16[96,128]{1,0:T(8,128)(2,1)} %get-tuple-element.36), channel_id=1, source_target_pairs={{0,2},{1,3},{2,0},{3,1},{4,6},{5,7},{6,4},{7,5},{8,10},{9,11},{10,... | collective-permute-start | bytes 73736 | tf_op jit(solution)/shard_map/ppermute | solution.py:23
  12.1 1.7 %collective-permute-start.3 = (bf16[96,128]{1,0:T(8,128)(2,1)}, bf16[96,128]{1,0:T(8,128)(2,1)S(1)}, u32[]{:S(2)}, u32[]{:S(2)}) collective-permute-start(bf16[96,128]{1,0:T(8,128)(2,1)} %get-tuple-element.37), channel_id=1, source_target_pairs={{2,4},{3,5},{4,2},{5,3},{6,8},{7,9},{8,6},{9,7},{10,12},{11,13},{1... | collective-permute-start | bytes 73736 | tf_op jit(solution)/shard_map/ppermute | solution.py:23
  13.8 1.0 copy-start.8
  14.8 32.7 %copy-start.1 = (bf16[8,128,256]{2,1,0:T(8,128)(2,1)S(1)}, bf16[8,128,256]{2,1,0:T(8,128)(2,1)}, u32[]{:S(2)}) copy-start(bf16[8,128,256]{2,1,0:T(8,128)(2,1)} %refs_6_.4) | copy-start | bytes 1572868
  14.8 32.7 %copy-start.3 = (bf16[256,256]{1,0:T(8,128)(2,1)S(1)}, bf16[256,256]{1,0:T(8,128)(2,1)}, u32[]{:S(2)}) copy-start(bf16[256,256]{1,0:T(8,128)(2,1)} %refs_7_.3) | copy-start | bytes 393220
  14.8 32.7 %copy-start.5 = (s32[8,256]{1,0:T(8,128)S(1)}, s32[8,256]{1,0:T(8,128)}, u32[]{:S(2)}) copy-start(s32[8,256]{1,0:T(8,128)} %refs_5_.3) | copy-start | bytes 24580
  37.1 10.0 %collective-permute-start.4 = (bf16[32,128]{1,0:T(8,128)(2,1)S(1)}, bf16[32,128]{1,0:T(8,128)(2,1)S(1)}, u32[]{:S(2)}, u32[]{:S(2)}) collective-permute-start(bf16[32,128]{1,0:T(8,128)(2,1)S(1)} %get-tuple-element.39), channel_id=1, source_target_pairs={{0,1},{1,0},{2,3},{3,2},{4,5},{5,4},{6,7},{7,6},{8,9},{9,8},{10,11... | collective-permute-start | bytes 24584 | tf_op jit(solution)/shard_map/ppermute | solution.py:23
  37.2 9.9 %collective-permute-start.5 = (bf16[32,128]{1,0:T(8,128)(2,1)S(1)}, bf16[32,128]{1,0:T(8,128)(2,1)S(1)}, u32[]{:S(2)}, u32[]{:S(2)}) collective-permute-start(bf16[32,128]{1,0:T(8,128)(2,1)S(1)} %get-tuple-element.40), channel_id=1, source_target_pairs={{1,2},{2,1},{3,4},{4,3},{5,6},{6,5},{7,8},{8,7},{9,10},{10,9},{11,... | collective-permute-start | bytes 24584 | tf_op jit(solution)/shard_map/ppermute | solution.py:23
  43.9 3.6 %collective-permute-start.6 = (bf16[32,128]{1,0:T(8,128)(2,1)S(1)}, bf16[32,128]{1,0:T(8,128)(2,1)S(1)}, u32[]{:S(2)}, u32[]{:S(2)}) collective-permute-start(bf16[32,128]{1,0:T(8,128)(2,1)S(1)} %get-tuple-element.41), channel_id=1, source_target_pairs={{0,2},{1,3},{2,0},{3,1},{4,6},{5,7},{6,4},{7,5},{8,10},{9,11},{10,... | collective-permute-start | bytes 24584 | tf_op jit(solution)/shard_map/ppermute | solution.py:23
  46.4 1.0 collective-permute-start.7
  50.0 2.2 %collective-permute-start.8 = (bf16[2816,128]{1,0:T(8,128)(2,1)S(1)}, bf16[2816,128]{1,0:T(8,128)(2,1)S(1)}, u32[]{:S(2)}, u32[]{:S(2)}) collective-permute-start(bf16[2816,128]{1,0:T(8,128)(2,1)S(1)} %get-tuple-element.47), channel_id=1, source_target_pairs={{0,1},{1,0},{2,3},{3,2},{4,5},{5,4},{6,7},{7,6},{8,9},{9,8},{10,11... | collective-permute-start | bytes 2162696 | tf_op jit(solution)/shard_map/ppermute | solution.py:391
  53.3 34.0 %all-to-all-start = ((bf16[32,88,128]{2,1,0:T(8,128)(2,1)}), bf16[32,88,128]{2,1,0:T(8,128)(2,1)S(1)}, u32[]{:S(2)}, u32[]{:S(2)}) async-start(bf16[32,88,128]{2,1,0:T(8,128)(2,1)} %bitcast), calls=%async_computation | async-start | bytes 1441792 | tf_op jit(solution)/shard_map/all_to_all | solution.py:395
  87.3 14.2 %copy-start.7 = (s32[4,64]{1,0:T(4,128)S(1)}, s32[4,64]{1,0:T(4,128)}, u32[]{:S(2)}) copy-start(s32[4,64]{1,0:T(4,128)} %refs_6_.5) | copy-start | bytes 3076
  88.3 24.8 %all-to-all-start.1 = ((bf16[32,88,128]{2,1,0:T(8,128)(2,1)}), bf16[32,88,128]{2,1,0:T(8,128)(2,1)S(1)}, u32[]{:S(2)}, u32[]{:S(2)}) async-start(bf16[32,88,128]{2,1,0:T(8,128)(2,1)} %bitcast.2), calls=%async_computation.1 | async-start | bytes 1441792 | tf_op jit(solution)/shard_map/all_to_all | solution.py:395
  94.1 5.7 %collective-permute-start.9 = (bf16[64,128]{1,0:T(8,128)(2,1)S(1)}, bf16[64,128]{1,0:T(8,128)(2,1)S(1)}, u32[]{:S(2)}, u32[]{:S(2)}) collective-permute-start(bf16[64,128]{1,0:T(8,128)(2,1)S(1)} %get-tuple-element.54.after_ref), channel_id=1, source_target_pairs={{0,1},{1,0},{2,3},{3,2},{4,5},{5,4},{6,7},{7,6},{8,9},{9,8},{10,11... | collective-permute-start | bytes 49160 | tf_op jit(solution)/shard_map/ppermute | solution.py:23
  94.4 5.4 %collective-permute-start.10 = (bf16[64,128]{1,0:T(8,128)(2,1)S(1)}, bf16[64,128]{1,0:T(8,128)(2,1)S(1)}, u32[]{:S(2)}, u32[]{:S(2)}) collective-permute-start(bf16[64,128]{1,0:T(8,128)(2,1)S(1)} %get-tuple-element.55), channel_id=1, source_target_pairs={{1,2},{2,1},{3,4},{4,3},{5,6},{6,5},{7,8},{8,7},{9,10},{10,9},{11,... | collective-permute-start | bytes 49160 | tf_op jit(solution)/shard_map/ppermute | solution.py:23
  97.9 3.6 %collective-permute-start.11 = (bf16[64,128]{1,0:T(8,128)(2,1)S(1)}, bf16[64,128]{1,0:T(8,128)(2,1)S(1)}, u32[]{:S(2)}, u32[]{:S(2)}) collective-permute-start(bf16[64,128]{1,0:T(8,128)(2,1)S(1)} %get-tuple-element.56), channel_id=1, source_target_pairs={{0,2},{1,3},{2,0},{3,1},{4,6},{5,7},{6,4},{7,5},{8,10},{9,11},{10,... | collective-permute-start | bytes 49160 | tf_op jit(solution)/shard_map/ppermute | solution.py:23
  99.1 2.4 %collective-permute-start.12 = (bf16[64,128]{1,0:T(8,128)(2,1)S(1)}, bf16[64,128]{1,0:T(8,128)(2,1)S(1)}, u32[]{:S(2)}, u32[]{:S(2)}) collective-permute-start(bf16[64,128]{1,0:T(8,128)(2,1)S(1)} %get-tuple-element.57), channel_id=1, source_target_pairs={{2,4},{3,5},{4,2},{5,3},{6,8},{7,9},{8,6},{9,7},{10,12},{11,13},{1... | collective-permute-start | bytes 49160 | tf_op jit(solution)/shard_map/ppermute | solution.py:23
  113.1 2.5 %collective-permute-start.13 = (bf16[2816,128]{1,0:T(8,128)(2,1)S(1)}, bf16[2816,128]{1,0:T(8,128)(2,1)S(1)}, u32[]{:S(2)}, u32[]{:S(2)}) collective-permute-start(bf16[2816,128]{1,0:T(8,128)(2,1)S(1)} %bitcast.6), channel_id=1, source_target_pairs={{0,1},{1,0},{2,3},{3,2},{4,5},{5,4},{6,7},{7,6},{8,9},{9,8},{10,11... | collective-permute-start | bytes 2162696 | tf_op jit(solution)/shard_map/ppermute | solution.py:391

commit v5 on v4

--- a/solution.py
+++ b/solution.py
@@ -138,14 +138,15 @@
     for copy in copies[2:]:
         copy.wait()
     upstream = out_grad_ref[...]
-    both = jnp.zeros((table_rows, 2 * LANES), F32)
     codes = encode(child_map_ref[...]).astype(BF16)
+    choosers, parts = [], []
     for o in range(octants):
         part = matmul_rt(upstream, down_ref[o])
         high = part.astype(BF16)
         low = (part - high.astype(F32)).astype(BF16)
-        chooser = one_hot_columns(codes[o : o + 1, :], table_rows)
-        both = both + matmul(chooser, jnp.concatenate([high, low], axis=1))
+        choosers.append(one_hot_columns(codes[o : o + 1, :], table_rows))
+        parts.append(jnp.concatenate([high, low], axis=1))
+    both = matmul(jnp.concatenate(choosers, axis=1), jnp.concatenate(parts, axis=0))
     total = both[:, :LANES] + both[:, LANES:]
     back_ref[...] = total[:voxels]
     for send, block in zip(sends, to_steps(jnp.split(total[voxels:].astype(BF16), slots), True)):
@@ -169,7 +170,8 @@
     (features_ref, map_ref, weight_ref, child_ref, back_hbm) = refs[slots : slots + 5]
     (hidden_ref, hgrad_ref, pgrad_ref, cgrad_ref) = refs[slots + 5 : slots + 9]
     sends = refs[slots + 9 : 2 * slots + 9]
-    (table_ref, stacked_ref, acc_ref, back_ref, sem) = refs[2 * slots + 9 :]
+    (table_ref, stacked_ref, acc_ref, back_ref, sem) = refs[2 * slots + 9 : 2 * slots + 14]
+    chooser_refs, col_refs = refs[2 * slots + 14 : 2 * slots + 16], refs[2 * slots + 16 :]
     back_copy = pltpu.make_async_copy(back_hbm, back_ref, sem)
     back_copy.start()
     voxels = features_ref.shape[0]
@@ -187,22 +189,39 @@
         table_ref[place : place + cap, side : side + LANES] = block
     table_rows = half + half_halo
 
-    def gather(k):
-        codes = half_codes(map_ref[pl.ds(k, 1), :], voxels, slots * cap).astype(BF16)
-        picked = pick_rows(column(codes), table_ref[...])
-        stacked_ref[k] = picked
-        return picked
+    def build(j, side):
+        for n, k in enumerate((j, j + middle + 1)):
+            codes = half_codes(map_ref[pl.ds(k, 1), :], voxels, slots * cap).astype(BF16)
+            col = column(codes)
+            col_refs[side][n] = col
+            chooser_refs[side][n] = one_hot_rows(jnp.abs(col), table_rows)
+
+    def use(j, side):
+        pair = []
+        for n, k in enumerate((j, j + middle + 1)):
+            both = matmul(chooser_refs[side][n], table_ref[...]).astype(BF16)
+            right = col_refs[side][n] < jnp.zeros((voxels, LANES), BF16)
+            pair.append(jnp.where(right, both[:, LANES:], both[:, :LANES]))
+            stacked_ref[k] = pair[n]
+        return pair
+
+    def convolve(j, pair):
+        kernel = jnp.concatenate([weight_ref[j], weight_ref[j + middle + 1]], axis=0)
+        acc_ref[...] += matmul(jnp.concatenate(pair, axis=1), kernel)
 
     acc_ref[...] = matmul(features, weight_ref[middle])
-
-    def step(j, carry):
-        near, far = gather(j), gather(j + middle + 1)
-        pair = jnp.concatenate([near, far], axis=1)
-        kernel = jnp.concatenate([weight_ref[j], weight_ref[j + middle + 1]], axis=0)
-        acc_ref[...] += matmul(pair, kernel)
+    build(0, 0)
+
+    def step(i, carry):
+        for side in range(2):
+            j = 2 * i + side
+            pair = use(j, side)
+            build(j + 1, 1 - side)
+            convolve(j, pair)
         return carry
 
-    lax.fori_loop(0, middle, step, 0)
+    lax.fori_loop(0, middle // 2, step, 0)
+    convolve(middle - 1, use(middle - 1, 0))
     pre = acc_ref[...]
     sig = jax.nn.sigmoid(pre)
     hidden = (features.astype(F32) + pre * sig).astype(BF16)
@@ -232,12 +251,13 @@
         put(j + middle + 1, both[:, LANES:])
         return carry
 
-    lax.fori_loop(0, middle, weight_step, 0)
+    for j in range(middle):
+        weight_step(j, 0)
 
 
 def spread_kernel(slots, pgrad_ref, map_ref, weight_ref, after_ref, back_ref, *sends):
-    acc_ref, codes_ref = sends[-2:]
-    sends = sends[:-2]
+    acc_ref = sends[-1]
+    sends = sends[:-1]
     voxels = pgrad_ref.shape[0]
     kernel_count = map_ref.shape[0]
     middle = kernel_count // 2
@@ -250,29 +270,17 @@
     acc_ref[0:half, LANES:] = own[half:]
     acc_ref[half:, :] = jnp.zeros((table_rows - half, 2 * LANES), F32)
 
-    codes_ref[...] = jnp.zeros(codes_ref.shape, F32)
-    codes_ref[0:kernel_count, :] = half_codes(map_ref[...], voxels, slots * cap)
-    turned = jnp.concatenate(
-        [
-            jnp.transpose(codes_ref[:, first : first + LANES]).astype(BF16)
-            for first in range(0, voxels, LANES)
-        ],
-        axis=0,
-    )
-    number = lax.broadcasted_iota(jnp.int32, (LANES, LANES), 0)
-
-    def parts(k, spread_codes):
+    def parts(k):
+        codes = half_codes(map_ref[pl.ds(k, 1), :], voxels, slots * cap)
         terms = matmul_rt(pgrad, weight_ref[k])
-        right = spread_codes < 0.0
+        right = column(codes) < 0.0
         sides = [jnp.where(right, 0.0, terms), jnp.where(right, terms, 0.0)]
-        codes = jnp.abs(codes_ref[pl.ds(k, 1), :]).astype(BF16)
-        return one_hot_columns(codes, table_rows), jnp.concatenate(sides, axis=1).astype(BF16)
+        chooser = one_hot_columns(jnp.abs(codes).astype(BF16), table_rows)
+        return chooser, jnp.concatenate(sides, axis=1).astype(BF16)
 
     def step(j, carry):
-        chosen = [pick_one(number == k) for k in (j, j + middle + 1)]
-        both = matmul(turned, jnp.concatenate(chosen, axis=1))
-        near_chooser, near_terms = parts(j, both[:, :LANES])
-        far_chooser, far_terms = parts(j + middle + 1, both[:, LANES:])
+        near_chooser, near_terms = parts(j)
+        far_chooser, far_terms = parts(j + middle + 1)
         acc_ref[...] += matmul(near_chooser, near_terms) + matmul(far_chooser, far_terms)
         return carry
 
@@ -444,7 +452,9 @@
             pltpu.VMEM((voxels, channels), F32),
             pltpu.VMEM((voxels, channels), F32),
             pltpu.SemaphoreType.DMA(()),
-        ],
+        ]
+        + [pltpu.VMEM((2, voxels, (voxels + slots * cap) // 2), BF16)] * 2
+        + [pltpu.VMEM((2, voxels, LANES), BF16)] * 2,
         limit=48,
         flops=12 * giga,
         in_hbm=(slots + 4,),
@@ -472,10 +482,7 @@
         functools.partial(spread_kernel, slots),
         (pre_grad, neighbour_map, conv_weight, pair_terms),
         [((voxels, channels), F32)] + [((cap, channels), BF16)] * slots,
-        scratch=[
-            pltpu.VMEM((voxels // 2 + slots * cap // 2, 2 * channels), F32),
-            pltpu.VMEM((LANES, voxels), F32),
-        ],
+        scratch=[pltpu.VMEM((voxels // 2 + slots * cap // 2, 2 * channels), F32)],
         flops=20 * giga,
         in_hbm=(3,),
     )
@@ -487,14 +494,13 @@
         in_hbm=(1,),
     )
     summed, *returning = lax.optimization_barrier((summed, *spread[1:]))
-    returned = swaps(returning, reach)
+    mine, *returned = lax.optimization_barrier((exchange(summed), *swaps(returning, reach)))
     (input_grad,) = call(
         functools.partial(tail_kernel, slots),
         (*returned, hidden_grad, spread[0], halo_rows),
         [((voxels, channels), F32)],
         flops=giga,
     )
-    mine, input_grad = lax.optimization_barrier((exchange(summed), input_grad))
     conv_grad, down_grad = call(
         final_kernel,
         (mine, swap_cores(mine, devices)),

time: 118 us -> 109 us (0.924)
  Pallas kernels: 57.8 us -> 46.9 us
  waiting for transfers between devices: 17.4 us -> 21.5 us
  starting transfers between devices: 40.2 us -> 38.2 us
    pallas_call x8, Pallas kernels: 57.8 us -> 46.9 us  [call(): pl.pallas_call(kernel, out_shape=[jax.ShapeDtypeStruct(s, d) for s, d in...]
    all_to_all x2, waiting for transfers between devices: 10.4 us -> 15.6 us  [exchange(): return lax.all_to_all(value, 'shard', 0, 0, tiled=True)]
    all_to_all x2, starting transfers between devices: 17.4 us -> 15.4 us  [exchange(): return lax.all_to_all(value, 'shard', 0, 0, tiled=True)]
    ppermute x2, waiting for transfers between devices: 4.01 us -> 2.77 us  [swap_cores(): lax.ppermute(value, 'shard', [(i, i + 1 - 2 * (i % 2)) for i in range(dev...]
  transfers between devices with their start and end apart: 16 -> 16, of which waited for: 7 -> 8; matrix products, arithmetic and copies ran while one was open for 0% -> 0% of each run, Pallas kernels for 20% -> 15%
where the time goes in v5:
time: 109 us
  Pallas kernels  46.9 us (43%)
  starting transfers between devices  38.2 us (35%)
  waiting for transfers between devices  21.5 us (20%)
    pallas_call x8, Pallas kernels, call(): pl.pallas_call(kernel, out_shape=[jax.ShapeDtypeStruct(s, d) for s, d in...  46.9 us
    ppermute x12, starting transfers between devices, swaps(): moved.append(lax.ppermute(by_step[len(moved)], 'shard', pairs))  22.1 us
    all_to_all x2, waiting for transfers between devices, exchange(): return lax.all_to_all(value, 'shard', 0, 0, tiled=True)  15.6 us
    all_to_all x2, starting transfers between devices, exchange(): return lax.all_to_all(value, 'shard', 0, 0, tiled=True)  15.4 us
    ppermute x12, waiting for transfers between devices, swaps(): moved.append(lax.ppermute(by_step[len(moved)], 'shard', pairs))  3.06 us
    ppermute x2, waiting for transfers between devices, swap_cores(): lax.ppermute(value, 'shard', [(i, i + 1 - 2 * (i % 2)) for i in range(dev...  2.77 us
  transfers between devices with their start and end apart: 16, of which 8 were waited for; matrix products, arithmetic and copies ran while one was open for 0% of the time, Pallas kernels for 15%

profile of v5, /device:TPU:1, one launch (start us, length us, event | category | flops | bytes accessed | tf_op | source)
XLA Modules:
  0.0 108.5 jit_solution(4417131868691410954)
XLA Ops:
  0.6 0.0 copy-start.2
  0.6 0.0 copy-start.4
  0.7 0.0 copy-start
  0.7 0.0 copy-start.6
  0.7 4.1 %shard_map.111 = (bf16[96,128]{1,0:T(8,128)(2,1)}, bf16[96,128]{1,0:T(8,128)(2,1)}, bf16[96,128]{1,0:T(8,128)(2,1)}, bf16[96,128]{1,0:T(8,128)(2,1)}, f32[1024,128]{1,0:T(8,128)}) custom-call(bf16[1024,128]{1,0:T(8,128)(2,1)} %refs_4_.1, s32[4,64]{1,0:T(4,128)} %refs_6_.5, s32[8,256]{1,0:T(8,128)} %refs_5_.3, bf16[256,256]{1,0:T(8,128)(2,1)} %refs_7_.3, ...), custom_call_target="tpu_custom_call" | custom-call | flops 1000000000 | bytes 4194304 | tf_op jit(solution)/shard_map/pallas_call | solution.py:387
  4.7 0.1 collective-permute-start
  4.9 4.5 %collective-permute-start.1 = (bf16[96,128]{1,0:T(8,128)(2,1)}, bf16[96,128]{1,0:T(8,128)(2,1)S(1)}, u32[]{:S(2)}, u32[]{:S(2)}) collective-permute-start(bf16[96,128]{1,0:T(8,128)(2,1)} %get-tuple-element.38), channel_id=1, source_target_pairs={{1,2},{2,1},{3,4},{4,3},{5,6},{6,5},{7,8},{8,7},{9,10},{10,9},{11,... | collective-permute-start | bytes 73736 | tf_op jit(solution)/shard_map/ppermute | solution.py:23
  9.3 1.3 %collective-permute-start.2 = (bf16[96,128]{1,0:T(8,128)(2,1)}, bf16[96,128]{1,0:T(8,128)(2,1)S(1)}, u32[]{:S(2)}, u32[]{:S(2)}) collective-permute-start(bf16[96,128]{1,0:T(8,128)(2,1)} %get-tuple-element.39), channel_id=1, source_target_pairs={{0,2},{1,3},{2,0},{3,1},{4,6},{5,7},{6,4},{7,5},{8,10},{9,11},{10,... | collective-permute-start | bytes 73736 | tf_op jit(solution)/shard_map/ppermute | solution.py:23
  10.6 0.7 collective-permute-start.3
  11.3 0.0 collective-permute-done.refs_0_
  11.3 0.0 collective-permute-done.1.refs_1_
  11.3 1.0 collective-permute-done.2.refs_2_
  12.3 0.0 collective-permute-done.3.refs_3_
  12.3 0.0 copy-done.2
  12.3 0.0 copy-done.4
  12.3 0.0 copy-done
  12.3 0.0 copy-done.6
  12.3 0.0 copy-start.8
  12.3 1.0 copy-done.8
  13.4 0.0 copy-start.1
  13.4 0.0 copy-start.3
  13.4 0.0 copy-start.5
  13.4 20.4 %shard_map.112 = (bf16[1024,128]{1,0:T(8,128)(2,1)S(1)}, f32[1024,128]{1,0:T(8,128)S(1)}, bf16[1024,128]{1,0:T(8,128)(2,1)S(1)}, bf16[3456,128]{1,0:T(8,128)(2,1...) custom-call(bf16[96,128]{1,0:T(8,128)(2,1)S(1)} %collective-permute-, ...), custom_call_target="tpu_custom_call" | custom-call | flops 12000000000 | bytes 4194304 | tf_op jit(solution)/shard_map/pallas_call | solution.py:387
  33.8 0.1 collective-permute-start.4
  33.9 6.7 %collective-permute-start.5 = (bf16[32,128]{1,0:T(8,128)(2,1)S(1)}, bf16[32,128]{1,0:T(8,128)(2,1)S(1)}, u32[]{:S(2)}, u32[]{:S(2)}) collective-permute-start(bf16[32,128]{1,0:T(8,128)(2,1)S(1)} %get-tuple-element.43), channel_id=1, source_target_pairs={{1,2},{2,1},{3,4},{4,3},{5,6},{6,5},{7,8},{8,7},{9,10},{10,9},{11,... | collective-permute-start | bytes 24584 | tf_op jit(solution)/shard_map/ppermute | solution.py:23
  40.6 2.5 %collective-permute-start.6 = (bf16[32,128]{1,0:T(8,128)(2,1)S(1)}, bf16[32,128]{1,0:T(8,128)(2,1)S(1)}, u32[]{:S(2)}, u32[]{:S(2)}) collective-permute-start(bf16[32,128]{1,0:T(8,128)(2,1)S(1)} %get-tuple-element.44), channel_id=1, source_target_pairs={{0,2},{1,3},{2,0},{3,1},{4,6},{5,7},{6,4},{7,5},{8,10},{9,11},{10,... | collective-permute-start | bytes 24584 | tf_op jit(solution)/shard_map/ppermute | solution.py:23
  43.1 0.6 collective-permute-start.7
  43.8 0.0 collective-permute-done.4.refs_0_
  43.8 0.0 collective-permute-done.5.refs_1_
  43.8 0.4 collective-permute-done.6.refs_2_
  44.1 0.0 collective-permute-done.7.refs_3_
  44.1 0.0 copy-done.1
  44.1 0.0 copy-done.3
  44.2 0.0 copy-done.5
  44.2 2.5 %shard_map.113 = (bf16[256,256]{1,0:T(8,128)(2,1)}, bf16[5632,128]{1,0:T(8,128)(2,1)S(1)}, bf16[2816,128]{1,0:T(8,128)(2,1)S(1)}) custom-call(bf16[32,128]{1,0:T(8,128)(2,1)S(1)} %collective-permute-done.4.refs_0_, bf16[32,128]{1,0:T(8,128)(2,1)S(1)} %collective-permute-done.5.refs_1_, bf16[32,128]{1,0:T(8,128)(2,1)S(1)} %collective-permute-done.6.refs_2_, ...), custom_call_target="tpu_custom_call" | custom-call | flops 2000000000 | bytes 4194304 | tf_op jit(solution)/shard_map/pallas_call | solution.py:387
  46.7 0.0 collective-permute-start.8
  46.7 2.2 %collective-permute-done.8.other_ref = bf16[2816,128]{1,0:T(8,128)(2,1)S(1)} collective-permute-done((bf16[2816,128]{1,0:T(8,128)(2,1)S(1)}, bf16[2816,128]{1,0:T(8,128)(2,1)S(1)}, u32[]{:S(2)}, u32[]{:S(2)}) %collective-permute-start.8) | collective-permute-done | bytes 720928 | tf_op jit(solution)/shard_map/ppermute | solution.py:399
  48.9 1.0 shard_map.114.after_ref
  49.9 11.5 %all-to-all-start = ((bf16[32,88,128]{2,1,0:T(8,128)(2,1)}), bf16[32,88,128]{2,1,0:T(8,128)(2,1)S(1)}, u32[]{:S(2)}, u32[]{:S(2)}) async-start(bf16[32,88,128]{2,1,0:T(8,128)(2,1)} %bitcast), calls=%async_computation | async-start | bytes 1441792 | tf_op jit(solution)/shard_map/all_to_all | solution.py:403
  61.5 14.9 %shard_map.115 = (f32[1024,128]{1,0:T(8,128)S(1)}, bf16[64,128]{1,0:T(8,128)(2,1)S(1)}, bf16[64,128]{1,0:T(8,128)(2,1)S(1)}, bf16[64,128]{1,0:T(8,128)(2,1)S(1)}, bf16[64,128]{1,0:T(8,128)(2,1)S(1)}) custom-call(bf16[1024,128]{1,0:T(8,128)(2,1)S(1)} %get-tuple-element.51.pgrad_ref, s32[27,1024]{1,0:T(8,128)S(1)} %copy-done.4, ...), custom_call_target="tpu_custom_call" | custom-call | flops 20000000000 | bytes 4194304 | tf_op jit(solution)/shard_map/pallas_call | solution.py:387
  76.4 0.0 copy-start.7
  76.4 4.0 %all-to-all-done = bf16[32,88,128]{2,1,0:T(8,128)(2,1)S(1)} async-done(((bf16[32,88,128]{2,1,0:T(8,128)(2,1)}), bf16[32,88,128]{2,1,0:T(8,128)(2,1)S(1)}, u32[]{:S(2)}, u32[]{:S(2)}) %all-to-all-start) | async-done | bytes 720928 | tf_op jit(solution)/shard_map/all_to_all | solution.py:403
  80.4 1.0 shard_map.116
  81.4 3.9 %all-to-all-start.1 = ((bf16[32,88,128]{2,1,0:T(8,128)(2,1)}), bf16[32,88,128]{2,1,0:T(8,128)(2,1)S(1)}, u32[]{:S(2)}, u32[]{:S(2)}) async-start(bf16[32,88,128]{2,1,0:T(8,128)(2,1)} %bitcast.2), calls=%async_computation.1 | async-start | bytes 1441792 | tf_op jit(solution)/shard_map/all_to_all | solution.py:403
  85.3 0.3 collective-permute-start.9
  85.6 3.4 %collective-permute-start.10 = (bf16[64,128]{1,0:T(8,128)(2,1)S(1)}, bf16[64,128]{1,0:T(8,128)(2,1)S(1)}, u32[]{:S(2)}, u32[]{:S(2)}) collective-permute-start(bf16[64,128]{1,0:T(8,128)(2,1)S(1)} %get-tuple-element.58), channel_id=1, source_target_pairs={{1,2},{2,1},{3,4},{4,3},{5,6},{6,5},{7,8},{8,7},{9,10},{10,9},{11,... | collective-permute-start | bytes 49160 | tf_op jit(solution)/shard_map/ppermute | solution.py:23
  89.0 1.2 %collective-permute-start.11 = (bf16[64,128]{1,0:T(8,128)(2,1)S(1)}, bf16[64,128]{1,0:T(8,128)(2,1)S(1)}, u32[]{:S(2)}, u32[]{:S(2)}) collective-permute-start(bf16[64,128]{1,0:T(8,128)(2,1)S(1)} %get-tuple-element.59), channel_id=1, source_target_pairs={{0,2},{1,3},{2,0},{3,1},{4,6},{5,7},{6,4},{7,5},{8,10},{9,11},{10,... | collective-permute-start | bytes 49160 | tf_op jit(solution)/shard_map/ppermute | solution.py:23
  90.3 0.7 collective-permute-start.12
  90.9 0.0 collective-permute-done.9.refs_0_
  90.9 0.1 collective-permute-done.10.refs_1_
  91.0 1.6 %collective-permute-done.11.refs_2_ = bf16[64,128]{1,0:T(8,128)(2,1)S(1)} collective-permute-done((bf16[64,128]{1,0:T(8,128)(2,1)S(1)}, bf16[64,128]{1,0:T(8,128)(2,1)S(1)}, u32[]{:S(2)}, u32[]{:S(2)}) %collective-permute-start.11) | collective-permute-done | bytes 16416 | tf_op jit(solution)/shard_map/ppermute | solution.py:23
  92.6 0.0 collective-permute-done.12.refs_3_
  92.6 11.6 %all-to-all-done.1 = bf16[32,88,128]{2,1,0:T(8,128)(2,1)S(1)} async-done(((bf16[32,88,128]{2,1,0:T(8,128)(2,1)}), bf16[32,88,128]{2,1,0:T(8,128)(2,1)S(1)}, u32[]{:S(2)}, u32[]{:S(2)}) %all-to-all-start.1) | async-done | bytes 720928 | tf_op jit(solution)/shard_map/all_to_all | solution.py:403
  104.2 0.7 collective-permute-start.13
  104.9 0.0 copy-done.7
  104.9 1.2 %shard_map.117 = f32[1024,128]{1,0:T(8,128)} custom-call(bf16[64,128]{1,0:T(8,128)(2,1)S(1)} %collective-permute-done.9.refs_0_, bf16[64,128]{1,0:T(8,128)(2,1)S(1)} %collective-permute-done.10.refs_1_, bf16[64,128]{1,0:T(8,128)(2,1)S(1)} %collective-permute-done.11.refs_2_, bf16[64,128]{1,0:T(8,128)(2,1)S(1)} %collective-permute-done.12.refs_3_, ...), custom_call_target="tpu_custom_call" | custom-call | flops 1000000000 | bytes 4194304 | tf_op jit(solution)/shard_map/pallas_call | solution.py:387
  106.2 0.6 collective-permute-done.13.other_ref
  106.7 1.8 %shard_map.118 = (f32[3456,128]{1,0:T(8,128)}, f32[1024,256]{1,0:T(8,128)}) custom-call(bf16[2816,128]{1,0:T(8,128)(2,1)S(1)} %bitcast.7, bf16[2816,128]{1,0:T(8,128)(2,1)S(1)} %collective-permute-done.13.other_ref), custom_call_target="tpu_custom_call" | custom-call | flops 1000000 | bytes 4194304 | tf_op jit(solution)/shard_map/pallas_call | solution.py:387
Async XLA Ops:
  0.6 11.7 %copy-start.2 = (bf16[1024,128]{1,0:T(8,128)(2,1)S(1)}, bf16[1024,128]{1,0:T(8,128)(2,1)}, u32[]{:S(2)}) copy-start(bf16[1024,128]{1,0:T(8,128)(2,1)} %refs_4_.1) | copy-start | bytes 786436
  0.6 11.6 %copy-start.4 = (s32[27,1024]{1,0:T(8,128)S(1)}, s32[27,1024]{1,0:T(8,128)}, u32[]{:S(2)}) copy-start(s32[27,1024]{1,0:T(8,128)} %map_ref.1) | copy-start | bytes 331780
  0.7 11.6 %copy-start = (bf16[27,128,128]{2,1,0:T(8,128)(2,1)S(1)}, bf16[27,128,128]{2,1,0:T(8,128)(2,1)}, u32[]{:S(2)}) copy-start(bf16[27,128,128]{2,1,0:T(8,128)(2,1)} %weight_ref.1) | copy-start | bytes 2654212
  0.7 11.6 %copy-start.6 = (s32[4,32]{1,0:T(4,128)S(1)}, s32[4,32]{1,0:T(4,128)}, u32[]{:S(2)}) copy-start(s32[4,32]{1,0:T(4,128)} %refs_7_.2) | copy-start | bytes 1540
  4.7 6.5 %collective-permute-start = (bf16[96,128]{1,0:T(8,128)(2,1)}, bf16[96,128]{1,0:T(8,128)(2,1)S(1)}, u32[]{:S(2)}, u32[]{:S(2)}) collective-permute-start(bf16[96,128]{1,0:T(8,128)(2,1)} %get-tuple-element.37), channel_id=1, source_target_pairs={{0,1},{1,0},{2,3},{3,2},{4,5},{5,4},{6,7},{7,6},{8,9},{9,8},{10,11... | collective-permute-start | bytes 73736 | tf_op jit(solution)/shard_map/ppermute | solution.py:23
  4.9 6.4 %collective-permute-start.1 = (bf16[96,128]{1,0:T(8,128)(2,1)}, bf16[96,128]{1,0:T(8,128)(2,1)S(1)}, u32[]{:S(2)}, u32[]{:S(2)}) collective-permute-start(bf16[96,128]{1,0:T(8,128)(2,1)} %get-tuple-element.38), channel_id=1, source_target_pairs={{1,2},{2,1},{3,4},{4,3},{5,6},{6,5},{7,8},{8,7},{9,10},{10,9},{11,... | collective-permute-start | bytes 73736 | tf_op jit(solution)/shard_map/ppermute | solution.py:23
  9.3 3.0 %collective-permute-start.2 = (bf16[96,128]{1,0:T(8,128)(2,1)}, bf16[96,128]{1,0:T(8,128)(2,1)S(1)}, u32[]{:S(2)}, u32[]{:S(2)}) collective-permute-start(bf16[96,128]{1,0:T(8,128)(2,1)} %get-tuple-element.39), channel_id=1, source_target_pairs={{0,2},{1,3},{2,0},{3,1},{4,6},{5,7},{6,4},{7,5},{8,10},{9,11},{10,... | collective-permute-start | bytes 73736 | tf_op jit(solution)/shard_map/ppermute | solution.py:23
  10.6 1.7 %collective-permute-start.3 = (bf16[96,128]{1,0:T(8,128)(2,1)}, bf16[96,128]{1,0:T(8,128)(2,1)S(1)}, u32[]{:S(2)}, u32[]{:S(2)}) collective-permute-start(bf16[96,128]{1,0:T(8,128)(2,1)} %get-tuple-element.40), channel_id=1, source_target_pairs={{2,4},{3,5},{4,2},{5,3},{6,8},{7,9},{8,6},{9,7},{10,12},{11,13},{1... | collective-permute-start | bytes 73736 | tf_op jit(solution)/shard_map/ppermute | solution.py:23
  12.3 1.0 copy-start.8
  13.4 30.8 %copy-start.1 = (bf16[8,128,256]{2,1,0:T(8,128)(2,1)S(1)}, bf16[8,128,256]{2,1,0:T(8,128)(2,1)}, u32[]{:S(2)}) copy-start(bf16[8,128,256]{2,1,0:T(8,128)(2,1)} %refs_6_.4) | copy-start | bytes 1572868
  13.4 30.8 %copy-start.3 = (bf16[256,256]{1,0:T(8,128)(2,1)S(1)}, bf16[256,256]{1,0:T(8,128)(2,1)}, u32[]{:S(2)}) copy-start(bf16[256,256]{1,0:T(8,128)(2,1)} %refs_7_.3) | copy-start | bytes 393220
  13.4 30.8 %copy-start.5 = (s32[8,256]{1,0:T(8,128)S(1)}, s32[8,256]{1,0:T(8,128)}, u32[]{:S(2)}) copy-start(s32[8,256]{1,0:T(8,128)} %refs_5_.3) | copy-start | bytes 24580
  33.8 10.0 %collective-permute-start.4 = (bf16[32,128]{1,0:T(8,128)(2,1)S(1)}, bf16[32,128]{1,0:T(8,128)(2,1)S(1)}, u32[]{:S(2)}, u32[]{:S(2)}) collective-permute-start(bf16[32,128]{1,0:T(8,128)(2,1)S(1)} %get-tuple-element.42), channel_id=1, source_target_pairs={{0,1},{1,0},{2,3},{3,2},{4,5},{5,4},{6,7},{7,6},{8,9},{9,8},{10,11... | collective-permute-start | bytes 24584 | tf_op jit(solution)/shard_map/ppermute | solution.py:23
  33.9 9.9 %collective-permute-start.5 = (bf16[32,128]{1,0:T(8,128)(2,1)S(1)}, bf16[32,128]{1,0:T(8,128)(2,1)S(1)}, u32[]{:S(2)}, u32[]{:S(2)}) collective-permute-start(bf16[32,128]{1,0:T(8,128)(2,1)S(1)} %get-tuple-element.43), channel_id=1, source_target_pairs={{1,2},{2,1},{3,4},{4,3},{5,6},{6,5},{7,8},{8,7},{9,10},{10,9},{11,... | collective-permute-start | bytes 24584 | tf_op jit(solution)/shard_map/ppermute | solution.py:23
  40.6 3.6 %collective-permute-start.6 = (bf16[32,128]{1,0:T(8,128)(2,1)S(1)}, bf16[32,128]{1,0:T(8,128)(2,1)S(1)}, u32[]{:S(2)}, u32[]{:S(2)}) collective-permute-start(bf16[32,128]{1,0:T(8,128)(2,1)S(1)} %get-tuple-element.44), channel_id=1, source_target_pairs={{0,2},{1,3},{2,0},{3,1},{4,6},{5,7},{6,4},{7,5},{8,10},{9,11},{10,... | collective-permute-start | bytes 24584 | tf_op jit(solution)/shard_map/ppermute | solution.py:23
  43.1 1.0 collective-permute-start.7
  46.7 2.2 %collective-permute-start.8 = (bf16[2816,128]{1,0:T(8,128)(2,1)S(1)}, bf16[2816,128]{1,0:T(8,128)(2,1)S(1)}, u32[]{:S(2)}, u32[]{:S(2)}) collective-permute-start(bf16[2816,128]{1,0:T(8,128)(2,1)S(1)} %get-tuple-element.50), channel_id=1, source_target_pairs={{0,1},{1,0},{2,3},{3,2},{4,5},{5,4},{6,7},{7,6},{8,9},{9,8},{10,11... | collective-permute-start | bytes 2162696 | tf_op jit(solution)/shard_map/ppermute | solution.py:399
  49.9 30.5 %all-to-all-start = ((bf16[32,88,128]{2,1,0:T(8,128)(2,1)}), bf16[32,88,128]{2,1,0:T(8,128)(2,1)S(1)}, u32[]{:S(2)}, u32[]{:S(2)}) async-start(bf16[32,88,128]{2,1,0:T(8,128)(2,1)} %bitcast), calls=%async_computation | async-start | bytes 1441792 | tf_op jit(solution)/shard_map/all_to_all | solution.py:403
  76.4 28.5 %copy-start.7 = (s32[4,64]{1,0:T(4,128)S(1)}, s32[4,64]{1,0:T(4,128)}, u32[]{:S(2)}) copy-start(s32[4,64]{1,0:T(4,128)} %refs_6_.5) | copy-start | bytes 3076
  81.4 22.8 %all-to-all-start.1 = ((bf16[32,88,128]{2,1,0:T(8,128)(2,1)}), bf16[32,88,128]{2,1,0:T(8,128)(2,1)S(1)}, u32[]{:S(2)}, u32[]{:S(2)}) async-start(bf16[32,88,128]{2,1,0:T(8,128)(2,1)} %bitcast.2), calls=%async_computation.1 | async-start | bytes 1441792 | tf_op jit(solution)/shard_map/all_to_all | solution.py:403
  85.3 5.7 %collective-permute-start.9 = (bf16[64,128]{1,0:T(8,128)(2,1)S(1)}, bf16[64,128]{1,0:T(8,128)(2,1)S(1)}, u32[]{:S(2)}, u32[]{:S(2)}) collective-permute-start(bf16[64,128]{1,0:T(8,128)(2,1)S(1)} %get-tuple-element.57.after_ref), channel_id=1, source_target_pairs={{0,1},{1,0},{2,3},{3,2},{4,5},{5,4},{6,7},{7,6},{8,9},{9,8},{10,11... | collective-permute-start | bytes 49160 | tf_op jit(solution)/shard_map/ppermute | solution.py:23
  85.6 5.4 %collective-permute-start.10 = (bf16[64,128]{1,0:T(8,128)(2,1)S(1)}, bf16[64,128]{1,0:T(8,128)(2,1)S(1)}, u32[]{:S(2)}, u32[]{:S(2)}) collective-permute-start(bf16[64,128]{1,0:T(8,128)(2,1)S(1)} %get-tuple-element.58), channel_id=1, source_target_pairs={{1,2},{2,1},{3,4},{4,3},{5,6},{6,5},{7,8},{8,7},{9,10},{10,9},{11,... | collective-permute-start | bytes 49160 | tf_op jit(solution)/shard_map/ppermute | solution.py:23
  89.0 3.6 %collective-permute-start.11 = (bf16[64,128]{1,0:T(8,128)(2,1)S(1)}, bf16[64,128]{1,0:T(8,128)(2,1)S(1)}, u32[]{:S(2)}, u32[]{:S(2)}) collective-permute-start(bf16[64,128]{1,0:T(8,128)(2,1)S(1)} %get-tuple-element.59), channel_id=1, source_target_pairs={{0,2},{1,3},{2,0},{3,1},{4,6},{5,7},{6,4},{7,5},{8,10},{9,11},{10,... | collective-permute-start | bytes 49160 | tf_op jit(solution)/shard_map/ppermute | solution.py:23
  90.3 2.4 %collective-permute-start.12 = (bf16[64,128]{1,0:T(8,128)(2,1)S(1)}, bf16[64,128]{1,0:T(8,128)(2,1)S(1)}, u32[]{:S(2)}, u32[]{:S(2)}) collective-permute-start(bf16[64,128]{1,0:T(8,128)(2,1)S(1)} %get-tuple-element.60), channel_id=1, source_target_pairs={{2,4},{3,5},{4,2},{5,3},{6,8},{7,9},{8,6},{9,7},{10,12},{11,13},{1... | collective-permute-start | bytes 49160 | tf_op jit(solution)/shard_map/ppermute | solution.py:23
  104.2 2.5 %collective-permute-start.13 = (bf16[2816,128]{1,0:T(8,128)(2,1)S(1)}, bf16[2816,128]{1,0:T(8,128)(2,1)S(1)}, u32[]{:S(2)}, u32[]{:S(2)}) collective-permute-start(bf16[2816,128]{1,0:T(8,128)(2,1)S(1)} %bitcast.6), channel_id=1, source_target_pairs={{0,1},{1,0},{2,3},{3,2},{4,5},{5,4},{6,7},{7,6},{8,9},{9,8},{10,11... | collective-permute-start | bytes 2162696 | tf_op jit(solution)/shard_map/ppermute | solution.py:399

commit v6 on v5

--- a/solution.py
+++ b/solution.py
@@ -13,15 +13,15 @@
 LANES = 128
 
 
-def swaps(by_step, reach):
+def swaps(by_step, order):
     devices = lax.axis_size("shard")
-    moved = []
-    for m in range(1, reach + 1):
-        for phase in range(2):
-            sign = [1 if (i // m) % 2 == phase else -1 for i in range(devices)]
-            pairs = [(i, i + m * sign[i]) for i in range(devices) if 0 <= i + m * sign[i] < devices]
-            moved.append(lax.ppermute(by_step[len(moved)], "shard", pairs))
-    return moved
+    moved = {}
+    for step in order:
+        m, phase = step // 2 + 1, step % 2
+        sign = [1 if (i // m) % 2 == phase else -1 for i in range(devices)]
+        pairs = [(i, i + m * sign[i]) for i in range(devices) if 0 <= i + m * sign[i] < devices]
+        moved[step] = lax.ppermute(by_step[step], "shard", pairs)
+    return [moved[step] for step in range(len(by_step))]
 
 
 def is_even(m):
@@ -99,6 +99,17 @@
 def list_row(lists, first, per_row):
     pieces = [lists[first + n : first + n + 1, :] for n in range(per_row)]
     return pieces[0] if per_row == 1 else jnp.concatenate(pieces, axis=1)
+
+
+def add_lists(total, lists_ref, blocks):
+    slots, cap = lists_ref.shape
+    codes = encode(lists_ref[...]).astype(F32)
+    per_row = max(1, min(slots, LANES // cap))
+    for first in range(0, slots, per_row):
+        row = list_row(codes, first, per_row).astype(BF16)
+        rows = jnp.concatenate(blocks[first : first + per_row], axis=0)
+        total = total + matmul(one_hot_columns(row, total.shape[0]), rows)
+    return total
 
 
 def gather_lists(lists_ref, table):
@@ -167,13 +178,11 @@
 
 def forward_kernel(slots, *refs):
     received = refs[:slots]
-    (features_ref, map_ref, weight_ref, child_ref, back_hbm) = refs[slots : slots + 5]
-    (hidden_ref, hgrad_ref, pgrad_ref, cgrad_ref) = refs[slots + 5 : slots + 9]
-    sends = refs[slots + 9 : 2 * slots + 9]
-    (table_ref, stacked_ref, acc_ref, back_ref, sem) = refs[2 * slots + 9 : 2 * slots + 14]
-    chooser_refs, col_refs = refs[2 * slots + 14 : 2 * slots + 16], refs[2 * slots + 16 :]
-    back_copy = pltpu.make_async_copy(back_hbm, back_ref, sem)
-    back_copy.start()
+    features_ref, map_ref, weight_ref, child_ref = refs[slots : slots + 4]
+    hidden_ref, pre_ref, stacked_ref = refs[slots + 4 : slots + 7]
+    sends = refs[slots + 7 : 2 * slots + 7]
+    table_ref, acc_ref = refs[2 * slots + 7 : 2 * slots + 9]
+    chooser_refs, col_refs = refs[2 * slots + 9 : 2 * slots + 11], refs[2 * slots + 11 :]
     voxels = features_ref.shape[0]
     kernel_count = map_ref.shape[0]
     middle = kernel_count // 2
@@ -223,36 +232,39 @@
     lax.fori_loop(0, middle // 2, step, 0)
     convolve(middle - 1, use(middle - 1, 0))
     pre = acc_ref[...]
-    sig = jax.nn.sigmoid(pre)
-    hidden = (features.astype(F32) + pre * sig).astype(BF16)
+    pre_ref[...] = pre
+    hidden = (features.astype(F32) + pre * jax.nn.sigmoid(pre)).astype(BF16)
     hidden_ref[...] = hidden
     leaving = gather_lists(child_ref, hidden).astype(BF16)
     for send, block in zip(sends, to_steps(jnp.split(leaving, slots), False)):
         send[...] = block
-    back_copy.wait()
-    hgrad = back_ref[...]
-    lists = encode(child_ref[...]).astype(BF16)
-    for s, block in enumerate(to_slots([r[cap : cap + cap2, :] for r in received], True)):
-        hgrad = hgrad + matmul(one_hot_columns(lists[s : s + 1, :], voxels), block)
+
+
+def gradient_kernel(slots, *refs):
+    received = refs[:slots]
+    stacked_ref, pre_ref, features_ref, child_ref, back_ref = refs[slots : slots + 5]
+    hgrad_ref, pgrad_ref, cgrad_ref = refs[slots + 5 :]
+    cap2 = child_ref.shape[1]
+    cap = received[0].shape[0] - cap2
+    middle = stacked_ref.shape[0] // 2
+    blocks = to_slots([r[cap : cap + cap2, :] for r in received], True)
+    hgrad = add_lists(back_ref[...], child_ref, blocks)
     hgrad_ref[...] = hgrad
+    pre = pre_ref[...]
+    sig = jax.nn.sigmoid(pre)
     pgrad = hgrad * (sig * (1.0 + pre * (1.0 - sig)))
     pgrad_ref[...] = pgrad.astype(BF16)
     pgrad_t = jnp.transpose(pgrad).astype(BF16)
 
     def put(k, value):
-        cgrad_ref[pl.ds(pl.multiple_of(k * LANES, LANES), LANES), :] = jnp.transpose(value).astype(BF16)
-
-    put(middle, matmul(pgrad_t, features))
-
-    def weight_step(j, carry):
+        cgrad_ref[k * LANES : (k + 1) * LANES, :] = jnp.transpose(value).astype(BF16)
+
+    put(middle, matmul(pgrad_t, features_ref[...]))
+    for j in range(middle):
         pair = jnp.concatenate([stacked_ref[j], stacked_ref[j + middle + 1]], axis=1)
         both = matmul(pgrad_t, pair)
         put(j, both[:, :LANES])
         put(j + middle + 1, both[:, LANES:])
-        return carry
-
-    for j in range(middle):
-        weight_step(j, 0)
 
 
 def spread_kernel(slots, pgrad_ref, map_ref, weight_ref, after_ref, back_ref, *sends):
@@ -374,12 +386,8 @@
 def tail_kernel(slots, *refs):
     received = refs[:slots]
     hgrad_ref, back_ref, halo_ref, out_ref = refs[slots:]
-    voxels = hgrad_ref.shape[0]
-    total = hgrad_ref[...] + back_ref[...]
-    lists = encode(halo_ref[...]).astype(BF16)
-    for s, block in enumerate(to_slots([r[...] for r in received], True)):
-        total = total + matmul(one_hot_columns(lists[s : s + 1, :], voxels), block)
-    out_ref[...] = total
+    blocks = to_slots([r[...] for r in received], True)
+    out_ref[...] = add_lists(hgrad_ref[...] + back_ref[...], halo_ref, blocks)
 
 
 def call(kernel, operands, outs, scratch=(), limit=32, flops=0, in_hbm=()):
@@ -412,7 +420,6 @@
     octants = down_weight.shape[0]
     slots, cap = halo_rows.shape
     cap2 = child_rows.shape[1]
-    reach = slots // 2
     devices = lax.axis_size("shard")
     scale = 1.0 / math.sqrt(voxels * devices)
     giga = 10**9
@@ -431,35 +438,40 @@
         in_hbm=range(5),
     )
     back_h = first[-1]
-    received = swaps(first[:-1], reach)
+    received = swaps(first[:-1], (2, 3, 1, 0))
     conv_rows = kernel_count * channels
     down_rows = octants * channels * coarse_channels // LANES
     grain = 8 * devices
     half_rows = -(-(conv_rows + down_rows) // (2 * grain)) * grain
-    hidden, hidden_grad, pre_grad, conv_terms, *leaving = call(
+    hidden, pre_act, stacked, *leaving = call(
         functools.partial(forward_kernel, slots),
-        (*received, features, neighbour_map, conv_weight, child_rows, back_h),
+        (*received, features, neighbour_map, conv_weight, child_rows),
         [
             ((voxels, channels), BF16),
             ((voxels, channels), F32),
-            ((voxels, channels), BF16),
-            ((conv_rows, channels), BF16),
+            ((kernel_count, voxels, channels), BF16),
         ]
         + [((cap2, channels), BF16)] * slots,
         scratch=[
             pltpu.VMEM((voxels // 2 + slots * cap // 2, 2 * channels), BF16),
-            pltpu.VMEM((kernel_count, voxels, channels), BF16),
             pltpu.VMEM((voxels, channels), F32),
-            pltpu.VMEM((voxels, channels), F32),
-            pltpu.SemaphoreType.DMA(()),
         ]
         + [pltpu.VMEM((2, voxels, (voxels + slots * cap) // 2), BF16)] * 2
         + [pltpu.VMEM((2, voxels, LANES), BF16)] * 2,
-        limit=48,
+        limit=32,
         flops=12 * giga,
-        in_hbm=(slots + 4,),
-    )
-    received_h = swaps(leaving, reach)
+    )
+    hidden_grad, pre_grad, conv_terms = call(
+        functools.partial(gradient_kernel, slots),
+        (*received, stacked, pre_act, features, child_rows, back_h),
+        [
+            ((voxels, channels), F32),
+            ((voxels, channels), BF16),
+            ((conv_rows, channels), BF16),
+        ],
+        flops=3 * giga,
+    )
+    received_h = swaps(leaving, (1, 3, 2, 0))
     coarse, terms, leaving_terms = call(
         functools.partial(down_kernel, slots),
         (*received_h, hidden, child_map, down_weight, out_grad, conv_terms),
@@ -494,7 +506,7 @@
         in_hbm=(1,),
     )
     summed, *returning = lax.optimization_barrier((summed, *spread[1:]))
-    mine, *returned = lax.optimization_barrier((exchange(summed), *swaps(returning, reach)))
+    mine, *returned = lax.optimization_barrier((exchange(summed), *swaps(returning, (3, 1, 0, 2))))
     (input_grad,) = call(
         functools.partial(tail_kernel, slots),
         (*returned, hidden_grad, spread[0], halo_rows),

time: 109 us -> 106 us (0.972)
    all_to_all x2, starting transfers between devices: 15.4 us -> 14.1 us  [exchange(): return lax.all_to_all(value, 'shard', 0, 0, tiled=True)]
    pallas_call x8 -> x9, Pallas kernels: 46.9 us -> 46.3 us  [call(): pl.pallas_call(kernel, out_shape=[jax.ShapeDtypeStruct(s, d) for s, d in...]
  transfers between devices with their start and end apart: 16 -> 16, of which waited for: 8 -> 7; matrix products, arithmetic and copies ran while one was open for 0% -> 0% of each run, Pallas kernels for 15% -> 17%
where the time goes in v6:
time: 106 us; the launch traced here: 105 us
  Pallas kernels  46.3 us (44%)
  starting transfers between devices  37.2 us (35%)
  waiting for transfers between devices  21 us (20%)
    pallas_call x9, Pallas kernels, call(): pl.pallas_call(kernel, out_shape=[jax.ShapeDtypeStruct(s, d) for s, d in...  46.3 us
    ppermute x12, starting transfers between devices, swaps(): moved[step] = lax.ppermute(by_step[step], 'shard', pairs)  22.4 us
    all_to_all x2, waiting for transfers between devices, exchange(): return lax.all_to_all(value, 'shard', 0, 0, tiled=True)  15.6 us
    all_to_all x2, starting transfers between devices, exchange(): return lax.all_to_all(value, 'shard', 0, 0, tiled=True)  14.1 us
    ppermute x2, waiting for transfers between devices, swap_cores(): lax.ppermute(value, 'shard', [(i, i + 1 - 2 * (i % 2)) for i in range(dev...  2.85 us
    ppermute x12, waiting for transfers between devices, swaps(): moved[step] = lax.ppermute(by_step[step], 'shard', pairs)  2.57 us
  transfers between devices with their start and end apart: 16, of which 7 were waited for; matrix products, arithmetic and copies ran while one was open for 0% of the time, Pallas kernels for 17%

profile of v6, /device:TPU:1, one launch (start us, length us, event | category | flops | bytes accessed | tf_op | source)
XLA Modules:
  0.0 105.5 jit_solution(16708974357558497265)
XLA Ops:
  0.6 0.0 copy-start.2
  0.6 0.0 copy-start.6
  0.7 0.0 copy-start.4
  0.7 0.0 copy-start
  0.7 4.1 %shard_map.111 = (bf16[96,128]{1,0:T(8,128)(2,1)}, bf16[96,128]{1,0:T(8,128)(2,1)}, bf16[96,128]{1,0:T(8,128)(2,1)}, bf16[96,128]{1,0:T(8,128)(2,1)}, f32[1024,128]{1,0:T(8,128)}) custom-call(bf16[1024,128]{1,0:T(8,128)(2,1)} %refs_6_.5, s32[4,64]{1,0:T(4,128)} %refs_6_.7, s32[8,256]{1,0:T(8,128)} %refs_5_.3, bf16[256,256]{1,0:T(8,128)(2,1)} %refs_7_.5, ...), custom_call_target="tpu_custom_call" | custom-call | flops 1000000000 | bytes 4194304 | tf_op jit(solution)/shard_map/pallas_call | solution.py:395
  4.7 0.1 collective-permute-start
  4.9 4.5 %collective-permute-start.1 = (bf16[96,128]{1,0:T(8,128)(2,1)}, bf16[96,128]{1,0:T(8,128)(2,1)S(1)}, u32[]{:S(2)}, u32[]{:S(2)}) collective-permute-start(bf16[96,128]{1,0:T(8,128)(2,1)} %get-tuple-element.40), channel_id=1, source_target_pairs={{1,2},{2,1},{3,4},{4,3},{5,6},{6,5},{7,8},{8,7},{9,10},{10,9},{11,... | collective-permute-start | bytes 73736 | tf_op jit(solution)/shard_map/ppermute | solution.py:23
  9.3 1.3 %collective-permute-start.2 = (bf16[96,128]{1,0:T(8,128)(2,1)}, bf16[96,128]{1,0:T(8,128)(2,1)S(1)}, u32[]{:S(2)}, u32[]{:S(2)}) collective-permute-start(bf16[96,128]{1,0:T(8,128)(2,1)} %get-tuple-element.41), channel_id=1, source_target_pairs={{0,2},{1,3},{2,0},{3,1},{4,6},{5,7},{6,4},{7,5},{8,10},{9,11},{10,... | collective-permute-start | bytes 73736 | tf_op jit(solution)/shard_map/ppermute | solution.py:23
  10.6 0.0 copy-start.8
  10.6 0.8 collective-permute-start.3
  11.4 0.0 collective-permute-done.refs_0_
  11.4 0.0 collective-permute-done.1.refs_1_
  11.4 0.9 collective-permute-done.2.refs_2_
  12.3 0.0 collective-permute-done.3.refs_3_
  12.3 0.0 copy-done.2
  12.3 0.0 copy-done.6
  12.3 0.0 copy-done.4
  12.3 0.0 copy-done
  12.3 18.3 %shard_map.112 = (bf16[1024,128]{1,0:T(8,128)(2,1)S(1)}, f32[1024,128]{1,0:T(8,128)S(1)}, bf16[27,1024,128]{2,1,0:T(8,128)(2,1)S(1)}, bf16[32,128]{1,0:T(8,128)(...) custom-call(bf16[96,128]{1,0:T(8,128)(2,1)S(1)} %collective-permute-done.refs_0_, ...), custom_call_target="tpu_custom_call" | custom-call | flops 12000000000 | bytes 4194304 | tf_op jit(solution)/shard_map/pallas_call | solution.py:395
  30.6 0.1 collective-permute-start.4
  30.7 6.8 %collective-permute-start.5 = (bf16[32,128]{1,0:T(8,128)(2,1)S(1)}, bf16[32,128]{1,0:T(8,128)(2,1)S(1)}, u32[]{:S(2)}, u32[]{:S(2)}) collective-permute-start(bf16[32,128]{1,0:T(8,128)(2,1)S(1)} %get-tuple-element.44), channel_id=1, source_target_pairs={{1,2},{2,1},{3,4},{4,3},{5,6},{6,5},{7,8},{8,7},{9,10},{10,9},{11,... | collective-permute-start | bytes 24584 | tf_op jit(solution)/shard_map/ppermute | solution.py:23
  37.5 2.5 %collective-permute-start.6 = (bf16[32,128]{1,0:T(8,128)(2,1)S(1)}, bf16[32,128]{1,0:T(8,128)(2,1)S(1)}, u32[]{:S(2)}, u32[]{:S(2)}) collective-permute-start(bf16[32,128]{1,0:T(8,128)(2,1)S(1)} %get-tuple-element.45), channel_id=1, source_target_pairs={{0,2},{1,3},{2,0},{3,1},{4,6},{5,7},{6,4},{7,5},{8,10},{9,11},{10,... | collective-permute-start | bytes 24584 | tf_op jit(solution)/shard_map/ppermute | solution.py:23
  40.1 0.6 collective-permute-start.7
  40.7 0.0 copy-done.8
  40.7 0.0 copy-start.1
  40.7 0.0 copy-start.3
  40.7 0.0 copy-start.5
  40.8 1.6 %shard_map.113 = (f32[1024,128]{1,0:T(8,128)S(1)}, bf16[1024,128]{1,0:T(8,128)(2,1)S(1)}, bf16[3456,128]{1,0:T(8,128)(2,1)S(1)}) custom-call(bf16[96,128]{1,0:T(8,128)(2,1)S(1)} %collective-permute-done.refs_0_, bf16[96,128]{1,0:T(8,128)(2,1)S(1)} %collective-permute-done.1.refs_1_, bf16[96,128]{1,0:T(8,128)(2,1)S(1)} %collective-permute-done.2.refs_2_, ...), custom_call_target="tpu_custom_call" | custom-call | flops 3000000000 | bytes 4194304 | tf_op jit(solution)/shard_map/pallas_call | solution.py:395
  42.3 0.0 collective-permute-done.4.refs_0_
  42.3 0.0 collective-permute-done.5.refs_1_
  42.3 0.0 collective-permute-done.6.refs_2_
  42.4 0.0 collective-permute-done.7.refs_3_
  42.4 0.0 copy-done.1
  42.4 0.0 copy-done.3
  42.4 0.0 copy-done.5
  42.4 2.5 %shard_map.114 = (bf16[256,256]{1,0:T(8,128)(2,1)}, bf16[5632,128]{1,0:T(8,128)(2,1)S(1)}, bf16[2816,128]{1,0:T(8,128)(2,1)S(1)}) custom-call(bf16[32,128]{1,0:T(8,128)(2,1)S(1)} %collective-permute-done.4.refs_0_, bf16[32,128]{1,0:T(8,128)(2,1)S(1)} %collective-permute-done.5.refs_1_, bf16[32,128]{1,0:T(8,128)(2,1)S(1)} %collective-permute-done.6.refs_2_, ...), custom_call_target="tpu_custom_call" | custom-call | flops 2000000000 | bytes 4194304 | tf_op jit(solution)/shard_map/pallas_call | solution.py:395
  44.9 0.0 collective-permute-start.8
  44.9 2.2 %collective-permute-done.8.other_ref = bf16[2816,128]{1,0:T(8,128)(2,1)S(1)} collective-permute-done((bf16[2816,128]{1,0:T(8,128)(2,1)S(1)}, bf16[2816,128]{1,0:T(8,128)(2,1)S(1)}, u32[]{:S(2)}, u32[]{:S(2)}) %collective-permute-start.8) | collective-permute-done | bytes 720928 | tf_op jit(solution)/shard_map/ppermute | solution.py:407
  47.1 1.0 shard_map.115.after_ref
  48.2 10.2 %all-to-all-start = ((bf16[32,88,128]{2,1,0:T(8,128)(2,1)}), bf16[32,88,128]{2,1,0:T(8,128)(2,1)S(1)}, u32[]{:S(2)}, u32[]{:S(2)}) async-start(bf16[32,88,128]{2,1,0:T(8,128)(2,1)} %bitcast), calls=%async_computation | async-start | bytes 1441792 | tf_op jit(solution)/shard_map/all_to_all | solution.py:411
  58.4 14.9 %shard_map.116 = (f32[1024,128]{1,0:T(8,128)S(1)}, bf16[64,128]{1,0:T(8,128)(2,1)S(1)}, bf16[64,128]{1,0:T(8,128)(2,1)S(1)}, bf16[64,128]{1,0:T(8,128)(2,1)S(1)}, bf16[64,128]{1,0:T(8,128)(2,1)S(1)}) custom-call(bf16[1024,128]{1,0:T(8,128)(2,1)S(1)} %get-tuple-element.55.pgrad_ref, s32[27,1024]{1,0:T(8,128)S(1)} %copy-done.4, ...), custom_call_target="tpu_custom_call" | custom-call | flops 20000000000 | bytes 4194304 | tf_op jit(solution)/shard_map/pallas_call | solution.py:395
  73.4 0.0 copy-start.7
  73.4 4.0 %all-to-all-done = bf16[32,88,128]{2,1,0:T(8,128)(2,1)S(1)} async-done(((bf16[32,88,128]{2,1,0:T(8,128)(2,1)}), bf16[32,88,128]{2,1,0:T(8,128)(2,1)S(1)}, u32[]{:S(2)}, u32[]{:S(2)}) %all-to-all-start) | async-done | bytes 720928 | tf_op jit(solution)/shard_map/all_to_all | solution.py:411
  77.4 1.0 shard_map.117
  78.4 3.9 %all-to-all-start.1 = ((bf16[32,88,128]{2,1,0:T(8,128)(2,1)}), bf16[32,88,128]{2,1,0:T(8,128)(2,1)S(1)}, u32[]{:S(2)}, u32[]{:S(2)}) async-start(bf16[32,88,128]{2,1,0:T(8,128)(2,1)} %bitcast.2), calls=%async_computation.1 | async-start | bytes 1441792 | tf_op jit(solution)/shard_map/all_to_all | solution.py:411
  82.2 0.3 collective-permute-start.9
  82.6 3.4 %collective-permute-start.10 = (bf16[64,128]{1,0:T(8,128)(2,1)S(1)}, bf16[64,128]{1,0:T(8,128)(2,1)S(1)}, u32[]{:S(2)}, u32[]{:S(2)}) collective-permute-start(bf16[64,128]{1,0:T(8,128)(2,1)S(1)} %get-tuple-element.62), channel_id=1, source_target_pairs={{1,2},{2,1},{3,4},{4,3},{5,6},{6,5},{7,8},{8,7},{9,10},{10,9},{11,... | collective-permute-start | bytes 49160 | tf_op jit(solution)/shard_map/ppermute | solution.py:23
  86.0 1.2 %collective-permute-start.11 = (bf16[64,128]{1,0:T(8,128)(2,1)S(1)}, bf16[64,128]{1,0:T(8,128)(2,1)S(1)}, u32[]{:S(2)}, u32[]{:S(2)}) collective-permute-start(bf16[64,128]{1,0:T(8,128)(2,1)S(1)} %get-tuple-element.63), channel_id=1, source_target_pairs={{0,2},{1,3},{2,0},{3,1},{4,6},{5,7},{6,4},{7,5},{8,10},{9,11},{10,... | collective-permute-start | bytes 49160 | tf_op jit(solution)/shard_map/ppermute | solution.py:23
  87.2 0.7 collective-permute-start.12
  87.9 0.0 collective-permute-done.9.refs_0_
  87.9 0.1 collective-permute-done.10.refs_1_
  88.0 1.6 %collective-permute-done.11.refs_2_ = bf16[64,128]{1,0:T(8,128)(2,1)S(1)} collective-permute-done((bf16[64,128]{1,0:T(8,128)(2,1)S(1)}, bf16[64,128]{1,0:T(8,128)(2,1)S(1)}, u32[]{:S(2)}, u32[]{:S(2)}) %collective-permute-start.11) | collective-permute-done | bytes 16416 | tf_op jit(solution)/shard_map/ppermute | solution.py:23
  89.6 0.0 collective-permute-done.12.refs_3_
  89.6 11.6 %all-to-all-done.1 = bf16[32,88,128]{2,1,0:T(8,128)(2,1)S(1)} async-done(((bf16[32,88,128]{2,1,0:T(8,128)(2,1)}), bf16[32,88,128]{2,1,0:T(8,128)(2,1)S(1)}, u32[]{:S(2)}, u32[]{:S(2)}) %all-to-all-start.1) | async-done | bytes 720928 | tf_op jit(solution)/shard_map/all_to_all | solution.py:411
  101.2 0.7 collective-permute-start.13
  101.9 0.0 copy-done.7
  101.9 1.2 %shard_map.118 = f32[1024,128]{1,0:T(8,128)} custom-call(bf16[64,128]{1,0:T(8,128)(2,1)S(1)} %collective-permute-done.9.refs_0_, bf16[64,128]{1,0:T(8,128)(2,1)S(1)} %collective-permute-done.10.refs_1_, bf16[64,128]{1,0:T(8,128)(2,1)S(1)} %collective-permute-done.11.refs_2_, bf16[64,128]{1,0:T(8,128)(2,1)S(1)} %collective-permute-done.12.refs_3_, ...), custom_call_target="tpu_custom_call" | custom-call | flops 1000000000 | bytes 4194304 | tf_op jit(solution)/shard_map/pallas_call | solution.py:395
  103.0 0.7 collective-permute-done.13.other_ref
  103.7 1.8 %shard_map.119 = (f32[3456,128]{1,0:T(8,128)}, f32[1024,256]{1,0:T(8,128)}) custom-call(bf16[2816,128]{1,0:T(8,128)(2,1)S(1)} %bitcast.7, bf16[2816,128]{1,0:T(8,128)(2,1)S(1)} %collective-permute-done.13.other_ref), custom_call_target="tpu_custom_call" | custom-call | flops 1000000 | bytes 4194304 | tf_op jit(solution)/shard_map/pallas_call | solution.py:395
Async XLA Ops:
  0.6 11.7 %copy-start.2 = (bf16[1024,128]{1,0:T(8,128)(2,1)S(1)}, bf16[1024,128]{1,0:T(8,128)(2,1)}, u32[]{:S(2)}) copy-start(bf16[1024,128]{1,0:T(8,128)(2,1)} %refs_6_.5) | copy-start | bytes 786436
  0.6 11.6 %copy-start.6 = (s32[4,32]{1,0:T(4,128)S(1)}, s32[4,32]{1,0:T(4,128)}, u32[]{:S(2)}) copy-start(s32[4,32]{1,0:T(4,128)} %refs_7_.4) | copy-start | bytes 1540
  0.7 11.6 %copy-start.4 = (s32[27,1024]{1,0:T(8,128)S(1)}, s32[27,1024]{1,0:T(8,128)}, u32[]{:S(2)}) copy-start(s32[27,1024]{1,0:T(8,128)} %map_ref.1) | copy-start | bytes 331780
  0.7 11.6 %copy-start = (bf16[27,128,128]{2,1,0:T(8,128)(2,1)S(1)}, bf16[27,128,128]{2,1,0:T(8,128)(2,1)}, u32[]{:S(2)}) copy-start(bf16[27,128,128]{2,1,0:T(8,128)(2,1)} %weight_ref.1) | copy-start | bytes 2654212
  4.7 6.7 %collective-permute-start = (bf16[96,128]{1,0:T(8,128)(2,1)}, bf16[96,128]{1,0:T(8,128)(2,1)S(1)}, u32[]{:S(2)}, u32[]{:S(2)}) collective-permute-start(bf16[96,128]{1,0:T(8,128)(2,1)} %get-tuple-element.39), channel_id=1, source_target_pairs={{0,1},{1,0},{2,3},{3,2},{4,5},{5,4},{6,7},{7,6},{8,9},{9,8},{10,11... | collective-permute-start | bytes 73736 | tf_op jit(solution)/shard_map/ppermute | solution.py:23
  4.9 6.6 %collective-permute-start.1 = (bf16[96,128]{1,0:T(8,128)(2,1)}, bf16[96,128]{1,0:T(8,128)(2,1)S(1)}, u32[]{:S(2)}, u32[]{:S(2)}) collective-permute-start(bf16[96,128]{1,0:T(8,128)(2,1)} %get-tuple-element.40), channel_id=1, source_target_pairs={{1,2},{2,1},{3,4},{4,3},{5,6},{6,5},{7,8},{8,7},{9,10},{10,9},{11,... | collective-permute-start | bytes 73736 | tf_op jit(solution)/shard_map/ppermute | solution.py:23
  9.3 3.0 %collective-permute-start.2 = (bf16[96,128]{1,0:T(8,128)(2,1)}, bf16[96,128]{1,0:T(8,128)(2,1)S(1)}, u32[]{:S(2)}, u32[]{:S(2)}) collective-permute-start(bf16[96,128]{1,0:T(8,128)(2,1)} %get-tuple-element.41), channel_id=1, source_target_pairs={{0,2},{1,3},{2,0},{3,1},{4,6},{5,7},{6,4},{7,5},{8,10},{9,11},{10,... | collective-permute-start | bytes 73736 | tf_op jit(solution)/shard_map/ppermute | solution.py:23
  10.6 30.1 %copy-start.8 = (f32[1024,128]{1,0:T(8,128)S(1)}, f32[1024,128]{1,0:T(8,128)}, u32[]{:S(2)}) copy-start(f32[1024,128]{1,0:T(8,128)} %get-tuple-element.50.refs_8_) | copy-start | bytes 1572868
  10.6 1.7 %collective-permute-start.3 = (bf16[96,128]{1,0:T(8,128)(2,1)}, bf16[96,128]{1,0:T(8,128)(2,1)S(1)}, u32[]{:S(2)}, u32[]{:S(2)}) collective-permute-start(bf16[96,128]{1,0:T(8,128)(2,1)} %get-tuple-element.42), channel_id=1, source_target_pairs={{2,4},{3,5},{4,2},{5,3},{6,8},{7,9},{8,6},{9,7},{10,12},{11,13},{1... | collective-permute-start | bytes 73736 | tf_op jit(solution)/shard_map/ppermute | solution.py:23
  30.6 11.7 %collective-permute-start.4 = (bf16[32,128]{1,0:T(8,128)(2,1)S(1)}, bf16[32,128]{1,0:T(8,128)(2,1)S(1)}, u32[]{:S(2)}, u32[]{:S(2)}) collective-permute-start(bf16[32,128]{1,0:T(8,128)(2,1)S(1)} %get-tuple-element.43), channel_id=1, source_target_pairs={{0,1},{1,0},{2,3},{3,2},{4,5},{5,4},{6,7},{7,6},{8,9},{9,8},{10,11... | collective-permute-start | bytes 24584 | tf_op jit(solution)/shard_map/ppermute | solution.py:23
  30.7 11.6 %collective-permute-start.5 = (bf16[32,128]{1,0:T(8,128)(2,1)S(1)}, bf16[32,128]{1,0:T(8,128)(2,1)S(1)}, u32[]{:S(2)}, u32[]{:S(2)}) collective-permute-start(bf16[32,128]{1,0:T(8,128)(2,1)S(1)} %get-tuple-element.44), channel_id=1, source_target_pairs={{1,2},{2,1},{3,4},{4,3},{5,6},{6,5},{7,8},{8,7},{9,10},{10,9},{11,... | collective-permute-start | bytes 24584 | tf_op jit(solution)/shard_map/ppermute | solution.py:23
  37.5 4.8 %collective-permute-start.6 = (bf16[32,128]{1,0:T(8,128)(2,1)S(1)}, bf16[32,128]{1,0:T(8,128)(2,1)S(1)}, u32[]{:S(2)}, u32[]{:S(2)}) collective-permute-start(bf16[32,128]{1,0:T(8,128)(2,1)S(1)} %get-tuple-element.45), channel_id=1, source_target_pairs={{0,2},{1,3},{2,0},{3,1},{4,6},{5,7},{6,4},{7,5},{8,10},{9,11},{10,... | collective-permute-start | bytes 24584 | tf_op jit(solution)/shard_map/ppermute | solution.py:23
  40.1 2.3 %collective-permute-start.7 = (bf16[32,128]{1,0:T(8,128)(2,1)S(1)}, bf16[32,128]{1,0:T(8,128)(2,1)S(1)}, u32[]{:S(2)}, u32[]{:S(2)}) collective-permute-start(bf16[32,128]{1,0:T(8,128)(2,1)S(1)} %get-tuple-element.46), channel_id=1, source_target_pairs={{2,4},{3,5},{4,2},{5,3},{6,8},{7,9},{8,6},{9,7},{10,12},{11,13},{1... | collective-permute-start | bytes 24584 | tf_op jit(solution)/shard_map/ppermute | solution.py:23
  40.7 1.6 %copy-start.1 = (bf16[8,128,256]{2,1,0:T(8,128)(2,1)S(1)}, bf16[8,128,256]{2,1,0:T(8,128)(2,1)}, u32[]{:S(2)}) copy-start(bf16[8,128,256]{2,1,0:T(8,128)(2,1)} %refs_6_.6) | copy-start | bytes 1572868
  40.7 1.6 %copy-start.3 = (bf16[256,256]{1,0:T(8,128)(2,1)S(1)}, bf16[256,256]{1,0:T(8,128)(2,1)}, u32[]{:S(2)}) copy-start(bf16[256,256]{1,0:T(8,128)(2,1)} %refs_7_.5) | copy-start | bytes 393220
  40.7 1.6 %copy-start.5 = (s32[8,256]{1,0:T(8,128)S(1)}, s32[8,256]{1,0:T(8,128)}, u32[]{:S(2)}) copy-start(s32[8,256]{1,0:T(8,128)} %refs_5_.3) | copy-start | bytes 24580
  44.9 2.2 %collective-permute-start.8 = (bf16[2816,128]{1,0:T(8,128)(2,1)S(1)}, bf16[2816,128]{1,0:T(8,128)(2,1)S(1)}, u32[]{:S(2)}, u32[]{:S(2)}) collective-permute-start(bf16[2816,128]{1,0:T(8,128)(2,1)S(1)} %get-tuple-element.54), channel_id=1, source_target_pairs={{0,1},{1,0},{2,3},{3,2},{4,5},{5,4},{6,7},{7,6},{8,9},{9,8},{10,11... | collective-permute-start | bytes 2162696 | tf_op jit(solution)/shard_map/ppermute | solution.py:407
  48.2 29.2 %all-to-all-start = ((bf16[32,88,128]{2,1,0:T(8,128)(2,1)}), bf16[32,88,128]{2,1,0:T(8,128)(2,1)S(1)}, u32[]{:S(2)}, u32[]{:S(2)}) async-start(bf16[32,88,128]{2,1,0:T(8,128)(2,1)} %bitcast), calls=%async_computation | async-start | bytes 1441792 | tf_op jit(solution)/shard_map/all_to_all | solution.py:411
  73.4 28.5 %copy-start.7 = (s32[4,64]{1,0:T(4,128)S(1)}, s32[4,64]{1,0:T(4,128)}, u32[]{:S(2)}) copy-start(s32[4,64]{1,0:T(4,128)} %refs_6_.7) | copy-start | bytes 3076
  78.4 22.8 %all-to-all-start.1 = ((bf16[32,88,128]{2,1,0:T(8,128)(2,1)}), bf16[32,88,128]{2,1,0:T(8,128)(2,1)S(1)}, u32[]{:S(2)}, u32[]{:S(2)}) async-start(bf16[32,88,128]{2,1,0:T(8,128)(2,1)} %bitcast.2), calls=%async_computation.1 | async-start | bytes 1441792 | tf_op jit(solution)/shard_map/all_to_all | solution.py:411
  82.2 5.7 %collective-permute-start.9 = (bf16[64,128]{1,0:T(8,128)(2,1)S(1)}, bf16[64,128]{1,0:T(8,128)(2,1)S(1)}, u32[]{:S(2)}, u32[]{:S(2)}) collective-permute-start(bf16[64,128]{1,0:T(8,128)(2,1)S(1)} %get-tuple-element.61.after_ref), channel_id=1, source_target_pairs={{0,1},{1,0},{2,3},{3,2},{4,5},{5,4},{6,7},{7,6},{8,9},{9,8},{10,11... | collective-permute-start | bytes 49160 | tf_op jit(solution)/shard_map/ppermute | solution.py:23
  82.6 5.4 %collective-permute-start.10 = (bf16[64,128]{1,0:T(8,128)(2,1)S(1)}, bf16[64,128]{1,0:T(8,128)(2,1)S(1)}, u32[]{:S(2)}, u32[]{:S(2)}) collective-permute-start(bf16[64,128]{1,0:T(8,128)(2,1)S(1)} %get-tuple-element.62), channel_id=1, source_target_pairs={{1,2},{2,1},{3,4},{4,3},{5,6},{6,5},{7,8},{8,7},{9,10},{10,9},{11,... | collective-permute-start | bytes 49160 | tf_op jit(solution)/shard_map/ppermute | solution.py:23
  86.0 3.6 %collective-permute-start.11 = (bf16[64,128]{1,0:T(8,128)(2,1)S(1)}, bf16[64,128]{1,0:T(8,128)(2,1)S(1)}, u32[]{:S(2)}, u32[]{:S(2)}) collective-permute-start(bf16[64,128]{1,0:T(8,128)(2,1)S(1)} %get-tuple-element.63), channel_id=1, source_target_pairs={{0,2},{1,3},{2,0},{3,1},{4,6},{5,7},{6,4},{7,5},{8,10},{9,11},{10,... | collective-permute-start | bytes 49160 | tf_op jit(solution)/shard_map/ppermute | solution.py:23
  87.2 2.4 %collective-permute-start.12 = (bf16[64,128]{1,0:T(8,128)(2,1)S(1)}, bf16[64,128]{1,0:T(8,128)(2,1)S(1)}, u32[]{:S(2)}, u32[]{:S(2)}) collective-permute-start(bf16[64,128]{1,0:T(8,128)(2,1)S(1)} %get-tuple-element.64), channel_id=1, source_target_pairs={{2,4},{3,5},{4,2},{5,3},{6,8},{7,9},{8,6},{9,7},{10,12},{11,13},{1... | collective-permute-start | bytes 49160 | tf_op jit(solution)/shard_map/ppermute | solution.py:23
  101.2 2.5 %collective-permute-start.13 = (bf16[2816,128]{1,0:T(8,128)(2,1)S(1)}, bf16[2816,128]{1,0:T(8,128)(2,1)S(1)}, u32[]{:S(2)}, u32[]{:S(2)}) collective-permute-start(bf16[2816,128]{1,0:T(8,128)(2,1)S(1)} %bitcast.6), channel_id=1, source_target_pairs={{0,1},{1,0},{2,3},{3,2},{4,5},{5,4},{6,7},{7,6},{8,9},{9,8},{10,11... | collective-permute-start | bytes 2162696 | tf_op jit(solution)/shard_map/ppermute | solution.py:407

commit v7 on v6

--- a/solution.py
+++ b/solution.py
@@ -176,64 +176,66 @@
     return code * jnp.where(outside, far_sign, near_sign)
 
 
+def offset_of(n, middle):
+    return n + jnp.where(n >= middle, 1, 0)
+
+
+def turn_kernel(features_ref, weight_ref, features_t_ref, weight_t_ref):
+    kernel_count = weight_ref.shape[0]
+    middle = kernel_count // 2
+    for first in range(0, features_ref.shape[0], LANES):
+        block = jnp.transpose(features_ref[first : first + LANES, :].astype(F32))
+        features_t_ref[:, first : first + LANES] = block.astype(BF16)
+    order = [k for k in range(kernel_count) if k != middle] + [middle]
+    for n, k in enumerate(order):
+        block = jnp.transpose(weight_ref[k].astype(F32))
+        weight_t_ref[:, n * LANES : (n + 1) * LANES] = block.astype(BF16)
+
+
 def forward_kernel(slots, *refs):
     received = refs[:slots]
-    features_ref, map_ref, weight_ref, child_ref = refs[slots : slots + 4]
-    hidden_ref, pre_ref, stacked_ref = refs[slots + 4 : slots + 7]
-    sends = refs[slots + 7 : 2 * slots + 7]
-    table_ref, acc_ref = refs[2 * slots + 7 : 2 * slots + 9]
-    chooser_refs, col_refs = refs[2 * slots + 9 : 2 * slots + 11], refs[2 * slots + 11 :]
+    features_ref, features_t_ref, map_ref, weight_t_ref, child_ref = refs[slots : slots + 5]
+    hidden_ref, pre_ref, stacked_ref = refs[slots + 5 : slots + 8]
+    sends = refs[slots + 8 : 2 * slots + 8]
+    table_ref, pattern_ref, *chooser_refs = refs[2 * slots + 8 :]
     voxels = features_ref.shape[0]
-    kernel_count = map_ref.shape[0]
-    middle = kernel_count // 2
+    gathers = map_ref.shape[0] - 1
+    middle = gathers // 2
     cap2 = child_ref.shape[1]
     cap = received[0].shape[0] - cap2
-    half, half_halo = voxels // 2, slots * cap // 2
-    features = features_ref[...]
-    table_ref[0:half, 0:LANES] = features[0:half]
-    table_ref[0:half, LANES : 2 * LANES] = features[half:voxels]
-    for s, block in enumerate(to_slots([r[0:cap, :] for r in received], False)):
-        place = half + (s % (slots // 2)) * cap
-        side = (s // (slots // 2)) * LANES
-        table_ref[place : place + cap, side : side + LANES] = block
-    table_rows = half + half_halo
-
-    def build(j, side):
-        for n, k in enumerate((j, j + middle + 1)):
-            codes = half_codes(map_ref[pl.ds(k, 1), :], voxels, slots * cap).astype(BF16)
-            col = column(codes)
-            col_refs[side][n] = col
-            chooser_refs[side][n] = one_hot_rows(jnp.abs(col), table_rows)
-
-    def use(j, side):
-        pair = []
-        for n, k in enumerate((j, j + middle + 1)):
-            both = matmul(chooser_refs[side][n], table_ref[...]).astype(BF16)
-            right = col_refs[side][n] < jnp.zeros((voxels, LANES), BF16)
-            pair.append(jnp.where(right, both[:, LANES:], both[:, :LANES]))
-            stacked_ref[k] = pair[n]
-        return pair
-
-    def convolve(j, pair):
-        kernel = jnp.concatenate([weight_ref[j], weight_ref[j + middle + 1]], axis=0)
-        acc_ref[...] += matmul(jnp.concatenate(pair, axis=1), kernel)
-
-    acc_ref[...] = matmul(features, weight_ref[middle])
-    build(0, 0)
+    table_ref[:, 0:voxels] = features_t_ref[...]
+    halo = jnp.concatenate(to_slots([r[0:cap, :] for r in received], False), axis=0)
+    table_ref[:, voxels:] = jnp.transpose(halo.astype(F32)).astype(BF16)
+    place = lax.broadcasted_iota(jnp.int32, pattern_ref.shape, 0)
+    pattern_ref[...] = encode(place).astype(BF16)
+
+    def build(n, side):
+        k = offset_of(n, middle)
+        codes = encode(map_ref[pl.ds(k, 1), :]).astype(BF16)
+        for start in range(0, voxels, LANES):
+            block = jnp.broadcast_to(codes[:, start : start + LANES], pattern_ref.shape)
+            chooser_refs[side][:, start : start + LANES] = pick_one(block == pattern_ref[...])
+
+    def use(n, side):
+        rows = pl.ds(pl.multiple_of(n * LANES, LANES), LANES)
+        stacked_ref[rows, :] = matmul(table_ref[...], chooser_refs[side][...]).astype(BF16)
 
     def step(i, carry):
         for side in range(2):
-            j = 2 * i + side
-            pair = use(j, side)
-            build(j + 1, 1 - side)
-            convolve(j, pair)
+            n = 2 * i + side
+            use(n, side)
+            build(n + 1, 1 - side)
         return carry
 
-    lax.fori_loop(0, middle // 2, step, 0)
-    convolve(middle - 1, use(middle - 1, 0))
-    pre = acc_ref[...]
+    build(0, 0)
+    lax.fori_loop(0, gathers // 2 - 1, step, 0)
+    use(gathers - 2, 0)
+    build(gathers - 1, 1)
+    use(gathers - 1, 1)
+    stacked_ref[gathers * LANES :, :] = features_t_ref[...]
+    pre = jnp.transpose(matmul(weight_t_ref[...], stacked_ref[...]))
     pre_ref[...] = pre
-    hidden = (features.astype(F32) + pre * jax.nn.sigmoid(pre)).astype(BF16)
+    hidden = (features_ref[...].astype(F32) + pre * jax.nn.sigmoid(pre)).astype(BF16)
     hidden_ref[...] = hidden
     leaving = gather_lists(child_ref, hidden).astype(BF16)
     for send, block in zip(sends, to_steps(jnp.split(leaving, slots), False)):
@@ -242,29 +244,22 @@
 
 def gradient_kernel(slots, *refs):
     received = refs[:slots]
-    stacked_ref, pre_ref, features_ref, child_ref, back_ref = refs[slots : slots + 5]
-    hgrad_ref, pgrad_ref, cgrad_ref = refs[slots + 5 :]
+    stacked_ref, pre_ref, child_ref, back_ref = refs[slots : slots + 4]
+    hgrad_ref, pgrad_ref, cgrad_ref = refs[slots + 4 :]
     cap2 = child_ref.shape[1]
     cap = received[0].shape[0] - cap2
-    middle = stacked_ref.shape[0] // 2
     blocks = to_slots([r[cap : cap + cap2, :] for r in received], True)
     hgrad = add_lists(back_ref[...], child_ref, blocks)
     hgrad_ref[...] = hgrad
     pre = pre_ref[...]
     sig = jax.nn.sigmoid(pre)
-    pgrad = hgrad * (sig * (1.0 + pre * (1.0 - sig)))
-    pgrad_ref[...] = pgrad.astype(BF16)
-    pgrad_t = jnp.transpose(pgrad).astype(BF16)
-
-    def put(k, value):
-        cgrad_ref[k * LANES : (k + 1) * LANES, :] = jnp.transpose(value).astype(BF16)
-
-    put(middle, matmul(pgrad_t, features_ref[...]))
-    for j in range(middle):
-        pair = jnp.concatenate([stacked_ref[j], stacked_ref[j + middle + 1]], axis=1)
-        both = matmul(pgrad_t, pair)
-        put(j, both[:, :LANES])
-        put(j + middle + 1, both[:, LANES:])
+    pgrad = (hgrad * (sig * (1.0 + pre * (1.0 - sig)))).astype(BF16)
+    pgrad_ref[...] = pgrad
+    terms = matmul(stacked_ref[...], pgrad).astype(BF16)
+    last = terms.shape[0] - LANES
+    cgrad_ref[0 : last // 2, :] = terms[0 : last // 2]
+    cgrad_ref[last // 2 : last // 2 + LANES, :] = terms[last:]
+    cgrad_ref[last // 2 + LANES :, :] = terms[last // 2 : last]
 
 
 def spread_kernel(slots, pgrad_ref, map_ref, weight_ref, after_ref, back_ref, *sends):
@@ -443,27 +438,32 @@
     down_rows = octants * channels * coarse_channels // LANES
     grain = 8 * devices
     half_rows = -(-(conv_rows + down_rows) // (2 * grain)) * grain
+    features_t, weight_t = call(
+        turn_kernel,
+        (features, conv_weight),
+        [((channels, voxels), BF16), ((channels, conv_rows), BF16)],
+        flops=giga,
+    )
     hidden, pre_act, stacked, *leaving = call(
         functools.partial(forward_kernel, slots),
-        (*received, features, neighbour_map, conv_weight, child_rows),
+        (*received, features, features_t, neighbour_map, weight_t, child_rows),
         [
             ((voxels, channels), BF16),
             ((voxels, channels), F32),
-            ((kernel_count, voxels, channels), BF16),
+            ((conv_rows, voxels), BF16),
         ]
         + [((cap2, channels), BF16)] * slots,
         scratch=[
-            pltpu.VMEM((voxels // 2 + slots * cap // 2, 2 * channels), BF16),
-            pltpu.VMEM((voxels, channels), F32),
+            pltpu.VMEM((channels, voxels + slots * cap), BF16),
+            pltpu.VMEM((voxels + slots * cap, LANES), BF16),
         ]
-        + [pltpu.VMEM((2, voxels, (voxels + slots * cap) // 2), BF16)] * 2
-        + [pltpu.VMEM((2, voxels, LANES), BF16)] * 2,
+        + [pltpu.VMEM((voxels + slots * cap, voxels), BF16)] * 2,
         limit=32,
         flops=12 * giga,
     )
     hidden_grad, pre_grad, conv_terms = call(
         functools.partial(gradient_kernel, slots),
-        (*received, stacked, pre_act, features, child_rows, back_h),
+        (*received, stacked, pre_act, child_rows, back_h),
         [
             ((voxels, channels), F32),
             ((voxels, channels), BF16),

time: 106 us -> 109 us (1.028)
  Pallas kernels: 46.3 us -> 50 us
    pallas_call x9 -> x10, Pallas kernels: 46.3 us -> 50 us  [call(): pl.pallas_call(kernel, out_shape=[jax.ShapeDtypeStruct(s, d) for s, d in...]
where the time goes in v7:
time: 109 us; the launch traced here: 108 us
  Pallas kernels  50 us (46%)
  starting transfers between devices  36.4 us (33%)
  waiting for transfers between devices  20.6 us (19%)
    pallas_call x10, Pallas kernels, call(): pl.pallas_call(kernel, out_shape=[jax.ShapeDtypeStruct(s, d) for s, d in...  50 us
    ppermute x12, starting transfers between devices, swaps(): moved[step] = lax.ppermute(by_step[step], 'shard', pairs)  22.4 us
    all_to_all x2, waiting for transfers between devices, exchange(): return lax.all_to_all(value, 'shard', 0, 0, tiled=True)  15.6 us
    all_to_all x2, starting transfers between devices, exchange(): return lax.all_to_all(value, 'shard', 0, 0, tiled=True)  13.3 us
    ppermute x2, waiting for transfers between devices, swap_cores(): lax.ppermute(value, 'shard', [(i, i + 1 - 2 * (i % 2)) for i in range(dev...  2.85 us
  transfers between devices with their start and end apart: 16, of which 7 were waited for; matrix products, arithmetic and copies ran while one was open for 0% of the time, Pallas kernels for 17%

profile of v7, /device:TPU:1, one launch (start us, length us, event | category | flops | bytes accessed | tf_op | source)
XLA Modules:
  0.0 107.9 jit_solution(16665483915015835115)
XLA Ops:
  0.6 0.0 copy-start.2
  0.6 0.0 copy-start
  0.7 4.0 %shard_map.111 = (bf16[96,128]{1,0:T(8,128)(2,1)}, bf16[96,128]{1,0:T(8,128)(2,1)}, bf16[96,128]{1,0:T(8,128)(2,1)}, bf16[96,128]{1,0:T(8,128)(2,1)}, f32[1024,128]{1,0:T(8,128)}) custom-call(bf16[1024,128]{1,0:T(8,128)(2,1)} %refs_4_.1, s32[4,64]{1,0:T(4,128)} %refs_6_.7, s32[8,256]{1,0:T(8,128)} %refs_5_.1, bf16[256,256]{1,0:T(8,128)(2,1)} %refs_7_.1, ...), custom_call_target="tpu_custom_call" | custom-call | flops 1000000000 | bytes 4194304 | tf_op jit(solution)/shard_map/pallas_call | solution.py:390
  4.7 0.1 collective-permute-start
  4.8 4.5 %collective-permute-start.1 = (bf16[96,128]{1,0:T(8,128)(2,1)}, bf16[96,128]{1,0:T(8,128)(2,1)S(1)}, u32[]{:S(2)}, u32[]{:S(2)}) collective-permute-start(bf16[96,128]{1,0:T(8,128)(2,1)} %get-tuple-element.42), channel_id=1, source_target_pairs={{1,2},{2,1},{3,4},{4,3},{5,6},{6,5},{7,8},{8,7},{9,10},{10,9},{11,... | collective-permute-start | bytes 73736 | tf_op jit(solution)/shard_map/ppermute | solution.py:23
  9.3 1.3 %collective-permute-start.2 = (bf16[96,128]{1,0:T(8,128)(2,1)}, bf16[96,128]{1,0:T(8,128)(2,1)S(1)}, u32[]{:S(2)}, u32[]{:S(2)}) collective-permute-start(bf16[96,128]{1,0:T(8,128)(2,1)} %get-tuple-element.43), channel_id=1, source_target_pairs={{0,2},{1,3},{2,0},{3,1},{4,6},{5,7},{6,4},{7,5},{8,10},{9,11},{10,... | collective-permute-start | bytes 73736 | tf_op jit(solution)/shard_map/ppermute | solution.py:23
  10.6 0.0 copy-start.4
  10.6 0.0 copy-start.6
  10.6 0.8 collective-permute-start.3
  11.4 0.0 copy-done.2
  11.4 0.0 copy-done
  11.4 0.4 shard_map.112
  11.8 0.0 collective-permute-done.refs_0_
  11.8 0.0 collective-permute-done.1.refs_1_
  11.8 0.5 collective-permute-done.2.refs_2_
  12.3 0.0 collective-permute-done.3.refs_3_
  12.3 0.0 copy-done.4
  12.3 0.0 copy-done.6
  12.3 0.0 copy-start.8
  12.3 20.8 %shard_map.113 = (bf16[1024,128]{1,0:T(8,128)(2,1)S(1)}, f32[1024,128]{1,0:T(8,128)S(1)}, bf16[3456,1024]{1,0:T(8,128)(2,1)S(1)}, bf16[32,128]{1,0:T(8,128)(2,1)...) custom-call(bf16[96,128]{1,0:T(8,128)(2,1)S(1)} %collective-permute-done.refs_0_, ...), custom_call_target="tpu_custom_call" | custom-call | flops 12000000000 | bytes 4194304 | tf_op jit(solution)/shard_map/pallas_call | solution.py:390
  33.1 0.1 collective-permute-start.4
  33.1 6.8 %collective-permute-start.5 = (bf16[32,128]{1,0:T(8,128)(2,1)S(1)}, bf16[32,128]{1,0:T(8,128)(2,1)S(1)}, u32[]{:S(2)}, u32[]{:S(2)}) collective-permute-start(bf16[32,128]{1,0:T(8,128)(2,1)S(1)} %get-tuple-element.48), channel_id=1, source_target_pairs={{1,2},{2,1},{3,4},{4,3},{5,6},{6,5},{7,8},{8,7},{9,10},{10,9},{11,... | collective-permute-start | bytes 24584 | tf_op jit(solution)/shard_map/ppermute | solution.py:23
  39.9 2.6 %collective-permute-start.6 = (bf16[32,128]{1,0:T(8,128)(2,1)S(1)}, bf16[32,128]{1,0:T(8,128)(2,1)S(1)}, u32[]{:S(2)}, u32[]{:S(2)}) collective-permute-start(bf16[32,128]{1,0:T(8,128)(2,1)S(1)} %get-tuple-element.49), channel_id=1, source_target_pairs={{0,2},{1,3},{2,0},{3,1},{4,6},{5,7},{6,4},{7,5},{8,10},{9,11},{10,... | collective-permute-start | bytes 24584 | tf_op jit(solution)/shard_map/ppermute | solution.py:23
  42.5 0.6 collective-permute-start.7
  43.2 0.0 copy-done.8
  43.2 0.0 copy-start.1
  43.2 0.0 copy-start.3
  43.2 0.0 copy-start.5
  43.2 2.3 %shard_map.114 = (f32[1024,128]{1,0:T(8,128)S(1)}, bf16[1024,128]{1,0:T(8,128)(2,1)S(1)}, bf16[3456,128]{1,0:T(8,128)(2,1)S(1)}) custom-call(bf16[96,128]{1,0:T(8,128)(2,1)S(1)} %collective-permute-done.refs_0_, bf16[96,128]{1,0:T(8,128)(2,1)S(1)} %collective-permute-done.1.refs_1_, bf16[96,128]{1,0:T(8,128)(2,1)S(1)} %collective-permute-done.2.refs_2_, ...), custom_call_target="tpu_custom_call" | custom-call | flops 3000000000 | bytes 4194304 | tf_op jit(solution)/shard_map/pallas_call | solution.py:390
  45.6 0.0 collective-permute-done.4.refs_0_
  45.6 0.0 collective-permute-done.5.refs_1_
  45.6 0.0 collective-permute-done.6.refs_2_
  45.6 0.0 collective-permute-done.7.refs_3_
  45.6 0.0 copy-done.1
  45.6 0.0 copy-done.3
  45.6 0.0 copy-done.5
  45.6 2.5 %shard_map.115 = (bf16[256,256]{1,0:T(8,128)(2,1)}, bf16[5632,128]{1,0:T(8,128)(2,1)S(1)}, bf16[2816,128]{1,0:T(8,128)(2,1)S(1)}) custom-call(bf16[32,128]{1,0:T(8,128)(2,1)S(1)} %collective-permute-done.4.refs_0_, bf16[32,128]{1,0:T(8,128)(2,1)S(1)} %collective-permute-done.5.refs_1_, bf16[32,128]{1,0:T(8,128)(2,1)S(1)} %collective-permute-done.6.refs_2_, ...), custom_call_target="tpu_custom_call" | custom-call | flops 2000000000 | bytes 4194304 | tf_op jit(solution)/shard_map/pallas_call | solution.py:390
  48.2 0.0 collective-permute-start.8
  48.2 2.2 %collective-permute-done.8.other_ref = bf16[2816,128]{1,0:T(8,128)(2,1)S(1)} collective-permute-done((bf16[2816,128]{1,0:T(8,128)(2,1)S(1)}, bf16[2816,128]{1,0:T(8,128)(2,1)S(1)}, u32[]{:S(2)}, u32[]{:S(2)}) %collective-permute-start.8) | collective-permute-done | bytes 720928 | tf_op jit(solution)/shard_map/ppermute | solution.py:402
  50.4 1.0 shard_map.116.after_ref
  51.4 9.5 %all-to-all-start = ((bf16[32,88,128]{2,1,0:T(8,128)(2,1)}), bf16[32,88,128]{2,1,0:T(8,128)(2,1)S(1)}, u32[]{:S(2)}, u32[]{:S(2)}) async-start(bf16[32,88,128]{2,1,0:T(8,128)(2,1)} %bitcast), calls=%async_computation | async-start | bytes 1441792 | tf_op jit(solution)/shard_map/all_to_all | solution.py:406
  60.9 14.9 %shard_map.117 = (f32[1024,128]{1,0:T(8,128)S(1)}, bf16[64,128]{1,0:T(8,128)(2,1)S(1)}, bf16[64,128]{1,0:T(8,128)(2,1)S(1)}, bf16[64,128]{1,0:T(8,128)(2,1)S(1)}, bf16[64,128]{1,0:T(8,128)(2,1)S(1)}) custom-call(bf16[1024,128]{1,0:T(8,128)(2,1)S(1)} %get-tuple-element.59.pgrad_ref, s32[27,1024]{1,0:T(8,128)S(1)} %copy-done.4, ...), custom_call_target="tpu_custom_call" | custom-call | flops 20000000000 | bytes 4194304 | tf_op jit(solution)/shard_map/pallas_call | solution.py:390
  75.8 0.0 copy-start.7
  75.8 4.0 %all-to-all-done = bf16[32,88,128]{2,1,0:T(8,128)(2,1)S(1)} async-done(((bf16[32,88,128]{2,1,0:T(8,128)(2,1)}), bf16[32,88,128]{2,1,0:T(8,128)(2,1)S(1)}, u32[]{:S(2)}, u32[]{:S(2)}) %all-to-all-start) | async-done | bytes 720928 | tf_op jit(solution)/shard_map/all_to_all | solution.py:406
  79.8 1.0 shard_map.118
  80.8 3.9 %all-to-all-start.1 = ((bf16[32,88,128]{2,1,0:T(8,128)(2,1)}), bf16[32,88,128]{2,1,0:T(8,128)(2,1)S(1)}, u32[]{:S(2)}, u32[]{:S(2)}) async-start(bf16[32,88,128]{2,1,0:T(8,128)(2,1)} %bitcast.2), calls=%async_computation.1 | async-start | bytes 1441792 | tf_op jit(solution)/shard_map/all_to_all | solution.py:406
  84.7 0.3 collective-permute-start.9
  85.0 3.4 %collective-permute-start.10 = (bf16[64,128]{1,0:T(8,128)(2,1)S(1)}, bf16[64,128]{1,0:T(8,128)(2,1)S(1)}, u32[]{:S(2)}, u32[]{:S(2)}) collective-permute-start(bf16[64,128]{1,0:T(8,128)(2,1)S(1)} %get-tuple-element.66), channel_id=1, source_target_pairs={{1,2},{2,1},{3,4},{4,3},{5,6},{6,5},{7,8},{8,7},{9,10},{10,9},{11,... | collective-permute-start | bytes 49160 | tf_op jit(solution)/shard_map/ppermute | solution.py:23
  88.4 1.2 %collective-permute-start.11 = (bf16[64,128]{1,0:T(8,128)(2,1)S(1)}, bf16[64,128]{1,0:T(8,128)(2,1)S(1)}, u32[]{:S(2)}, u32[]{:S(2)}) collective-permute-start(bf16[64,128]{1,0:T(8,128)(2,1)S(1)} %get-tuple-element.67), channel_id=1, source_target_pairs={{0,2},{1,3},{2,0},{3,1},{4,6},{5,7},{6,4},{7,5},{8,10},{9,11},{10,... | collective-permute-start | bytes 49160 | tf_op jit(solution)/shard_map/ppermute | solution.py:23
  89.7 0.7 collective-permute-start.12
  90.3 0.0 collective-permute-done.9.refs_0_
  90.3 0.1 collective-permute-done.10.refs_1_
  90.4 1.6 %collective-permute-done.11.refs_2_ = bf16[64,128]{1,0:T(8,128)(2,1)S(1)} collective-permute-done((bf16[64,128]{1,0:T(8,128)(2,1)S(1)}, bf16[64,128]{1,0:T(8,128)(2,1)S(1)}, u32[]{:S(2)}, u32[]{:S(2)}) %collective-permute-start.11) | collective-permute-done | bytes 16416 | tf_op jit(solution)/shard_map/ppermute | solution.py:23
  92.0 0.0 collective-permute-done.12.refs_3_
  92.0 11.6 %all-to-all-done.1 = bf16[32,88,128]{2,1,0:T(8,128)(2,1)S(1)} async-done(((bf16[32,88,128]{2,1,0:T(8,128)(2,1)}), bf16[32,88,128]{2,1,0:T(8,128)(2,1)S(1)}, u32[]{:S(2)}, u32[]{:S(2)}) %all-to-all-start.1) | async-done | bytes 720928 | tf_op jit(solution)/shard_map/all_to_all | solution.py:406
  103.6 0.7 collective-permute-start.13
  104.3 0.0 copy-done.7
  104.3 1.2 %shard_map.119 = f32[1024,128]{1,0:T(8,128)} custom-call(bf16[64,128]{1,0:T(8,128)(2,1)S(1)} %collective-permute-done.9.refs_0_, bf16[64,128]{1,0:T(8,128)(2,1)S(1)} %collective-permute-done.10.refs_1_, bf16[64,128]{1,0:T(8,128)(2,1)S(1)} %collective-permute-done.11.refs_2_, bf16[64,128]{1,0:T(8,128)(2,1)S(1)} %collective-permute-done.12.refs_3_, ...), custom_call_target="tpu_custom_call" | custom-call | flops 1000000000 | bytes 4194304 | tf_op jit(solution)/shard_map/pallas_call | solution.py:390
  105.5 0.7 collective-permute-done.13.other_ref
  106.1 1.8 %shard_map.120 = (f32[3456,128]{1,0:T(8,128)}, f32[1024,256]{1,0:T(8,128)}) custom-call(bf16[2816,128]{1,0:T(8,128)(2,1)S(1)} %bitcast.7, bf16[2816,128]{1,0:T(8,128)(2,1)S(1)} %collective-permute-done.13.other_ref), custom_call_target="tpu_custom_call" | custom-call | flops 1000000 | bytes 4194304 | tf_op jit(solution)/shard_map/pallas_call | solution.py:390
Async XLA Ops:
  0.6 10.7 %copy-start.2 = (bf16[1024,128]{1,0:T(8,128)(2,1)S(1)}, bf16[1024,128]{1,0:T(8,128)(2,1)}, u32[]{:S(2)}) copy-start(bf16[1024,128]{1,0:T(8,128)(2,1)} %refs_4_.1) | copy-start | bytes 786436
  0.6 10.7 %copy-start = (bf16[27,128,128]{2,1,0:T(8,128)(2,1)S(1)}, bf16[27,128,128]{2,1,0:T(8,128)(2,1)}, u32[]{:S(2)}) copy-start(bf16[27,128,128]{2,1,0:T(8,128)(2,1)} %weight_ref.3) | copy-start | bytes 2654212
  4.7 7.1 %collective-permute-start = (bf16[96,128]{1,0:T(8,128)(2,1)}, bf16[96,128]{1,0:T(8,128)(2,1)S(1)}, u32[]{:S(2)}, u32[]{:S(2)}) collective-permute-start(bf16[96,128]{1,0:T(8,128)(2,1)} %get-tuple-element.41), channel_id=1, source_target_pairs={{0,1},{1,0},{2,3},{3,2},{4,5},{5,4},{6,7},{7,6},{8,9},{9,8},{10,11... | collective-permute-start | bytes 73736 | tf_op jit(solution)/shard_map/ppermute | solution.py:23
  4.8 7.0 %collective-permute-start.1 = (bf16[96,128]{1,0:T(8,128)(2,1)}, bf16[96,128]{1,0:T(8,128)(2,1)S(1)}, u32[]{:S(2)}, u32[]{:S(2)}) collective-permute-start(bf16[96,128]{1,0:T(8,128)(2,1)} %get-tuple-element.42), channel_id=1, source_target_pairs={{1,2},{2,1},{3,4},{4,3},{5,6},{6,5},{7,8},{8,7},{9,10},{10,9},{11,... | collective-permute-start | bytes 73736 | tf_op jit(solution)/shard_map/ppermute | solution.py:23
  9.3 3.0 %collective-permute-start.2 = (bf16[96,128]{1,0:T(8,128)(2,1)}, bf16[96,128]{1,0:T(8,128)(2,1)S(1)}, u32[]{:S(2)}, u32[]{:S(2)}) collective-permute-start(bf16[96,128]{1,0:T(8,128)(2,1)} %get-tuple-element.43), channel_id=1, source_target_pairs={{0,2},{1,3},{2,0},{3,1},{4,6},{5,7},{6,4},{7,5},{8,10},{9,11},{10,... | collective-permute-start | bytes 73736 | tf_op jit(solution)/shard_map/ppermute | solution.py:23
  10.6 1.7 %copy-start.4 = (s32[27,1024]{1,0:T(8,128)S(1)}, s32[27,1024]{1,0:T(8,128)}, u32[]{:S(2)}) copy-start(s32[27,1024]{1,0:T(8,128)} %map_ref.1) | copy-start | bytes 331780
  10.6 1.7 %copy-start.6 = (s32[4,32]{1,0:T(4,128)S(1)}, s32[4,32]{1,0:T(4,128)}, u32[]{:S(2)}) copy-start(s32[4,32]{1,0:T(4,128)} %refs_6_.5) | copy-start | bytes 1540
  10.6 1.7 %collective-permute-start.3 = (bf16[96,128]{1,0:T(8,128)(2,1)}, bf16[96,128]{1,0:T(8,128)(2,1)S(1)}, u32[]{:S(2)}, u32[]{:S(2)}) collective-permute-start(bf16[96,128]{1,0:T(8,128)(2,1)} %get-tuple-element.44), channel_id=1, source_target_pairs={{2,4},{3,5},{4,2},{5,3},{6,8},{7,9},{8,6},{9,7},{10,12},{11,13},{1... | collective-permute-start | bytes 73736 | tf_op jit(solution)/shard_map/ppermute | solution.py:23
  12.3 30.9 %copy-start.8 = (f32[1024,128]{1,0:T(8,128)S(1)}, f32[1024,128]{1,0:T(8,128)}, u32[]{:S(2)}) copy-start(f32[1024,128]{1,0:T(8,128)} %get-tuple-element.54.refs_7_) | copy-start | bytes 1572868
  33.1 12.5 %collective-permute-start.4 = (bf16[32,128]{1,0:T(8,128)(2,1)S(1)}, bf16[32,128]{1,0:T(8,128)(2,1)S(1)}, u32[]{:S(2)}, u32[]{:S(2)}) collective-permute-start(bf16[32,128]{1,0:T(8,128)(2,1)S(1)} %get-tuple-element.47), channel_id=1, source_target_pairs={{0,1},{1,0},{2,3},{3,2},{4,5},{5,4},{6,7},{7,6},{8,9},{9,8},{10,11... | collective-permute-start | bytes 24584 | tf_op jit(solution)/shard_map/ppermute | solution.py:23
  33.1 12.4 %collective-permute-start.5 = (bf16[32,128]{1,0:T(8,128)(2,1)S(1)}, bf16[32,128]{1,0:T(8,128)(2,1)S(1)}, u32[]{:S(2)}, u32[]{:S(2)}) collective-permute-start(bf16[32,128]{1,0:T(8,128)(2,1)S(1)} %get-tuple-element.48), channel_id=1, source_target_pairs={{1,2},{2,1},{3,4},{4,3},{5,6},{6,5},{7,8},{8,7},{9,10},{10,9},{11,... | collective-permute-start | bytes 24584 | tf_op jit(solution)/shard_map/ppermute | solution.py:23
  39.9 5.6 %collective-permute-start.6 = (bf16[32,128]{1,0:T(8,128)(2,1)S(1)}, bf16[32,128]{1,0:T(8,128)(2,1)S(1)}, u32[]{:S(2)}, u32[]{:S(2)}) collective-permute-start(bf16[32,128]{1,0:T(8,128)(2,1)S(1)} %get-tuple-element.49), channel_id=1, source_target_pairs={{0,2},{1,3},{2,0},{3,1},{4,6},{5,7},{6,4},{7,5},{8,10},{9,11},{10,... | collective-permute-start | bytes 24584 | tf_op jit(solution)/shard_map/ppermute | solution.py:23
  42.5 3.1 %collective-permute-start.7 = (bf16[32,128]{1,0:T(8,128)(2,1)S(1)}, bf16[32,128]{1,0:T(8,128)(2,1)S(1)}, u32[]{:S(2)}, u32[]{:S(2)}) collective-permute-start(bf16[32,128]{1,0:T(8,128)(2,1)S(1)} %get-tuple-element.50), channel_id=1, source_target_pairs={{2,4},{3,5},{4,2},{5,3},{6,8},{7,9},{8,6},{9,7},{10,12},{11,13},{1... | collective-permute-start | bytes 24584 | tf_op jit(solution)/shard_map/ppermute | solution.py:23
  43.2 2.4 %copy-start.1 = (bf16[8,128,256]{2,1,0:T(8,128)(2,1)S(1)}, bf16[8,128,256]{2,1,0:T(8,128)(2,1)}, u32[]{:S(2)}) copy-start(bf16[8,128,256]{2,1,0:T(8,128)(2,1)} %refs_6_.6) | copy-start | bytes 1572868
  43.2 2.4 %copy-start.3 = (bf16[256,256]{1,0:T(8,128)(2,1)S(1)}, bf16[256,256]{1,0:T(8,128)(2,1)}, u32[]{:S(2)}) copy-start(bf16[256,256]{1,0:T(8,128)(2,1)} %refs_7_.1) | copy-start | bytes 393220
  43.2 2.4 %copy-start.5 = (s32[8,256]{1,0:T(8,128)S(1)}, s32[8,256]{1,0:T(8,128)}, u32[]{:S(2)}) copy-start(s32[8,256]{1,0:T(8,128)} %refs_5_.1) | copy-start | bytes 24580
  48.2 2.2 %collective-permute-start.8 = (bf16[2816,128]{1,0:T(8,128)(2,1)S(1)}, bf16[2816,128]{1,0:T(8,128)(2,1)S(1)}, u32[]{:S(2)}, u32[]{:S(2)}) collective-permute-start(bf16[2816,128]{1,0:T(8,128)(2,1)S(1)} %get-tuple-element.58), channel_id=1, source_target_pairs={{0,1},{1,0},{2,3},{3,2},{4,5},{5,4},{6,7},{7,6},{8,9},{9,8},{10,11... | collective-permute-start | bytes 2162696 | tf_op jit(solution)/shard_map/ppermute | solution.py:402
  51.4 28.4 %all-to-all-start = ((bf16[32,88,128]{2,1,0:T(8,128)(2,1)}), bf16[32,88,128]{2,1,0:T(8,128)(2,1)S(1)}, u32[]{:S(2)}, u32[]{:S(2)}) async-start(bf16[32,88,128]{2,1,0:T(8,128)(2,1)} %bitcast), calls=%async_computation | async-start | bytes 1441792 | tf_op jit(solution)/shard_map/all_to_all | solution.py:406
  75.8 28.5 %copy-start.7 = (s32[4,64]{1,0:T(4,128)S(1)}, s32[4,64]{1,0:T(4,128)}, u32[]{:S(2)}) copy-start(s32[4,64]{1,0:T(4,128)} %refs_6_.7) | copy-start | bytes 3076
  80.8 22.8 %all-to-all-start.1 = ((bf16[32,88,128]{2,1,0:T(8,128)(2,1)}), bf16[32,88,128]{2,1,0:T(8,128)(2,1)S(1)}, u32[]{:S(2)}, u32[]{:S(2)}) async-start(bf16[32,88,128]{2,1,0:T(8,128)(2,1)} %bitcast.2), calls=%async_computation.1 | async-start | bytes 1441792 | tf_op jit(solution)/shard_map/all_to_all | solution.py:406
  84.7 5.7 %collective-permute-start.9 = (bf16[64,128]{1,0:T(8,128)(2,1)S(1)}, bf16[64,128]{1,0:T(8,128)(2,1)S(1)}, u32[]{:S(2)}, u32[]{:S(2)}) collective-permute-start(bf16[64,128]{1,0:T(8,128)(2,1)S(1)} %get-tuple-element.65.after_ref), channel_id=1, source_target_pairs={{0,1},{1,0},{2,3},{3,2},{4,5},{5,4},{6,7},{7,6},{8,9},{9,8},{10,11... | collective-permute-start | bytes 49160 | tf_op jit(solution)/shard_map/ppermute | solution.py:23
  85.0 5.4 %collective-permute-start.10 = (bf16[64,128]{1,0:T(8,128)(2,1)S(1)}, bf16[64,128]{1,0:T(8,128)(2,1)S(1)}, u32[]{:S(2)}, u32[]{:S(2)}) collective-permute-start(bf16[64,128]{1,0:T(8,128)(2,1)S(1)} %get-tuple-element.66), channel_id=1, source_target_pairs={{1,2},{2,1},{3,4},{4,3},{5,6},{6,5},{7,8},{8,7},{9,10},{10,9},{11,... | collective-permute-start | bytes 49160 | tf_op jit(solution)/shard_map/ppermute | solution.py:23
  88.4 3.6 %collective-permute-start.11 = (bf16[64,128]{1,0:T(8,128)(2,1)S(1)}, bf16[64,128]{1,0:T(8,128)(2,1)S(1)}, u32[]{:S(2)}, u32[]{:S(2)}) collective-permute-start(bf16[64,128]{1,0:T(8,128)(2,1)S(1)} %get-tuple-element.67), channel_id=1, source_target_pairs={{0,2},{1,3},{2,0},{3,1},{4,6},{5,7},{6,4},{7,5},{8,10},{9,11},{10,... | collective-permute-start | bytes 49160 | tf_op jit(solution)/shard_map/ppermute | solution.py:23
  89.7 2.4 %collective-permute-start.12 = (bf16[64,128]{1,0:T(8,128)(2,1)S(1)}, bf16[64,128]{1,0:T(8,128)(2,1)S(1)}, u32[]{:S(2)}, u32[]{:S(2)}) collective-permute-start(bf16[64,128]{1,0:T(8,128)(2,1)S(1)} %get-tuple-element.68), channel_id=1, source_target_pairs={{2,4},{3,5},{4,2},{5,3},{6,8},{7,9},{8,6},{9,7},{10,12},{11,13},{1... | collective-permute-start | bytes 49160 | tf_op jit(solution)/shard_map/ppermute | solution.py:23
  103.6 2.5 %collective-permute-start.13 = (bf16[2816,128]{1,0:T(8,128)(2,1)S(1)}, bf16[2816,128]{1,0:T(8,128)(2,1)S(1)}, u32[]{:S(2)}, u32[]{:S(2)}) collective-permute-start(bf16[2816,128]{1,0:T(8,128)(2,1)S(1)} %bitcast.6), channel_id=1, source_target_pairs={{0,1},{1,0},{2,3},{3,2},{4,5},{5,4},{6,7},{7,6},{8,9},{9,8},{10,11... | collective-permute-start | bytes 2162696 | tf_op jit(solution)/shard_map/ppermute | solution.py:402

commit v8 on v6

--- a/solution.py
+++ b/solution.py
@@ -76,10 +76,10 @@
     return pieces[0] if len(pieces) == 1 else jnp.concatenate(pieces, axis=0)
 
 
-def one_hot_rows(col, width):
+def one_hot_rows(col, width, first=0):
     lane = lax.broadcasted_iota(jnp.int32, (16, LANES), 1)
     blocks = []
-    for start in range(0, width, LANES):
+    for start in range(first, first + width, LANES):
         pattern = jnp.broadcast_to(encode(lane + start).astype(BF16)[0:1], col.shape)
         blocks.append(pick_one(col == pattern))
     return jnp.concatenate(blocks, axis=1)
@@ -176,62 +176,73 @@
     return code * jnp.where(outside, far_sign, near_sign)
 
 
+def offset_of(n, middle):
+    return n + jnp.where(n >= middle, 1, 0)
+
+
 def forward_kernel(slots, *refs):
     received = refs[:slots]
     features_ref, map_ref, weight_ref, child_ref = refs[slots : slots + 4]
     hidden_ref, pre_ref, stacked_ref = refs[slots + 4 : slots + 7]
     sends = refs[slots + 7 : 2 * slots + 7]
-    table_ref, acc_ref = refs[2 * slots + 7 : 2 * slots + 9]
-    chooser_refs, col_refs = refs[2 * slots + 9 : 2 * slots + 11], refs[2 * slots + 11 :]
+    table_ref, halo_ref, kernel_ref = refs[2 * slots + 7 : 2 * slots + 10]
+    own_refs, far_refs, col_refs = (
+        refs[2 * slots + 10 + 2 * n : 2 * slots + 12 + 2 * n] for n in range(3)
+    )
     voxels = features_ref.shape[0]
-    kernel_count = map_ref.shape[0]
-    middle = kernel_count // 2
+    gathers = map_ref.shape[0] - 1
+    middle = gathers // 2
     cap2 = child_ref.shape[1]
     cap = received[0].shape[0] - cap2
     half, half_halo = voxels // 2, slots * cap // 2
     features = features_ref[...]
-    table_ref[0:half, 0:LANES] = features[0:half]
-    table_ref[0:half, LANES : 2 * LANES] = features[half:voxels]
+    table_ref[:, 0:LANES] = features[0:half]
+    table_ref[:, LANES:] = features[half:voxels]
+    halo_ref[...] = jnp.zeros(halo_ref.shape, BF16)
     for s, block in enumerate(to_slots([r[0:cap, :] for r in received], False)):
-        place = half + (s % (slots // 2)) * cap
+        place = (s % (slots // 2)) * cap
         side = (s // (slots // 2)) * LANES
-        table_ref[place : place + cap, side : side + LANES] = block
-    table_rows = half + half_halo
+        for n in range(2):
+            row, lane = n * half_halo + place, 2 * n * LANES + side
+            halo_ref[row : row + cap, lane : lane + LANES] = block
+    kernel_ref[0:middle] = weight_ref[0:middle]
+    kernel_ref[middle:gathers] = weight_ref[middle + 1 :]
+    kernel_ref[gathers] = weight_ref[middle]
 
     def build(j, side):
-        for n, k in enumerate((j, j + middle + 1)):
+        for n in range(2):
+            k = offset_of(2 * j + n, middle)
             codes = half_codes(map_ref[pl.ds(k, 1), :], voxels, slots * cap).astype(BF16)
             col = column(codes)
             col_refs[side][n] = col
-            chooser_refs[side][n] = one_hot_rows(jnp.abs(col), table_rows)
+            col = jnp.abs(col)
+            own_refs[side][n] = one_hot_rows(col, half)
+            lanes = slice(n * half_halo, (n + 1) * half_halo)
+            far_refs[side][:, lanes] = one_hot_rows(col, half_halo, half)
 
     def use(j, side):
+        far = matmul(far_refs[side][...], halo_ref[...])
         pair = []
-        for n, k in enumerate((j, j + middle + 1)):
-            both = matmul(chooser_refs[side][n], table_ref[...]).astype(BF16)
+        for n in range(2):
+            both = matmul(own_refs[side][n], table_ref[...])
+            both = (both + far[:, 2 * n * LANES : 2 * (n + 1) * LANES]).astype(BF16)
             right = col_refs[side][n] < jnp.zeros((voxels, LANES), BF16)
             pair.append(jnp.where(right, both[:, LANES:], both[:, :LANES]))
-            stacked_ref[k] = pair[n]
-        return pair
-
-    def convolve(j, pair):
-        kernel = jnp.concatenate([weight_ref[j], weight_ref[j + middle + 1]], axis=0)
-        acc_ref[...] += matmul(jnp.concatenate(pair, axis=1), kernel)
-
-    acc_ref[...] = matmul(features, weight_ref[middle])
-    build(0, 0)
+        lanes = pl.ds(pl.multiple_of(2 * j * LANES, 2 * LANES), 2 * LANES)
+        stacked_ref[:, lanes] = jnp.concatenate(pair, axis=1)
 
     def step(i, carry):
         for side in range(2):
             j = 2 * i + side
-            pair = use(j, side)
+            use(j, side)
             build(j + 1, 1 - side)
-            convolve(j, pair)
         return carry
 
+    build(0, 0)
     lax.fori_loop(0, middle // 2, step, 0)
-    convolve(middle - 1, use(middle - 1, 0))
-    pre = acc_ref[...]
+    use(middle - 1, 0)
+    stacked_ref[:, gathers * LANES :] = features
+    pre = matmul(stacked_ref[...], kernel_ref[...].reshape(-1, LANES))
     pre_ref[...] = pre
     hidden = (features.astype(F32) + pre * jax.nn.sigmoid(pre)).astype(BF16)
     hidden_ref[...] = hidden
@@ -242,11 +253,12 @@
 
 def gradient_kernel(slots, *refs):
     received = refs[:slots]
-    stacked_ref, pre_ref, features_ref, child_ref, back_ref = refs[slots : slots + 5]
-    hgrad_ref, pgrad_ref, cgrad_ref = refs[slots + 5 :]
+    stacked_ref, pre_ref, child_ref, back_ref = refs[slots : slots + 4]
+    hgrad_ref, pgrad_ref, cgrad_ref = refs[slots + 4 :]
     cap2 = child_ref.shape[1]
     cap = received[0].shape[0] - cap2
-    middle = stacked_ref.shape[0] // 2
+    kernel_count = cgrad_ref.shape[0] // LANES
+    middle = kernel_count // 2
     blocks = to_slots([r[cap : cap + cap2, :] for r in received], True)
     hgrad = add_lists(back_ref[...], child_ref, blocks)
     hgrad_ref[...] = hgrad
@@ -254,17 +266,11 @@
     sig = jax.nn.sigmoid(pre)
     pgrad = hgrad * (sig * (1.0 + pre * (1.0 - sig)))
     pgrad_ref[...] = pgrad.astype(BF16)
-    pgrad_t = jnp.transpose(pgrad).astype(BF16)
-
-    def put(k, value):
-        cgrad_ref[k * LANES : (k + 1) * LANES, :] = jnp.transpose(value).astype(BF16)
-
-    put(middle, matmul(pgrad_t, features_ref[...]))
-    for j in range(middle):
-        pair = jnp.concatenate([stacked_ref[j], stacked_ref[j + middle + 1]], axis=1)
-        both = matmul(pgrad_t, pair)
-        put(j, both[:, :LANES])
-        put(j + middle + 1, both[:, LANES:])
+    terms = matmul(jnp.transpose(pgrad).astype(BF16), stacked_ref[...])
+    order = [k for k in range(kernel_count) if k != middle] + [middle]
+    for n, k in enumerate(order):
+        block = jnp.transpose(terms[:, n * LANES : (n + 1) * LANES])
+        cgrad_ref[k * LANES : (k + 1) * LANES, :] = block.astype(BF16)
 
 
 def spread_kernel(slots, pgrad_ref, map_ref, weight_ref, after_ref, back_ref, *sends):
@@ -449,21 +455,23 @@
         [
             ((voxels, channels), BF16),
             ((voxels, channels), F32),
-            ((kernel_count, voxels, channels), BF16),
+            ((voxels, conv_rows), BF16),
         ]
         + [((cap2, channels), BF16)] * slots,
         scratch=[
-            pltpu.VMEM((voxels // 2 + slots * cap // 2, 2 * channels), BF16),
-            pltpu.VMEM((voxels, channels), F32),
+            pltpu.VMEM((voxels // 2, 2 * channels), BF16),
+            pltpu.VMEM((slots * cap, 4 * channels), BF16),
+            pltpu.VMEM(conv_weight.shape, BF16),
         ]
-        + [pltpu.VMEM((2, voxels, (voxels + slots * cap) // 2), BF16)] * 2
+        + [pltpu.VMEM((2, voxels, voxels // 2), BF16)] * 2
+        + [pltpu.VMEM((voxels, slots * cap), BF16)] * 2
         + [pltpu.VMEM((2, voxels, LANES), BF16)] * 2,
         limit=32,
         flops=12 * giga,
     )
     hidden_grad, pre_grad, conv_terms = call(
         functools.partial(gradient_kernel, slots),
-        (*received, stacked, pre_act, features, child_rows, back_h),
+        (*received, stacked, pre_act, child_rows, back_h),
         [
             ((voxels, channels), F32),
             ((voxels, channels), BF16),

time: 106 us -> 104 us (0.981)
  Pallas kernels: 46.3 us -> 44.3 us
    pallas_call x9, Pallas kernels: 46.3 us -> 44.3 us  [call(): pl.pallas_call(kernel, out_shape=[jax.ShapeDtypeStruct(s, d) for s, d in...]
where the time goes in v8:
time: 104 us; the launch traced here: 103 us
  Pallas kernels  44.3 us (43%)
  starting transfers between devices  37.2 us (36%)
  waiting for transfers between devices  21 us (20%)
    pallas_call x9, Pallas kernels, call(): pl.pallas_call(kernel, out_shape=[jax.ShapeDtypeStruct(s, d) for s, d in...  44.3 us
    ppermute x12, starting transfers between devices, swaps(): moved[step] = lax.ppermute(by_step[step], 'shard', pairs)  22.4 us
    all_to_all x2, waiting for transfers between devices, exchange(): return lax.all_to_all(value, 'shard', 0, 0, tiled=True)  15.6 us
    all_to_all x2, starting transfers between devices, exchange(): return lax.all_to_all(value, 'shard', 0, 0, tiled=True)  14.1 us
    ppermute x2, waiting for transfers between devices, swap_cores(): lax.ppermute(value, 'shard', [(i, i + 1 - 2 * (i % 2)) for i in range(dev...  2.85 us
    ppermute x12, waiting for transfers between devices, swaps(): moved[step] = lax.ppermute(by_step[step], 'shard', pairs)  2.57 us
  transfers between devices with their start and end apart: 16, of which 7 were waited for; matrix products, arithmetic and copies ran while one was open for 0% of the time, Pallas kernels for 17%

profile of v8, /device:TPU:1, one launch (start us, length us, event | category | flops | bytes accessed | tf_op | source)
XLA Modules:
  0.0 103.5 jit_solution(6313148744071465455)
XLA Ops:
  0.6 0.0 copy-start.2
  0.6 0.0 copy-start.6
  0.7 0.0 copy-start.4
  0.7 0.0 copy-start
  0.7 4.1 %shard_map.111 = (bf16[96,128]{1,0:T(8,128)(2,1)}, bf16[96,128]{1,0:T(8,128)(2,1)}, bf16[96,128]{1,0:T(8,128)(2,1)}, bf16[96,128]{1,0:T(8,128)(2,1)}, f32[1024,128]{1,0:T(8,128)}) custom-call(bf16[1024,128]{1,0:T(8,128)(2,1)} %refs_4_.1, s32[4,64]{1,0:T(4,128)} %refs_6_.7, s32[8,256]{1,0:T(8,128)} %refs_5_.3, bf16[256,256]{1,0:T(8,128)(2,1)} %refs_7_.3, ...), custom_call_target="tpu_custom_call" | custom-call | flops 1000000000 | bytes 4194304 | tf_op jit(solution)/shard_map/pallas_call | solution.py:401
  4.7 0.1 collective-permute-start
  4.9 4.5 %collective-permute-start.1 = (bf16[96,128]{1,0:T(8,128)(2,1)}, bf16[96,128]{1,0:T(8,128)(2,1)S(1)}, u32[]{:S(2)}, u32[]{:S(2)}) collective-permute-start(bf16[96,128]{1,0:T(8,128)(2,1)} %get-tuple-element.40), channel_id=1, source_target_pairs={{1,2},{2,1},{3,4},{4,3},{5,6},{6,5},{7,8},{8,7},{9,10},{10,9},{11,... | collective-permute-start | bytes 73736 | tf_op jit(solution)/shard_map/ppermute | solution.py:23
  9.3 1.3 %collective-permute-start.2 = (bf16[96,128]{1,0:T(8,128)(2,1)}, bf16[96,128]{1,0:T(8,128)(2,1)S(1)}, u32[]{:S(2)}, u32[]{:S(2)}) collective-permute-start(bf16[96,128]{1,0:T(8,128)(2,1)} %get-tuple-element.41), channel_id=1, source_target_pairs={{0,2},{1,3},{2,0},{3,1},{4,6},{5,7},{6,4},{7,5},{8,10},{9,11},{10,... | collective-permute-start | bytes 73736 | tf_op jit(solution)/shard_map/ppermute | solution.py:23
  10.6 0.0 copy-start.8
  10.6 0.8 collective-permute-start.3
  11.4 0.0 collective-permute-done.refs_0_
  11.4 0.0 collective-permute-done.1.refs_1_
  11.4 0.9 collective-permute-done.2.refs_2_
  12.3 0.0 collective-permute-done.3.refs_3_
  12.3 0.0 copy-done.2
  12.3 0.0 copy-done.6
  12.3 0.0 copy-done.4
  12.3 0.0 copy-done
  12.3 16.3 %shard_map.112 = (bf16[1024,128]{1,0:T(8,128)(2,1)S(1)}, f32[1024,128]{1,0:T(8,128)S(1)}, bf16[1024,3456]{1,0:T(8,128)(2,1)S(1)}, bf16[32,128]{1,0:T(8,128)(2,1)...) custom-call(bf16[96,128]{1,0:T(8,128)(2,1)S(1)} %collective-permute-done.refs_0_, ...), custom_call_target="tpu_custom_call" | custom-call | flops 12000000000 | bytes 4194304 | tf_op jit(solution)/shard_map/pallas_call | solution.py:401
  28.6 0.1 collective-permute-start.4
  28.7 6.8 %collective-permute-start.5 = (bf16[32,128]{1,0:T(8,128)(2,1)S(1)}, bf16[32,128]{1,0:T(8,128)(2,1)S(1)}, u32[]{:S(2)}, u32[]{:S(2)}) collective-permute-start(bf16[32,128]{1,0:T(8,128)(2,1)S(1)} %get-tuple-element.44), channel_id=1, source_target_pairs={{1,2},{2,1},{3,4},{4,3},{5,6},{6,5},{7,8},{8,7},{9,10},{10,9},{11,... | collective-permute-start | bytes 24584 | tf_op jit(solution)/shard_map/ppermute | solution.py:23
  35.5 2.5 %collective-permute-start.6 = (bf16[32,128]{1,0:T(8,128)(2,1)S(1)}, bf16[32,128]{1,0:T(8,128)(2,1)S(1)}, u32[]{:S(2)}, u32[]{:S(2)}) collective-permute-start(bf16[32,128]{1,0:T(8,128)(2,1)S(1)} %get-tuple-element.45), channel_id=1, source_target_pairs={{0,2},{1,3},{2,0},{3,1},{4,6},{5,7},{6,4},{7,5},{8,10},{9,11},{10,... | collective-permute-start | bytes 24584 | tf_op jit(solution)/shard_map/ppermute | solution.py:23
  38.0 0.6 collective-permute-start.7
  38.7 0.0 copy-done.8
  38.7 0.0 copy-start.1
  38.7 0.0 copy-start.3
  38.7 0.0 copy-start.5
  38.8 1.6 %shard_map.113 = (f32[1024,128]{1,0:T(8,128)S(1)}, bf16[1024,128]{1,0:T(8,128)(2,1)S(1)}, bf16[3456,128]{1,0:T(8,128)(2,1)S(1)}) custom-call(bf16[96,128]{1,0:T(8,128)(2,1)S(1)} %collective-permute-done.refs_0_, bf16[96,128]{1,0:T(8,128)(2,1)S(1)} %collective-permute-done.1.refs_1_, bf16[96,128]{1,0:T(8,128)(2,1)S(1)} %collective-permute-done.2.refs_2_, ...), custom_call_target="tpu_custom_call" | custom-call | flops 3000000000 | bytes 4194304 | tf_op jit(solution)/shard_map/pallas_call | solution.py:401
  40.3 0.0 collective-permute-done.4.refs_0_
  40.3 0.0 collective-permute-done.5.refs_1_
  40.3 0.0 collective-permute-done.6.refs_2_
  40.3 0.0 collective-permute-done.7.refs_3_
  40.4 0.0 copy-done.1
  40.4 0.0 copy-done.3
  40.4 0.0 copy-done.5
  40.4 2.5 %shard_map.114 = (bf16[256,256]{1,0:T(8,128)(2,1)}, bf16[5632,128]{1,0:T(8,128)(2,1)S(1)}, bf16[2816,128]{1,0:T(8,128)(2,1)S(1)}) custom-call(bf16[32,128]{1,0:T(8,128)(2,1)S(1)} %collective-permute-done.4.refs_0_, bf16[32,128]{1,0:T(8,128)(2,1)S(1)} %collective-permute-done.5.refs_1_, bf16[32,128]{1,0:T(8,128)(2,1)S(1)} %collective-permute-done.6.refs_2_, ...), custom_call_target="tpu_custom_call" | custom-call | flops 2000000000 | bytes 4194304 | tf_op jit(solution)/shard_map/pallas_call | solution.py:401
  42.9 0.0 collective-permute-start.8
  42.9 2.2 %collective-permute-done.8.other_ref = bf16[2816,128]{1,0:T(8,128)(2,1)S(1)} collective-permute-done((bf16[2816,128]{1,0:T(8,128)(2,1)S(1)}, bf16[2816,128]{1,0:T(8,128)(2,1)S(1)}, u32[]{:S(2)}, u32[]{:S(2)}) %collective-permute-start.8) | collective-permute-done | bytes 720928 | tf_op jit(solution)/shard_map/ppermute | solution.py:413
  45.1 1.0 %shard_map.115.after_ref = bf16[2816,128]{1,0:T(8,128)(2,1)} custom-call(bf16[5632,128]{1,0:T(8,128)(2,1)S(1)} %get-tuple-element.53.terms_ref, bf16[2816,128]{1,0:T(8,128)(2,1)S(1)} %collective-permute-done.8.other_ref), custom_call_target="tpu_custom_call" | custom-call | flops 1000000 | bytes 4194304 | tf_op jit(solution)/shard_map/pallas_call | solution.py:401
  46.2 10.3 %all-to-all-start = ((bf16[32,88,128]{2,1,0:T(8,128)(2,1)}), bf16[32,88,128]{2,1,0:T(8,128)(2,1)S(1)}, u32[]{:S(2)}, u32[]{:S(2)}) async-start(bf16[32,88,128]{2,1,0:T(8,128)(2,1)} %bitcast), calls=%async_computation | async-start | bytes 1441792 | tf_op jit(solution)/shard_map/all_to_all | solution.py:417
  56.4 14.9 %shard_map.116 = (f32[1024,128]{1,0:T(8,128)S(1)}, bf16[64,128]{1,0:T(8,128)(2,1)S(1)}, bf16[64,128]{1,0:T(8,128)(2,1)S(1)}, bf16[64,128]{1,0:T(8,128)(2,1)S(1)}, bf16[64,128]{1,0:T(8,128)(2,1)S(1)}) custom-call(bf16[1024,128]{1,0:T(8,128)(2,1)S(1)} %get-tuple-element.55.pgrad_ref, s32[27,1024]{1,0:T(8,128)S(1)} %copy-done.4, ...), custom_call_target="tpu_custom_call" | custom-call | flops 20000000000 | bytes 4194304 | tf_op jit(solution)/shard_map/pallas_call | solution.py:401
  71.3 0.0 copy-start.7
  71.4 4.0 %all-to-all-done = bf16[32,88,128]{2,1,0:T(8,128)(2,1)S(1)} async-done(((bf16[32,88,128]{2,1,0:T(8,128)(2,1)}), bf16[32,88,128]{2,1,0:T(8,128)(2,1)S(1)}, u32[]{:S(2)}, u32[]{:S(2)}) %all-to-all-start) | async-done | bytes 720928 | tf_op jit(solution)/shard_map/all_to_all | solution.py:417
  75.4 1.0 shard_map.117
  76.3 3.9 %all-to-all-start.1 = ((bf16[32,88,128]{2,1,0:T(8,128)(2,1)}), bf16[32,88,128]{2,1,0:T(8,128)(2,1)S(1)}, u32[]{:S(2)}, u32[]{:S(2)}) async-start(bf16[32,88,128]{2,1,0:T(8,128)(2,1)} %bitcast.2), calls=%async_computation.1 | async-start | bytes 1441792 | tf_op jit(solution)/shard_map/all_to_all | solution.py:417
  80.2 0.3 collective-permute-start.9
  80.5 3.4 %collective-permute-start.10 = (bf16[64,128]{1,0:T(8,128)(2,1)S(1)}, bf16[64,128]{1,0:T(8,128)(2,1)S(1)}, u32[]{:S(2)}, u32[]{:S(2)}) collective-permute-start(bf16[64,128]{1,0:T(8,128)(2,1)S(1)} %get-tuple-element.62), channel_id=1, source_target_pairs={{1,2},{2,1},{3,4},{4,3},{5,6},{6,5},{7,8},{8,7},{9,10},{10,9},{11,... | collective-permute-start | bytes 49160 | tf_op jit(solution)/shard_map/ppermute | solution.py:23
  84.0 1.2 %collective-permute-start.11 = (bf16[64,128]{1,0:T(8,128)(2,1)S(1)}, bf16[64,128]{1,0:T(8,128)(2,1)S(1)}, u32[]{:S(2)}, u32[]{:S(2)}) collective-permute-start(bf16[64,128]{1,0:T(8,128)(2,1)S(1)} %get-tuple-element.63), channel_id=1, source_target_pairs={{0,2},{1,3},{2,0},{3,1},{4,6},{5,7},{6,4},{7,5},{8,10},{9,11},{10,... | collective-permute-start | bytes 49160 | tf_op jit(solution)/shard_map/ppermute | solution.py:23
  85.2 0.7 collective-permute-start.12
  85.9 0.0 collective-permute-done.9.refs_0_
  85.9 0.1 collective-permute-done.10.refs_1_
  85.9 1.6 %collective-permute-done.11.refs_2_ = bf16[64,128]{1,0:T(8,128)(2,1)S(1)} collective-permute-done((bf16[64,128]{1,0:T(8,128)(2,1)S(1)}, bf16[64,128]{1,0:T(8,128)(2,1)S(1)}, u32[]{:S(2)}, u32[]{:S(2)}) %collective-permute-start.11) | collective-permute-done | bytes 16416 | tf_op jit(solution)/shard_map/ppermute | solution.py:23
  87.6 0.0 collective-permute-done.12.refs_3_
  87.6 11.6 %all-to-all-done.1 = bf16[32,88,128]{2,1,0:T(8,128)(2,1)S(1)} async-done(((bf16[32,88,128]{2,1,0:T(8,128)(2,1)}), bf16[32,88,128]{2,1,0:T(8,128)(2,1)S(1)}, u32[]{:S(2)}, u32[]{:S(2)}) %all-to-all-start.1) | async-done | bytes 720928 | tf_op jit(solution)/shard_map/all_to_all | solution.py:417
  99.2 0.7 collective-permute-start.13
  99.9 0.0 copy-done.7
  99.9 1.2 %shard_map.118 = f32[1024,128]{1,0:T(8,128)} custom-call(bf16[64,128]{1,0:T(8,128)(2,1)S(1)} %collective-permute-done.9.refs_0_, bf16[64,128]{1,0:T(8,128)(2,1)S(1)} %collective-permute-done.10.refs_1_, bf16[64,128]{1,0:T(8,128)(2,1)S(1)} %collective-permute-done.11.refs_2_, bf16[64,128]{1,0:T(8,128)(2,1)S(1)} %collective-permute-done.12.refs_3_, ...), custom_call_target="tpu_custom_call" | custom-call | flops 1000000000 | bytes 4194304 | tf_op jit(solution)/shard_map/pallas_call | solution.py:401
  101.0 0.7 collective-permute-done.13.other_ref
  101.7 1.8 %shard_map.119 = (f32[3456,128]{1,0:T(8,128)}, f32[1024,256]{1,0:T(8,128)}) custom-call(bf16[2816,128]{1,0:T(8,128)(2,1)S(1)} %bitcast.7, bf16[2816,128]{1,0:T(8,128)(2,1)S(1)} %collective-permute-done.13.other_ref), custom_call_target="tpu_custom_call" | custom-call | flops 1000000 | bytes 4194304 | tf_op jit(solution)/shard_map/pallas_call | solution.py:401
Async XLA Ops:
  0.6 11.7 %copy-start.2 = (bf16[1024,128]{1,0:T(8,128)(2,1)S(1)}, bf16[1024,128]{1,0:T(8,128)(2,1)}, u32[]{:S(2)}) copy-start(bf16[1024,128]{1,0:T(8,128)(2,1)} %refs_4_.1) | copy-start | bytes 786436
  0.6 11.6 %copy-start.6 = (s32[4,32]{1,0:T(4,128)S(1)}, s32[4,32]{1,0:T(4,128)}, u32[]{:S(2)}) copy-start(s32[4,32]{1,0:T(4,128)} %refs_6_.5) | copy-start | bytes 1540
  0.7 11.6 %copy-start.4 = (s32[27,1024]{1,0:T(8,128)S(1)}, s32[27,1024]{1,0:T(8,128)}, u32[]{:S(2)}) copy-start(s32[27,1024]{1,0:T(8,128)} %map_ref.1) | copy-start | bytes 331780
  0.7 11.6 %copy-start = (bf16[27,128,128]{2,1,0:T(8,128)(2,1)S(1)}, bf16[27,128,128]{2,1,0:T(8,128)(2,1)}, u32[]{:S(2)}) copy-start(bf16[27,128,128]{2,1,0:T(8,128)(2,1)} %weight_ref.1) | copy-start | bytes 2654212
  4.7 6.7 %collective-permute-start = (bf16[96,128]{1,0:T(8,128)(2,1)}, bf16[96,128]{1,0:T(8,128)(2,1)S(1)}, u32[]{:S(2)}, u32[]{:S(2)}) collective-permute-start(bf16[96,128]{1,0:T(8,128)(2,1)} %get-tuple-element.39), channel_id=1, source_target_pairs={{0,1},{1,0},{2,3},{3,2},{4,5},{5,4},{6,7},{7,6},{8,9},{9,8},{10,11... | collective-permute-start | bytes 73736 | tf_op jit(solution)/shard_map/ppermute | solution.py:23
  4.9 6.6 %collective-permute-start.1 = (bf16[96,128]{1,0:T(8,128)(2,1)}, bf16[96,128]{1,0:T(8,128)(2,1)S(1)}, u32[]{:S(2)}, u32[]{:S(2)}) collective-permute-start(bf16[96,128]{1,0:T(8,128)(2,1)} %get-tuple-element.40), channel_id=1, source_target_pairs={{1,2},{2,1},{3,4},{4,3},{5,6},{6,5},{7,8},{8,7},{9,10},{10,9},{11,... | collective-permute-start | bytes 73736 | tf_op jit(solution)/shard_map/ppermute | solution.py:23
  9.3 3.0 %collective-permute-start.2 = (bf16[96,128]{1,0:T(8,128)(2,1)}, bf16[96,128]{1,0:T(8,128)(2,1)S(1)}, u32[]{:S(2)}, u32[]{:S(2)}) collective-permute-start(bf16[96,128]{1,0:T(8,128)(2,1)} %get-tuple-element.41), channel_id=1, source_target_pairs={{0,2},{1,3},{2,0},{3,1},{4,6},{5,7},{6,4},{7,5},{8,10},{9,11},{10,... | collective-permute-start | bytes 73736 | tf_op jit(solution)/shard_map/ppermute | solution.py:23
  10.6 28.1 %copy-start.8 = (f32[1024,128]{1,0:T(8,128)S(1)}, f32[1024,128]{1,0:T(8,128)}, u32[]{:S(2)}) copy-start(f32[1024,128]{1,0:T(8,128)} %get-tuple-element.50.refs_7_) | copy-start | bytes 1572868
  10.6 1.7 %collective-permute-start.3 = (bf16[96,128]{1,0:T(8,128)(2,1)}, bf16[96,128]{1,0:T(8,128)(2,1)S(1)}, u32[]{:S(2)}, u32[]{:S(2)}) collective-permute-start(bf16[96,128]{1,0:T(8,128)(2,1)} %get-tuple-element.42), channel_id=1, source_target_pairs={{2,4},{3,5},{4,2},{5,3},{6,8},{7,9},{8,6},{9,7},{10,12},{11,13},{1... | collective-permute-start | bytes 73736 | tf_op jit(solution)/shard_map/ppermute | solution.py:23
  28.6 11.7 %collective-permute-start.4 = (bf16[32,128]{1,0:T(8,128)(2,1)S(1)}, bf16[32,128]{1,0:T(8,128)(2,1)S(1)}, u32[]{:S(2)}, u32[]{:S(2)}) collective-permute-start(bf16[32,128]{1,0:T(8,128)(2,1)S(1)} %get-tuple-element.43), channel_id=1, source_target_pairs={{0,1},{1,0},{2,3},{3,2},{4,5},{5,4},{6,7},{7,6},{8,9},{9,8},{10,11... | collective-permute-start | bytes 24584 | tf_op jit(solution)/shard_map/ppermute | solution.py:23
  28.7 11.6 %collective-permute-start.5 = (bf16[32,128]{1,0:T(8,128)(2,1)S(1)}, bf16[32,128]{1,0:T(8,128)(2,1)S(1)}, u32[]{:S(2)}, u32[]{:S(2)}) collective-permute-start(bf16[32,128]{1,0:T(8,128)(2,1)S(1)} %get-tuple-element.44), channel_id=1, source_target_pairs={{1,2},{2,1},{3,4},{4,3},{5,6},{6,5},{7,8},{8,7},{9,10},{10,9},{11,... | collective-permute-start | bytes 24584 | tf_op jit(solution)/shard_map/ppermute | solution.py:23
  35.5 4.8 %collective-permute-start.6 = (bf16[32,128]{1,0:T(8,128)(2,1)S(1)}, bf16[32,128]{1,0:T(8,128)(2,1)S(1)}, u32[]{:S(2)}, u32[]{:S(2)}) collective-permute-start(bf16[32,128]{1,0:T(8,128)(2,1)S(1)} %get-tuple-element.45), channel_id=1, source_target_pairs={{0,2},{1,3},{2,0},{3,1},{4,6},{5,7},{6,4},{7,5},{8,10},{9,11},{10,... | collective-permute-start | bytes 24584 | tf_op jit(solution)/shard_map/ppermute | solution.py:23
  38.0 2.3 %collective-permute-start.7 = (bf16[32,128]{1,0:T(8,128)(2,1)S(1)}, bf16[32,128]{1,0:T(8,128)(2,1)S(1)}, u32[]{:S(2)}, u32[]{:S(2)}) collective-permute-start(bf16[32,128]{1,0:T(8,128)(2,1)S(1)} %get-tuple-element.46), channel_id=1, source_target_pairs={{2,4},{3,5},{4,2},{5,3},{6,8},{7,9},{8,6},{9,7},{10,12},{11,13},{1... | collective-permute-start | bytes 24584 | tf_op jit(solution)/shard_map/ppermute | solution.py:23
  38.7 1.6 %copy-start.1 = (bf16[8,128,256]{2,1,0:T(8,128)(2,1)S(1)}, bf16[8,128,256]{2,1,0:T(8,128)(2,1)}, u32[]{:S(2)}) copy-start(bf16[8,128,256]{2,1,0:T(8,128)(2,1)} %refs_6_.6) | copy-start | bytes 1572868
  38.7 1.6 %copy-start.3 = (bf16[256,256]{1,0:T(8,128)(2,1)S(1)}, bf16[256,256]{1,0:T(8,128)(2,1)}, u32[]{:S(2)}) copy-start(bf16[256,256]{1,0:T(8,128)(2,1)} %refs_7_.3) | copy-start | bytes 393220
  38.7 1.6 %copy-start.5 = (s32[8,256]{1,0:T(8,128)S(1)}, s32[8,256]{1,0:T(8,128)}, u32[]{:S(2)}) copy-start(s32[8,256]{1,0:T(8,128)} %refs_5_.3) | copy-start | bytes 24580
  42.9 2.2 %collective-permute-start.8 = (bf16[2816,128]{1,0:T(8,128)(2,1)S(1)}, bf16[2816,128]{1,0:T(8,128)(2,1)S(1)}, u32[]{:S(2)}, u32[]{:S(2)}) collective-permute-start(bf16[2816,128]{1,0:T(8,128)(2,1)S(1)} %get-tuple-element.54), channel_id=1, source_target_pairs={{0,1},{1,0},{2,3},{3,2},{4,5},{5,4},{6,7},{7,6},{8,9},{9,8},{10,11... | collective-permute-start | bytes 2162696 | tf_op jit(solution)/shard_map/ppermute | solution.py:413
  46.2 29.2 %all-to-all-start = ((bf16[32,88,128]{2,1,0:T(8,128)(2,1)}), bf16[32,88,128]{2,1,0:T(8,128)(2,1)S(1)}, u32[]{:S(2)}, u32[]{:S(2)}) async-start(bf16[32,88,128]{2,1,0:T(8,128)(2,1)} %bitcast), calls=%async_computation | async-start | bytes 1441792 | tf_op jit(solution)/shard_map/all_to_all | solution.py:417
  71.3 28.5 %copy-start.7 = (s32[4,64]{1,0:T(4,128)S(1)}, s32[4,64]{1,0:T(4,128)}, u32[]{:S(2)}) copy-start(s32[4,64]{1,0:T(4,128)} %refs_6_.7) | copy-start | bytes 3076
  76.3 22.8 %all-to-all-start.1 = ((bf16[32,88,128]{2,1,0:T(8,128)(2,1)}), bf16[32,88,128]{2,1,0:T(8,128)(2,1)S(1)}, u32[]{:S(2)}, u32[]{:S(2)}) async-start(bf16[32,88,128]{2,1,0:T(8,128)(2,1)} %bitcast.2), calls=%async_computation.1 | async-start | bytes 1441792 | tf_op jit(solution)/shard_map/all_to_all | solution.py:417
  80.2 5.7 %collective-permute-start.9 = (bf16[64,128]{1,0:T(8,128)(2,1)S(1)}, bf16[64,128]{1,0:T(8,128)(2,1)S(1)}, u32[]{:S(2)}, u32[]{:S(2)}) collective-permute-start(bf16[64,128]{1,0:T(8,128)(2,1)S(1)} %get-tuple-element.61.after_ref), channel_id=1, source_target_pairs={{0,1},{1,0},{2,3},{3,2},{4,5},{5,4},{6,7},{7,6},{8,9},{9,8},{10,11... | collective-permute-start | bytes 49160 | tf_op jit(solution)/shard_map/ppermute | solution.py:23
  80.5 5.4 %collective-permute-start.10 = (bf16[64,128]{1,0:T(8,128)(2,1)S(1)}, bf16[64,128]{1,0:T(8,128)(2,1)S(1)}, u32[]{:S(2)}, u32[]{:S(2)}) collective-permute-start(bf16[64,128]{1,0:T(8,128)(2,1)S(1)} %get-tuple-element.62), channel_id=1, source_target_pairs={{1,2},{2,1},{3,4},{4,3},{5,6},{6,5},{7,8},{8,7},{9,10},{10,9},{11,... | collective-permute-start | bytes 49160 | tf_op jit(solution)/shard_map/ppermute | solution.py:23
  84.0 3.6 %collective-permute-start.11 = (bf16[64,128]{1,0:T(8,128)(2,1)S(1)}, bf16[64,128]{1,0:T(8,128)(2,1)S(1)}, u32[]{:S(2)}, u32[]{:S(2)}) collective-permute-start(bf16[64,128]{1,0:T(8,128)(2,1)S(1)} %get-tuple-element.63), channel_id=1, source_target_pairs={{0,2},{1,3},{2,0},{3,1},{4,6},{5,7},{6,4},{7,5},{8,10},{9,11},{10,... | collective-permute-start | bytes 49160 | tf_op jit(solution)/shard_map/ppermute | solution.py:23
  85.2 2.4 %collective-permute-start.12 = (bf16[64,128]{1,0:T(8,128)(2,1)S(1)}, bf16[64,128]{1,0:T(8,128)(2,1)S(1)}, u32[]{:S(2)}, u32[]{:S(2)}) collective-permute-start(bf16[64,128]{1,0:T(8,128)(2,1)S(1)} %get-tuple-element.64), channel_id=1, source_target_pairs={{2,4},{3,5},{4,2},{5,3},{6,8},{7,9},{8,6},{9,7},{10,12},{11,13},{1... | collective-permute-start | bytes 49160 | tf_op jit(solution)/shard_map/ppermute | solution.py:23
  99.2 2.5 %collective-permute-start.13 = (bf16[2816,128]{1,0:T(8,128)(2,1)S(1)}, bf16[2816,128]{1,0:T(8,128)(2,1)S(1)}, u32[]{:S(2)}, u32[]{:S(2)}) collective-permute-start(bf16[2816,128]{1,0:T(8,128)(2,1)S(1)} %bitcast.6), channel_id=1, source_target_pairs={{0,1},{1,0},{2,3},{3,2},{4,5},{5,4},{6,7},{7,6},{8,9},{9,8},{10,11... | collective-permute-start | bytes 2162696 | tf_op jit(solution)/shard_map/ppermute | solution.py:413

commit v9 on v8

--- a/solution.py
+++ b/solution.py
@@ -180,14 +180,34 @@
     return n + jnp.where(n >= middle, 1, 0)
 
 
+def code_column(map_ref, k, voxels, received):
+    return column(half_codes(map_ref[pl.ds(k, 1), :], voxels, received).astype(BF16))
+
+
+def pick_side(col, both):
+    return jnp.where(col < jnp.zeros(col.shape, BF16), both[:, LANES:], both[:, :LANES])
+
+
+def local_kernel(received, features_ref, map_ref, early_ref, table_ref):
+    voxels = features_ref.shape[0]
+    half = voxels // 2
+    table_ref[:, 0:LANES] = features_ref[0:half, :]
+    table_ref[:, LANES:] = features_ref[half:, :]
+    middle = map_ref.shape[0] // 2
+    for n in range(early_ref.shape[1] // LANES):
+        col = code_column(map_ref, offset_of(n, middle), voxels, received)
+        both = matmul(one_hot_rows(jnp.abs(col), half), table_ref[...]).astype(BF16)
+        early_ref[:, n * LANES : (n + 1) * LANES] = pick_side(col, both)
+
+
 def forward_kernel(slots, *refs):
     received = refs[:slots]
-    features_ref, map_ref, weight_ref, child_ref = refs[slots : slots + 4]
-    hidden_ref, pre_ref, stacked_ref = refs[slots + 4 : slots + 7]
-    sends = refs[slots + 7 : 2 * slots + 7]
-    table_ref, halo_ref, kernel_ref = refs[2 * slots + 7 : 2 * slots + 10]
+    features_ref, map_ref, weight_ref, child_ref, early_ref = refs[slots : slots + 5]
+    hidden_ref, pre_ref, stacked_ref = refs[slots + 5 : slots + 8]
+    sends = refs[slots + 8 : 2 * slots + 8]
+    table_ref, halo_ref, kernel_ref = refs[2 * slots + 8 : 2 * slots + 11]
     own_refs, far_refs, col_refs = (
-        refs[2 * slots + 10 + 2 * n : 2 * slots + 12 + 2 * n] for n in range(3)
+        refs[2 * slots + 11 + 2 * n : 2 * slots + 13 + 2 * n] for n in range(3)
     )
     voxels = features_ref.shape[0]
     gathers = map_ref.shape[0] - 1
@@ -211,9 +231,7 @@
 
     def build(j, side):
         for n in range(2):
-            k = offset_of(2 * j + n, middle)
-            codes = half_codes(map_ref[pl.ds(k, 1), :], voxels, slots * cap).astype(BF16)
-            col = column(codes)
+            col = code_column(map_ref, offset_of(2 * j + n, middle), voxels, slots * cap)
             col_refs[side][n] = col
             col = jnp.abs(col)
             own_refs[side][n] = one_hot_rows(col, half)
@@ -226,21 +244,37 @@
         for n in range(2):
             both = matmul(own_refs[side][n], table_ref[...])
             both = (both + far[:, 2 * n * LANES : 2 * (n + 1) * LANES]).astype(BF16)
-            right = col_refs[side][n] < jnp.zeros((voxels, LANES), BF16)
-            pair.append(jnp.where(right, both[:, LANES:], both[:, :LANES]))
+            pair.append(pick_side(col_refs[side][n], both))
         lanes = pl.ds(pl.multiple_of(2 * j * LANES, 2 * LANES), 2 * LANES)
         stacked_ref[:, lanes] = jnp.concatenate(pair, axis=1)
 
+    begun = early_ref.shape[1] // (2 * LANES)
+    for j in range(begun):
+        cols = [
+            code_column(map_ref, offset_of(2 * j + n, middle), voxels, slots * cap)
+            for n in range(2)
+        ]
+        choosers = [one_hot_rows(jnp.abs(col), half_halo, half) for col in cols]
+        far = matmul(jnp.concatenate(choosers, axis=1), halo_ref[...]).astype(BF16)
+        for n in range(2):
+            picked = pick_side(cols[n], far[:, 2 * n * LANES : 2 * (n + 1) * LANES])
+            lanes = slice((2 * j + n) * LANES, (2 * j + n + 1) * LANES)
+            stacked_ref[:, lanes] = early_ref[:, lanes] + picked
+
     def step(i, carry):
         for side in range(2):
-            j = 2 * i + side
+            j = begun + 2 * i + side
             use(j, side)
             build(j + 1, 1 - side)
         return carry
 
-    build(0, 0)
-    lax.fori_loop(0, middle // 2, step, 0)
-    use(middle - 1, 0)
+    left = middle - begun
+    build(begun, 0)
+    lax.fori_loop(0, (left - 1) // 2, step, 0)
+    if left % 2 == 0:
+        use(middle - 2, 0)
+        build(middle - 1, 1)
+    use(middle - 1, 1 - left % 2)
     stacked_ref[:, gathers * LANES :] = features
     pre = matmul(stacked_ref[...], kernel_ref[...].reshape(-1, LANES))
     pre_ref[...] = pre
@@ -375,18 +409,45 @@
             out_ref[d * rows : (d + 1) * rows, :] = total
 
 
-def final_kernel(mine_ref, other_ref, conv_ref, down_ref, whole_ref):
-    rows = mine_ref.shape[0]
-    mine, other = my_half(rows)
-    whole_ref[pl.ds(mine, rows), :] = mine_ref[...]
-    whole_ref[pl.ds(other, rows), :] = other_ref[...]
-    row = conv_ref.shape[0]
-    conv_ref[...] = whole_ref[0:row, :].astype(F32)
-    for first in range(0, down_ref.shape[0], LANES):
-        for start in range(0, down_ref.shape[1], LANES):
-            block = whole_ref[row : row + LANES, :].astype(F32)
-            down_ref[first : first + LANES, start : start + LANES] = block
-            row += LANES
+def final_kernel(own, *refs):
+    block_ref, conv_hbm, down_hbm = refs[0], *refs[-5:-3]
+    conv_ref, down_ref, sems = refs[-3:]
+    rows = block_ref.shape[0]
+    conv_rows = conv_hbm.shape[0]
+    core = lax.rem(lax.axis_index("shard"), 2)
+    piece = 4 * LANES
+    assert rows <= conv_rows <= 2 * rows and rows % LANES == 0
+
+    def write(half):
+        first, last = half * rows, (half + 1) * rows
+        copies = []
+        for start in range(first, min(last, conv_rows), piece):
+            size = min(piece, last - start, conv_rows - start)
+            place = pl.ds(start, size)
+            value = block_ref[start - first : start - first + size, :]
+            conv_ref[place, :] = value.astype(F32)
+            sem = sems.at[len(copies)]
+            copies.append(pltpu.make_async_copy(conv_ref.at[place], conv_hbm.at[place], sem))
+            copies[-1].start()
+        across = down_hbm.shape[1] // LANES
+        for down in range(0, down_hbm.shape[0], LANES):
+            row = conv_rows + down * across
+            for side in range(across):
+                start = row + side * LANES
+                if first <= start < last:
+                    value = block_ref[start - first : start - first + LANES, :]
+                    lanes = slice(side * LANES, (side + 1) * LANES)
+                    down_ref[down : down + LANES, lanes] = value.astype(F32)
+            if first <= row < last:
+                place = pl.ds(down, LANES)
+                sem = sems.at[len(copies)]
+                copies.append(pltpu.make_async_copy(down_ref.at[place], down_hbm.at[place], sem))
+                copies[-1].start()
+        for copy in copies:
+            copy.wait()
+
+    for half in range(2):
+        pl.when(core == (half if own else 1 - half))(functools.partial(write, half))
 
 
 def tail_kernel(slots, *refs):
@@ -396,13 +457,16 @@
     out_ref[...] = add_lists(hgrad_ref[...] + back_ref[...], halo_ref, blocks)
 
 
-def call(kernel, operands, outs, scratch=(), limit=32, flops=0, in_hbm=()):
+def call(
+    kernel, operands, outs, scratch=(), limit=32, flops=0, in_hbm=(), out_hbm=False, aliases={}
+):
     spaces = [pl.ANY if n in in_hbm else pltpu.VMEM for n in range(len(operands))]
     return pl.pallas_call(
         kernel,
         out_shape=[jax.ShapeDtypeStruct(s, d) for s, d in outs],
         in_specs=[pl.BlockSpec(memory_space=space) for space in spaces],
-        out_specs=[pl.BlockSpec(memory_space=pltpu.VMEM) for _ in outs],
+        out_specs=[pl.BlockSpec(memory_space=pl.ANY if out_hbm else pltpu.VMEM) for _ in outs],
+        input_output_aliases=aliases,
         scratch_shapes=list(scratch),
         compiler_params=pltpu.CompilerParams(vmem_limit_bytes=limit * 2**20),
         cost_estimate=pl.CostEstimate(flops=flops, bytes_accessed=4 * 2**20, transcendentals=0),
@@ -449,9 +513,16 @@
     down_rows = octants * channels * coarse_channels // LANES
     grain = 8 * devices
     half_rows = -(-(conv_rows + down_rows) // (2 * grain)) * grain
+    (early,) = call(
+        functools.partial(local_kernel, slots * cap),
+        (features, neighbour_map),
+        [((voxels, 8 * channels), BF16)],
+        scratch=[pltpu.VMEM((voxels // 2, 2 * channels), BF16)],
+        flops=4 * giga,
+    )
     hidden, pre_act, stacked, *leaving = call(
         functools.partial(forward_kernel, slots),
-        (*received, features, neighbour_map, conv_weight, child_rows),
+        (*received, features, neighbour_map, conv_weight, child_rows, early),
         [
             ((voxels, channels), BF16),
             ((voxels, channels), F32),
@@ -521,13 +592,24 @@
         [((voxels, channels), F32)],
         flops=giga,
     )
-    conv_grad, down_grad = call(
-        final_kernel,
-        (mine, swap_cores(mine, devices)),
-        [((conv_rows, LANES), F32), ((octants * channels, coarse_channels), F32)],
-        scratch=[pltpu.VMEM((2 * half_rows, LANES), BF16)],
-        flops=10**6,
-    )
+    other = swap_cores(mine, devices)
+    gradients = ()
+    for own, block in ((True, mine), (False, other)):
+        gradients = call(
+            functools.partial(final_kernel, own),
+            (block, *gradients),
+            [((conv_rows, LANES), F32), ((octants * channels, coarse_channels), F32)],
+            scratch=[
+                pltpu.VMEM((conv_rows, LANES), F32),
+                pltpu.VMEM((octants * channels, coarse_channels), F32),
+                pltpu.SemaphoreType.DMA((32,)),
+            ],
+            flops=10**6,
+            in_hbm=(1, 2),
+            out_hbm=True,
+            aliases={1: 0, 2: 1} if gradients else {},
+        )
+    conv_grad, down_grad = gradients
     conv_grad = conv_grad.reshape(conv_weight.shape)
     return (coarse, input_grad, conv_grad, down_grad.reshape(down_weight.shape))
 

time: 104 us -> 101 us (0.971)
  starting transfers between devices: 37.2 us -> 35.6 us
  waiting for transfers between devices: 21 us -> 19.5 us
    ppermute x12, starting transfers between devices: 22.4 us -> 20.9 us  [swaps(): moved[step] = lax.ppermute(by_step[step], 'shard', pairs)]
    pallas_call x9 -> x11, Pallas kernels: 44.3 us -> 44.6 us  [call(): pl.pallas_call(kernel, out_shape=[jax.ShapeDtypeStruct(s, d) for s, d in...]
  transfers between devices with their start and end apart: 16 -> 16, of which waited for: 7 -> 5; matrix products, arithmetic and copies ran while one was open for 0% -> 0% of each run, Pallas kernels for 17% -> 21%
where the time goes in v9:
time: 101 us
  Pallas kernels  44.6 us (44%)
  starting transfers between devices  35.6 us (35%)
  waiting for transfers between devices  19.5 us (19%)
  between operations  1.1 us (1%)
    pallas_call x11, Pallas kernels, call(): pl.pallas_call(kernel, out_shape=[jax.ShapeDtypeStruct(s, d) for s, d in...  44.6 us
    ppermute x12, starting transfers between devices, swaps(): moved[step] = lax.ppermute(by_step[step], 'shard', pairs)  20.9 us
    all_to_all x2, waiting for transfers between devices, exchange(): return lax.all_to_all(value, 'shard', 0, 0, tiled=True)  15.6 us
    all_to_all x2, starting transfers between devices, exchange(): return lax.all_to_all(value, 'shard', 0, 0, tiled=True)  14 us
    ppermute x2, waiting for transfers between devices, swap_cores(): lax.ppermute(value, 'shard', [(i, i + 1 - 2 * (i % 2)) for i in range(dev...  2.19 us
  transfers between devices with their start and end apart: 16, of which 5 were waited for; matrix products, arithmetic and copies ran while one was open for 0% of the time, Pallas kernels for 21%

profile of v9, /device:TPU:1, one launch (start us, length us, event | category | flops | bytes accessed | tf_op | source)
XLA Modules:
  0.0 100.8 jit_solution(14437516323236653355)
XLA Ops:
  0.6 0.0 copy-start.2
  0.6 0.0 copy-start.4
  0.7 4.0 %shard_map.111 = (bf16[96,128]{1,0:T(8,128)(2,1)}, bf16[96,128]{1,0:T(8,128)(2,1)}, bf16[96,128]{1,0:T(8,128)(2,1)}, bf16[96,128]{1,0:T(8,128)(2,1)}, f32[1024,128]{1,0:T(8,128)}) custom-call(bf16[1024,128]{1,0:T(8,128)(2,1)} %refs_4_.1, s32[4,64]{1,0:T(4,128)} %refs_6_.7, s32[8,256]{1,0:T(8,128)} %refs_5_.3, bf16[256,256]{1,0:T(8,128)(2,1)} %refs_7_.3, ...), custom_call_target="tpu_custom_call" | custom-call | flops 1000000000 | bytes 4194304 | tf_op jit(solution)/shard_map/pallas_call | solution.py:464
  4.7 0.1 collective-permute-start
  4.8 4.5 %collective-permute-start.1 = (bf16[96,128]{1,0:T(8,128)(2,1)}, bf16[96,128]{1,0:T(8,128)(2,1)S(1)}, u32[]{:S(2)}, u32[]{:S(2)}) collective-permute-start(bf16[96,128]{1,0:T(8,128)(2,1)} %get-tuple-element.42), channel_id=1, source_target_pairs={{1,2},{2,1},{3,4},{4,3},{5,6},{6,5},{7,8},{8,7},{9,10},{10,9},{11,... | collective-permute-start | bytes 73736 | tf_op jit(solution)/shard_map/ppermute | solution.py:23
  9.3 1.3 %collective-permute-start.2 = (bf16[96,128]{1,0:T(8,128)(2,1)}, bf16[96,128]{1,0:T(8,128)(2,1)S(1)}, u32[]{:S(2)}, u32[]{:S(2)}) collective-permute-start(bf16[96,128]{1,0:T(8,128)(2,1)} %get-tuple-element.43), channel_id=1, source_target_pairs={{0,2},{1,3},{2,0},{3,1},{4,6},{5,7},{6,4},{7,5},{8,10},{9,11},{10,... | collective-permute-start | bytes 73736 | tf_op jit(solution)/shard_map/ppermute | solution.py:23
  10.5 0.0 copy-start
  10.5 0.0 copy-start.6
  10.5 0.8 collective-permute-start.3
  11.3 0.0 copy-done.2
  11.3 0.0 copy-done.4
  11.3 2.4 %shard_map.112.refs_8_ = bf16[1024,1024]{1,0:T(8,128)(2,1)S(1)} custom-call(bf16[1024,128]{1,0:T(8,128)(2,1)S(1)} %copy-done.2, s32[27,1024]{1,0:T(8,128)S(1)} %copy-done.4), custom_call_target="tpu_custom_call" | custom-call | flops 4000000000 | bytes 4194304 | tf_op jit(solution)/shard_map/pallas_call | solution.py:464
  13.8 0.0 copy-start.8
  13.8 0.0 collective-permute-done.refs_0_
  13.8 0.0 collective-permute-done.1.refs_1_
  13.8 0.0 collective-permute-done.2.refs_2_
  13.8 0.0 collective-permute-done.3.refs_3_
  13.8 0.0 copy-done
  13.8 0.0 copy-done.6
  13.8 13.2 %shard_map.113 = (bf16[1024,128]{1,0:T(8,128)(2,1)S(1)}, f32[1024,128]{1,0:T(8,128)S(1)}, bf16[1024,3456]{1,0:T(8,128)(2,1)S(1)}, bf16[32,128]{1,0:T(8,128)(2,1)...) custom-call(bf16[96,128]{1,0:T(8,128)(2,1)S(1)} %collective-permute-done.refs_0_, ...), custom_call_target="tpu_custom_call" | custom-call | flops 12000000000 | bytes 4194304 | tf_op jit(solution)/shard_map/pallas_call | solution.py:464
  27.1 0.1 collective-permute-start.4
  27.2 5.9 %collective-permute-start.5 = (bf16[32,128]{1,0:T(8,128)(2,1)S(1)}, bf16[32,128]{1,0:T(8,128)(2,1)S(1)}, u32[]{:S(2)}, u32[]{:S(2)}) collective-permute-start(bf16[32,128]{1,0:T(8,128)(2,1)S(1)} %get-tuple-element.46), channel_id=1, source_target_pairs={{1,2},{2,1},{3,4},{4,3},{5,6},{6,5},{7,8},{8,7},{9,10},{10,9},{11,... | collective-permute-start | bytes 24584 | tf_op jit(solution)/shard_map/ppermute | solution.py:23
  33.1 1.8 %collective-permute-start.6 = (bf16[32,128]{1,0:T(8,128)(2,1)S(1)}, bf16[32,128]{1,0:T(8,128)(2,1)S(1)}, u32[]{:S(2)}, u32[]{:S(2)}) collective-permute-start(bf16[32,128]{1,0:T(8,128)(2,1)S(1)} %get-tuple-element.47), channel_id=1, source_target_pairs={{0,2},{1,3},{2,0},{3,1},{4,6},{5,7},{6,4},{7,5},{8,10},{9,11},{10,... | collective-permute-start | bytes 24584 | tf_op jit(solution)/shard_map/ppermute | solution.py:23
  34.9 0.8 collective-permute-start.7
  35.7 0.0 copy-done.8
  35.8 0.0 copy-start.1
  35.8 0.0 copy-start.3
  35.8 0.0 copy-start.5
  35.8 1.6 %shard_map.114 = (f32[1024,128]{1,0:T(8,128)S(1)}, bf16[1024,128]{1,0:T(8,128)(2,1)S(1)}, bf16[3456,128]{1,0:T(8,128)(2,1)S(1)}) custom-call(bf16[96,128]{1,0:T(8,128)(2,1)S(1)} %collective-permute-done.refs_0_, bf16[96,128]{1,0:T(8,128)(2,1)S(1)} %collective-permute-done.1.refs_1_, bf16[96,128]{1,0:T(8,128)(2,1)S(1)} %collective-permute-done.2.refs_2_, ...), custom_call_target="tpu_custom_call" | custom-call | flops 3000000000 | bytes 4194304 | tf_op jit(solution)/shard_map/pallas_call | solution.py:464
  37.4 0.0 collective-permute-done.4.refs_0_
  37.4 0.0 collective-permute-done.5.refs_1_
  37.4 0.0 collective-permute-done.6.refs_2_
  37.4 0.0 collective-permute-done.7.refs_3_
  37.4 0.0 copy-done.1
  37.4 0.0 copy-done.3
  37.4 0.0 copy-done.5
  37.4 2.5 %shard_map.115 = (bf16[256,256]{1,0:T(8,128)(2,1)}, bf16[5632,128]{1,0:T(8,128)(2,1)S(1)}, bf16[2816,128]{1,0:T(8,128)(2,1)S(1)}) custom-call(bf16[32,128]{1,0:T(8,128)(2,1)S(1)} %collective-permute-done.4.refs_0_, bf16[32,128]{1,0:T(8,128)(2,1)S(1)} %collective-permute-done.5.refs_1_, bf16[32,128]{1,0:T(8,128)(2,1)S(1)} %collective-permute-done.6.refs_2_, ...), custom_call_target="tpu_custom_call" | custom-call | flops 2000000000 | bytes 4194304 | tf_op jit(solution)/shard_map/pallas_call | solution.py:464
  40.0 0.0 collective-permute-start.8
  40.0 2.2 %collective-permute-done.8.other_ref = bf16[2816,128]{1,0:T(8,128)(2,1)S(1)} collective-permute-done((bf16[2816,128]{1,0:T(8,128)(2,1)S(1)}, bf16[2816,128]{1,0:T(8,128)(2,1)S(1)}, u32[]{:S(2)}, u32[]{:S(2)}) %collective-permute-start.8) | collective-permute-done | bytes 720928 | tf_op jit(solution)/shard_map/ppermute | solution.py:477
  42.2 1.0 %shard_map.116.after_ref = bf16[2816,128]{1,0:T(8,128)(2,1)} custom-call(bf16[5632,128]{1,0:T(8,128)(2,1)S(1)} %get-tuple-element.55.terms_ref, bf16[2816,128]{1,0:T(8,128)(2,1)S(1)} %collective-permute-done.8.other_ref), custom_call_target="tpu_custom_call" | custom-call | flops 1000000 | bytes 4194304 | tf_op jit(solution)/shard_map/pallas_call | solution.py:464
  43.2 10.1 %all-to-all-start = ((bf16[32,88,128]{2,1,0:T(8,128)(2,1)}), bf16[32,88,128]{2,1,0:T(8,128)(2,1)S(1)}, u32[]{:S(2)}, u32[]{:S(2)}) async-start(bf16[32,88,128]{2,1,0:T(8,128)(2,1)} %bitcast), calls=%async_computation | async-start | bytes 1441792 | tf_op jit(solution)/shard_map/all_to_all | solution.py:481
  53.3 14.9 %shard_map.117 = (f32[1024,128]{1,0:T(8,128)S(1)}, bf16[64,128]{1,0:T(8,128)(2,1)S(1)}, bf16[64,128]{1,0:T(8,128)(2,1)S(1)}, bf16[64,128]{1,0:T(8,128)(2,1)S(1)}, bf16[64,128]{1,0:T(8,128)(2,1)S(1)}) custom-call(bf16[1024,128]{1,0:T(8,128)(2,1)S(1)} %get-tuple-element.57.pgrad_ref, s32[27,1024]{1,0:T(8,128)S(1)} %copy-done.4, ...), custom_call_target="tpu_custom_call" | custom-call | flops 20000000000 | bytes 4194304 | tf_op jit(solution)/shard_map/pallas_call | solution.py:464
  68.2 4.0 %all-to-all-done = bf16[32,88,128]{2,1,0:T(8,128)(2,1)S(1)} async-done(((bf16[32,88,128]{2,1,0:T(8,128)(2,1)}), bf16[32,88,128]{2,1,0:T(8,128)(2,1)S(1)}, u32[]{:S(2)}, u32[]{:S(2)}) %all-to-all-start) | async-done | bytes 720928 | tf_op jit(solution)/shard_map/all_to_all | solution.py:481
  72.2 0.0 copy-start.7
  72.2 1.0 shard_map.118
  73.2 3.9 %all-to-all-start.1 = ((bf16[32,88,128]{2,1,0:T(8,128)(2,1)}), bf16[32,88,128]{2,1,0:T(8,128)(2,1)S(1)}, u32[]{:S(2)}, u32[]{:S(2)}) async-start(bf16[32,88,128]{2,1,0:T(8,128)(2,1)} %bitcast.2), calls=%async_computation.1 | async-start | bytes 1441792 | tf_op jit(solution)/shard_map/all_to_all | solution.py:481
  77.1 0.3 collective-permute-start.9
  77.4 3.4 %collective-permute-start.10 = (bf16[64,128]{1,0:T(8,128)(2,1)S(1)}, bf16[64,128]{1,0:T(8,128)(2,1)S(1)}, u32[]{:S(2)}, u32[]{:S(2)}) collective-permute-start(bf16[64,128]{1,0:T(8,128)(2,1)S(1)} %get-tuple-element.64), channel_id=1, source_target_pairs={{1,2},{2,1},{3,4},{4,3},{5,6},{6,5},{7,8},{8,7},{9,10},{10,9},{11,... | collective-permute-start | bytes 49160 | tf_op jit(solution)/shard_map/ppermute | solution.py:23
  80.8 1.2 %collective-permute-start.11 = (bf16[64,128]{1,0:T(8,128)(2,1)S(1)}, bf16[64,128]{1,0:T(8,128)(2,1)S(1)}, u32[]{:S(2)}, u32[]{:S(2)}) collective-permute-start(bf16[64,128]{1,0:T(8,128)(2,1)S(1)} %get-tuple-element.65), channel_id=1, source_target_pairs={{0,2},{1,3},{2,0},{3,1},{4,6},{5,7},{6,4},{7,5},{8,10},{9,11},{10,... | collective-permute-start | bytes 49160 | tf_op jit(solution)/shard_map/ppermute | solution.py:23
  82.1 0.7 collective-permute-start.12
  82.8 0.0 collective-permute-done.9.refs_0_
  82.8 0.1 collective-permute-done.10.refs_1_
  82.8 1.6 %collective-permute-done.11.refs_2_ = bf16[64,128]{1,0:T(8,128)(2,1)S(1)} collective-permute-done((bf16[64,128]{1,0:T(8,128)(2,1)S(1)}, bf16[64,128]{1,0:T(8,128)(2,1)S(1)}, u32[]{:S(2)}, u32[]{:S(2)}) %collective-permute-start.11) | collective-permute-done | bytes 16416 | tf_op jit(solution)/shard_map/ppermute | solution.py:23
  84.5 0.0 collective-permute-done.12.refs_3_
  84.5 11.6 %all-to-all-done.1 = bf16[32,88,128]{2,1,0:T(8,128)(2,1)S(1)} async-done(((bf16[32,88,128]{2,1,0:T(8,128)(2,1)}), bf16[32,88,128]{2,1,0:T(8,128)(2,1)S(1)}, u32[]{:S(2)}, u32[]{:S(2)}) %all-to-all-start.1) | async-done | bytes 720928 | tf_op jit(solution)/shard_map/all_to_all | solution.py:481
  96.1 0.7 collective-permute-start.13
  96.7 1.4 %shard_map.120 = (f32[3456,128]{1,0:T(8,128)}, f32[1024,256]{1,0:T(8,128)}) custom-call(bf16[2816,128]{1,0:T(8,128)(2,1)S(1)} %bitcast.7), custom_call_target="tpu_custom_call" | custom-call | flops 1000000 | bytes 4194304 | tf_op jit(solution)/shard_map/pallas_call | solution.py:464
  98.1 0.0 copy-done.7
  98.1 1.2 %shard_map.119 = f32[1024,128]{1,0:T(8,128)} custom-call(bf16[64,128]{1,0:T(8,128)(2,1)S(1)} %collective-permute-done.9.refs_0_, bf16[64,128]{1,0:T(8,128)(2,1)S(1)} %collective-permute-done.10.refs_1_, bf16[64,128]{1,0:T(8,128)(2,1)S(1)} %collective-permute-done.11.refs_2_, bf16[64,128]{1,0:T(8,128)(2,1)S(1)} %collective-permute-done.12.refs_3_, ...), custom_call_target="tpu_custom_call" | custom-call | flops 1000000000 | bytes 4194304 | tf_op jit(solution)/shard_map/pallas_call | solution.py:464
  99.3 0.0 collective-permute-done.13.refs_0_
  99.3 1.4 %shard_map.121 = (f32[3456,128]{1,0:T(8,128)}, f32[1024,256]{1,0:T(8,128)}) custom-call(bf16[2816,128]{1,0:T(8,128)(2,1)S(1)} %collective-permute-done.13.refs_0_, f32[3456,128]{1,0:T(8,128)} %get-tuple-element.74.refs_1_, f32[1024,256]{1,0:T(8,128)} %get-tuple-element.75.refs_2_), custom_call_target="tpu_custom_call", output_to_operand_aliasing={{0}: (1, {}), {1}: (2, {})} | custom-call | flops 1000000 | bytes 4194304 | tf_op jit(solution)/shard_map/pallas_call | solution.py:464
Async XLA Ops:
  0.6 10.7 %copy-start.2 = (bf16[1024,128]{1,0:T(8,128)(2,1)S(1)}, bf16[1024,128]{1,0:T(8,128)(2,1)}, u32[]{:S(2)}) copy-start(bf16[1024,128]{1,0:T(8,128)(2,1)} %refs_4_.1) | copy-start | bytes 786436
  0.6 10.7 %copy-start.4 = (s32[27,1024]{1,0:T(8,128)S(1)}, s32[27,1024]{1,0:T(8,128)}, u32[]{:S(2)}) copy-start(s32[27,1024]{1,0:T(8,128)} %map_ref.3) | copy-start | bytes 331780
  4.7 9.1 %collective-permute-start = (bf16[96,128]{1,0:T(8,128)(2,1)}, bf16[96,128]{1,0:T(8,128)(2,1)S(1)}, u32[]{:S(2)}, u32[]{:S(2)}) collective-permute-start(bf16[96,128]{1,0:T(8,128)(2,1)} %get-tuple-element.41), channel_id=1, source_target_pairs={{0,1},{1,0},{2,3},{3,2},{4,5},{5,4},{6,7},{7,6},{8,9},{9,8},{10,11... | collective-permute-start | bytes 73736 | tf_op jit(solution)/shard_map/ppermute | solution.py:23
  4.8 9.0 %collective-permute-start.1 = (bf16[96,128]{1,0:T(8,128)(2,1)}, bf16[96,128]{1,0:T(8,128)(2,1)S(1)}, u32[]{:S(2)}, u32[]{:S(2)}) collective-permute-start(bf16[96,128]{1,0:T(8,128)(2,1)} %get-tuple-element.42), channel_id=1, source_target_pairs={{1,2},{2,1},{3,4},{4,3},{5,6},{6,5},{7,8},{8,7},{9,10},{10,9},{11,... | collective-permute-start | bytes 73736 | tf_op jit(solution)/shard_map/ppermute | solution.py:23
  9.3 4.5 %collective-permute-start.2 = (bf16[96,128]{1,0:T(8,128)(2,1)}, bf16[96,128]{1,0:T(8,128)(2,1)S(1)}, u32[]{:S(2)}, u32[]{:S(2)}) collective-permute-start(bf16[96,128]{1,0:T(8,128)(2,1)} %get-tuple-element.43), channel_id=1, source_target_pairs={{0,2},{1,3},{2,0},{3,1},{4,6},{5,7},{6,4},{7,5},{8,10},{9,11},{10,... | collective-permute-start | bytes 73736 | tf_op jit(solution)/shard_map/ppermute | solution.py:23
  10.5 3.3 %copy-start = (bf16[27,128,128]{2,1,0:T(8,128)(2,1)S(1)}, bf16[27,128,128]{2,1,0:T(8,128)(2,1)}, u32[]{:S(2)}) copy-start(bf16[27,128,128]{2,1,0:T(8,128)(2,1)} %weight_ref.1) | copy-start | bytes 2654212
  10.5 3.3 %copy-start.6 = (s32[4,32]{1,0:T(4,128)S(1)}, s32[4,32]{1,0:T(4,128)}, u32[]{:S(2)}) copy-start(s32[4,32]{1,0:T(4,128)} %refs_6_.5) | copy-start | bytes 1540
  10.5 3.3 %collective-permute-start.3 = (bf16[96,128]{1,0:T(8,128)(2,1)}, bf16[96,128]{1,0:T(8,128)(2,1)S(1)}, u32[]{:S(2)}, u32[]{:S(2)}) collective-permute-start(bf16[96,128]{1,0:T(8,128)(2,1)} %get-tuple-element.44), channel_id=1, source_target_pairs={{2,4},{3,5},{4,2},{5,3},{6,8},{7,9},{8,6},{9,7},{10,12},{11,13},{1... | collective-permute-start | bytes 73736 | tf_op jit(solution)/shard_map/ppermute | solution.py:23
  13.8 22.0 %copy-start.8 = (f32[1024,128]{1,0:T(8,128)S(1)}, f32[1024,128]{1,0:T(8,128)}, u32[]{:S(2)}) copy-start(f32[1024,128]{1,0:T(8,128)} %get-tuple-element.52.refs_7_) | copy-start | bytes 1572868
  27.1 10.3 %collective-permute-start.4 = (bf16[32,128]{1,0:T(8,128)(2,1)S(1)}, bf16[32,128]{1,0:T(8,128)(2,1)S(1)}, u32[]{:S(2)}, u32[]{:S(2)}) collective-permute-start(bf16[32,128]{1,0:T(8,128)(2,1)S(1)} %get-tuple-element.45), channel_id=1, source_target_pairs={{0,1},{1,0},{2,3},{3,2},{4,5},{5,4},{6,7},{7,6},{8,9},{9,8},{10,11... | collective-permute-start | bytes 24584 | tf_op jit(solution)/shard_map/ppermute | solution.py:23
  27.2 10.2 %collective-permute-start.5 = (bf16[32,128]{1,0:T(8,128)(2,1)S(1)}, bf16[32,128]{1,0:T(8,128)(2,1)S(1)}, u32[]{:S(2)}, u32[]{:S(2)}) collective-permute-start(bf16[32,128]{1,0:T(8,128)(2,1)S(1)} %get-tuple-element.46), channel_id=1, source_target_pairs={{1,2},{2,1},{3,4},{4,3},{5,6},{6,5},{7,8},{8,7},{9,10},{10,9},{11,... | collective-permute-start | bytes 24584 | tf_op jit(solution)/shard_map/ppermute | solution.py:23
  33.1 4.3 %collective-permute-start.6 = (bf16[32,128]{1,0:T(8,128)(2,1)S(1)}, bf16[32,128]{1,0:T(8,128)(2,1)S(1)}, u32[]{:S(2)}, u32[]{:S(2)}) collective-permute-start(bf16[32,128]{1,0:T(8,128)(2,1)S(1)} %get-tuple-element.47), channel_id=1, source_target_pairs={{0,2},{1,3},{2,0},{3,1},{4,6},{5,7},{6,4},{7,5},{8,10},{9,11},{10,... | collective-permute-start | bytes 24584 | tf_op jit(solution)/shard_map/ppermute | solution.py:23
  34.9 2.5 %collective-permute-start.7 = (bf16[32,128]{1,0:T(8,128)(2,1)S(1)}, bf16[32,128]{1,0:T(8,128)(2,1)S(1)}, u32[]{:S(2)}, u32[]{:S(2)}) collective-permute-start(bf16[32,128]{1,0:T(8,128)(2,1)S(1)} %get-tuple-element.48), channel_id=1, source_target_pairs={{2,4},{3,5},{4,2},{5,3},{6,8},{7,9},{8,6},{9,7},{10,12},{11,13},{1... | collective-permute-start | bytes 24584 | tf_op jit(solution)/shard_map/ppermute | solution.py:23
  35.8 1.6 %copy-start.1 = (bf16[8,128,256]{2,1,0:T(8,128)(2,1)S(1)}, bf16[8,128,256]{2,1,0:T(8,128)(2,1)}, u32[]{:S(2)}) copy-start(bf16[8,128,256]{2,1,0:T(8,128)(2,1)} %refs_6_.6) | copy-start | bytes 1572868
  35.8 1.6 %copy-start.3 = (bf16[256,256]{1,0:T(8,128)(2,1)S(1)}, bf16[256,256]{1,0:T(8,128)(2,1)}, u32[]{:S(2)}) copy-start(bf16[256,256]{1,0:T(8,128)(2,1)} %refs_7_.3) | copy-start | bytes 393220
  35.8 1.6 %copy-start.5 = (s32[8,256]{1,0:T(8,128)S(1)}, s32[8,256]{1,0:T(8,128)}, u32[]{:S(2)}) copy-start(s32[8,256]{1,0:T(8,128)} %refs_5_.3) | copy-start | bytes 24580
  40.0 2.2 %collective-permute-start.8 = (bf16[2816,128]{1,0:T(8,128)(2,1)S(1)}, bf16[2816,128]{1,0:T(8,128)(2,1)S(1)}, u32[]{:S(2)}, u32[]{:S(2)}) collective-permute-start(bf16[2816,128]{1,0:T(8,128)(2,1)S(1)} %get-tuple-element.56), channel_id=1, source_target_pairs={{0,1},{1,0},{2,3},{3,2},{4,5},{5,4},{6,7},{7,6},{8,9},{9,8},{10,11... | collective-permute-start | bytes 2162696 | tf_op jit(solution)/shard_map/ppermute | solution.py:477
  43.2 29.1 %all-to-all-start = ((bf16[32,88,128]{2,1,0:T(8,128)(2,1)}), bf16[32,88,128]{2,1,0:T(8,128)(2,1)S(1)}, u32[]{:S(2)}, u32[]{:S(2)}) async-start(bf16[32,88,128]{2,1,0:T(8,128)(2,1)} %bitcast), calls=%async_computation | async-start | bytes 1441792 | tf_op jit(solution)/shard_map/all_to_all | solution.py:481
  72.2 25.9 %copy-start.7 = (s32[4,64]{1,0:T(4,128)S(1)}, s32[4,64]{1,0:T(4,128)}, u32[]{:S(2)}) copy-start(s32[4,64]{1,0:T(4,128)} %refs_6_.7) | copy-start | bytes 3076
  73.2 22.8 %all-to-all-start.1 = ((bf16[32,88,128]{2,1,0:T(8,128)(2,1)}), bf16[32,88,128]{2,1,0:T(8,128)(2,1)S(1)}, u32[]{:S(2)}, u32[]{:S(2)}) async-start(bf16[32,88,128]{2,1,0:T(8,128)(2,1)} %bitcast.2), calls=%async_computation.1 | async-start | bytes 1441792 | tf_op jit(solution)/shard_map/all_to_all | solution.py:481
  77.1 5.7 %collective-permute-start.9 = (bf16[64,128]{1,0:T(8,128)(2,1)S(1)}, bf16[64,128]{1,0:T(8,128)(2,1)S(1)}, u32[]{:S(2)}, u32[]{:S(2)}) collective-permute-start(bf16[64,128]{1,0:T(8,128)(2,1)S(1)} %get-tuple-element.63.after_ref), channel_id=1, source_target_pairs={{0,1},{1,0},{2,3},{3,2},{4,5},{5,4},{6,7},{7,6},{8,9},{9,8},{10,11... | collective-permute-start | bytes 49160 | tf_op jit(solution)/shard_map/ppermute | solution.py:23
  77.4 5.4 %collective-permute-start.10 = (bf16[64,128]{1,0:T(8,128)(2,1)S(1)}, bf16[64,128]{1,0:T(8,128)(2,1)S(1)}, u32[]{:S(2)}, u32[]{:S(2)}) collective-permute-start(bf16[64,128]{1,0:T(8,128)(2,1)S(1)} %get-tuple-element.64), channel_id=1, source_target_pairs={{1,2},{2,1},{3,4},{4,3},{5,6},{6,5},{7,8},{8,7},{9,10},{10,9},{11,... | collective-permute-start | bytes 49160 | tf_op jit(solution)/shard_map/ppermute | solution.py:23
  80.8 3.6 %collective-permute-start.11 = (bf16[64,128]{1,0:T(8,128)(2,1)S(1)}, bf16[64,128]{1,0:T(8,128)(2,1)S(1)}, u32[]{:S(2)}, u32[]{:S(2)}) collective-permute-start(bf16[64,128]{1,0:T(8,128)(2,1)S(1)} %get-tuple-element.65), channel_id=1, source_target_pairs={{0,2},{1,3},{2,0},{3,1},{4,6},{5,7},{6,4},{7,5},{8,10},{9,11},{10,... | collective-permute-start | bytes 49160 | tf_op jit(solution)/shard_map/ppermute | solution.py:23
  82.1 2.4 %collective-permute-start.12 = (bf16[64,128]{1,0:T(8,128)(2,1)S(1)}, bf16[64,128]{1,0:T(8,128)(2,1)S(1)}, u32[]{:S(2)}, u32[]{:S(2)}) collective-permute-start(bf16[64,128]{1,0:T(8,128)(2,1)S(1)} %get-tuple-element.66), channel_id=1, source_target_pairs={{2,4},{3,5},{4,2},{5,3},{6,8},{7,9},{8,6},{9,7},{10,12},{11,13},{1... | collective-permute-start | bytes 49160 | tf_op jit(solution)/shard_map/ppermute | solution.py:23
  96.1 3.2 %collective-permute-start.13 = (bf16[2816,128]{1,0:T(8,128)(2,1)S(1)}, bf16[2816,128]{1,0:T(8,128)(2,1)S(1)}, u32[]{:S(2)}, u32[]{:S(2)}) collective-permute-start(bf16[2816,128]{1,0:T(8,128)(2,1)S(1)} %bitcast.6), channel_id=1, source_target_pairs={{0,1},{1,0},{2,3},{3,2},{4,5},{5,4},{6,7},{7,6},{8,9},{9,8},{10,11... | collective-permute-start | bytes 2162696 | tf_op jit(solution)/shard_map/ppermute | solution.py:477

commit v10 on v9

--- a/solution.py
+++ b/solution.py
@@ -205,10 +205,7 @@
     features_ref, map_ref, weight_ref, child_ref, early_ref = refs[slots : slots + 5]
     hidden_ref, pre_ref, stacked_ref = refs[slots + 5 : slots + 8]
     sends = refs[slots + 8 : 2 * slots + 8]
-    table_ref, halo_ref, kernel_ref = refs[2 * slots + 8 : 2 * slots + 11]
-    own_refs, far_refs, col_refs = (
-        refs[2 * slots + 11 + 2 * n : 2 * slots + 13 + 2 * n] for n in range(3)
-    )
+    table_ref, halo_ref, kernel_ref = refs[2 * slots + 8 :]
     voxels = features_ref.shape[0]
     gathers = map_ref.shape[0] - 1
     middle = gathers // 2
@@ -229,52 +226,23 @@
     kernel_ref[middle:gathers] = weight_ref[middle + 1 :]
     kernel_ref[gathers] = weight_ref[middle]
 
-    def build(j, side):
-        for n in range(2):
-            col = code_column(map_ref, offset_of(2 * j + n, middle), voxels, slots * cap)
-            col_refs[side][n] = col
-            col = jnp.abs(col)
-            own_refs[side][n] = one_hot_rows(col, half)
-            lanes = slice(n * half_halo, (n + 1) * half_halo)
-            far_refs[side][:, lanes] = one_hot_rows(col, half_halo, half)
-
-    def use(j, side):
-        far = matmul(far_refs[side][...], halo_ref[...])
-        pair = []
-        for n in range(2):
-            both = matmul(own_refs[side][n], table_ref[...])
-            both = (both + far[:, 2 * n * LANES : 2 * (n + 1) * LANES]).astype(BF16)
-            pair.append(pick_side(col_refs[side][n], both))
-        lanes = pl.ds(pl.multiple_of(2 * j * LANES, 2 * LANES), 2 * LANES)
-        stacked_ref[:, lanes] = jnp.concatenate(pair, axis=1)
-
     begun = early_ref.shape[1] // (2 * LANES)
-    for j in range(begun):
-        cols = [
-            code_column(map_ref, offset_of(2 * j + n, middle), voxels, slots * cap)
-            for n in range(2)
-        ]
+    for j in range(middle):
+        numbers = (2 * j, 2 * j + 1)
+        cols = [code_column(map_ref, offset_of(n, middle), voxels, slots * cap) for n in numbers]
         choosers = [one_hot_rows(jnp.abs(col), half_halo, half) for col in cols]
-        far = matmul(jnp.concatenate(choosers, axis=1), halo_ref[...]).astype(BF16)
-        for n in range(2):
-            picked = pick_side(cols[n], far[:, 2 * n * LANES : 2 * (n + 1) * LANES])
-            lanes = slice((2 * j + n) * LANES, (2 * j + n + 1) * LANES)
-            stacked_ref[:, lanes] = early_ref[:, lanes] + picked
-
-    def step(i, carry):
-        for side in range(2):
-            j = begun + 2 * i + side
-            use(j, side)
-            build(j + 1, 1 - side)
-        return carry
-
-    left = middle - begun
-    build(begun, 0)
-    lax.fori_loop(0, (left - 1) // 2, step, 0)
-    if left % 2 == 0:
-        use(middle - 2, 0)
-        build(middle - 1, 1)
-    use(middle - 1, 1 - left % 2)
+        far = matmul(jnp.concatenate(choosers, axis=1), halo_ref[...])
+        for n in numbers:
+            col = cols[n % 2]
+            both = far[:, 2 * (n % 2) * LANES : 2 * (n % 2 + 1) * LANES]
+            lanes = slice(n * LANES, (n + 1) * LANES)
+            if j < begun:
+                picked = pick_side(col, both.astype(BF16)) + early_ref[:, lanes]
+            else:
+                own = matmul(one_hot_rows(jnp.abs(col), half), table_ref[...])
+                picked = pick_side(col, (both + own).astype(BF16))
+            stacked_ref[:, lanes] = picked
+
     stacked_ref[:, gathers * LANES :] = features
     pre = matmul(stacked_ref[...], kernel_ref[...].reshape(-1, LANES))
     pre_ref[...] = pre
@@ -288,7 +256,8 @@
 def gradient_kernel(slots, *refs):
     received = refs[:slots]
     stacked_ref, pre_ref, child_ref, back_ref = refs[slots : slots + 4]
-    hgrad_ref, pgrad_ref, cgrad_ref = refs[slots + 4 :]
+    hidden_ref, child_map_ref, out_grad_ref = refs[slots + 4 : slots + 7]
+    hgrad_ref, pgrad_ref, cgrad_ref, early_ref, upstream_t_ref = refs[slots + 7 :]
     cap2 = child_ref.shape[1]
     cap = received[0].shape[0] - cap2
     kernel_count = cgrad_ref.shape[0] // LANES
@@ -305,6 +274,15 @@
     for n, k in enumerate(order):
         block = jnp.transpose(terms[:, n * LANES : (n + 1) * LANES])
         cgrad_ref[k * LANES : (k + 1) * LANES, :] = block.astype(BF16)
+    voxels, parents = hidden_ref.shape[0], out_grad_ref.shape[0]
+    half = voxels // 2
+    hidden = hidden_ref[...]
+    table = jnp.concatenate([hidden[0:half], hidden[half:]], axis=1)
+    for o in range(child_map_ref.shape[0]):
+        col = code_column(child_map_ref, o, voxels, slots * cap2)
+        both = matmul(one_hot_rows(jnp.abs(col), half), table).astype(BF16)
+        early_ref[:, o * LANES : (o + 1) * LANES] = pick_side(col, both)
+    upstream_t_ref[...] = jnp.transpose(out_grad_ref[...].astype(F32)).astype(BF16)
 
 
 def spread_kernel(slots, pgrad_ref, map_ref, weight_ref, after_ref, back_ref, *sends):
@@ -353,33 +331,25 @@
     return pl.multiple_of(core * rows, 16), pl.multiple_of((1 - core) * rows, 16)
 
 
-def down_kernel(slots, *refs):
+def down_kernel(slots, voxels, *refs):
     received = refs[:slots]
-    (hidden_ref, map_ref, down_ref, out_grad_ref, cgrad_ref) = refs[slots : slots + 5]
-    coarse_ref, terms_ref, send_ref, table_ref = refs[slots + 5 :]
-    voxels = hidden_ref.shape[0]
+    (early_ref, map_ref, down_ref, upstream_t_ref, cgrad_ref) = refs[slots : slots + 5]
+    coarse_ref, terms_ref, send_ref = refs[slots + 5 :]
     cap2 = received[0].shape[0]
-    half, half_halo = voxels // 2, slots * cap2 // 2
+    octants, parents = map_ref.shape
     blocks = to_slots([r[...] for r in received], False)
-    table_ref[0:half, 0:LANES] = hidden_ref[0:half, :]
-    table_ref[0:half, LANES:] = hidden_ref[half:, :]
-    for s, block in enumerate(blocks):
-        place = half + (s % (slots // 2)) * cap2
-        side = (s // (slots // 2)) * LANES
-        table_ref[place : place + cap2, side : side + LANES] = block
-    padding = table_ref.shape[0] - half - half_halo
-    table_ref[half + half_halo :, :] = jnp.zeros((padding, 2 * LANES), BF16)
-    upstream = out_grad_ref[...]
-    parents = upstream.shape[0]
-    octants = map_ref.shape[0]
-    upstream_t = jnp.transpose(upstream.astype(F32)).astype(BF16)
-    codes = half_codes(map_ref[...], voxels, slots * cap2)
-    col = jnp.concatenate([column(codes[o : o + 1, :]) for o in range(octants)], axis=0)
-    picked = pick_rows(col.astype(BF16), table_ref[...])
-    picked = jnp.concatenate(jnp.split(picked, octants), axis=1)
+    halo = jnp.concatenate(blocks, axis=0)
+    rows = map_ref[...]
+    codes = encode(jnp.where(rows >= voxels, rows - voxels, slots * cap2))
+    picked = []
+    for o in range(octants):
+        chooser = one_hot_rows(column(codes[o : o + 1, :]).astype(BF16), slots * cap2)
+        far = matmul(chooser, halo).astype(BF16)
+        picked.append(far + early_ref[:, o * LANES : (o + 1) * LANES])
+    picked = jnp.concatenate(picked, axis=1)
     row = cgrad_ref.shape[0]
     terms_ref[0:row, :] = cgrad_ref[...]
-    terms = matmul(upstream_t, picked)
+    terms = matmul(upstream_t_ref[...], picked)
     for o in range(octants):
         for start in range(0, terms.shape[0], LANES):
             block = terms[start : start + LANES, o * LANES : (o + 1) * LANES]
@@ -516,7 +486,7 @@
     (early,) = call(
         functools.partial(local_kernel, slots * cap),
         (features, neighbour_map),
-        [((voxels, 8 * channels), BF16)],
+        [((voxels, 12 * channels), BF16)],
         scratch=[pltpu.VMEM((voxels // 2, 2 * channels), BF16)],
         flops=4 * giga,
     )
@@ -533,33 +503,31 @@
             pltpu.VMEM((voxels // 2, 2 * channels), BF16),
             pltpu.VMEM((slots * cap, 4 * channels), BF16),
             pltpu.VMEM(conv_weight.shape, BF16),
-        ]
-        + [pltpu.VMEM((2, voxels, voxels // 2), BF16)] * 2
-        + [pltpu.VMEM((voxels, slots * cap), BF16)] * 2
-        + [pltpu.VMEM((2, voxels, LANES), BF16)] * 2,
+        ],
         limit=32,
         flops=12 * giga,
     )
-    hidden_grad, pre_grad, conv_terms = call(
+    hidden_grad, pre_grad, conv_terms, early_h, out_grad_t = call(
         functools.partial(gradient_kernel, slots),
-        (*received, stacked, pre_act, child_rows, back_h),
+        (*received, stacked, pre_act, child_rows, back_h, hidden, child_map, out_grad),
         [
             ((voxels, channels), F32),
             ((voxels, channels), BF16),
             ((conv_rows, channels), BF16),
+            ((parents, octants * channels), BF16),
+            ((coarse_channels, parents), BF16),
         ],
         flops=3 * giga,
     )
     received_h = swaps(leaving, (1, 3, 2, 0))
     coarse, terms, leaving_terms = call(
-        functools.partial(down_kernel, slots),
-        (*received_h, hidden, child_map, down_weight, out_grad, conv_terms),
+        functools.partial(down_kernel, slots, voxels),
+        (*received_h, early_h, child_map, down_weight, out_grad_t, conv_terms),
         [
             ((parents, coarse_channels), BF16),
             ((2 * half_rows, LANES), BF16),
             ((half_rows, LANES), BF16),
         ],
-        scratch=[pltpu.VMEM((-(-(voxels + slots * cap2) // 256) * 128, 2 * channels), BF16)],
         flops=2 * giga,
     )
     (pair_terms,) = call(
@@ -585,13 +553,14 @@
         in_hbm=(1,),
     )
     summed, *returning = lax.optimization_barrier((summed, *spread[1:]))
-    mine, *returned = lax.optimization_barrier((exchange(summed), *swaps(returning, (3, 1, 0, 2))))
+    returned = swaps(returning, (0, 1, 2, 3))
     (input_grad,) = call(
         functools.partial(tail_kernel, slots),
         (*returned, hidden_grad, spread[0], halo_rows),
         [((voxels, channels), F32)],
         flops=giga,
     )
+    mine, input_grad = lax.optimization_barrier((exchange(summed), input_grad))
     other = swap_cores(mine, devices)
     gradients = ()
     for own, block in ((True, mine), (False, other)):

time: 101 us -> 96.5 us (0.955)
  Pallas kernels: 44.6 us -> 41.7 us
  starting transfers between devices: 35.6 us -> 34.1 us
    pallas_call x11, Pallas kernels: 44.6 us -> 41.7 us  [call(): pl.pallas_call(kernel, out_shape=[jax.ShapeDtypeStruct(s, d) for s, d in...]
    all_to_all x2, waiting for transfers between devices: 15.6 us -> 14.5 us  [exchange(): return lax.all_to_all(value, 'shard', 0, 0, tiled=True)]
    ppermute x12, starting transfers between devices: 20.9 us -> 19.8 us  [swaps(): moved[step] = lax.ppermute(by_step[step], 'shard', pairs)]
  transfers between devices with their start and end apart: 16 -> 16, of which waited for: 5 -> 6; matrix products, arithmetic and copies ran while one was open for 0% -> 0% of each run, Pallas kernels for 21% -> 24%
where the time goes in v10:
time: 96.5 us; the launch traced here: 95.8 us
  Pallas kernels  41.7 us (43%)
  starting transfers between devices  34.1 us (35%)
  waiting for transfers between devices  18.8 us (19%)
  between operations  1.11 us (1%)
    pallas_call x11, Pallas kernels, call(): pl.pallas_call(kernel, out_shape=[jax.ShapeDtypeStruct(s, d) for s, d in...  41.7 us
    ppermute x12, starting transfers between devices, swaps(): moved[step] = lax.ppermute(by_step[step], 'shard', pairs)  19.8 us
    all_to_all x2, waiting for transfers between devices, exchange(): return lax.all_to_all(value, 'shard', 0, 0, tiled=True)  14.5 us
    all_to_all x2, starting transfers between devices, exchange(): return lax.all_to_all(value, 'shard', 0, 0, tiled=True)  13.6 us
    ppermute x2, waiting for transfers between devices, swap_cores(): lax.ppermute(value, 'shard', [(i, i + 1 - 2 * (i % 2)) for i in range(dev...  2.64 us
  transfers between devices with their start and end apart: 16, of which 6 were waited for; matrix products, arithmetic and copies ran while one was open for 0% of the time, Pallas kernels for 24%

profile of v10, /device:TPU:1, one launch (start us, length us, event | category | flops | bytes accessed | tf_op | source)
XLA Modules:
  0.0 95.8 jit_solution(5041445916284199040)
XLA Ops:
  0.6 0.0 copy-start.2
  0.6 0.0 copy-start.4
  0.7 4.0 %shard_map.111 = (bf16[96,128]{1,0:T(8,128)(2,1)}, bf16[96,128]{1,0:T(8,128)(2,1)}, bf16[96,128]{1,0:T(8,128)(2,1)}, bf16[96,128]{1,0:T(8,128)(2,1)}, f32[1024,128]{1,0:T(8,128)}) custom-call(bf16[1024,128]{1,0:T(8,128)(2,1)} %refs_4_.1, s32[4,64]{1,0:T(4,128)} %refs_6_.7, s32[8,256]{1,0:T(8,128)} %refs_5_.3, bf16[256,256]{1,0:T(8,128)(2,1)} %refs_10_.1, ...), custom_call_target="tpu_custom_call" | custom-call | flops 1000000000 | bytes 4194304 | tf_op jit(solution)/shard_map/pallas_call | solution.py:434
  4.7 0.1 collective-permute-start
  4.8 4.5 %collective-permute-start.1 = (bf16[96,128]{1,0:T(8,128)(2,1)}, bf16[96,128]{1,0:T(8,128)(2,1)S(1)}, u32[]{:S(2)}, u32[]{:S(2)}) collective-permute-start(bf16[96,128]{1,0:T(8,128)(2,1)} %get-tuple-element.41), channel_id=1, source_target_pairs={{1,2},{2,1},{3,4},{4,3},{5,6},{6,5},{7,8},{8,7},{9,10},{10,9},{11,... | collective-permute-start | bytes 73736 | tf_op jit(solution)/shard_map/ppermute | solution.py:23
  9.3 1.3 %collective-permute-start.2 = (bf16[96,128]{1,0:T(8,128)(2,1)}, bf16[96,128]{1,0:T(8,128)(2,1)S(1)}, u32[]{:S(2)}, u32[]{:S(2)}) collective-permute-start(bf16[96,128]{1,0:T(8,128)(2,1)} %get-tuple-element.42), channel_id=1, source_target_pairs={{0,2},{1,3},{2,0},{3,1},{4,6},{5,7},{6,4},{7,5},{8,10},{9,11},{10,... | collective-permute-start | bytes 73736 | tf_op jit(solution)/shard_map/ppermute | solution.py:23
  10.5 0.0 copy-start
  10.5 0.0 copy-start.6
  10.5 0.8 collective-permute-start.3
  11.3 0.0 copy-done.2
  11.3 0.0 copy-done.4
  11.3 3.5 %shard_map.112.refs_8_ = bf16[1024,1536]{1,0:T(8,128)(2,1)S(1)} custom-call(bf16[1024,128]{1,0:T(8,128)(2,1)S(1)} %copy-done.2, s32[27,1024]{1,0:T(8,128)S(1)} %copy-done.4), custom_call_target="tpu_custom_call" | custom-call | flops 4000000000 | bytes 4194304 | tf_op jit(solution)/shard_map/pallas_call | solution.py:434
  14.9 0.0 copy-start.3
  14.9 0.0 copy-start.5
  14.9 0.0 copy-start.8
  14.9 0.0 collective-permute-done.refs_0_
  14.9 0.0 collective-permute-done.1.refs_1_
  14.9 0.0 collective-permute-done.2.refs_2_
  14.9 0.0 collective-permute-done.3.refs_3_
  14.9 0.0 copy-done
  14.9 0.0 copy-done.6
  15.0 9.9 %shard_map.113 = (bf16[1024,128]{1,0:T(8,128)(2,1)S(1)}, f32[1024,128]{1,0:T(8,128)S(1)}, bf16[1024,3456]{1,0:T(8,128)(2,1)S(1)}, bf16[32,128]{1,0:T(8,128)(2,1)...) custom-call(bf16[96,128]{1,0:T(8,128)(2,1)S(1)} %collective-permute-done.refs_0_, ...), custom_call_target="tpu_custom_call" | custom-call | flops 12000000000 | bytes 4194304 | tf_op jit(solution)/shard_map/pallas_call | solution.py:434
  24.8 0.3 collective-permute-start.4
  25.1 5.9 %collective-permute-start.5 = (bf16[32,128]{1,0:T(8,128)(2,1)S(1)}, bf16[32,128]{1,0:T(8,128)(2,1)S(1)}, u32[]{:S(2)}, u32[]{:S(2)}) collective-permute-start(bf16[32,128]{1,0:T(8,128)(2,1)S(1)} %get-tuple-element.45), channel_id=1, source_target_pairs={{1,2},{2,1},{3,4},{4,3},{5,6},{6,5},{7,8},{8,7},{9,10},{10,9},{11,... | collective-permute-start | bytes 24584 | tf_op jit(solution)/shard_map/ppermute | solution.py:23
  31.1 0.7 collective-permute-start.6
  31.7 0.6 collective-permute-start.7
  32.4 0.0 copy-done.3
  32.4 0.0 copy-done.5
  32.4 0.0 copy-done.8
  32.4 0.0 copy-start.1
  32.4 2.1 %shard_map.114 = (f32[1024,128]{1,0:T(8,128)S(1)}, bf16[1024,128]{1,0:T(8,128)(2,1)S(1)}, bf16[3456,128]{1,0:T(8,128)(2,1)S(1)}, bf16[256,1024]{1,0:T(8,128)(2,1)S(1)}, bf16[256,256]{1,0:T(8,128)(2,1)S(1)}) custom-call(bf16[96,128]{1,0:T(8,128)(2,1)S(1)} %collective-permute-done.refs_0_, bf16[96,128]{1,0:T(8,128)(2,1)S(1)} %collective-permute-done.1.refs_1_, ...), custom_call_target="tpu_custom_call" | custom-call | flops 3000000000 | bytes 4194304 | tf_op jit(solution)/shard_map/pallas_call | solution.py:434
  34.5 0.0 collective-permute-done.4.refs_0_
  34.5 0.0 collective-permute-done.5.refs_1_
  34.6 0.0 collective-permute-done.6.refs_2_
  34.6 0.0 collective-permute-done.7.refs_3_
  34.6 0.0 copy-done.1
  34.6 1.4 %shard_map.115 = (bf16[256,256]{1,0:T(8,128)(2,1)}, bf16[5632,128]{1,0:T(8,128)(2,1)S(1)}, bf16[2816,128]{1,0:T(8,128)(2,1)S(1)}) custom-call(bf16[32,128]{1,0:T(8,128)(2,1)S(1)} %collective-permute-done.4.refs_0_, bf16[32,128]{1,0:T(8,128)(2,1)S(1)} %collective-permute-done.5.refs_1_, bf16[32,128]{1,0:T(8,128)(2,1)S(1)} %collective-permute-done.6.refs_2_, ...), custom_call_target="tpu_custom_call" | custom-call | flops 2000000000 | bytes 4194304 | tf_op jit(solution)/shard_map/pallas_call | solution.py:434
  36.0 0.0 collective-permute-start.8
  36.0 2.2 %collective-permute-done.8.other_ref = bf16[2816,128]{1,0:T(8,128)(2,1)S(1)} collective-permute-done((bf16[2816,128]{1,0:T(8,128)(2,1)S(1)}, bf16[2816,128]{1,0:T(8,128)(2,1)S(1)}, u32[]{:S(2)}, u32[]{:S(2)}) %collective-permute-start.8) | collective-permute-done | bytes 720928 | tf_op jit(solution)/shard_map/ppermute | solution.py:447
  38.2 1.0 %shard_map.116.after_ref = bf16[2816,128]{1,0:T(8,128)(2,1)} custom-call(bf16[5632,128]{1,0:T(8,128)(2,1)S(1)} %get-tuple-element.56.terms_ref, bf16[2816,128]{1,0:T(8,128)(2,1)S(1)} %collective-permute-done.8.other_ref), custom_call_target="tpu_custom_call" | custom-call | flops 1000000 | bytes 4194304 | tf_op jit(solution)/shard_map/pallas_call | solution.py:434
  39.2 9.7 %all-to-all-start = ((bf16[32,88,128]{2,1,0:T(8,128)(2,1)}), bf16[32,88,128]{2,1,0:T(8,128)(2,1)S(1)}, u32[]{:S(2)}, u32[]{:S(2)}) async-start(bf16[32,88,128]{2,1,0:T(8,128)(2,1)} %bitcast), calls=%async_computation | async-start | bytes 1441792 | tf_op jit(solution)/shard_map/all_to_all | solution.py:451
  48.9 14.9 %shard_map.117 = (f32[1024,128]{1,0:T(8,128)S(1)}, bf16[64,128]{1,0:T(8,128)(2,1)S(1)}, bf16[64,128]{1,0:T(8,128)(2,1)S(1)}, bf16[64,128]{1,0:T(8,128)(2,1)S(1)}, bf16[64,128]{1,0:T(8,128)(2,1)S(1)}) custom-call(bf16[1024,128]{1,0:T(8,128)(2,1)S(1)} %get-tuple-element.58.pgrad_ref, s32[27,1024]{1,0:T(8,128)S(1)} %copy-done.4, ...), custom_call_target="tpu_custom_call" | custom-call | flops 20000000000 | bytes 4194304 | tf_op jit(solution)/shard_map/pallas_call | solution.py:434
  63.9 0.0 copy-start.7
  63.9 4.0 %all-to-all-done = bf16[32,88,128]{2,1,0:T(8,128)(2,1)S(1)} async-done(((bf16[32,88,128]{2,1,0:T(8,128)(2,1)}), bf16[32,88,128]{2,1,0:T(8,128)(2,1)S(1)}, u32[]{:S(2)}, u32[]{:S(2)}) %all-to-all-start) | async-done | bytes 720928 | tf_op jit(solution)/shard_map/all_to_all | solution.py:451
  67.9 1.0 %shard_map.118 = bf16[2816,128]{1,0:T(8,128)(2,1)} custom-call(bf16[2816,128]{1,0:T(8,128)(2,1)S(1)} %bitcast.8, bf16[64,128]{1,0:T(8,128)(2,1)S(1)} %get-tuple-element.64.after_ref), custom_call_target="tpu_custom_call" | custom-call | flops 1000000 | bytes 4194304 | tf_op jit(solution)/shard_map/pallas_call | solution.py:434
  68.9 3.9 %all-to-all-start.1 = ((bf16[32,88,128]{2,1,0:T(8,128)(2,1)}), bf16[32,88,128]{2,1,0:T(8,128)(2,1)S(1)}, u32[]{:S(2)}, u32[]{:S(2)}) async-start(bf16[32,88,128]{2,1,0:T(8,128)(2,1)} %bitcast.2), calls=%async_computation.1 | async-start | bytes 1441792 | tf_op jit(solution)/shard_map/all_to_all | solution.py:451
  72.7 0.3 collective-permute-start.9
  73.1 3.4 %collective-permute-start.10 = (bf16[64,128]{1,0:T(8,128)(2,1)S(1)}, bf16[64,128]{1,0:T(8,128)(2,1)S(1)}, u32[]{:S(2)}, u32[]{:S(2)}) collective-permute-start(bf16[64,128]{1,0:T(8,128)(2,1)S(1)} %get-tuple-element.65), channel_id=1, source_target_pairs={{1,2},{2,1},{3,4},{4,3},{5,6},{6,5},{7,8},{8,7},{9,10},{10,9},{11,... | collective-permute-start | bytes 49160 | tf_op jit(solution)/shard_map/ppermute | solution.py:23
  76.5 1.2 %collective-permute-start.11 = (bf16[64,128]{1,0:T(8,128)(2,1)S(1)}, bf16[64,128]{1,0:T(8,128)(2,1)S(1)}, u32[]{:S(2)}, u32[]{:S(2)}) collective-permute-start(bf16[64,128]{1,0:T(8,128)(2,1)S(1)} %get-tuple-element.66), channel_id=1, source_target_pairs={{0,2},{1,3},{2,0},{3,1},{4,6},{5,7},{6,4},{7,5},{8,10},{9,11},{10,... | collective-permute-start | bytes 49160 | tf_op jit(solution)/shard_map/ppermute | solution.py:23
  77.7 0.7 collective-permute-start.12
  78.4 0.0 collective-permute-done.9.refs_0_
  78.4 0.1 collective-permute-done.10.refs_1_
  78.5 1.6 %collective-permute-done.11.refs_2_ = bf16[64,128]{1,0:T(8,128)(2,1)S(1)} collective-permute-done((bf16[64,128]{1,0:T(8,128)(2,1)S(1)}, bf16[64,128]{1,0:T(8,128)(2,1)S(1)}, u32[]{:S(2)}, u32[]{:S(2)}) %collective-permute-start.11) | collective-permute-done | bytes 16416 | tf_op jit(solution)/shard_map/ppermute | solution.py:23
  80.1 0.0 collective-permute-done.12.refs_3_
  80.1 0.0 copy-done.7
  80.1 1.2 %shard_map.119 = f32[1024,128]{1,0:T(8,128)} custom-call(bf16[64,128]{1,0:T(8,128)(2,1)S(1)} %collective-permute-done.9.refs_0_, bf16[64,128]{1,0:T(8,128)(2,1)S(1)} %collective-permute-done.10.refs_1_, bf16[64,128]{1,0:T(8,128)(2,1)S(1)} %collective-permute-done.11.refs_2_, bf16[64,128]{1,0:T(8,128)(2,1)S(1)} %collective-permute-done.12.refs_3_, ...), custom_call_target="tpu_custom_call" | custom-call | flops 1000000000 | bytes 4194304 | tf_op jit(solution)/shard_map/pallas_call | solution.py:434
  81.3 10.4 %all-to-all-done.1 = bf16[32,88,128]{2,1,0:T(8,128)(2,1)S(1)} async-done(((bf16[32,88,128]{2,1,0:T(8,128)(2,1)}), bf16[32,88,128]{2,1,0:T(8,128)(2,1)S(1)}, u32[]{:S(2)}, u32[]{:S(2)}) %all-to-all-start.1) | async-done | bytes 720928 | tf_op jit(solution)/shard_map/all_to_all | solution.py:451
  91.7 0.7 collective-permute-start.13
  92.4 1.4 %shard_map.120 = (f32[3456,128]{1,0:T(8,128)}, f32[1024,256]{1,0:T(8,128)}) custom-call(bf16[2816,128]{1,0:T(8,128)(2,1)S(1)} %bitcast.7), custom_call_target="tpu_custom_call" | custom-call | flops 1000000 | bytes 4194304 | tf_op jit(solution)/shard_map/pallas_call | solution.py:434
  93.8 0.4 collective-permute-done.13.refs_0_
  94.2 1.4 %shard_map.121 = (f32[3456,128]{1,0:T(8,128)}, f32[1024,256]{1,0:T(8,128)}) custom-call(bf16[2816,128]{1,0:T(8,128)(2,1)S(1)} %collective-permute-done.13.refs_0_, f32[3456,128]{1,0:T(8,128)} %get-tuple-element.72.refs_1_, f32[1024,256]{1,0:T(8,128)} %get-tuple-element.73.refs_2_), custom_call_target="tpu_custom_call", output_to_operand_aliasing={{0}: (1, {}), {1}: (2, {})} | custom-call | flops 1000000 | bytes 4194304 | tf_op jit(solution)/shard_map/pallas_call | solution.py:434
Async XLA Ops:
  0.6 10.7 %copy-start.2 = (bf16[1024,128]{1,0:T(8,128)(2,1)S(1)}, bf16[1024,128]{1,0:T(8,128)(2,1)}, u32[]{:S(2)}) copy-start(bf16[1024,128]{1,0:T(8,128)(2,1)} %refs_4_.1) | copy-start | bytes 786436
  0.6 10.7 %copy-start.4 = (s32[27,1024]{1,0:T(8,128)S(1)}, s32[27,1024]{1,0:T(8,128)}, u32[]{:S(2)}) copy-start(s32[27,1024]{1,0:T(8,128)} %map_ref.3) | copy-start | bytes 331780
  4.7 10.2 %collective-permute-start = (bf16[96,128]{1,0:T(8,128)(2,1)}, bf16[96,128]{1,0:T(8,128)(2,1)S(1)}, u32[]{:S(2)}, u32[]{:S(2)}) collective-permute-start(bf16[96,128]{1,0:T(8,128)(2,1)} %get-tuple-element.40), channel_id=1, source_target_pairs={{0,1},{1,0},{2,3},{3,2},{4,5},{5,4},{6,7},{7,6},{8,9},{9,8},{10,11... | collective-permute-start | bytes 73736 | tf_op jit(solution)/shard_map/ppermute | solution.py:23
  4.8 10.1 %collective-permute-start.1 = (bf16[96,128]{1,0:T(8,128)(2,1)}, bf16[96,128]{1,0:T(8,128)(2,1)S(1)}, u32[]{:S(2)}, u32[]{:S(2)}) collective-permute-start(bf16[96,128]{1,0:T(8,128)(2,1)} %get-tuple-element.41), channel_id=1, source_target_pairs={{1,2},{2,1},{3,4},{4,3},{5,6},{6,5},{7,8},{8,7},{9,10},{10,9},{11,... | collective-permute-start | bytes 73736 | tf_op jit(solution)/shard_map/ppermute | solution.py:23
  9.3 5.7 %collective-permute-start.2 = (bf16[96,128]{1,0:T(8,128)(2,1)}, bf16[96,128]{1,0:T(8,128)(2,1)S(1)}, u32[]{:S(2)}, u32[]{:S(2)}) collective-permute-start(bf16[96,128]{1,0:T(8,128)(2,1)} %get-tuple-element.42), channel_id=1, source_target_pairs={{0,2},{1,3},{2,0},{3,1},{4,6},{5,7},{6,4},{7,5},{8,10},{9,11},{10,... | collective-permute-start | bytes 73736 | tf_op jit(solution)/shard_map/ppermute | solution.py:23
  10.5 4.4 %copy-start = (bf16[27,128,128]{2,1,0:T(8,128)(2,1)S(1)}, bf16[27,128,128]{2,1,0:T(8,128)(2,1)}, u32[]{:S(2)}) copy-start(bf16[27,128,128]{2,1,0:T(8,128)(2,1)} %weight_ref.1) | copy-start | bytes 2654212
  10.5 4.4 %copy-start.6 = (s32[4,32]{1,0:T(4,128)S(1)}, s32[4,32]{1,0:T(4,128)}, u32[]{:S(2)}) copy-start(s32[4,32]{1,0:T(4,128)} %refs_6_.5) | copy-start | bytes 1540
  10.5 4.4 %collective-permute-start.3 = (bf16[96,128]{1,0:T(8,128)(2,1)}, bf16[96,128]{1,0:T(8,128)(2,1)S(1)}, u32[]{:S(2)}, u32[]{:S(2)}) collective-permute-start(bf16[96,128]{1,0:T(8,128)(2,1)} %get-tuple-element.43), channel_id=1, source_target_pairs={{2,4},{3,5},{4,2},{5,3},{6,8},{7,9},{8,6},{9,7},{10,12},{11,13},{1... | collective-permute-start | bytes 73736 | tf_op jit(solution)/shard_map/ppermute | solution.py:23
  14.9 17.5 %copy-start.3 = (bf16[256,256]{1,0:T(8,128)(2,1)S(1)}, bf16[256,256]{1,0:T(8,128)(2,1)}, u32[]{:S(2)}) copy-start(bf16[256,256]{1,0:T(8,128)(2,1)} %refs_10_.1) | copy-start | bytes 393220
  14.9 17.5 %copy-start.5 = (s32[8,256]{1,0:T(8,128)S(1)}, s32[8,256]{1,0:T(8,128)}, u32[]{:S(2)}) copy-start(s32[8,256]{1,0:T(8,128)} %refs_5_.3) | copy-start | bytes 24580
  14.9 17.5 %copy-start.8 = (f32[1024,128]{1,0:T(8,128)S(1)}, f32[1024,128]{1,0:T(8,128)}, u32[]{:S(2)}) copy-start(f32[1024,128]{1,0:T(8,128)} %get-tuple-element.50.refs_7_) | copy-start | bytes 1572868
  24.8 9.7 %collective-permute-start.4 = (bf16[32,128]{1,0:T(8,128)(2,1)S(1)}, bf16[32,128]{1,0:T(8,128)(2,1)S(1)}, u32[]{:S(2)}, u32[]{:S(2)}) collective-permute-start(bf16[32,128]{1,0:T(8,128)(2,1)S(1)} %get-tuple-element.44), channel_id=1, source_target_pairs={{0,1},{1,0},{2,3},{3,2},{4,5},{5,4},{6,7},{7,6},{8,9},{9,8},{10,11... | collective-permute-start | bytes 24584 | tf_op jit(solution)/shard_map/ppermute | solution.py:23
  25.1 9.4 %collective-permute-start.5 = (bf16[32,128]{1,0:T(8,128)(2,1)S(1)}, bf16[32,128]{1,0:T(8,128)(2,1)S(1)}, u32[]{:S(2)}, u32[]{:S(2)}) collective-permute-start(bf16[32,128]{1,0:T(8,128)(2,1)S(1)} %get-tuple-element.45), channel_id=1, source_target_pairs={{1,2},{2,1},{3,4},{4,3},{5,6},{6,5},{7,8},{8,7},{9,10},{10,9},{11,... | collective-permute-start | bytes 24584 | tf_op jit(solution)/shard_map/ppermute | solution.py:23
  31.1 3.5 %collective-permute-start.6 = (bf16[32,128]{1,0:T(8,128)(2,1)S(1)}, bf16[32,128]{1,0:T(8,128)(2,1)S(1)}, u32[]{:S(2)}, u32[]{:S(2)}) collective-permute-start(bf16[32,128]{1,0:T(8,128)(2,1)S(1)} %get-tuple-element.46), channel_id=1, source_target_pairs={{0,2},{1,3},{2,0},{3,1},{4,6},{5,7},{6,4},{7,5},{8,10},{9,11},{10,... | collective-permute-start | bytes 24584 | tf_op jit(solution)/shard_map/ppermute | solution.py:23
  31.7 2.8 %collective-permute-start.7 = (bf16[32,128]{1,0:T(8,128)(2,1)S(1)}, bf16[32,128]{1,0:T(8,128)(2,1)S(1)}, u32[]{:S(2)}, u32[]{:S(2)}) collective-permute-start(bf16[32,128]{1,0:T(8,128)(2,1)S(1)} %get-tuple-element.47), channel_id=1, source_target_pairs={{2,4},{3,5},{4,2},{5,3},{6,8},{7,9},{8,6},{9,7},{10,12},{11,13},{1... | collective-permute-start | bytes 24584 | tf_op jit(solution)/shard_map/ppermute | solution.py:23
  32.4 2.1 %copy-start.1 = (bf16[8,128,256]{2,1,0:T(8,128)(2,1)S(1)}, bf16[8,128,256]{2,1,0:T(8,128)(2,1)}, u32[]{:S(2)}) copy-start(bf16[8,128,256]{2,1,0:T(8,128)(2,1)} %refs_6_.6) | copy-start | bytes 1572868
  36.0 2.2 %collective-permute-start.8 = (bf16[2816,128]{1,0:T(8,128)(2,1)S(1)}, bf16[2816,128]{1,0:T(8,128)(2,1)S(1)}, u32[]{:S(2)}, u32[]{:S(2)}) collective-permute-start(bf16[2816,128]{1,0:T(8,128)(2,1)S(1)} %get-tuple-element.57), channel_id=1, source_target_pairs={{0,1},{1,0},{2,3},{3,2},{4,5},{5,4},{6,7},{7,6},{8,9},{9,8},{10,11... | collective-permute-start | bytes 2162696 | tf_op jit(solution)/shard_map/ppermute | solution.py:447
  39.2 28.7 %all-to-all-start = ((bf16[32,88,128]{2,1,0:T(8,128)(2,1)}), bf16[32,88,128]{2,1,0:T(8,128)(2,1)S(1)}, u32[]{:S(2)}, u32[]{:S(2)}) async-start(bf16[32,88,128]{2,1,0:T(8,128)(2,1)} %bitcast), calls=%async_computation | async-start | bytes 1441792 | tf_op jit(solution)/shard_map/all_to_all | solution.py:451
  63.9 16.2 %copy-start.7 = (s32[4,64]{1,0:T(4,128)S(1)}, s32[4,64]{1,0:T(4,128)}, u32[]{:S(2)}) copy-start(s32[4,64]{1,0:T(4,128)} %refs_6_.7) | copy-start | bytes 3076
  68.9 22.8 %all-to-all-start.1 = ((bf16[32,88,128]{2,1,0:T(8,128)(2,1)}), bf16[32,88,128]{2,1,0:T(8,128)(2,1)S(1)}, u32[]{:S(2)}, u32[]{:S(2)}) async-start(bf16[32,88,128]{2,1,0:T(8,128)(2,1)} %bitcast.2), calls=%async_computation.1 | async-start | bytes 1441792 | tf_op jit(solution)/shard_map/all_to_all | solution.py:451
  72.7 5.7 %collective-permute-start.9 = (bf16[64,128]{1,0:T(8,128)(2,1)S(1)}, bf16[64,128]{1,0:T(8,128)(2,1)S(1)}, u32[]{:S(2)}, u32[]{:S(2)}) collective-permute-start(bf16[64,128]{1,0:T(8,128)(2,1)S(1)} %get-tuple-element.64.after_ref), channel_id=1, source_target_pairs={{0,1},{1,0},{2,3},{3,2},{4,5},{5,4},{6,7},{7,6},{8,9},{9,8},{10,11... | collective-permute-start | bytes 49160 | tf_op jit(solution)/shard_map/ppermute | solution.py:23
  73.1 5.4 %collective-permute-start.10 = (bf16[64,128]{1,0:T(8,128)(2,1)S(1)}, bf16[64,128]{1,0:T(8,128)(2,1)S(1)}, u32[]{:S(2)}, u32[]{:S(2)}) collective-permute-start(bf16[64,128]{1,0:T(8,128)(2,1)S(1)} %get-tuple-element.65), channel_id=1, source_target_pairs={{1,2},{2,1},{3,4},{4,3},{5,6},{6,5},{7,8},{8,7},{9,10},{10,9},{11,... | collective-permute-start | bytes 49160 | tf_op jit(solution)/shard_map/ppermute | solution.py:23
  76.5 3.6 %collective-permute-start.11 = (bf16[64,128]{1,0:T(8,128)(2,1)S(1)}, bf16[64,128]{1,0:T(8,128)(2,1)S(1)}, u32[]{:S(2)}, u32[]{:S(2)}) collective-permute-start(bf16[64,128]{1,0:T(8,128)(2,1)S(1)} %get-tuple-element.66), channel_id=1, source_target_pairs={{0,2},{1,3},{2,0},{3,1},{4,6},{5,7},{6,4},{7,5},{8,10},{9,11},{10,... | collective-permute-start | bytes 49160 | tf_op jit(solution)/shard_map/ppermute | solution.py:23
  77.7 2.4 %collective-permute-start.12 = (bf16[64,128]{1,0:T(8,128)(2,1)S(1)}, bf16[64,128]{1,0:T(8,128)(2,1)S(1)}, u32[]{:S(2)}, u32[]{:S(2)}) collective-permute-start(bf16[64,128]{1,0:T(8,128)(2,1)S(1)} %get-tuple-element.67), channel_id=1, source_target_pairs={{2,4},{3,5},{4,2},{5,3},{6,8},{7,9},{8,6},{9,7},{10,12},{11,13},{1... | collective-permute-start | bytes 49160 | tf_op jit(solution)/shard_map/ppermute | solution.py:23
  91.7 2.5 %collective-permute-start.13 = (bf16[2816,128]{1,0:T(8,128)(2,1)S(1)}, bf16[2816,128]{1,0:T(8,128)(2,1)S(1)}, u32[]{:S(2)}, u32[]{:S(2)}) collective-permute-start(bf16[2816,128]{1,0:T(8,128)(2,1)S(1)} %bitcast.6), channel_id=1, source_target_pairs={{0,1},{1,0},{2,3},{3,2},{4,5},{5,4},{6,7},{7,6},{8,9},{9,8},{10,11... | collective-permute-start | bytes 2162696 | tf_op jit(solution)/shard_map/ppermute | solution.py:447

commit v11 on v10

--- a/solution.py
+++ b/solution.py
@@ -300,21 +300,21 @@
     acc_ref[0:half, LANES:] = own[half:]
     acc_ref[half:, :] = jnp.zeros((table_rows - half, 2 * LANES), F32)
 
-    def parts(k):
-        codes = half_codes(map_ref[pl.ds(k, 1), :], voxels, slots * cap)
-        terms = matmul_rt(pgrad, weight_ref[k])
-        right = column(codes) < 0.0
-        sides = [jnp.where(right, 0.0, terms), jnp.where(right, terms, 0.0)]
-        chooser = one_hot_columns(jnp.abs(codes).astype(BF16), table_rows)
-        return chooser, jnp.concatenate(sides, axis=1).astype(BF16)
-
-    def step(j, carry):
-        near_chooser, near_terms = parts(j)
-        far_chooser, far_terms = parts(j + middle + 1)
-        acc_ref[...] += matmul(near_chooser, near_terms) + matmul(far_chooser, far_terms)
-        return carry
-
-    lax.fori_loop(0, middle, step, 0)
+    for j in range(middle):
+        numbers = (j, j + middle + 1)
+        kernels = jnp.concatenate([weight_ref[k] for k in numbers], axis=0)
+        terms = matmul_rt(pgrad, kernels).astype(BF16)
+        choosers, sides = [], []
+        for n, k in enumerate(numbers):
+            codes = half_codes(map_ref[k : k + 1, :], voxels, slots * cap).astype(BF16)
+            right = column(codes) < jnp.zeros((voxels, LANES), BF16)
+            mine = terms[:, n * LANES : (n + 1) * LANES]
+            none = jnp.zeros(mine.shape, BF16)
+            pair = [jnp.where(right, none, mine), jnp.where(right, mine, none)]
+            sides.append(jnp.concatenate(pair, axis=1))
+            choosers.append(one_hot_columns(jnp.abs(codes), table_rows))
+        acc_ref[...] += matmul(choosers[0], sides[0]) + matmul(choosers[1], sides[1])
+
     back_ref[0:half, :] = acc_ref[0:half, 0:LANES]
     back_ref[half:, :] = acc_ref[0:half, LANES:]
     blocks = []
@@ -367,57 +367,40 @@
     out_ref[...] = (mine + other_ref[...].astype(F32)).astype(BF16)
 
 
-def sum_kernel(devices, scale, parts_ref, after_ref, out_ref):
+def sum_kernel(devices, scale, parts_ref, out_ref):
     rows = parts_ref.shape[0] // devices
     for core in range(2):
-        mine = range(core, devices, 2)
         total = jnp.zeros((rows, LANES), F32)
-        for d in mine:
+        for d in range(core, devices, 2):
             total = total + parts_ref[d * rows : (d + 1) * rows, :].astype(F32)
-        total = (total * scale).astype(BF16)
-        for d in mine:
-            out_ref[d * rows : (d + 1) * rows, :] = total
-
-
-def final_kernel(own, *refs):
-    block_ref, conv_hbm, down_hbm = refs[0], *refs[-5:-3]
-    conv_ref, down_ref, sems = refs[-3:]
-    rows = block_ref.shape[0]
-    conv_rows = conv_hbm.shape[0]
+        out_ref[core * rows : (core + 1) * rows, :] = (total * scale).astype(BF16)
+
+
+def final_kernel(chips, inner, mine_ref, other_ref, conv_hbm, down_hbm, whole_ref, down_ref, sems):
+    half = mine_ref.shape[0]
+    rows = half // (2 * chips)
     core = lax.rem(lax.axis_index("shard"), 2)
-    piece = 4 * LANES
-    assert rows <= conv_rows <= 2 * rows and rows % LANES == 0
-
-    def write(half):
-        first, last = half * rows, (half + 1) * rows
-        copies = []
-        for start in range(first, min(last, conv_rows), piece):
-            size = min(piece, last - start, conv_rows - start)
-            place = pl.ds(start, size)
-            value = block_ref[start - first : start - first + size, :]
-            conv_ref[place, :] = value.astype(F32)
-            sem = sems.at[len(copies)]
-            copies.append(pltpu.make_async_copy(conv_ref.at[place], conv_hbm.at[place], sem))
-            copies[-1].start()
-        across = down_hbm.shape[1] // LANES
-        for down in range(0, down_hbm.shape[0], LANES):
-            row = conv_rows + down * across
-            for side in range(across):
-                start = row + side * LANES
-                if first <= start < last:
-                    value = block_ref[start - first : start - first + LANES, :]
-                    lanes = slice(side * LANES, (side + 1) * LANES)
-                    down_ref[down : down + LANES, lanes] = value.astype(F32)
-            if first <= row < last:
-                place = pl.ds(down, LANES)
-                sem = sems.at[len(copies)]
-                copies.append(pltpu.make_async_copy(down_ref.at[place], down_hbm.at[place], sem))
-                copies[-1].start()
-        for copy in copies:
-            copy.wait()
-
-    for half in range(2):
-        pl.when(core == (half if own else 1 - half))(functools.partial(write, half))
+    outer = chips // inner
+    for block_ref, side in ((mine_ref, core), (other_ref, 1 - core)):
+        for place in range(chips):
+            chip = place % outer * inner + place // outer
+            for h in range(2):
+                first = (2 * place + h) * rows
+                target = pl.multiple_of(h * half + (2 * chip + side) * rows, 8)
+                value = block_ref[first : first + rows, :].astype(F32)
+                whole_ref[pl.ds(target, rows), :] = value
+    row = conv_hbm.shape[0]
+    conv_copy = pltpu.make_async_copy(whole_ref.at[pl.ds(0, row)], conv_hbm, sems.at[0])
+    conv_copy.start()
+    for down in range(0, down_ref.shape[0], LANES):
+        for start in range(0, down_ref.shape[1], LANES):
+            block = whole_ref[row : row + LANES, :]
+            down_ref[down : down + LANES, start : start + LANES] = block
+            row += LANES
+    down_copy = pltpu.make_async_copy(down_ref, down_hbm, sems.at[1])
+    down_copy.start()
+    conv_copy.wait()
+    down_copy.wait()
 
 
 def tail_kernel(slots, *refs):
@@ -427,16 +410,13 @@
     out_ref[...] = add_lists(hgrad_ref[...] + back_ref[...], halo_ref, blocks)
 
 
-def call(
-    kernel, operands, outs, scratch=(), limit=32, flops=0, in_hbm=(), out_hbm=False, aliases={}
-):
+def call(kernel, operands, outs, scratch=(), limit=32, flops=0, in_hbm=(), out_hbm=False):
     spaces = [pl.ANY if n in in_hbm else pltpu.VMEM for n in range(len(operands))]
     return pl.pallas_call(
         kernel,
         out_shape=[jax.ShapeDtypeStruct(s, d) for s, d in outs],
         in_specs=[pl.BlockSpec(memory_space=space) for space in spaces],
         out_specs=[pl.BlockSpec(memory_space=pl.ANY if out_hbm else pltpu.VMEM) for _ in outs],
-        input_output_aliases=aliases,
         scratch_shapes=list(scratch),
         compiler_params=pltpu.CompilerParams(vmem_limit_bytes=limit * 2**20),
         cost_estimate=pl.CostEstimate(flops=flops, bytes_accessed=4 * 2**20, transcendentals=0),
@@ -445,6 +425,17 @@
 
 def swap_cores(value, devices):
     return lax.ppermute(value, "shard", [(i, i + 1 - 2 * (i % 2)) for i in range(devices)])
+
+
+def gather_blocks(value, devices, inner):
+    chips = devices // 2
+    far = [[2 * c + q for c in range(i, chips, inner)] for i in range(inner) for q in range(2)]
+    near = [
+        [2 * (o + i) + q for i in range(inner)] for o in range(0, chips, inner) for q in range(2)
+    ]
+    for groups in (far, near):
+        value = lax.all_gather(value, "shard", axis_index_groups=groups, axis=0, tiled=True)
+    return value
 
 
 def exchange(value):
@@ -545,40 +536,34 @@
         flops=20 * giga,
         in_hbm=(3,),
     )
-    (summed,) = call(
-        functools.partial(sum_kernel, devices, scale),
-        (parts, spread[1]),
-        [((half_rows, LANES), BF16)],
-        flops=10**6,
-        in_hbm=(1,),
-    )
-    summed, *returning = lax.optimization_barrier((summed, *spread[1:]))
-    returned = swaps(returning, (0, 1, 2, 3))
+    returned = swaps(spread[1:], (0, 1, 2, 3))
+    parts, *returned = lax.optimization_barrier((parts, *returned))
     (input_grad,) = call(
         functools.partial(tail_kernel, slots),
         (*returned, hidden_grad, spread[0], halo_rows),
         [((voxels, channels), F32)],
         flops=giga,
     )
-    mine, input_grad = lax.optimization_barrier((exchange(summed), input_grad))
-    other = swap_cores(mine, devices)
-    gradients = ()
-    for own, block in ((True, mine), (False, other)):
-        gradients = call(
-            functools.partial(final_kernel, own),
-            (block, *gradients),
-            [((conv_rows, LANES), F32), ((octants * channels, coarse_channels), F32)],
-            scratch=[
-                pltpu.VMEM((conv_rows, LANES), F32),
-                pltpu.VMEM((octants * channels, coarse_channels), F32),
-                pltpu.SemaphoreType.DMA((32,)),
-            ],
-            flops=10**6,
-            in_hbm=(1, 2),
-            out_hbm=True,
-            aliases={1: 0, 2: 1} if gradients else {},
-        )
-    conv_grad, down_grad = gradients
+    (summed,) = call(
+        functools.partial(sum_kernel, devices, scale),
+        (parts,),
+        [((2 * half_rows // devices, LANES), BF16)],
+        flops=10**6,
+    )
+    inner = 4
+    mine = gather_blocks(summed, devices, inner)
+    conv_grad, down_grad = call(
+        functools.partial(final_kernel, devices // 2, inner),
+        (mine, swap_cores(mine, devices)),
+        [((conv_rows, LANES), F32), ((octants * channels, coarse_channels), F32)],
+        scratch=[
+            pltpu.VMEM((2 * half_rows, LANES), F32),
+            pltpu.VMEM((octants * channels, coarse_channels), F32),
+            pltpu.SemaphoreType.DMA((2,)),
+        ],
+        flops=10**6,
+        out_hbm=True,
+    )
     conv_grad = conv_grad.reshape(conv_weight.shape)
     return (coarse, input_grad, conv_grad, down_grad.reshape(down_weight.shape))
 

time: 96.5 us -> 110 us (1.14)
  blocking collectives: 0 us -> 25.2 us
  waiting for transfers between devices: 18.8 us -> 3.6 us
  Pallas kernels: 41.7 us -> 44.1 us
    all_gather x0 -> x2, blocking collectives: none -> 25.2 us  [gather_blocks(): lax.all_gather(value, 'shard', axis_index_groups=groups, axis=0, tiled=True)]
    all_to_all x2 -> x1, waiting for transfers between devices: 14.5 us -> 0.01 us  [exchange(): return lax.all_to_all(value, 'shard', 0, 0, tiled=True)]
    ppermute x2, starting transfers between devices: 0.69 us -> 5.37 us  [swap_cores(): lax.ppermute(value, 'shard', [(i, i + 1 - 2 * (i % 2)) for i in range(dev...]
    all_to_all x2 -> x1, starting transfers between devices: 13.6 us -> 9.72 us  [exchange(): return lax.all_to_all(value, 'shard', 0, 0, tiled=True)]
    pallas_call x11 -> x10, Pallas kernels: 41.7 us -> 44.1 us  [call(): pl.pallas_call(kernel, out_shape=[jax.ShapeDtypeStruct(s, d) for s, d in...]
  transfers between devices with their start and end apart: 16 -> 15, of which waited for: 6 -> 3; matrix products, arithmetic and copies ran while one was open for 0% -> 0% of each run, Pallas kernels for 24% -> 24%
where the time goes in v11:
time: 110 us; the launch traced here: 109 us
  Pallas kernels  44.1 us (40%)
  starting transfers between devices  34.9 us (32%)
  blocking collectives  25.2 us (23%)
  waiting for transfers between devices  3.6 us (3%)
  between operations  1.1 us (1%)
    pallas_call x10, Pallas kernels, call(): pl.pallas_call(kernel, out_shape=[jax.ShapeDtypeStruct(s, d) for s, d in...  44.1 us
    all_gather x2, blocking collectives, gather_blocks(): lax.all_gather(value, 'shard', axis_index_groups=groups, axis=0, tiled=True)  25.2 us
    ppermute x12, starting transfers between devices, swaps(): moved[step] = lax.ppermute(by_step[step], 'shard', pairs)  19.8 us
    all_to_all x1, starting transfers between devices, exchange(): return lax.all_to_all(value, 'shard', 0, 0, tiled=True)  9.72 us
    ppermute x2, starting transfers between devices, swap_cores(): lax.ppermute(value, 'shard', [(i, i + 1 - 2 * (i % 2)) for i in range(dev...  5.37 us
    ppermute x2, waiting for transfers between devices, swap_cores(): lax.ppermute(value, 'shard', [(i, i + 1 - 2 * (i % 2)) for i in range(dev...  2.85 us
  transfers between devices with their start and end apart: 15, of which 3 were waited for; matrix products, arithmetic and copies ran while one was open for 0% of the time, Pallas kernels for 24%

profile of v11, /device:TPU:1, one launch (start us, length us, event | category | flops | bytes accessed | tf_op | source)
XLA Modules:
  0.0 108.9 jit_solution(6950382750866018694)
XLA Ops:
  0.6 0.0 copy-start.2
  0.6 0.0 copy-start.4
  0.7 4.0 %shard_map.111 = (bf16[96,128]{1,0:T(8,128)(2,1)}, bf16[96,128]{1,0:T(8,128)(2,1)}, bf16[96,128]{1,0:T(8,128)(2,1)}, bf16[96,128]{1,0:T(8,128)(2,1)}, f32[1024,128]{1,0:T(8,128)}) custom-call(bf16[1024,128]{1,0:T(8,128)(2,1)} %refs_4_.1, s32[4,64]{1,0:T(4,128)} %refs_6_.7, s32[8,256]{1,0:T(8,128)} %refs_5_.3, bf16[256,256]{1,0:T(8,128)(2,1)} %refs_10_.1, ...), custom_call_target="tpu_custom_call" | custom-call | flops 1000000000 | bytes 4194304 | tf_op jit(solution)/shard_map/pallas_call | solution.py:415
  4.7 0.1 collective-permute-start
  4.8 4.5 %collective-permute-start.1 = (bf16[96,128]{1,0:T(8,128)(2,1)}, bf16[96,128]{1,0:T(8,128)(2,1)S(1)}, u32[]{:S(2)}, u32[]{:S(2)}) collective-permute-start(bf16[96,128]{1,0:T(8,128)(2,1)} %get-tuple-element.37), channel_id=1, source_target_pairs={{1,2},{2,1},{3,4},{4,3},{5,6},{6,5},{7,8},{8,7},{9,10},{10,9},{11,... | collective-permute-start | bytes 73736 | tf_op jit(solution)/shard_map/ppermute | solution.py:23
  9.3 1.3 %collective-permute-start.2 = (bf16[96,128]{1,0:T(8,128)(2,1)}, bf16[96,128]{1,0:T(8,128)(2,1)S(1)}, u32[]{:S(2)}, u32[]{:S(2)}) collective-permute-start(bf16[96,128]{1,0:T(8,128)(2,1)} %get-tuple-element.38), channel_id=1, source_target_pairs={{0,2},{1,3},{2,0},{3,1},{4,6},{5,7},{6,4},{7,5},{8,10},{9,11},{10,... | collective-permute-start | bytes 73736 | tf_op jit(solution)/shard_map/ppermute | solution.py:23
  10.5 0.0 copy-start
  10.5 0.0 copy-start.6
  10.5 0.8 collective-permute-start.3
  11.3 0.0 copy-done.2
  11.3 0.0 copy-done.4
  11.3 3.5 %shard_map.112.refs_8_ = bf16[1024,1536]{1,0:T(8,128)(2,1)S(1)} custom-call(bf16[1024,128]{1,0:T(8,128)(2,1)S(1)} %copy-done.2, s32[27,1024]{1,0:T(8,128)S(1)} %copy-done.4), custom_call_target="tpu_custom_call" | custom-call | flops 4000000000 | bytes 4194304 | tf_op jit(solution)/shard_map/pallas_call | solution.py:415
  14.9 0.0 copy-start.3
  14.9 0.0 copy-start.5
  14.9 0.0 copy-start.8
  14.9 0.0 collective-permute-done.refs_0_
  14.9 0.0 collective-permute-done.1.refs_1_
  14.9 0.0 collective-permute-done.2.refs_2_
  14.9 0.0 collective-permute-done.3.refs_3_
  14.9 0.0 copy-done
  14.9 0.0 copy-done.6
  15.0 9.9 %shard_map.113 = (bf16[1024,128]{1,0:T(8,128)(2,1)S(1)}, f32[1024,128]{1,0:T(8,128)S(1)}, bf16[1024,3456]{1,0:T(8,128)(2,1)S(1)}, bf16[32,128]{1,0:T(8,128)(2,1)...) custom-call(bf16[96,128]{1,0:T(8,128)(2,1)S(1)} %collective-permute-done.refs_0_, ...), custom_call_target="tpu_custom_call" | custom-call | flops 12000000000 | bytes 4194304 | tf_op jit(solution)/shard_map/pallas_call | solution.py:415
  24.8 0.3 collective-permute-start.4
  25.1 5.9 %collective-permute-start.5 = (bf16[32,128]{1,0:T(8,128)(2,1)S(1)}, bf16[32,128]{1,0:T(8,128)(2,1)S(1)}, u32[]{:S(2)}, u32[]{:S(2)}) collective-permute-start(bf16[32,128]{1,0:T(8,128)(2,1)S(1)} %get-tuple-element.41), channel_id=1, source_target_pairs={{1,2},{2,1},{3,4},{4,3},{5,6},{6,5},{7,8},{8,7},{9,10},{10,9},{11,... | collective-permute-start | bytes 24584 | tf_op jit(solution)/shard_map/ppermute | solution.py:23
  31.1 0.7 collective-permute-start.6
  31.7 0.6 collective-permute-start.7
  32.4 0.0 copy-done.3
  32.4 0.0 copy-done.5
  32.4 0.0 copy-done.8
  32.4 0.0 copy-start.1
  32.4 2.1 %shard_map.114 = (f32[1024,128]{1,0:T(8,128)S(1)}, bf16[1024,128]{1,0:T(8,128)(2,1)S(1)}, bf16[3456,128]{1,0:T(8,128)(2,1)S(1)}, bf16[256,1024]{1,0:T(8,128)(2,1)S(1)}, bf16[256,256]{1,0:T(8,128)(2,1)S(1)}) custom-call(bf16[96,128]{1,0:T(8,128)(2,1)S(1)} %collective-permute-done.refs_0_, bf16[96,128]{1,0:T(8,128)(2,1)S(1)} %collective-permute-done.1.refs_1_, ...), custom_call_target="tpu_custom_call" | custom-call | flops 3000000000 | bytes 4194304 | tf_op jit(solution)/shard_map/pallas_call | solution.py:415
  34.5 0.0 collective-permute-done.4.refs_0_
  34.5 0.0 collective-permute-done.5.refs_1_
  34.6 0.0 collective-permute-done.6.refs_2_
  34.6 0.0 collective-permute-done.7.refs_3_
  34.6 0.0 copy-done.1
  34.6 1.4 %shard_map.115 = (bf16[256,256]{1,0:T(8,128)(2,1)}, bf16[5632,128]{1,0:T(8,128)(2,1)S(1)}, bf16[2816,128]{1,0:T(8,128)(2,1)S(1)}) custom-call(bf16[32,128]{1,0:T(8,128)(2,1)S(1)} %collective-permute-done.4.refs_0_, bf16[32,128]{1,0:T(8,128)(2,1)S(1)} %collective-permute-done.5.refs_1_, bf16[32,128]{1,0:T(8,128)(2,1)S(1)} %collective-permute-done.6.refs_2_, ...), custom_call_target="tpu_custom_call" | custom-call | flops 2000000000 | bytes 4194304 | tf_op jit(solution)/shard_map/pallas_call | solution.py:415
  36.0 0.0 collective-permute-start.8
  36.0 2.2 %collective-permute-done.8.other_ref = bf16[2816,128]{1,0:T(8,128)(2,1)S(1)} collective-permute-done((bf16[2816,128]{1,0:T(8,128)(2,1)S(1)}, bf16[2816,128]{1,0:T(8,128)(2,1)S(1)}, u32[]{:S(2)}, u32[]{:S(2)}) %collective-permute-start.8) | collective-permute-done | bytes 720928 | tf_op jit(solution)/shard_map/ppermute | solution.py:427
  38.2 1.0 shard_map.116.after_ref
  39.2 9.7 %all-to-all-start = ((bf16[32,88,128]{2,1,0:T(8,128)(2,1)}), bf16[32,88,128]{2,1,0:T(8,128)(2,1)S(1)}, u32[]{:S(2)}, u32[]{:S(2)}) async-start(bf16[32,88,128]{2,1,0:T(8,128)(2,1)} %bitcast), calls=%async_computation | async-start | bytes 1441792 | tf_op jit(solution)/shard_map/all_to_all | solution.py:442
  48.9 0.0 copy-start.7
  48.9 19.1 %shard_map.117 = (f32[1024,128]{1,0:T(8,128)S(1)}, bf16[64,128]{1,0:T(8,128)(2,1)S(1)}, bf16[64,128]{1,0:T(8,128)(2,1)S(1)}, bf16[64,128]{1,0:T(8,128)(2,1)S(1)}, bf16[64,128]{1,0:T(8,128)(2,1)S(1)}) custom-call(bf16[1024,128]{1,0:T(8,128)(2,1)S(1)} %get-tuple-element.54.pgrad_ref, s32[27,1024]{1,0:T(8,128)S(1)} %copy-done.4, ...), custom_call_target="tpu_custom_call" | custom-call | flops 20000000000 | bytes 4194304 | tf_op jit(solution)/shard_map/pallas_call | solution.py:415
  68.0 0.3 collective-permute-start.9
  68.4 3.4 %collective-permute-start.10 = (bf16[64,128]{1,0:T(8,128)(2,1)S(1)}, bf16[64,128]{1,0:T(8,128)(2,1)S(1)}, u32[]{:S(2)}, u32[]{:S(2)}) collective-permute-start(bf16[64,128]{1,0:T(8,128)(2,1)S(1)} %get-tuple-element.56), channel_id=1, source_target_pairs={{1,2},{2,1},{3,4},{4,3},{5,6},{6,5},{7,8},{8,7},{9,10},{10,9},{11,... | collective-permute-start | bytes 49160 | tf_op jit(solution)/shard_map/ppermute | solution.py:23
  71.8 1.2 %collective-permute-start.11 = (bf16[64,128]{1,0:T(8,128)(2,1)S(1)}, bf16[64,128]{1,0:T(8,128)(2,1)S(1)}, u32[]{:S(2)}, u32[]{:S(2)}) collective-permute-start(bf16[64,128]{1,0:T(8,128)(2,1)S(1)} %get-tuple-element.57), channel_id=1, source_target_pairs={{0,2},{1,3},{2,0},{3,1},{4,6},{5,7},{6,4},{7,5},{8,10},{9,11},{10,... | collective-permute-start | bytes 49160 | tf_op jit(solution)/shard_map/ppermute | solution.py:23
  73.0 0.7 collective-permute-start.12
  73.7 0.0 collective-permute-done.9.refs_0_
  73.7 0.0 collective-permute-done.10.refs_1_
  73.7 0.7 collective-permute-done.11.refs_2_
  74.5 0.0 collective-permute-done.12.refs_3_
  74.5 0.0 all-to-all-done
  74.5 0.1 shard_map.119
  74.6 16.0 %all_gather.6 = bf16[704,128]{1,0:T(8,128)(2,1)S(1)} all-gather(bf16[176,128]{1,0:T(8,128)(2,1)S(1)} %shard_map.119), channel_id=1, replica_groups={{0,8,16,24},{1,9,17,25},{2,10,18,26},{3,11,19,27},{4,12,20,28},{5,13,21..., dimensions={0}, use_global_device_ids=true | all-gather | bytes 225280 | tf_op jit(solution)/shard_map/all_gather | solution.py:437
  90.5 9.2 %all_gather.7.mine_ref = bf16[2816,128]{1,0:T(8,128)(2,1)S(1)} all-gather(bf16[704,128]{1,0:T(8,128)(2,1)S(1)} %all_gather.6), channel_id=1, replica_groups={{0,2,4,6},{1,3,5,7},{8,10,12,14},{9,11,13,15},{16,18,20,22},{17,19,21,2..., dimensions={0}, use_global_device_ids=true | all-gather | bytes 901120 | tf_op jit(solution)/shard_map/all_gather | solution.py:437
  99.7 5.4 %collective-permute-start.13 = (bf16[2816,128]{1,0:T(8,128)(2,1)S(1)}, bf16[2816,128]{1,0:T(8,128)(2,1)S(1)}, u32[]{:S(2)}, u32[]{:S(2)}) collective-permute-start(bf16[2816,128]{1,0:T(8,128)(2,1)S(1)} %all_gather.7.mine_ref), channel_id=1, source_target_pairs={{0,1},{1,0},{2,3},{3,2},{4,5},{5,4},{6,7},{7,6},{8,9},{9,8},{10,11... | collective-permute-start | bytes 2162696 | tf_op jit(solution)/shard_map/ppermute | solution.py:427
  105.1 0.0 copy-done.7
  105.1 1.2 %shard_map.118 = f32[1024,128]{1,0:T(8,128)} custom-call(bf16[64,128]{1,0:T(8,128)(2,1)S(1)} %collective-permute-done.9.refs_0_, bf16[64,128]{1,0:T(8,128)(2,1)S(1)} %collective-permute-done.10.refs_1_, bf16[64,128]{1,0:T(8,128)(2,1)S(1)} %collective-permute-done.11.refs_2_, bf16[64,128]{1,0:T(8,128)(2,1)S(1)} %collective-permute-done.12.refs_3_, ...), custom_call_target="tpu_custom_call" | custom-call | flops 1000000000 | bytes 4194304 | tf_op jit(solution)/shard_map/pallas_call | solution.py:415
  106.3 0.7 collective-permute-done.13.other_ref
  106.9 1.9 %shard_map.120 = (f32[3456,128]{1,0:T(8,128)}, f32[1024,256]{1,0:T(8,128)}) custom-call(bf16[2816,128]{1,0:T(8,128)(2,1)S(1)} %all_gather.7.mine_ref, bf16[2816,128]{1,0:T(8,128)(2,1)S(1)} %collective-permute-done.13.other_ref), custom_call_target="tpu_custom_call" | custom-call | flops 1000000 | bytes 4194304 | tf_op jit(solution)/shard_map/pallas_call | solution.py:415
Async XLA Ops:
  0.6 10.7 %copy-start.2 = (bf16[1024,128]{1,0:T(8,128)(2,1)S(1)}, bf16[1024,128]{1,0:T(8,128)(2,1)}, u32[]{:S(2)}) copy-start(bf16[1024,128]{1,0:T(8,128)(2,1)} %refs_4_.1) | copy-start | bytes 786436
  0.6 10.7 %copy-start.4 = (s32[27,1024]{1,0:T(8,128)S(1)}, s32[27,1024]{1,0:T(8,128)}, u32[]{:S(2)}) copy-start(s32[27,1024]{1,0:T(8,128)} %map_ref.3) | copy-start | bytes 331780
  4.7 10.2 %collective-permute-start = (bf16[96,128]{1,0:T(8,128)(2,1)}, bf16[96,128]{1,0:T(8,128)(2,1)S(1)}, u32[]{:S(2)}, u32[]{:S(2)}) collective-permute-start(bf16[96,128]{1,0:T(8,128)(2,1)} %get-tuple-element.36), channel_id=1, source_target_pairs={{0,1},{1,0},{2,3},{3,2},{4,5},{5,4},{6,7},{7,6},{8,9},{9,8},{10,11... | collective-permute-start | bytes 73736 | tf_op jit(solution)/shard_map/ppermute | solution.py:23
  4.8 10.1 %collective-permute-start.1 = (bf16[96,128]{1,0:T(8,128)(2,1)}, bf16[96,128]{1,0:T(8,128)(2,1)S(1)}, u32[]{:S(2)}, u32[]{:S(2)}) collective-permute-start(bf16[96,128]{1,0:T(8,128)(2,1)} %get-tuple-element.37), channel_id=1, source_target_pairs={{1,2},{2,1},{3,4},{4,3},{5,6},{6,5},{7,8},{8,7},{9,10},{10,9},{11,... | collective-permute-start | bytes 73736 | tf_op jit(solution)/shard_map/ppermute | solution.py:23
  9.3 5.7 %collective-permute-start.2 = (bf16[96,128]{1,0:T(8,128)(2,1)}, bf16[96,128]{1,0:T(8,128)(2,1)S(1)}, u32[]{:S(2)}, u32[]{:S(2)}) collective-permute-start(bf16[96,128]{1,0:T(8,128)(2,1)} %get-tuple-element.38), channel_id=1, source_target_pairs={{0,2},{1,3},{2,0},{3,1},{4,6},{5,7},{6,4},{7,5},{8,10},{9,11},{10,... | collective-permute-start | bytes 73736 | tf_op jit(solution)/shard_map/ppermute | solution.py:23
  10.5 4.4 %copy-start = (bf16[27,128,128]{2,1,0:T(8,128)(2,1)S(1)}, bf16[27,128,128]{2,1,0:T(8,128)(2,1)}, u32[]{:S(2)}) copy-start(bf16[27,128,128]{2,1,0:T(8,128)(2,1)} %weight_ref.1) | copy-start | bytes 2654212
  10.5 4.4 %copy-start.6 = (s32[4,32]{1,0:T(4,128)S(1)}, s32[4,32]{1,0:T(4,128)}, u32[]{:S(2)}) copy-start(s32[4,32]{1,0:T(4,128)} %refs_6_.5) | copy-start | bytes 1540
  10.5 4.4 %collective-permute-start.3 = (bf16[96,128]{1,0:T(8,128)(2,1)}, bf16[96,128]{1,0:T(8,128)(2,1)S(1)}, u32[]{:S(2)}, u32[]{:S(2)}) collective-permute-start(bf16[96,128]{1,0:T(8,128)(2,1)} %get-tuple-element.39), channel_id=1, source_target_pairs={{2,4},{3,5},{4,2},{5,3},{6,8},{7,9},{8,6},{9,7},{10,12},{11,13},{1... | collective-permute-start | bytes 73736 | tf_op jit(solution)/shard_map/ppermute | solution.py:23
  14.9 17.5 %copy-start.3 = (bf16[256,256]{1,0:T(8,128)(2,1)S(1)}, bf16[256,256]{1,0:T(8,128)(2,1)}, u32[]{:S(2)}) copy-start(bf16[256,256]{1,0:T(8,128)(2,1)} %refs_10_.1) | copy-start | bytes 393220
  14.9 17.5 %copy-start.5 = (s32[8,256]{1,0:T(8,128)S(1)}, s32[8,256]{1,0:T(8,128)}, u32[]{:S(2)}) copy-start(s32[8,256]{1,0:T(8,128)} %refs_5_.3) | copy-start | bytes 24580
  14.9 17.5 %copy-start.8 = (f32[1024,128]{1,0:T(8,128)S(1)}, f32[1024,128]{1,0:T(8,128)}, u32[]{:S(2)}) copy-start(f32[1024,128]{1,0:T(8,128)} %get-tuple-element.46.refs_7_) | copy-start | bytes 1572868
  24.8 9.7 %collective-permute-start.4 = (bf16[32,128]{1,0:T(8,128)(2,1)S(1)}, bf16[32,128]{1,0:T(8,128)(2,1)S(1)}, u32[]{:S(2)}, u32[]{:S(2)}) collective-permute-start(bf16[32,128]{1,0:T(8,128)(2,1)S(1)} %get-tuple-element.40), channel_id=1, source_target_pairs={{0,1},{1,0},{2,3},{3,2},{4,5},{5,4},{6,7},{7,6},{8,9},{9,8},{10,11... | collective-permute-start | bytes 24584 | tf_op jit(solution)/shard_map/ppermute | solution.py:23
  25.1 9.4 %collective-permute-start.5 = (bf16[32,128]{1,0:T(8,128)(2,1)S(1)}, bf16[32,128]{1,0:T(8,128)(2,1)S(1)}, u32[]{:S(2)}, u32[]{:S(2)}) collective-permute-start(bf16[32,128]{1,0:T(8,128)(2,1)S(1)} %get-tuple-element.41), channel_id=1, source_target_pairs={{1,2},{2,1},{3,4},{4,3},{5,6},{6,5},{7,8},{8,7},{9,10},{10,9},{11,... | collective-permute-start | bytes 24584 | tf_op jit(solution)/shard_map/ppermute | solution.py:23
  31.1 3.5 %collective-permute-start.6 = (bf16[32,128]{1,0:T(8,128)(2,1)S(1)}, bf16[32,128]{1,0:T(8,128)(2,1)S(1)}, u32[]{:S(2)}, u32[]{:S(2)}) collective-permute-start(bf16[32,128]{1,0:T(8,128)(2,1)S(1)} %get-tuple-element.42), channel_id=1, source_target_pairs={{0,2},{1,3},{2,0},{3,1},{4,6},{5,7},{6,4},{7,5},{8,10},{9,11},{10,... | collective-permute-start | bytes 24584 | tf_op jit(solution)/shard_map/ppermute | solution.py:23
  31.7 2.8 %collective-permute-start.7 = (bf16[32,128]{1,0:T(8,128)(2,1)S(1)}, bf16[32,128]{1,0:T(8,128)(2,1)S(1)}, u32[]{:S(2)}, u32[]{:S(2)}) collective-permute-start(bf16[32,128]{1,0:T(8,128)(2,1)S(1)} %get-tuple-element.43), channel_id=1, source_target_pairs={{2,4},{3,5},{4,2},{5,3},{6,8},{7,9},{8,6},{9,7},{10,12},{11,13},{1... | collective-permute-start | bytes 24584 | tf_op jit(solution)/shard_map/ppermute | solution.py:23
  32.4 2.1 %copy-start.1 = (bf16[8,128,256]{2,1,0:T(8,128)(2,1)S(1)}, bf16[8,128,256]{2,1,0:T(8,128)(2,1)}, u32[]{:S(2)}) copy-start(bf16[8,128,256]{2,1,0:T(8,128)(2,1)} %refs_6_.6) | copy-start | bytes 1572868
  36.0 2.2 %collective-permute-start.8 = (bf16[2816,128]{1,0:T(8,128)(2,1)S(1)}, bf16[2816,128]{1,0:T(8,128)(2,1)S(1)}, u32[]{:S(2)}, u32[]{:S(2)}) collective-permute-start(bf16[2816,128]{1,0:T(8,128)(2,1)S(1)} %get-tuple-element.53), channel_id=1, source_target_pairs={{0,1},{1,0},{2,3},{3,2},{4,5},{5,4},{6,7},{7,6},{8,9},{9,8},{10,11... | collective-permute-start | bytes 2162696 | tf_op jit(solution)/shard_map/ppermute | solution.py:427
  39.2 35.2 %all-to-all-start = ((bf16[32,88,128]{2,1,0:T(8,128)(2,1)}), bf16[32,88,128]{2,1,0:T(8,128)(2,1)S(1)}, u32[]{:S(2)}, u32[]{:S(2)}) async-start(bf16[32,88,128]{2,1,0:T(8,128)(2,1)} %bitcast), calls=%async_computation | async-start | bytes 1441792 | tf_op jit(solution)/shard_map/all_to_all | solution.py:442
  48.9 56.2 %copy-start.7 = (s32[4,64]{1,0:T(4,128)S(1)}, s32[4,64]{1,0:T(4,128)}, u32[]{:S(2)}) copy-start(s32[4,64]{1,0:T(4,128)} %refs_6_.7) | copy-start | bytes 3076
  68.0 5.7 %collective-permute-start.9 = (bf16[64,128]{1,0:T(8,128)(2,1)S(1)}, bf16[64,128]{1,0:T(8,128)(2,1)S(1)}, u32[]{:S(2)}, u32[]{:S(2)}) collective-permute-start(bf16[64,128]{1,0:T(8,128)(2,1)S(1)} %get-tuple-element.55), channel_id=1, source_target_pairs={{0,1},{1,0},{2,3},{3,2},{4,5},{5,4},{6,7},{7,6},{8,9},{9,8},{10,11... | collective-permute-start | bytes 49160 | tf_op jit(solution)/shard_map/ppermute | solution.py:23
  68.4 5.3 %collective-permute-start.10 = (bf16[64,128]{1,0:T(8,128)(2,1)S(1)}, bf16[64,128]{1,0:T(8,128)(2,1)S(1)}, u32[]{:S(2)}, u32[]{:S(2)}) collective-permute-start(bf16[64,128]{1,0:T(8,128)(2,1)S(1)} %get-tuple-element.56), channel_id=1, source_target_pairs={{1,2},{2,1},{3,4},{4,3},{5,6},{6,5},{7,8},{8,7},{9,10},{10,9},{11,... | collective-permute-start | bytes 49160 | tf_op jit(solution)/shard_map/ppermute | solution.py:23
  71.8 2.7 %collective-permute-start.11 = (bf16[64,128]{1,0:T(8,128)(2,1)S(1)}, bf16[64,128]{1,0:T(8,128)(2,1)S(1)}, u32[]{:S(2)}, u32[]{:S(2)}) collective-permute-start(bf16[64,128]{1,0:T(8,128)(2,1)S(1)} %get-tuple-element.57), channel_id=1, source_target_pairs={{0,2},{1,3},{2,0},{3,1},{4,6},{5,7},{6,4},{7,5},{8,10},{9,11},{10,... | collective-permute-start | bytes 49160 | tf_op jit(solution)/shard_map/ppermute | solution.py:23
  73.0 1.4 %collective-permute-start.12 = (bf16[64,128]{1,0:T(8,128)(2,1)S(1)}, bf16[64,128]{1,0:T(8,128)(2,1)S(1)}, u32[]{:S(2)}, u32[]{:S(2)}) collective-permute-start(bf16[64,128]{1,0:T(8,128)(2,1)S(1)} %get-tuple-element.58), channel_id=1, source_target_pairs={{2,4},{3,5},{4,2},{5,3},{6,8},{7,9},{8,6},{9,7},{10,12},{11,13},{1... | collective-permute-start | bytes 49160 | tf_op jit(solution)/shard_map/ppermute | solution.py:23
  99.7 7.2 %collective-permute-start.13 = (bf16[2816,128]{1,0:T(8,128)(2,1)S(1)}, bf16[2816,128]{1,0:T(8,128)(2,1)S(1)}, u32[]{:S(2)}, u32[]{:S(2)}) collective-permute-start(bf16[2816,128]{1,0:T(8,128)(2,1)S(1)} %all_gather.7.mine_ref), channel_id=1, source_target_pairs={{0,1},{1,0},{2,3},{3,2},{4,5},{5,4},{6,7},{7,6},{8,9},{9,8},{10,11... | collective-permute-start | bytes 2162696 | tf_op jit(solution)/shard_map/ppermute | solution.py:427

commit v12 on v10

--- a/solution.py
+++ b/solution.py
@@ -139,8 +139,9 @@
     slots, cap = halo_ref.shape
     voxels = features_ref.shape[0]
     octants = child_map_ref.shape[0]
-    table_rows = voxels + slots * (sends[0].shape[0] - cap)
-    cap2 = (table_rows - voxels) // slots
+    cap2 = sends[0].shape[0] - cap
+    cap2 //= 1 + octants * out_grad_ref.shape[1] // LANES
+    table_rows = voxels + slots * cap2
     copies[0].wait()
     copies[1].wait()
     listed = gather_lists(halo_ref, features_ref[...]).astype(BF16)
@@ -162,6 +163,18 @@
     back_ref[...] = total[:voxels]
     for send, block in zip(sends, to_steps(jnp.split(total[voxels:].astype(BF16), slots), True)):
         send[cap : cap + cap2, :] = block
+    sums = [matmul(chooser[voxels:], upstream).astype(BF16) for chooser in choosers]
+    blocks = []
+    for s in range(slots):
+        rows = slice(s * cap2, (s + 1) * cap2)
+        halves = [
+            sums[o][rows, start : start + LANES]
+            for o in range(octants)
+            for start in range(0, upstream.shape[1], LANES)
+        ]
+        blocks.append(jnp.concatenate(halves, axis=0))
+    for send, block in zip(sends, to_steps(blocks, True)):
+        send[cap + cap2 :, :] = block
 
 
 def half_codes(row, voxels, received):
@@ -200,21 +213,15 @@
         early_ref[:, n * LANES : (n + 1) * LANES] = pick_side(col, both)
 
 
-def forward_kernel(slots, *refs):
+def forward_kernel(slots, cap, *refs):
     received = refs[:slots]
     features_ref, map_ref, weight_ref, child_ref, early_ref = refs[slots : slots + 5]
-    hidden_ref, pre_ref, stacked_ref = refs[slots + 5 : slots + 8]
-    sends = refs[slots + 8 : 2 * slots + 8]
-    table_ref, halo_ref, kernel_ref = refs[2 * slots + 8 :]
+    hidden_ref, pre_ref, stacked_ref, leaving_ref, halo_ref, kernel_ref = refs[slots + 5 :]
     voxels = features_ref.shape[0]
     gathers = map_ref.shape[0] - 1
     middle = gathers // 2
-    cap2 = child_ref.shape[1]
-    cap = received[0].shape[0] - cap2
     half, half_halo = voxels // 2, slots * cap // 2
     features = features_ref[...]
-    table_ref[:, 0:LANES] = features[0:half]
-    table_ref[:, LANES:] = features[half:voxels]
     halo_ref[...] = jnp.zeros(halo_ref.shape, BF16)
     for s, block in enumerate(to_slots([r[0:cap, :] for r in received], False)):
         place = (s % (slots // 2)) * cap
@@ -226,41 +233,31 @@
     kernel_ref[middle:gathers] = weight_ref[middle + 1 :]
     kernel_ref[gathers] = weight_ref[middle]
 
-    begun = early_ref.shape[1] // (2 * LANES)
     for j in range(middle):
         numbers = (2 * j, 2 * j + 1)
         cols = [code_column(map_ref, offset_of(n, middle), voxels, slots * cap) for n in numbers]
         choosers = [one_hot_rows(jnp.abs(col), half_halo, half) for col in cols]
-        far = matmul(jnp.concatenate(choosers, axis=1), halo_ref[...])
+        far = matmul(jnp.concatenate(choosers, axis=1), halo_ref[...]).astype(BF16)
         for n in numbers:
-            col = cols[n % 2]
             both = far[:, 2 * (n % 2) * LANES : 2 * (n % 2 + 1) * LANES]
             lanes = slice(n * LANES, (n + 1) * LANES)
-            if j < begun:
-                picked = pick_side(col, both.astype(BF16)) + early_ref[:, lanes]
-            else:
-                own = matmul(one_hot_rows(jnp.abs(col), half), table_ref[...])
-                picked = pick_side(col, (both + own).astype(BF16))
-            stacked_ref[:, lanes] = picked
+            stacked_ref[:, lanes] = pick_side(cols[n % 2], both) + early_ref[:, lanes]
 
     stacked_ref[:, gathers * LANES :] = features
     pre = matmul(stacked_ref[...], kernel_ref[...].reshape(-1, LANES))
     pre_ref[...] = pre
     hidden = (features.astype(F32) + pre * jax.nn.sigmoid(pre)).astype(BF16)
     hidden_ref[...] = hidden
-    leaving = gather_lists(child_ref, hidden).astype(BF16)
-    for send, block in zip(sends, to_steps(jnp.split(leaving, slots), False)):
-        send[...] = block
-
-
-def gradient_kernel(slots, *refs):
+    leaving_ref[...] = gather_lists(child_ref, hidden).astype(BF16)
+
+
+def gradient_kernel(slots, cap, *refs):
     received = refs[:slots]
     stacked_ref, pre_ref, child_ref, back_ref = refs[slots : slots + 4]
-    hidden_ref, child_map_ref, out_grad_ref = refs[slots + 4 : slots + 7]
-    hgrad_ref, pgrad_ref, cgrad_ref, early_ref, upstream_t_ref = refs[slots + 7 :]
+    hidden_ref, leaving_ref, child_map_ref, out_grad_ref = refs[slots + 4 : slots + 8]
+    hgrad_ref, pgrad_ref, early_ref, terms_ref, send_ref = refs[slots + 8 :]
     cap2 = child_ref.shape[1]
-    cap = received[0].shape[0] - cap2
-    kernel_count = cgrad_ref.shape[0] // LANES
+    kernel_count = stacked_ref.shape[1] // LANES
     middle = kernel_count // 2
     blocks = to_slots([r[cap : cap + cap2, :] for r in received], True)
     hgrad = add_lists(back_ref[...], child_ref, blocks)
@@ -273,25 +270,48 @@
     order = [k for k in range(kernel_count) if k != middle] + [middle]
     for n, k in enumerate(order):
         block = jnp.transpose(terms[:, n * LANES : (n + 1) * LANES])
-        cgrad_ref[k * LANES : (k + 1) * LANES, :] = block.astype(BF16)
-    voxels, parents = hidden_ref.shape[0], out_grad_ref.shape[0]
+        terms_ref[k * LANES : (k + 1) * LANES, :] = block.astype(BF16)
+    voxels = hidden_ref.shape[0]
     half = voxels // 2
     hidden = hidden_ref[...]
     table = jnp.concatenate([hidden[0:half], hidden[half:]], axis=1)
-    for o in range(child_map_ref.shape[0]):
+    octants = child_map_ref.shape[0]
+    picked = []
+    for o in range(octants):
         col = code_column(child_map_ref, o, voxels, slots * cap2)
         both = matmul(one_hot_rows(jnp.abs(col), half), table).astype(BF16)
-        early_ref[:, o * LANES : (o + 1) * LANES] = pick_side(col, both)
-    upstream_t_ref[...] = jnp.transpose(out_grad_ref[...].astype(F32)).astype(BF16)
-
-
-def spread_kernel(slots, pgrad_ref, map_ref, weight_ref, after_ref, back_ref, *sends):
+        picked.append(pick_side(col, both))
+    picked = jnp.concatenate(picked, axis=1)
+    early_ref[...] = picked
+    upstream_t = jnp.transpose(out_grad_ref[...].astype(F32)).astype(BF16)
+    own = matmul(upstream_t, picked)
+    blocks = to_slots([r[cap + cap2 :, :] for r in received], True)
+    across = upstream_t.shape[0] // LANES
+    sums = []
+    for n in range(octants * across):
+        rows = slice(n * cap2, (n + 1) * cap2)
+        sums.append(jnp.concatenate([block[rows, :] for block in blocks], axis=0))
+    leaving_t = jnp.transpose(leaving_ref[...].astype(F32)).astype(BF16)
+    far = matmul(leaving_t, jnp.concatenate(sums, axis=1))
+    row = kernel_count * LANES
+    for n in range(octants * across):
+        o, side = n // across, n % across
+        block = own[side * LANES : (side + 1) * LANES, o * LANES : (o + 1) * LANES]
+        value = jnp.transpose(block) + far[:, n * LANES : (n + 1) * LANES]
+        terms_ref[row : row + LANES, :] = value.astype(BF16)
+        row += LANES
+    terms_ref[row:, :] = jnp.zeros((terms_ref.shape[0] - row, LANES), BF16)
+    send_ref[...] = terms_ref[pl.ds(my_half(send_ref.shape[0])[1], send_ref.shape[0]), :]
+
+
+def spread_kernel(
+    slots, cap, pgrad_ref, map_ref, weight_ref, leaving_ref, after_ref, back_ref, *sends
+):
     acc_ref = sends[-1]
     sends = sends[:-1]
     voxels = pgrad_ref.shape[0]
     kernel_count = map_ref.shape[0]
     middle = kernel_count // 2
-    cap = sends[0].shape[0]
     half = voxels // 2
     table_rows = half + slots * cap // 2
     pgrad = pgrad_ref[...]
@@ -323,42 +343,14 @@
         side = (s // (slots // 2)) * LANES
         blocks.append(acc_ref[first : first + cap, side : side + LANES].astype(BF16))
     for send, block in zip(sends, to_steps(blocks, True)):
-        send[...] = block
+        send[0:cap, :] = block
+    for send, block in zip(sends, to_steps(jnp.split(leaving_ref[...], slots), False)):
+        send[cap:, :] = block
 
 
 def my_half(rows):
     core = lax.rem(lax.axis_index("shard"), 2)
     return pl.multiple_of(core * rows, 16), pl.multiple_of((1 - core) * rows, 16)
-
-
-def down_kernel(slots, voxels, *refs):
-    received = refs[:slots]
-    (early_ref, map_ref, down_ref, upstream_t_ref, cgrad_ref) = refs[slots : slots + 5]
-    coarse_ref, terms_ref, send_ref = refs[slots + 5 :]
-    cap2 = received[0].shape[0]
-    octants, parents = map_ref.shape
-    blocks = to_slots([r[...] for r in received], False)
-    halo = jnp.concatenate(blocks, axis=0)
-    rows = map_ref[...]
-    codes = encode(jnp.where(rows >= voxels, rows - voxels, slots * cap2))
-    picked = []
-    for o in range(octants):
-        chooser = one_hot_rows(column(codes[o : o + 1, :]).astype(BF16), slots * cap2)
-        far = matmul(chooser, halo).astype(BF16)
-        picked.append(far + early_ref[:, o * LANES : (o + 1) * LANES])
-    picked = jnp.concatenate(picked, axis=1)
-    row = cgrad_ref.shape[0]
-    terms_ref[0:row, :] = cgrad_ref[...]
-    terms = matmul(upstream_t_ref[...], picked)
-    for o in range(octants):
-        for start in range(0, terms.shape[0], LANES):
-            block = terms[start : start + LANES, o * LANES : (o + 1) * LANES]
-            terms_ref[row : row + LANES, :] = jnp.transpose(block).astype(BF16)
-            row += LANES
-    total = matmul(picked, down_ref[...].reshape(octants * LANES, down_ref.shape[2]))
-    terms_ref[row:, :] = jnp.zeros((terms_ref.shape[0] - row, LANES), BF16)
-    coarse_ref[...] = total.astype(BF16)
-    send_ref[...] = terms_ref[pl.ds(my_half(send_ref.shape[0])[1], send_ref.shape[0]), :]
 
 
 def pair_kernel(terms_ref, other_ref, out_ref):
@@ -422,9 +414,24 @@
 
 def tail_kernel(slots, *refs):
     received = refs[:slots]
-    hgrad_ref, back_ref, halo_ref, out_ref = refs[slots:]
-    blocks = to_slots([r[...] for r in received], True)
+    hgrad_ref, back_ref, halo_ref, early_ref, map_ref, down_ref = refs[slots : slots + 6]
+    out_ref, coarse_ref = refs[slots + 6 :]
+    voxels = hgrad_ref.shape[0]
+    cap = halo_ref.shape[1]
+    cap2 = received[0].shape[0] - cap
+    blocks = to_slots([r[0:cap, :] for r in received], True)
     out_ref[...] = add_lists(hgrad_ref[...] + back_ref[...], halo_ref, blocks)
+    halo = jnp.concatenate(to_slots([r[cap:, :] for r in received], False), axis=0)
+    octants = map_ref.shape[0]
+    rows = map_ref[...]
+    codes = encode(jnp.where(rows >= voxels, rows - voxels, slots * cap2))
+    picked = []
+    for o in range(octants):
+        chooser = one_hot_rows(column(codes[o : o + 1, :]).astype(BF16), slots * cap2)
+        far = matmul(chooser, halo).astype(BF16)
+        picked.append(far + early_ref[:, o * LANES : (o + 1) * LANES])
+    kernel = down_ref[...].reshape(octants * LANES, down_ref.shape[2])
+    coarse_ref[...] = matmul(jnp.concatenate(picked, axis=1), kernel).astype(BF16)
 
 
 def call(
@@ -464,10 +471,15 @@
     scale = 1.0 / math.sqrt(voxels * devices)
     giga = 10**9
 
+    sum_rows = octants * cap2 * coarse_channels // LANES
+    conv_rows = kernel_count * channels
+    down_rows = octants * channels * coarse_channels // LANES
+    grain = 8 * devices
+    half_rows = -(-(conv_rows + down_rows) // (2 * grain)) * grain
     first = call(
         head_kernel,
         (features, halo_rows, child_map, out_grad, down_weight),
-        [((cap + cap2, channels), BF16)] * slots + [((voxels, channels), F32)],
+        [((cap + cap2 + sum_rows, channels), BF16)] * slots + [((voxels, channels), F32)],
         scratch=[
             pltpu.VMEM(value.shape, value.dtype)
             for value in (features, halo_rows, child_map, out_grad, down_weight)
@@ -479,56 +491,49 @@
     )
     back_h = first[-1]
     received = swaps(first[:-1], (2, 3, 1, 0))
-    conv_rows = kernel_count * channels
-    down_rows = octants * channels * coarse_channels // LANES
-    grain = 8 * devices
-    half_rows = -(-(conv_rows + down_rows) // (2 * grain)) * grain
     (early,) = call(
         functools.partial(local_kernel, slots * cap),
         (features, neighbour_map),
-        [((voxels, 12 * channels), BF16)],
+        [((voxels, conv_rows - channels), BF16)],
         scratch=[pltpu.VMEM((voxels // 2, 2 * channels), BF16)],
         flops=4 * giga,
     )
-    hidden, pre_act, stacked, *leaving = call(
-        functools.partial(forward_kernel, slots),
+    hidden, pre_act, stacked, leaving = call(
+        functools.partial(forward_kernel, slots, cap),
         (*received, features, neighbour_map, conv_weight, child_rows, early),
         [
             ((voxels, channels), BF16),
             ((voxels, channels), F32),
             ((voxels, conv_rows), BF16),
-        ]
-        + [((cap2, channels), BF16)] * slots,
+            ((slots * cap2, channels), BF16),
+        ],
         scratch=[
-            pltpu.VMEM((voxels // 2, 2 * channels), BF16),
             pltpu.VMEM((slots * cap, 4 * channels), BF16),
             pltpu.VMEM(conv_weight.shape, BF16),
         ],
-        limit=32,
         flops=12 * giga,
     )
-    hidden_grad, pre_grad, conv_terms, early_h, out_grad_t = call(
-        functools.partial(gradient_kernel, slots),
-        (*received, stacked, pre_act, child_rows, back_h, hidden, child_map, out_grad),
+    hidden_grad, pre_grad, early_h, terms, leaving_terms = call(
+        functools.partial(gradient_kernel, slots, cap),
+        (
+            *received,
+            stacked,
+            pre_act,
+            child_rows,
+            back_h,
+            hidden,
+            leaving,
+            child_map,
+            out_grad,
+        ),
         [
             ((voxels, channels), F32),
             ((voxels, channels), BF16),
-            ((conv_rows, channels), BF16),
             ((parents, octants * channels), BF16),
-            ((coarse_channels, parents), BF16),
-        ],
-        flops=3 * giga,
-    )
-    received_h = swaps(leaving, (1, 3, 2, 0))
-    coarse, terms, leaving_terms = call(
-        functools.partial(down_kernel, slots, voxels),
-        (*received_h, early_h, child_map, down_weight, out_grad_t, conv_terms),
-        [
-            ((parents, coarse_channels), BF16),
             ((2 * half_rows, LANES), BF16),
             ((half_rows, LANES), BF16),
         ],
-        flops=2 * giga,
+        flops=3 * giga,
     )
     (pair_terms,) = call(
         pair_kernel,
@@ -538,12 +543,12 @@
     )
     parts = exchange(pair_terms)
     spread = call(
-        functools.partial(spread_kernel, slots),
-        (pre_grad, neighbour_map, conv_weight, pair_terms),
-        [((voxels, channels), F32)] + [((cap, channels), BF16)] * slots,
+        functools.partial(spread_kernel, slots, cap),
+        (pre_grad, neighbour_map, conv_weight, leaving, pair_terms),
+        [((voxels, channels), F32)] + [((cap + cap2, channels), BF16)] * slots,
         scratch=[pltpu.VMEM((voxels // 2 + slots * cap // 2, 2 * channels), F32)],
         flops=20 * giga,
-        in_hbm=(3,),
+        in_hbm=(4,),
     )
     (summed,) = call(
         functools.partial(sum_kernel, devices, scale),
@@ -554,10 +559,10 @@
     )
     summed, *returning = lax.optimization_barrier((summed, *spread[1:]))
     returned = swaps(returning, (0, 1, 2, 3))
-    (input_grad,) = call(
+    input_grad, coarse = call(
         functools.partial(tail_kernel, slots),
-        (*returned, hidden_grad, spread[0], halo_rows),
-        [((voxels, channels), F32)],
+        (*returned, hidden_grad, spread[0], halo_rows, early_h, child_map, down_weight),
+        [((voxels, channels), F32), ((parents, coarse_channels), BF16)],
         flops=giga,
     )
     mine, input_grad = lax.optimization_barrier((exchange(summed), input_grad))

time: 96.5 us -> 87.8 us (0.910)
  starting transfers between devices: 34.1 us -> 23.9 us
    ppermute x12 -> x8, starting transfers between devices: 19.8 us -> 12.3 us  [swaps(): moved[step] = lax.ppermute(by_step[step], 'shard', pairs)]
    all_to_all x2, starting transfers between devices: 13.6 us -> 10.8 us  [exchange(): return lax.all_to_all(value, 'shard', 0, 0, tiled=True)]
    ppermute x12 -> x8, waiting for transfers between devices: 1.72 us -> 4.41 us  [swaps(): moved[step] = lax.ppermute(by_step[step], 'shard', pairs)]
    all_to_all x2, waiting for transfers between devices: 14.5 us -> 11.8 us  [exchange(): return lax.all_to_all(value, 'shard', 0, 0, tiled=True)]
    pallas_call x11 -> x10, Pallas kernels: 41.7 us -> 41.9 us  [call(): pl.pallas_call(kernel, out_shape=[jax.ShapeDtypeStruct(s, d) for s, d in...]
  transfers between devices with their start and end apart: 16 -> 12, of which waited for: 6 -> 7; matrix products, arithmetic and copies ran while one was open for 0% -> 0% of each run, Pallas kernels for 24% -> 29%
where the time goes in v12:
time: 87.8 us; the launch traced here: 86.7 us
  Pallas kernels  41.9 us (48%)
  starting transfers between devices  23.9 us (27%)
  waiting for transfers between devices  18.9 us (22%)
  between operations  1.04 us (1%)
  local copies, waits for them, and re-layouts  1 us (1%)
    pallas_call x10, Pallas kernels, call(): pl.pallas_call(kernel, out_shape=[jax.ShapeDtypeStruct(s, d) for s, d in...  41.9 us
    ppermute x8, starting transfers between devices, swaps(): moved[step] = lax.ppermute(by_step[step], 'shard', pairs)  12.3 us
    all_to_all x2, waiting for transfers between devices, exchange(): return lax.all_to_all(value, 'shard', 0, 0, tiled=True)  11.8 us
    all_to_all x2, starting transfers between devices, exchange(): return lax.all_to_all(value, 'shard', 0, 0, tiled=True)  10.8 us
    ppermute x8, waiting for transfers between devices, swaps(): moved[step] = lax.ppermute(by_step[step], 'shard', pairs)  4.41 us
    ppermute x2, waiting for transfers between devices, swap_cores(): lax.ppermute(value, 'shard', [(i, i + 1 - 2 * (i % 2)) for i in range(dev...  2.62 us
  transfers between devices with their start and end apart: 12, of which 7 were waited for; matrix products, arithmetic and copies ran while one was open for 0% of the time, Pallas kernels for 29%

profile of v12, /device:TPU:1, one launch (start us, length us, event | category | flops | bytes accessed | tf_op | source)
XLA Modules:
  0.0 86.7 jit_solution(17236221279733967813)
XLA Ops:
  0.6 0.0 copy-start.2
  0.6 0.0 copy-start.4
  0.7 4.3 %shard_map.111 = (bf16[608,128]{1,0:T(8,128)(2,1)}, bf16[608,128]{1,0:T(8,128)(2,1)}, bf16[608,128]{1,0:T(8,128)(2,1)}, bf16[608,128]{1,0:T(8,128)(2,1)}, f32[1024,128]{1,0:T(8,128)}) custom-call(bf16[1024,128]{1,0:T(8,128)(2,1)} %refs_4_.1, s32[4,64]{1,0:T(4,128)} %refs_6_.5, s32[8,256]{1,0:T(8,128)} %refs_8_.1, bf16[256,256]{1,0:T(8,128)(2,1)} %refs_11_.1, ...), custom_call_target="tpu_custom_call" | custom-call | flops 1000000000 | bytes 4194304 | tf_op jit(solution)/shard_map/pallas_call | solution.py:441
  4.9 0.1 collective-permute-start
  5.0 4.5 %collective-permute-start.1 = (bf16[608,128]{1,0:T(8,128)(2,1)}, bf16[608,128]{1,0:T(8,128)(2,1)S(1)}, u32[]{:S(2)}, u32[]{:S(2)}) collective-permute-start(bf16[608,128]{1,0:T(8,128)(2,1)} %get-tuple-element.37), channel_id=1, source_target_pairs={{1,2},{2,1},{3,4},{4,3},{5,6},{6,5},{7,8},{8,7},{9,10},{10,9},{11,... | collective-permute-start | bytes 466952 | tf_op jit(solution)/shard_map/ppermute | solution.py:23
  9.5 1.3 %collective-permute-start.2 = (bf16[608,128]{1,0:T(8,128)(2,1)}, bf16[608,128]{1,0:T(8,128)(2,1)S(1)}, u32[]{:S(2)}, u32[]{:S(2)}) collective-permute-start(bf16[608,128]{1,0:T(8,128)(2,1)} %get-tuple-element.38), channel_id=1, source_target_pairs={{0,2},{1,3},{2,0},{3,1},{4,6},{5,7},{6,4},{7,5},{8,10},{9,11},{10,... | collective-permute-start | bytes 466952 | tf_op jit(solution)/shard_map/ppermute | solution.py:23
  10.8 0.0 copy-start
  10.8 0.0 copy-start.6
  10.8 0.8 collective-permute-start.3
  11.6 0.0 copy-done.2
  11.6 0.0 copy-done.4
  11.6 7.3 %shard_map.112.refs_8_ = bf16[1024,3328]{1,0:T(8,128)(2,1)S(1)} custom-call(bf16[1024,128]{1,0:T(8,128)(2,1)S(1)} %copy-done.2, s32[27,1024]{1,0:T(8,128)S(1)} %copy-done.4), custom_call_target="tpu_custom_call" | custom-call | flops 4000000000 | bytes 4194304 | tf_op jit(solution)/shard_map/pallas_call | solution.py:441
  18.9 0.0 copy-start.3
  18.9 0.0 copy-start.5
  19.0 0.0 copy-start.8
  19.0 0.0 collective-permute-done.refs_0_
  19.0 0.0 collective-permute-done.1.refs_1_
  19.0 1.3 %collective-permute-done.2.refs_2_ = bf16[608,128]{1,0:T(8,128)(2,1)S(1)} collective-permute-done((bf16[608,128]{1,0:T(8,128)(2,1)}, bf16[608,128]{1,0:T(8,128)(2,1)S(1)}, u32[]{:S(2)}, u32[]{:S(2)}) %collective-permute-start.2) | collective-permute-done | bytes 155680 | tf_op jit(solution)/shard_map/ppermute | solution.py:23
  20.3 0.0 collective-permute-done.3.refs_3_
  20.3 0.0 copy-done
  20.3 0.0 copy-done.6
  20.3 6.6 %shard_map.113 = (bf16[1024,128]{1,0:T(8,128)(2,1)S(1)}, f32[1024,128]{1,0:T(8,128)S(1)}, bf16[1024,3456]{1,0:T(8,128)(2,1)S(1)}, bf16[128,128]{1,0:T(8,128)(2,1)S(1)}) custom-call(bf16[608,128]{1,0:T(8,128)(2,1)S(1)} %collective-permute-done.refs_0_, bf16[608,128]{1,0:T(8,128)(2,1)S(1)} %collective-permute-done.1.refs_1_, ...), custom_call_target="tpu_custom_call" | custom-call | flops 12000000000 | bytes 4194304 | tf_op jit(solution)/shard_map/pallas_call | solution.py:441
  26.9 0.0 copy-done.3
  26.9 0.0 copy-done.5
  26.9 0.0 copy-done.8
  27.0 2.6 %shard_map.114 = (f32[1024,128]{1,0:T(8,128)S(1)}, bf16[1024,128]{1,0:T(8,128)(2,1)S(1)}, bf16[256,1024]{1,0:T(8,128)(2,1)S(1)}, bf16[5632,128]{1,0:T(8,128)(2,1)S(1)}, bf16[2816,128]{1,0:T(8,128)(2,1)S(1)}) custom-call(bf16[608,128]{1,0:T(8,128)(2,1)S(1)} %collective-permute-done.refs_0_, bf16[608,128]{1,0:T(8,128)(2,1)S(1)} %collective-permute-done.1.refs_1_, ...), custom_call_target="tpu_custom_call" | custom-call | flops 3000000000 | bytes 4194304 | tf_op jit(solution)/shard_map/pallas_call | solution.py:441
  29.5 0.0 copy-start.9
  29.6 0.1 collective-permute-start.4
  29.6 2.2 %collective-permute-done.4.other_ref = bf16[2816,128]{1,0:T(8,128)(2,1)S(1)} collective-permute-done((bf16[2816,128]{1,0:T(8,128)(2,1)S(1)}, bf16[2816,128]{1,0:T(8,128)(2,1)S(1)}, u32[]{:S(2)}, u32[]{:S(2)}) %collective-permute-start.4) | collective-permute-done | bytes 720928 | tf_op jit(solution)/shard_map/ppermute | solution.py:454
  31.8 1.1 %shard_map.115.after_ref = bf16[2816,128]{1,0:T(8,128)(2,1)} custom-call(bf16[5632,128]{1,0:T(8,128)(2,1)S(1)} %get-tuple-element.45.terms_ref, bf16[2816,128]{1,0:T(8,128)(2,1)S(1)} %collective-permute-done.4.other_ref), custom_call_target="tpu_custom_call" | custom-call | flops 1000000 | bytes 4194304 | tf_op jit(solution)/shard_map/pallas_call | solution.py:441
  32.9 0.0 copy-done.9
  32.9 6.9 %all-to-all-start = ((bf16[32,88,128]{2,1,0:T(8,128)(2,1)}), bf16[32,88,128]{2,1,0:T(8,128)(2,1)S(1)}, u32[]{:S(2)}, u32[]{:S(2)}) async-start(bf16[32,88,128]{2,1,0:T(8,128)(2,1)} %bitcast), calls=%async_computation | async-start | bytes 1441792 | tf_op jit(solution)/shard_map/all_to_all | solution.py:458
  39.8 0.0 copy-start.10
  39.8 0.9 %copy-done.10 = bf16[1024,128]{1,0:T(8,128)(2,1)S(1)} copy-done((bf16[1024,128]{1,0:T(8,128)(2,1)S(1)}, bf16[1024,128]{1,0:T(8,128)(2,1)}, u32[]{:S(2)}) %copy-start.10) | copy-done | bytes 262168
  40.8 14.9 %shard_map.116 = (f32[1024,128]{1,0:T(8,128)S(1)}, bf16[96,128]{1,0:T(8,128)(2,1)S(1)}, bf16[96,128]{1,0:T(8,128)(2,1)S(1)}, bf16[96,128]{1,0:T(8,128)(2,1)S(1)}, bf16[96,128]{1,0:T(8,128)(2,1)S(1)}) custom-call(bf16[1024,128]{1,0:T(8,128)(2,1)S(1)} %copy-done.10, s32[27,1024]{1,0:T(8,128)S(1)} %copy-done.4, bf16[27,128,128]{2,1,0:T(8,128)(2,1)S(1)} %copy-done, ...), custom_call_target="tpu_custom_call" | custom-call | flops 20000000000 | bytes 4194304 | tf_op jit(solution)/shard_map/pallas_call | solution.py:441
  55.7 0.0 copy-start.1
  55.7 0.0 copy-start.7
  55.7 3.0 %all-to-all-done = bf16[32,88,128]{2,1,0:T(8,128)(2,1)S(1)} async-done(((bf16[32,88,128]{2,1,0:T(8,128)(2,1)}), bf16[32,88,128]{2,1,0:T(8,128)(2,1)S(1)}, u32[]{:S(2)}, u32[]{:S(2)}) %all-to-all-start) | async-done | bytes 720928 | tf_op jit(solution)/shard_map/all_to_all | solution.py:458
  58.8 1.0 %shard_map.117 = bf16[2816,128]{1,0:T(8,128)(2,1)} custom-call(bf16[2816,128]{1,0:T(8,128)(2,1)S(1)} %bitcast.8, bf16[96,128]{1,0:T(8,128)(2,1)S(1)} %get-tuple-element.52.after_ref), custom_call_target="tpu_custom_call" | custom-call | flops 1000000 | bytes 4194304 | tf_op jit(solution)/shard_map/pallas_call | solution.py:441
  59.7 3.9 %all-to-all-start.1 = ((bf16[32,88,128]{2,1,0:T(8,128)(2,1)}), bf16[32,88,128]{2,1,0:T(8,128)(2,1)S(1)}, u32[]{:S(2)}, u32[]{:S(2)}) async-start(bf16[32,88,128]{2,1,0:T(8,128)(2,1)} %bitcast.2), calls=%async_computation.1 | async-start | bytes 1441792 | tf_op jit(solution)/shard_map/all_to_all | solution.py:458
  63.6 0.3 collective-permute-start.5
  63.9 3.4 %collective-permute-start.6 = (bf16[96,128]{1,0:T(8,128)(2,1)S(1)}, bf16[96,128]{1,0:T(8,128)(2,1)S(1)}, u32[]{:S(2)}, u32[]{:S(2)}) collective-permute-start(bf16[96,128]{1,0:T(8,128)(2,1)S(1)} %get-tuple-element.53), channel_id=1, source_target_pairs={{1,2},{2,1},{3,4},{4,3},{5,6},{6,5},{7,8},{8,7},{9,10},{10,9},{11,... | collective-permute-start | bytes 73736 | tf_op jit(solution)/shard_map/ppermute | solution.py:23
  67.4 1.2 %collective-permute-start.7 = (bf16[96,128]{1,0:T(8,128)(2,1)S(1)}, bf16[96,128]{1,0:T(8,128)(2,1)S(1)}, u32[]{:S(2)}, u32[]{:S(2)}) collective-permute-start(bf16[96,128]{1,0:T(8,128)(2,1)S(1)} %get-tuple-element.54), channel_id=1, source_target_pairs={{0,2},{1,3},{2,0},{3,1},{4,6},{5,7},{6,4},{7,5},{8,10},{9,11},{10,... | collective-permute-start | bytes 73736 | tf_op jit(solution)/shard_map/ppermute | solution.py:23
  68.6 0.7 collective-permute-start.8
  69.3 0.0 collective-permute-done.5.refs_0_
  69.3 0.1 collective-permute-done.6.refs_1_
  69.4 2.9 %collective-permute-done.7.refs_2_ = bf16[96,128]{1,0:T(8,128)(2,1)S(1)} collective-permute-done((bf16[96,128]{1,0:T(8,128)(2,1)S(1)}, bf16[96,128]{1,0:T(8,128)(2,1)S(1)}, u32[]{:S(2)}, u32[]{:S(2)}) %collective-permute-start.7) | collective-permute-done | bytes 24608 | tf_op jit(solution)/shard_map/ppermute | solution.py:23
  72.3 0.0 collective-permute-done.8.refs_3_
  72.3 0.0 copy-done.1
  72.3 0.0 copy-done.7
  72.3 1.5 %shard_map.118 = (f32[1024,128]{1,0:T(8,128)}, bf16[256,256]{1,0:T(8,128)(2,1)}) custom-call(bf16[96,128]{1,0:T(8,128)(2,1)S(1)} %collective-permute-done.5.refs_0_, bf16[96,128]{1,0:T(8,128)(2,1)S(1)} %collective-permute-done.6.refs_1_, bf16[96,128]{1,0:T(8,128)(2,1)S(1)} %collective-permute-done.7.refs_2_, ...), custom_call_target="tpu_custom_call" | custom-call | flops 1000000000 | bytes 4194304 | tf_op jit(solution)/shard_map/pallas_call | solution.py:441
  73.8 8.8 %all-to-all-done.1 = bf16[32,88,128]{2,1,0:T(8,128)(2,1)S(1)} async-done(((bf16[32,88,128]{2,1,0:T(8,128)(2,1)}), bf16[32,88,128]{2,1,0:T(8,128)(2,1)S(1)}, u32[]{:S(2)}, u32[]{:S(2)}) %all-to-all-start.1) | async-done | bytes 720928 | tf_op jit(solution)/shard_map/all_to_all | solution.py:458
  82.6 0.8 collective-permute-start.9
  83.3 1.4 %shard_map.119 = (f32[3456,128]{1,0:T(8,128)}, f32[1024,256]{1,0:T(8,128)}) custom-call(bf16[2816,128]{1,0:T(8,128)(2,1)S(1)} %bitcast.7), custom_call_target="tpu_custom_call" | custom-call | flops 1000000 | bytes 4194304 | tf_op jit(solution)/shard_map/pallas_call | solution.py:441
  84.7 0.4 collective-permute-done.9.refs_0_
  85.2 1.4 %shard_map.120 = (f32[3456,128]{1,0:T(8,128)}, f32[1024,256]{1,0:T(8,128)}) custom-call(bf16[2816,128]{1,0:T(8,128)(2,1)S(1)} %collective-permute-done.9.refs_0_, f32[3456,128]{1,0:T(8,128)} %get-tuple-element.64.refs_1_, f32[1024,256]{1,0:T(8,128)} %get-tuple-element.65.refs_2_), custom_call_target="tpu_custom_call", output_to_operand_aliasing={{0}: (1, {}), {1}: (2, {})} | custom-call | flops 1000000 | bytes 4194304 | tf_op jit(solution)/shard_map/pallas_call | solution.py:441
Async XLA Ops:
  0.6 11.0 %copy-start.2 = (bf16[1024,128]{1,0:T(8,128)(2,1)S(1)}, bf16[1024,128]{1,0:T(8,128)(2,1)}, u32[]{:S(2)}) copy-start(bf16[1024,128]{1,0:T(8,128)(2,1)} %refs_4_.1) | copy-start | bytes 786436
  0.6 11.0 %copy-start.4 = (s32[27,1024]{1,0:T(8,128)S(1)}, s32[27,1024]{1,0:T(8,128)}, u32[]{:S(2)}) copy-start(s32[27,1024]{1,0:T(8,128)} %map_ref.3) | copy-start | bytes 331780
  4.9 14.0 %collective-permute-start = (bf16[608,128]{1,0:T(8,128)(2,1)}, bf16[608,128]{1,0:T(8,128)(2,1)S(1)}, u32[]{:S(2)}, u32[]{:S(2)}) collective-permute-start(bf16[608,128]{1,0:T(8,128)(2,1)} %get-tuple-element.36), channel_id=1, source_target_pairs={{0,1},{1,0},{2,3},{3,2},{4,5},{5,4},{6,7},{7,6},{8,9},{9,8},{10,11... | collective-permute-start | bytes 466952 | tf_op jit(solution)/shard_map/ppermute | solution.py:23
  5.0 13.9 %collective-permute-start.1 = (bf16[608,128]{1,0:T(8,128)(2,1)}, bf16[608,128]{1,0:T(8,128)(2,1)S(1)}, u32[]{:S(2)}, u32[]{:S(2)}) collective-permute-start(bf16[608,128]{1,0:T(8,128)(2,1)} %get-tuple-element.37), channel_id=1, source_target_pairs={{1,2},{2,1},{3,4},{4,3},{5,6},{6,5},{7,8},{8,7},{9,10},{10,9},{11,... | collective-permute-start | bytes 466952 | tf_op jit(solution)/shard_map/ppermute | solution.py:23
  9.5 10.8 %collective-permute-start.2 = (bf16[608,128]{1,0:T(8,128)(2,1)}, bf16[608,128]{1,0:T(8,128)(2,1)S(1)}, u32[]{:S(2)}, u32[]{:S(2)}) collective-permute-start(bf16[608,128]{1,0:T(8,128)(2,1)} %get-tuple-element.38), channel_id=1, source_target_pairs={{0,2},{1,3},{2,0},{3,1},{4,6},{5,7},{6,4},{7,5},{8,10},{9,11},{10,... | collective-permute-start | bytes 466952 | tf_op jit(solution)/shard_map/ppermute | solution.py:23
  10.8 9.5 %copy-start = (bf16[27,128,128]{2,1,0:T(8,128)(2,1)S(1)}, bf16[27,128,128]{2,1,0:T(8,128)(2,1)}, u32[]{:S(2)}) copy-start(bf16[27,128,128]{2,1,0:T(8,128)(2,1)} %weight_ref.1) | copy-start | bytes 2654212
  10.8 9.5 %copy-start.6 = (s32[4,32]{1,0:T(4,128)S(1)}, s32[4,32]{1,0:T(4,128)}, u32[]{:S(2)}) copy-start(s32[4,32]{1,0:T(4,128)} %refs_6_.4) | copy-start | bytes 1540
  10.8 9.5 %collective-permute-start.3 = (bf16[608,128]{1,0:T(8,128)(2,1)}, bf16[608,128]{1,0:T(8,128)(2,1)S(1)}, u32[]{:S(2)}, u32[]{:S(2)}) collective-permute-start(bf16[608,128]{1,0:T(8,128)(2,1)} %get-tuple-element.39), channel_id=1, source_target_pairs={{2,4},{3,5},{4,2},{5,3},{6,8},{7,9},{8,6},{9,7},{10,12},{11,13},{1... | collective-permute-start | bytes 466952 | tf_op jit(solution)/shard_map/ppermute | solution.py:23
  18.9 8.0 %copy-start.3 = (bf16[256,256]{1,0:T(8,128)(2,1)S(1)}, bf16[256,256]{1,0:T(8,128)(2,1)}, u32[]{:S(2)}) copy-start(bf16[256,256]{1,0:T(8,128)(2,1)} %refs_11_.1) | copy-start | bytes 393220
  18.9 8.0 %copy-start.5 = (s32[8,256]{1,0:T(8,128)S(1)}, s32[8,256]{1,0:T(8,128)}, u32[]{:S(2)}) copy-start(s32[8,256]{1,0:T(8,128)} %refs_8_.1) | copy-start | bytes 24580
  19.0 8.0 %copy-start.8 = (f32[1024,128]{1,0:T(8,128)S(1)}, f32[1024,128]{1,0:T(8,128)}, u32[]{:S(2)}) copy-start(f32[1024,128]{1,0:T(8,128)} %get-tuple-element.42.refs_7_) | copy-start | bytes 1572868
  29.5 3.3 %copy-start.9 = (bf16[1024,128]{1,0:T(8,128)(2,1)}, bf16[1024,128]{1,0:T(8,128)(2,1)S(1)}, u32[]{:S(2)}) copy-start(bf16[1024,128]{1,0:T(8,128)(2,1)S(1)} %get-tuple-element.47.pgrad_ref) | copy-start | bytes 786436
  29.6 2.3 %collective-permute-start.4 = (bf16[2816,128]{1,0:T(8,128)(2,1)S(1)}, bf16[2816,128]{1,0:T(8,128)(2,1)S(1)}, u32[]{:S(2)}, u32[]{:S(2)}) collective-permute-start(bf16[2816,128]{1,0:T(8,128)(2,1)S(1)} %get-tuple-element.46), channel_id=1, source_target_pairs={{0,1},{1,0},{2,3},{3,2},{4,5},{5,4},{6,7},{7,6},{8,9},{9,8},{10,11... | collective-permute-start | bytes 2162696 | tf_op jit(solution)/shard_map/ppermute | solution.py:454
  32.9 25.9 %all-to-all-start = ((bf16[32,88,128]{2,1,0:T(8,128)(2,1)}), bf16[32,88,128]{2,1,0:T(8,128)(2,1)S(1)}, u32[]{:S(2)}, u32[]{:S(2)}) async-start(bf16[32,88,128]{2,1,0:T(8,128)(2,1)} %bitcast), calls=%async_computation | async-start | bytes 1441792 | tf_op jit(solution)/shard_map/all_to_all | solution.py:458
  39.8 1.0 %copy-start.10 = (bf16[1024,128]{1,0:T(8,128)(2,1)S(1)}, bf16[1024,128]{1,0:T(8,128)(2,1)}, u32[]{:S(2)}) copy-start(bf16[1024,128]{1,0:T(8,128)(2,1)} %copy-done.9) | copy-start | bytes 786436
  55.7 16.6 %copy-start.1 = (bf16[8,128,256]{2,1,0:T(8,128)(2,1)S(1)}, bf16[8,128,256]{2,1,0:T(8,128)(2,1)}, u32[]{:S(2)}) copy-start(bf16[8,128,256]{2,1,0:T(8,128)(2,1)} %refs_9_.1) | copy-start | bytes 1572868
  55.7 16.6 %copy-start.7 = (s32[4,64]{1,0:T(4,128)S(1)}, s32[4,64]{1,0:T(4,128)}, u32[]{:S(2)}) copy-start(s32[4,64]{1,0:T(4,128)} %refs_6_.5) | copy-start | bytes 3076
  59.7 22.8 %all-to-all-start.1 = ((bf16[32,88,128]{2,1,0:T(8,128)(2,1)}), bf16[32,88,128]{2,1,0:T(8,128)(2,1)S(1)}, u32[]{:S(2)}, u32[]{:S(2)}) async-start(bf16[32,88,128]{2,1,0:T(8,128)(2,1)} %bitcast.2), calls=%async_computation.1 | async-start | bytes 1441792 | tf_op jit(solution)/shard_map/all_to_all | solution.py:458
  63.6 5.7 %collective-permute-start.5 = (bf16[96,128]{1,0:T(8,128)(2,1)S(1)}, bf16[96,128]{1,0:T(8,128)(2,1)S(1)}, u32[]{:S(2)}, u32[]{:S(2)}) collective-permute-start(bf16[96,128]{1,0:T(8,128)(2,1)S(1)} %get-tuple-element.52.after_ref), channel_id=1, source_target_pairs={{0,1},{1,0},{2,3},{3,2},{4,5},{5,4},{6,7},{7,6},{8,9},{9,8},{10,11... | collective-permute-start | bytes 73736 | tf_op jit(solution)/shard_map/ppermute | solution.py:23
  63.9 5.5 %collective-permute-start.6 = (bf16[96,128]{1,0:T(8,128)(2,1)S(1)}, bf16[96,128]{1,0:T(8,128)(2,1)S(1)}, u32[]{:S(2)}, u32[]{:S(2)}) collective-permute-start(bf16[96,128]{1,0:T(8,128)(2,1)S(1)} %get-tuple-element.53), channel_id=1, source_target_pairs={{1,2},{2,1},{3,4},{4,3},{5,6},{6,5},{7,8},{8,7},{9,10},{10,9},{11,... | collective-permute-start | bytes 73736 | tf_op jit(solution)/shard_map/ppermute | solution.py:23
  67.4 5.0 %collective-permute-start.7 = (bf16[96,128]{1,0:T(8,128)(2,1)S(1)}, bf16[96,128]{1,0:T(8,128)(2,1)S(1)}, u32[]{:S(2)}, u32[]{:S(2)}) collective-permute-start(bf16[96,128]{1,0:T(8,128)(2,1)S(1)} %get-tuple-element.54), channel_id=1, source_target_pairs={{0,2},{1,3},{2,0},{3,1},{4,6},{5,7},{6,4},{7,5},{8,10},{9,11},{10,... | collective-permute-start | bytes 73736 | tf_op jit(solution)/shard_map/ppermute | solution.py:23
  68.6 3.7 %collective-permute-start.8 = (bf16[96,128]{1,0:T(8,128)(2,1)S(1)}, bf16[96,128]{1,0:T(8,128)(2,1)S(1)}, u32[]{:S(2)}, u32[]{:S(2)}) collective-permute-start(bf16[96,128]{1,0:T(8,128)(2,1)S(1)} %get-tuple-element.55), channel_id=1, source_target_pairs={{2,4},{3,5},{4,2},{5,3},{6,8},{7,9},{8,6},{9,7},{10,12},{11,13},{1... | collective-permute-start | bytes 73736 | tf_op jit(solution)/shard_map/ppermute | solution.py:23
  82.6 2.6 %collective-permute-start.9 = (bf16[2816,128]{1,0:T(8,128)(2,1)S(1)}, bf16[2816,128]{1,0:T(8,128)(2,1)S(1)}, u32[]{:S(2)}, u32[]{:S(2)}) collective-permute-start(bf16[2816,128]{1,0:T(8,128)(2,1)S(1)} %bitcast.6), channel_id=1, source_target_pairs={{0,1},{1,0},{2,3},{3,2},{4,5},{5,4},{6,7},{7,6},{8,9},{9,8},{10,11... | collective-permute-start | bytes 2162696 | tf_op jit(solution)/shard_map/ppermute | solution.py:454

commit v13 on v12

--- a/solution.py
+++ b/solution.py
@@ -141,7 +141,6 @@
     octants = child_map_ref.shape[0]
     cap2 = sends[0].shape[0] - cap
     cap2 //= 1 + octants * out_grad_ref.shape[1] // LANES
-    table_rows = voxels + slots * cap2
     copies[0].wait()
     copies[1].wait()
     listed = gather_lists(halo_ref, features_ref[...]).astype(BF16)
@@ -150,20 +149,29 @@
     for copy in copies[2:]:
         copy.wait()
     upstream = out_grad_ref[...]
-    codes = encode(child_map_ref[...]).astype(BF16)
-    choosers, parts = [], []
+    rows = child_map_ref[...]
+    codes = half_codes(rows, voxels, slots * cap2)
+    half = voxels // 2
+    choosers, sides = [], []
     for o in range(octants):
-        part = matmul_rt(upstream, down_ref[o])
-        high = part.astype(BF16)
-        low = (part - high.astype(F32)).astype(BF16)
-        choosers.append(one_hot_columns(codes[o : o + 1, :], table_rows))
-        parts.append(jnp.concatenate([high, low], axis=1))
-    both = matmul(jnp.concatenate(choosers, axis=1), jnp.concatenate(parts, axis=0))
-    total = both[:, :LANES] + both[:, LANES:]
-    back_ref[...] = total[:voxels]
-    for send, block in zip(sends, to_steps(jnp.split(total[voxels:].astype(BF16), slots), True)):
+        part = matmul_rt(upstream, down_ref[o]).astype(BF16)
+        code = codes[o : o + 1, :].astype(BF16)
+        right = column(code) < jnp.zeros(part.shape, BF16)
+        none = jnp.zeros(part.shape, BF16)
+        pair = [jnp.where(right, none, part), jnp.where(right, part, none)]
+        sides.append(jnp.concatenate(pair, axis=1))
+        choosers.append(one_hot_columns(jnp.abs(code), half + slots * cap2 // 2))
+    both = matmul(jnp.concatenate(choosers, axis=1), jnp.concatenate(sides, axis=0))
+    back_ref[0:half, :] = both[0:half, :LANES]
+    back_ref[half:, :] = both[0:half, LANES:]
+    far = jnp.concatenate([both[half:, :LANES], both[half:, LANES:]], axis=0).astype(BF16)
+    for send, block in zip(sends, to_steps(jnp.split(far, slots), True)):
         send[cap : cap + cap2, :] = block
-    sums = [matmul(chooser[voxels:], upstream).astype(BF16) for chooser in choosers]
+    codes = encode(jnp.where(rows >= voxels, rows - voxels, slots * cap2)).astype(BF16)
+    sums = []
+    for o in range(octants):
+        chooser = one_hot_columns(codes[o : o + 1, :], slots * cap2)
+        sums.append(matmul(chooser, upstream).astype(BF16))
     blocks = []
     for s in range(slots):
         rows = slice(s * cap2, (s + 1) * cap2)
@@ -216,9 +224,13 @@
 def forward_kernel(slots, cap, *refs):
     received = refs[:slots]
     features_ref, map_ref, weight_ref, child_ref, early_ref = refs[slots : slots + 5]
-    hidden_ref, pre_ref, stacked_ref, leaving_ref, halo_ref, kernel_ref = refs[slots + 5 :]
+    back_ref, child_map_ref, out_grad_ref = refs[slots + 5 : slots + 8]
+    leaving_ref, hgrad_ref, pgrad_ref, early_h_ref, terms_ref, send_ref = refs[slots + 8 : slots + 14]
+    stacked_ref, halo_ref, kernel_ref = refs[slots + 14 :]
+    cap2 = child_ref.shape[1]
+    kernel_count = map_ref.shape[0]
     voxels = features_ref.shape[0]
-    gathers = map_ref.shape[0] - 1
+    gathers = kernel_count - 1
     middle = gathers // 2
     half, half_halo = voxels // 2, slots * cap // 2
     features = features_ref[...]
@@ -245,25 +257,14 @@
 
     stacked_ref[:, gathers * LANES :] = features
     pre = matmul(stacked_ref[...], kernel_ref[...].reshape(-1, LANES))
-    pre_ref[...] = pre
-    hidden = (features.astype(F32) + pre * jax.nn.sigmoid(pre)).astype(BF16)
-    hidden_ref[...] = hidden
-    leaving_ref[...] = gather_lists(child_ref, hidden).astype(BF16)
-
-
-def gradient_kernel(slots, cap, *refs):
-    received = refs[:slots]
-    stacked_ref, pre_ref, child_ref, back_ref = refs[slots : slots + 4]
-    hidden_ref, leaving_ref, child_map_ref, out_grad_ref = refs[slots + 4 : slots + 8]
-    hgrad_ref, pgrad_ref, early_ref, terms_ref, send_ref = refs[slots + 8 :]
-    cap2 = child_ref.shape[1]
-    kernel_count = stacked_ref.shape[1] // LANES
-    middle = kernel_count // 2
+    sig = jax.nn.sigmoid(pre)
+    hidden = (features.astype(F32) + pre * sig).astype(BF16)
+    leaving = gather_lists(child_ref, hidden).astype(BF16)
+    leaving_ref[...] = leaving
+
     blocks = to_slots([r[cap : cap + cap2, :] for r in received], True)
     hgrad = add_lists(back_ref[...], child_ref, blocks)
     hgrad_ref[...] = hgrad
-    pre = pre_ref[...]
-    sig = jax.nn.sigmoid(pre)
     pgrad = hgrad * (sig * (1.0 + pre * (1.0 - sig)))
     pgrad_ref[...] = pgrad.astype(BF16)
     terms = matmul(jnp.transpose(pgrad).astype(BF16), stacked_ref[...])
@@ -271,9 +272,6 @@
     for n, k in enumerate(order):
         block = jnp.transpose(terms[:, n * LANES : (n + 1) * LANES])
         terms_ref[k * LANES : (k + 1) * LANES, :] = block.astype(BF16)
-    voxels = hidden_ref.shape[0]
-    half = voxels // 2
-    hidden = hidden_ref[...]
     table = jnp.concatenate([hidden[0:half], hidden[half:]], axis=1)
     octants = child_map_ref.shape[0]
     picked = []
@@ -282,7 +280,7 @@
         both = matmul(one_hot_rows(jnp.abs(col), half), table).astype(BF16)
         picked.append(pick_side(col, both))
     picked = jnp.concatenate(picked, axis=1)
-    early_ref[...] = picked
+    early_h_ref[...] = picked
     upstream_t = jnp.transpose(out_grad_ref[...].astype(F32)).astype(BF16)
     own = matmul(upstream_t, picked)
     blocks = to_slots([r[cap + cap2 :, :] for r in received], True)
@@ -291,7 +289,7 @@
     for n in range(octants * across):
         rows = slice(n * cap2, (n + 1) * cap2)
         sums.append(jnp.concatenate([block[rows, :] for block in blocks], axis=0))
-    leaving_t = jnp.transpose(leaving_ref[...].astype(F32)).astype(BF16)
+    leaving_t = jnp.transpose(leaving.astype(F32)).astype(BF16)
     far = matmul(leaving_t, jnp.concatenate(sums, axis=1))
     row = kernel_count * LANES
     for n in range(octants * across):
@@ -498,42 +496,33 @@
         scratch=[pltpu.VMEM((voxels // 2, 2 * channels), BF16)],
         flops=4 * giga,
     )
-    hidden, pre_act, stacked, leaving = call(
+    leaving, hidden_grad, pre_grad, early_h, terms, leaving_terms = call(
         functools.partial(forward_kernel, slots, cap),
-        (*received, features, neighbour_map, conv_weight, child_rows, early),
-        [
-            ((voxels, channels), BF16),
-            ((voxels, channels), F32),
-            ((voxels, conv_rows), BF16),
-            ((slots * cap2, channels), BF16),
-        ],
-        scratch=[
-            pltpu.VMEM((slots * cap, 4 * channels), BF16),
-            pltpu.VMEM(conv_weight.shape, BF16),
-        ],
-        flops=12 * giga,
-    )
-    hidden_grad, pre_grad, early_h, terms, leaving_terms = call(
-        functools.partial(gradient_kernel, slots, cap),
         (
             *received,
-            stacked,
-            pre_act,
+            features,
+            neighbour_map,
+            conv_weight,
             child_rows,
+            early,
             back_h,
-            hidden,
-            leaving,
             child_map,
             out_grad,
         ),
         [
+            ((slots * cap2, channels), BF16),
             ((voxels, channels), F32),
             ((voxels, channels), BF16),
             ((parents, octants * channels), BF16),
             ((2 * half_rows, LANES), BF16),
             ((half_rows, LANES), BF16),
         ],
-        flops=3 * giga,
+        scratch=[
+            pltpu.VMEM((voxels, conv_rows), BF16),
+            pltpu.VMEM((slots * cap, 4 * channels), BF16),
+            pltpu.VMEM(conv_weight.shape, BF16),
+        ],
+        flops=15 * giga,
     )
     (pair_terms,) = call(
         pair_kernel,

time: 87.8 us -> 89.6 us (1.021)
  Pallas kernels: 41.9 us -> 43.6 us
    pallas_call x10 -> x9, Pallas kernels: 41.9 us -> 43.6 us  [call(): pl.pallas_call(kernel, out_shape=[jax.ShapeDtypeStruct(s, d) for s, d in...]
  transfers between devices with their start and end apart: 12 -> 12, of which waited for: 7 -> 7; matrix products, arithmetic and copies ran while one was open for 0% -> 0% of each run, Pallas kernels for 29% -> 28%
where the time goes in v13:
time: 89.6 us; the launch traced here: 88.5 us
  Pallas kernels  43.6 us (49%)
  starting transfers between devices  24 us (27%)
  waiting for transfers between devices  18.9 us (21%)
  between operations  1.02 us (1%)
  local copies, waits for them, and re-layouts  0.99 us (1%)
    pallas_call x9, Pallas kernels, call(): pl.pallas_call(kernel, out_shape=[jax.ShapeDtypeStruct(s, d) for s, d in...  43.6 us
    ppermute x8, starting transfers between devices, swaps(): moved[step] = lax.ppermute(by_step[step], 'shard', pairs)  12.3 us
    all_to_all x2, waiting for transfers between devices, exchange(): return lax.all_to_all(value, 'shard', 0, 0, tiled=True)  11.8 us
    all_to_all x2, starting transfers between devices, exchange(): return lax.all_to_all(value, 'shard', 0, 0, tiled=True)  10.8 us
    ppermute x8, waiting for transfers between devices, swaps(): moved[step] = lax.ppermute(by_step[step], 'shard', pairs)  4.42 us
    ppermute x2, waiting for transfers between devices, swap_cores(): lax.ppermute(value, 'shard', [(i, i + 1 - 2 * (i % 2)) for i in range(dev...  2.62 us
  transfers between devices with their start and end apart: 12, of which 7 were waited for; matrix products, arithmetic and copies ran while one was open for 0% of the time, Pallas kernels for 28%

profile of v13, /device:TPU:1, one launch (start us, length us, event | category | flops | bytes accessed | tf_op | source)
XLA Modules:
  0.0 88.5 jit_solution(9029551917353729013)
XLA Ops:
  0.6 0.0 copy-start.2
  0.6 0.0 copy-start.4
  0.7 3.7 %shard_map.111 = (bf16[608,128]{1,0:T(8,128)(2,1)}, bf16[608,128]{1,0:T(8,128)(2,1)}, bf16[608,128]{1,0:T(8,128)(2,1)}, bf16[608,128]{1,0:T(8,128)(2,1)}, f32[1024,128]{1,0:T(8,128)}) custom-call(bf16[1024,128]{1,0:T(8,128)(2,1)} %refs_4_.1, s32[4,64]{1,0:T(4,128)} %refs_6_.3, s32[8,256]{1,0:T(8,128)} %refs_8_.1, bf16[256,256]{1,0:T(8,128)(2,1)} %refs_11_.1, ...), custom_call_target="tpu_custom_call" | custom-call | flops 1000000000 | bytes 4194304 | tf_op jit(solution)/shard_map/pallas_call | solution.py:439
  4.4 0.1 collective-permute-start
  4.5 4.5 %collective-permute-start.1 = (bf16[608,128]{1,0:T(8,128)(2,1)}, bf16[608,128]{1,0:T(8,128)(2,1)S(1)}, u32[]{:S(2)}, u32[]{:S(2)}) collective-permute-start(bf16[608,128]{1,0:T(8,128)(2,1)} %get-tuple-element.34), channel_id=1, source_target_pairs={{1,2},{2,1},{3,4},{4,3},{5,6},{6,5},{7,8},{8,7},{9,10},{10,9},{11,... | collective-permute-start | bytes 466952 | tf_op jit(solution)/shard_map/ppermute | solution.py:23
  9.0 1.3 %collective-permute-start.2 = (bf16[608,128]{1,0:T(8,128)(2,1)}, bf16[608,128]{1,0:T(8,128)(2,1)S(1)}, u32[]{:S(2)}, u32[]{:S(2)}) collective-permute-start(bf16[608,128]{1,0:T(8,128)(2,1)} %get-tuple-element.35), channel_id=1, source_target_pairs={{0,2},{1,3},{2,0},{3,1},{4,6},{5,7},{6,4},{7,5},{8,10},{9,11},{10,... | collective-permute-start | bytes 466952 | tf_op jit(solution)/shard_map/ppermute | solution.py:23
  10.2 0.0 copy-start
  10.2 0.0 copy-start.3
  10.2 0.0 copy-start.5
  10.2 0.0 copy-start.6
  10.3 0.0 copy-start.8
  10.3 0.8 collective-permute-start.3
  11.1 0.0 copy-done.2
  11.1 0.0 copy-done.4
  11.1 7.3 %shard_map.112.refs_8_ = bf16[1024,3328]{1,0:T(8,128)(2,1)S(1)} custom-call(bf16[1024,128]{1,0:T(8,128)(2,1)S(1)} %copy-done.2, s32[27,1024]{1,0:T(8,128)S(1)} %copy-done.4), custom_call_target="tpu_custom_call" | custom-call | flops 4000000000 | bytes 4194304 | tf_op jit(solution)/shard_map/pallas_call | solution.py:439
  18.4 0.0 collective-permute-done.refs_0_
  18.4 0.0 collective-permute-done.1.refs_1_
  18.4 1.3 %collective-permute-done.2.refs_2_ = bf16[608,128]{1,0:T(8,128)(2,1)S(1)} collective-permute-done((bf16[608,128]{1,0:T(8,128)(2,1)}, bf16[608,128]{1,0:T(8,128)(2,1)S(1)}, u32[]{:S(2)}, u32[]{:S(2)}) %collective-permute-start.2) | collective-permute-done | bytes 155680 | tf_op jit(solution)/shard_map/ppermute | solution.py:23
  19.8 0.0 collective-permute-done.3.refs_3_
  19.8 0.0 copy-done
  19.8 0.0 copy-done.3
  19.8 0.0 copy-done.5
  19.8 0.0 copy-done.6
  19.8 0.0 copy-done.8
  19.8 11.5 %shard_map.113 = (bf16[128,128]{1,0:T(8,128)(2,1)S(1)}, f32[1024,128]{1,0:T(8,128)S(1)}, bf16[1024,128]{1,0:T(8,128)(2,1)S(1)}, bf16[256,1024]{1,0:T(8,128)(2,1)...) custom-call(bf16[608,128]{1,0:T(8,128)(2,1)S(1)} %collective-permute-done.refs_0_, ...), custom_call_target="tpu_custom_call" | custom-call | flops 15000000512 | bytes 4194304 | tf_op jit(solution)/shard_map/pallas_call | solution.py:439
  31.3 0.0 copy-start.9
  31.3 0.1 collective-permute-start.4
  31.4 2.2 %collective-permute-done.4.other_ref = bf16[2816,128]{1,0:T(8,128)(2,1)S(1)} collective-permute-done((bf16[2816,128]{1,0:T(8,128)(2,1)S(1)}, bf16[2816,128]{1,0:T(8,128)(2,1)S(1)}, u32[]{:S(2)}, u32[]{:S(2)}) %collective-permute-start.4) | collective-permute-done | bytes 720928 | tf_op jit(solution)/shard_map/ppermute | solution.py:452
  33.6 1.1 %shard_map.114.after_ref = bf16[2816,128]{1,0:T(8,128)(2,1)} custom-call(bf16[5632,128]{1,0:T(8,128)(2,1)S(1)} %get-tuple-element.38.terms_ref, bf16[2816,128]{1,0:T(8,128)(2,1)S(1)} %collective-permute-done.4.other_ref), custom_call_target="tpu_custom_call" | custom-call | flops 1000000 | bytes 4194304 | tf_op jit(solution)/shard_map/pallas_call | solution.py:439
  34.6 0.0 copy-done.9
  34.6 7.0 %all-to-all-start = ((bf16[32,88,128]{2,1,0:T(8,128)(2,1)}), bf16[32,88,128]{2,1,0:T(8,128)(2,1)S(1)}, u32[]{:S(2)}, u32[]{:S(2)}) async-start(bf16[32,88,128]{2,1,0:T(8,128)(2,1)} %bitcast), calls=%async_computation | async-start | bytes 1441792 | tf_op jit(solution)/shard_map/all_to_all | solution.py:456
  41.6 0.0 copy-start.10
  41.6 0.9 %copy-done.10 = bf16[1024,128]{1,0:T(8,128)(2,1)S(1)} copy-done((bf16[1024,128]{1,0:T(8,128)(2,1)S(1)}, bf16[1024,128]{1,0:T(8,128)(2,1)}, u32[]{:S(2)}) %copy-start.10) | copy-done | bytes 262168
  42.5 14.9 %shard_map.115 = (f32[1024,128]{1,0:T(8,128)S(1)}, bf16[96,128]{1,0:T(8,128)(2,1)S(1)}, bf16[96,128]{1,0:T(8,128)(2,1)S(1)}, bf16[96,128]{1,0:T(8,128)(2,1)S(1)}, bf16[96,128]{1,0:T(8,128)(2,1)S(1)}) custom-call(bf16[1024,128]{1,0:T(8,128)(2,1)S(1)} %copy-done.10, s32[27,1024]{1,0:T(8,128)S(1)} %copy-done.4, bf16[27,128,128]{2,1,0:T(8,128)(2,1)S(1)} %copy-done, ...), custom_call_target="tpu_custom_call" | custom-call | flops 20000000000 | bytes 4194304 | tf_op jit(solution)/shard_map/pallas_call | solution.py:439
  57.5 0.0 copy-start.1
  57.5 0.0 copy-start.7
  57.5 3.1 %all-to-all-done = bf16[32,88,128]{2,1,0:T(8,128)(2,1)S(1)} async-done(((bf16[32,88,128]{2,1,0:T(8,128)(2,1)}), bf16[32,88,128]{2,1,0:T(8,128)(2,1)S(1)}, u32[]{:S(2)}, u32[]{:S(2)}) %all-to-all-start) | async-done | bytes 720928 | tf_op jit(solution)/shard_map/all_to_all | solution.py:456
  60.5 1.0 %shard_map.116 = bf16[2816,128]{1,0:T(8,128)(2,1)} custom-call(bf16[2816,128]{1,0:T(8,128)(2,1)S(1)} %bitcast.8, bf16[96,128]{1,0:T(8,128)(2,1)S(1)} %get-tuple-element.46.after_ref), custom_call_target="tpu_custom_call" | custom-call | flops 1000000 | bytes 4194304 | tf_op jit(solution)/shard_map/pallas_call | solution.py:439
  61.5 3.9 %all-to-all-start.1 = ((bf16[32,88,128]{2,1,0:T(8,128)(2,1)}), bf16[32,88,128]{2,1,0:T(8,128)(2,1)S(1)}, u32[]{:S(2)}, u32[]{:S(2)}) async-start(bf16[32,88,128]{2,1,0:T(8,128)(2,1)} %bitcast.2), calls=%async_computation.1 | async-start | bytes 1441792 | tf_op jit(solution)/shard_map/all_to_all | solution.py:456
  65.4 0.3 collective-permute-start.5
  65.7 3.4 %collective-permute-start.6 = (bf16[96,128]{1,0:T(8,128)(2,1)S(1)}, bf16[96,128]{1,0:T(8,128)(2,1)S(1)}, u32[]{:S(2)}, u32[]{:S(2)}) collective-permute-start(bf16[96,128]{1,0:T(8,128)(2,1)S(1)} %get-tuple-element.47), channel_id=1, source_target_pairs={{1,2},{2,1},{3,4},{4,3},{5,6},{6,5},{7,8},{8,7},{9,10},{10,9},{11,... | collective-permute-start | bytes 73736 | tf_op jit(solution)/shard_map/ppermute | solution.py:23
  69.1 1.2 %collective-permute-start.7 = (bf16[96,128]{1,0:T(8,128)(2,1)S(1)}, bf16[96,128]{1,0:T(8,128)(2,1)S(1)}, u32[]{:S(2)}, u32[]{:S(2)}) collective-permute-start(bf16[96,128]{1,0:T(8,128)(2,1)S(1)} %get-tuple-element.48), channel_id=1, source_target_pairs={{0,2},{1,3},{2,0},{3,1},{4,6},{5,7},{6,4},{7,5},{8,10},{9,11},{10,... | collective-permute-start | bytes 73736 | tf_op jit(solution)/shard_map/ppermute | solution.py:23
  70.4 0.7 collective-permute-start.8
  71.0 0.0 collective-permute-done.5.refs_0_
  71.0 0.1 collective-permute-done.6.refs_1_
  71.2 2.9 %collective-permute-done.7.refs_2_ = bf16[96,128]{1,0:T(8,128)(2,1)S(1)} collective-permute-done((bf16[96,128]{1,0:T(8,128)(2,1)S(1)}, bf16[96,128]{1,0:T(8,128)(2,1)S(1)}, u32[]{:S(2)}, u32[]{:S(2)}) %collective-permute-start.7) | collective-permute-done | bytes 24608 | tf_op jit(solution)/shard_map/ppermute | solution.py:23
  74.1 0.0 collective-permute-done.8.refs_3_
  74.1 0.0 copy-done.1
  74.1 0.0 copy-done.7
  74.1 1.5 %shard_map.117 = (f32[1024,128]{1,0:T(8,128)}, bf16[256,256]{1,0:T(8,128)(2,1)}) custom-call(bf16[96,128]{1,0:T(8,128)(2,1)S(1)} %collective-permute-done.5.refs_0_, bf16[96,128]{1,0:T(8,128)(2,1)S(1)} %collective-permute-done.6.refs_1_, bf16[96,128]{1,0:T(8,128)(2,1)S(1)} %collective-permute-done.7.refs_2_, ...), custom_call_target="tpu_custom_call" | custom-call | flops 1000000000 | bytes 4194304 | tf_op jit(solution)/shard_map/pallas_call | solution.py:439
  75.6 8.8 %all-to-all-done.1 = bf16[32,88,128]{2,1,0:T(8,128)(2,1)S(1)} async-done(((bf16[32,88,128]{2,1,0:T(8,128)(2,1)}), bf16[32,88,128]{2,1,0:T(8,128)(2,1)S(1)}, u32[]{:S(2)}, u32[]{:S(2)}) %all-to-all-start.1) | async-done | bytes 720928 | tf_op jit(solution)/shard_map/all_to_all | solution.py:456
  84.3 0.8 collective-permute-start.9
  85.1 1.4 %shard_map.118 = (f32[3456,128]{1,0:T(8,128)}, f32[1024,256]{1,0:T(8,128)}) custom-call(bf16[2816,128]{1,0:T(8,128)(2,1)S(1)} %bitcast.7), custom_call_target="tpu_custom_call" | custom-call | flops 1000000 | bytes 4194304 | tf_op jit(solution)/shard_map/pallas_call | solution.py:439
  86.5 0.4 collective-permute-done.9.refs_0_
  86.9 1.4 %shard_map.119 = (f32[3456,128]{1,0:T(8,128)}, f32[1024,256]{1,0:T(8,128)}) custom-call(bf16[2816,128]{1,0:T(8,128)(2,1)S(1)} %collective-permute-done.9.refs_0_, f32[3456,128]{1,0:T(8,128)} %get-tuple-element.58.refs_1_, f32[1024,256]{1,0:T(8,128)} %get-tuple-element.59.refs_2_), custom_call_target="tpu_custom_call", output_to_operand_aliasing={{0}: (1, {}), {1}: (2, {})} | custom-call | flops 1000000 | bytes 4194304 | tf_op jit(solution)/shard_map/pallas_call | solution.py:439
Async XLA Ops:
  0.6 10.4 %copy-start.2 = (bf16[1024,128]{1,0:T(8,128)(2,1)S(1)}, bf16[1024,128]{1,0:T(8,128)(2,1)}, u32[]{:S(2)}) copy-start(bf16[1024,128]{1,0:T(8,128)(2,1)} %refs_4_.1) | copy-start | bytes 786436
  0.6 10.4 %copy-start.4 = (s32[27,1024]{1,0:T(8,128)S(1)}, s32[27,1024]{1,0:T(8,128)}, u32[]{:S(2)}) copy-start(s32[27,1024]{1,0:T(8,128)} %map_ref.3) | copy-start | bytes 331780
  4.4 14.0 %collective-permute-start = (bf16[608,128]{1,0:T(8,128)(2,1)}, bf16[608,128]{1,0:T(8,128)(2,1)S(1)}, u32[]{:S(2)}, u32[]{:S(2)}) collective-permute-start(bf16[608,128]{1,0:T(8,128)(2,1)} %get-tuple-element.33), channel_id=1, source_target_pairs={{0,1},{1,0},{2,3},{3,2},{4,5},{5,4},{6,7},{7,6},{8,9},{9,8},{10,11... | collective-permute-start | bytes 466952 | tf_op jit(solution)/shard_map/ppermute | solution.py:23
  4.5 13.9 %collective-permute-start.1 = (bf16[608,128]{1,0:T(8,128)(2,1)}, bf16[608,128]{1,0:T(8,128)(2,1)S(1)}, u32[]{:S(2)}, u32[]{:S(2)}) collective-permute-start(bf16[608,128]{1,0:T(8,128)(2,1)} %get-tuple-element.34), channel_id=1, source_target_pairs={{1,2},{2,1},{3,4},{4,3},{5,6},{6,5},{7,8},{8,7},{9,10},{10,9},{11,... | collective-permute-start | bytes 466952 | tf_op jit(solution)/shard_map/ppermute | solution.py:23
  9.0 10.8 %collective-permute-start.2 = (bf16[608,128]{1,0:T(8,128)(2,1)}, bf16[608,128]{1,0:T(8,128)(2,1)S(1)}, u32[]{:S(2)}, u32[]{:S(2)}) collective-permute-start(bf16[608,128]{1,0:T(8,128)(2,1)} %get-tuple-element.35), channel_id=1, source_target_pairs={{0,2},{1,3},{2,0},{3,1},{4,6},{5,7},{6,4},{7,5},{8,10},{9,11},{10,... | collective-permute-start | bytes 466952 | tf_op jit(solution)/shard_map/ppermute | solution.py:23
  10.2 9.5 %copy-start = (bf16[27,128,128]{2,1,0:T(8,128)(2,1)S(1)}, bf16[27,128,128]{2,1,0:T(8,128)(2,1)}, u32[]{:S(2)}) copy-start(bf16[27,128,128]{2,1,0:T(8,128)(2,1)} %weight_ref.1) | copy-start | bytes 2654212
  10.2 9.5 %copy-start.3 = (bf16[256,256]{1,0:T(8,128)(2,1)S(1)}, bf16[256,256]{1,0:T(8,128)(2,1)}, u32[]{:S(2)}) copy-start(bf16[256,256]{1,0:T(8,128)(2,1)} %refs_11_.1) | copy-start | bytes 393220
  10.2 9.5 %copy-start.5 = (s32[8,256]{1,0:T(8,128)S(1)}, s32[8,256]{1,0:T(8,128)}, u32[]{:S(2)}) copy-start(s32[8,256]{1,0:T(8,128)} %refs_8_.1) | copy-start | bytes 24580
  10.2 9.5 %copy-start.6 = (s32[4,32]{1,0:T(4,128)S(1)}, s32[4,32]{1,0:T(4,128)}, u32[]{:S(2)}) copy-start(s32[4,32]{1,0:T(4,128)} %refs_7_.1) | copy-start | bytes 1540
  10.3 9.5 %copy-start.8 = (f32[1024,128]{1,0:T(8,128)S(1)}, f32[1024,128]{1,0:T(8,128)}, u32[]{:S(2)}) copy-start(f32[1024,128]{1,0:T(8,128)} %get-tuple-element.37.refs_9_) | copy-start | bytes 1572868
  10.3 9.5 %collective-permute-start.3 = (bf16[608,128]{1,0:T(8,128)(2,1)}, bf16[608,128]{1,0:T(8,128)(2,1)S(1)}, u32[]{:S(2)}, u32[]{:S(2)}) collective-permute-start(bf16[608,128]{1,0:T(8,128)(2,1)} %get-tuple-element.36), channel_id=1, source_target_pairs={{2,4},{3,5},{4,2},{5,3},{6,8},{7,9},{8,6},{9,7},{10,12},{11,13},{1... | collective-permute-start | bytes 466952 | tf_op jit(solution)/shard_map/ppermute | solution.py:23
  31.3 3.3 %copy-start.9 = (bf16[1024,128]{1,0:T(8,128)(2,1)}, bf16[1024,128]{1,0:T(8,128)(2,1)S(1)}, u32[]{:S(2)}) copy-start(bf16[1024,128]{1,0:T(8,128)(2,1)S(1)} %get-tuple-element.40.pgrad_ref) | copy-start | bytes 786436
  31.3 2.3 %collective-permute-start.4 = (bf16[2816,128]{1,0:T(8,128)(2,1)S(1)}, bf16[2816,128]{1,0:T(8,128)(2,1)S(1)}, u32[]{:S(2)}, u32[]{:S(2)}) collective-permute-start(bf16[2816,128]{1,0:T(8,128)(2,1)S(1)} %get-tuple-element.39), channel_id=1, source_target_pairs={{0,1},{1,0},{2,3},{3,2},{4,5},{5,4},{6,7},{7,6},{8,9},{9,8},{10,11... | collective-permute-start | bytes 2162696 | tf_op jit(solution)/shard_map/ppermute | solution.py:452
  34.6 25.9 %all-to-all-start = ((bf16[32,88,128]{2,1,0:T(8,128)(2,1)}), bf16[32,88,128]{2,1,0:T(8,128)(2,1)S(1)}, u32[]{:S(2)}, u32[]{:S(2)}) async-start(bf16[32,88,128]{2,1,0:T(8,128)(2,1)} %bitcast), calls=%async_computation | async-start | bytes 1441792 | tf_op jit(solution)/shard_map/all_to_all | solution.py:456
  41.6 1.0 %copy-start.10 = (bf16[1024,128]{1,0:T(8,128)(2,1)S(1)}, bf16[1024,128]{1,0:T(8,128)(2,1)}, u32[]{:S(2)}) copy-start(bf16[1024,128]{1,0:T(8,128)(2,1)} %copy-done.9) | copy-start | bytes 786436
  57.5 16.7 %copy-start.1 = (bf16[8,128,256]{2,1,0:T(8,128)(2,1)S(1)}, bf16[8,128,256]{2,1,0:T(8,128)(2,1)}, u32[]{:S(2)}) copy-start(bf16[8,128,256]{2,1,0:T(8,128)(2,1)} %refs_9_.1) | copy-start | bytes 1572868
  57.5 16.6 %copy-start.7 = (s32[4,64]{1,0:T(4,128)S(1)}, s32[4,64]{1,0:T(4,128)}, u32[]{:S(2)}) copy-start(s32[4,64]{1,0:T(4,128)} %refs_6_.3) | copy-start | bytes 3076
  61.5 22.8 %all-to-all-start.1 = ((bf16[32,88,128]{2,1,0:T(8,128)(2,1)}), bf16[32,88,128]{2,1,0:T(8,128)(2,1)S(1)}, u32[]{:S(2)}, u32[]{:S(2)}) async-start(bf16[32,88,128]{2,1,0:T(8,128)(2,1)} %bitcast.2), calls=%async_computation.1 | async-start | bytes 1441792 | tf_op jit(solution)/shard_map/all_to_all | solution.py:456
  65.4 5.7 %collective-permute-start.5 = (bf16[96,128]{1,0:T(8,128)(2,1)S(1)}, bf16[96,128]{1,0:T(8,128)(2,1)S(1)}, u32[]{:S(2)}, u32[]{:S(2)}) collective-permute-start(bf16[96,128]{1,0:T(8,128)(2,1)S(1)} %get-tuple-element.46.after_ref), channel_id=1, source_target_pairs={{0,1},{1,0},{2,3},{3,2},{4,5},{5,4},{6,7},{7,6},{8,9},{9,8},{10,11... | collective-permute-start | bytes 73736 | tf_op jit(solution)/shard_map/ppermute | solution.py:23
  65.7 5.5 %collective-permute-start.6 = (bf16[96,128]{1,0:T(8,128)(2,1)S(1)}, bf16[96,128]{1,0:T(8,128)(2,1)S(1)}, u32[]{:S(2)}, u32[]{:S(2)}) collective-permute-start(bf16[96,128]{1,0:T(8,128)(2,1)S(1)} %get-tuple-element.47), channel_id=1, source_target_pairs={{1,2},{2,1},{3,4},{4,3},{5,6},{6,5},{7,8},{8,7},{9,10},{10,9},{11,... | collective-permute-start | bytes 73736 | tf_op jit(solution)/shard_map/ppermute | solution.py:23
  69.1 5.0 %collective-permute-start.7 = (bf16[96,128]{1,0:T(8,128)(2,1)S(1)}, bf16[96,128]{1,0:T(8,128)(2,1)S(1)}, u32[]{:S(2)}, u32[]{:S(2)}) collective-permute-start(bf16[96,128]{1,0:T(8,128)(2,1)S(1)} %get-tuple-element.48), channel_id=1, source_target_pairs={{0,2},{1,3},{2,0},{3,1},{4,6},{5,7},{6,4},{7,5},{8,10},{9,11},{10,... | collective-permute-start | bytes 73736 | tf_op jit(solution)/shard_map/ppermute | solution.py:23
  70.4 3.7 %collective-permute-start.8 = (bf16[96,128]{1,0:T(8,128)(2,1)S(1)}, bf16[96,128]{1,0:T(8,128)(2,1)S(1)}, u32[]{:S(2)}, u32[]{:S(2)}) collective-permute-start(bf16[96,128]{1,0:T(8,128)(2,1)S(1)} %get-tuple-element.49), channel_id=1, source_target_pairs={{2,4},{3,5},{4,2},{5,3},{6,8},{7,9},{8,6},{9,7},{10,12},{11,13},{1... | collective-permute-start | bytes 73736 | tf_op jit(solution)/shard_map/ppermute | solution.py:23
  84.3 2.6 %collective-permute-start.9 = (bf16[2816,128]{1,0:T(8,128)(2,1)S(1)}, bf16[2816,128]{1,0:T(8,128)(2,1)S(1)}, u32[]{:S(2)}, u32[]{:S(2)}) collective-permute-start(bf16[2816,128]{1,0:T(8,128)(2,1)S(1)} %bitcast.6), channel_id=1, source_target_pairs={{0,1},{1,0},{2,3},{3,2},{4,5},{5,4},{6,7},{7,6},{8,9},{9,8},{10,11... | collective-permute-start | bytes 2162696 | tf_op jit(solution)/shard_map/ppermute | solution.py:452

commit v14 on v12

--- a/solution.py
+++ b/solution.py
@@ -141,7 +141,6 @@
     octants = child_map_ref.shape[0]
     cap2 = sends[0].shape[0] - cap
     cap2 //= 1 + octants * out_grad_ref.shape[1] // LANES
-    table_rows = voxels + slots * cap2
     copies[0].wait()
     copies[1].wait()
     listed = gather_lists(halo_ref, features_ref[...]).astype(BF16)
@@ -150,20 +149,29 @@
     for copy in copies[2:]:
         copy.wait()
     upstream = out_grad_ref[...]
-    codes = encode(child_map_ref[...]).astype(BF16)
-    choosers, parts = [], []
+    rows = child_map_ref[...]
+    codes = half_codes(rows, voxels, slots * cap2)
+    half = voxels // 2
+    choosers, sides = [], []
     for o in range(octants):
-        part = matmul_rt(upstream, down_ref[o])
-        high = part.astype(BF16)
-        low = (part - high.astype(F32)).astype(BF16)
-        choosers.append(one_hot_columns(codes[o : o + 1, :], table_rows))
-        parts.append(jnp.concatenate([high, low], axis=1))
-    both = matmul(jnp.concatenate(choosers, axis=1), jnp.concatenate(parts, axis=0))
-    total = both[:, :LANES] + both[:, LANES:]
-    back_ref[...] = total[:voxels]
-    for send, block in zip(sends, to_steps(jnp.split(total[voxels:].astype(BF16), slots), True)):
+        part = matmul_rt(upstream, down_ref[o]).astype(BF16)
+        code = codes[o : o + 1, :].astype(BF16)
+        right = column(code) < jnp.zeros(part.shape, BF16)
+        none = jnp.zeros(part.shape, BF16)
+        pair = [jnp.where(right, none, part), jnp.where(right, part, none)]
+        sides.append(jnp.concatenate(pair, axis=1))
+        choosers.append(one_hot_columns(jnp.abs(code), half + slots * cap2 // 2))
+    both = matmul(jnp.concatenate(choosers, axis=1), jnp.concatenate(sides, axis=0))
+    back_ref[0:half, :] = both[0:half, :LANES]
+    back_ref[half:, :] = both[0:half, LANES:]
+    far = jnp.concatenate([both[half:, :LANES], both[half:, LANES:]], axis=0).astype(BF16)
+    for send, block in zip(sends, to_steps(jnp.split(far, slots), True)):
         send[cap : cap + cap2, :] = block
-    sums = [matmul(chooser[voxels:], upstream).astype(BF16) for chooser in choosers]
+    codes = encode(jnp.where(rows >= voxels, rows - voxels, slots * cap2)).astype(BF16)
+    sums = []
+    for o in range(octants):
+        chooser = one_hot_columns(codes[o : o + 1, :], slots * cap2)
+        sums.append(matmul(chooser, upstream).astype(BF16))
     blocks = []
     for s in range(slots):
         rows = slice(s * cap2, (s + 1) * cap2)
@@ -359,16 +367,16 @@
     out_ref[...] = (mine + other_ref[...].astype(F32)).astype(BF16)
 
 
-def sum_kernel(devices, scale, parts_ref, after_ref, out_ref):
-    rows = parts_ref.shape[0] // devices
+def sum_kernel(order, scale, parts_ref, after_ref, out_ref):
+    rows = parts_ref.shape[0] // len(order)
     for core in range(2):
-        mine = range(core, devices, 2)
+        mine = [n for n in range(len(order)) if order[n] % 2 == core]
         total = jnp.zeros((rows, LANES), F32)
-        for d in mine:
-            total = total + parts_ref[d * rows : (d + 1) * rows, :].astype(F32)
+        for n in mine:
+            total = total + parts_ref[n * rows : (n + 1) * rows, :].astype(F32)
         total = (total * scale).astype(BF16)
-        for d in mine:
-            out_ref[d * rows : (d + 1) * rows, :] = total
+        for n in mine:
+            out_ref[n * rows : (n + 1) * rows, :] = total
 
 
 def final_kernel(own, *refs):
@@ -454,8 +462,15 @@
     return lax.ppermute(value, "shard", [(i, i + 1 - 2 * (i % 2)) for i in range(devices)])
 
 
-def exchange(value):
-    return lax.all_to_all(value, "shard", 0, 0, tiled=True)
+def far_order(devices):
+    order = [0]
+    while len(order) < devices:
+        order = [2 * n for n in order] + [2 * n + 1 for n in order]
+    return order if len(order) == devices else list(range(devices))
+
+
+def exchange(value, order):
+    return lax.all_to_all(value, "shard", 0, 0, axis_index_groups=[order], tiled=True)
 
 
 def local(
@@ -541,7 +556,8 @@
         [((half_rows, LANES), BF16)],
         flops=10**6,
     )
-    parts = exchange(pair_terms)
+    order = far_order(devices)
+    parts = exchange(pair_terms, order)
     spread = call(
         functools.partial(spread_kernel, slots, cap),
         (pre_grad, neighbour_map, conv_weight, leaving, pair_terms),
@@ -551,7 +567,7 @@
         in_hbm=(4,),
     )
     (summed,) = call(
-        functools.partial(sum_kernel, devices, scale),
+        functools.partial(sum_kernel, order, scale),
         (parts, spread[1]),
         [((half_rows, LANES), BF16)],
         flops=10**6,
@@ -565,7 +581,7 @@
         [((voxels, channels), F32), ((parents, coarse_channels), BF16)],
         flops=giga,
     )
-    mine, input_grad = lax.optimization_barrier((exchange(summed), input_grad))
+    mine, input_grad = lax.optimization_barrier((exchange(summed, order), input_grad))
     other = swap_cores(mine, devices)
     gradients = ()
     for own, block in ((True, mine), (False, other)):

time: 87.8 us -> 88.3 us (level)
  waiting for transfers between devices: 18.9 us -> 22.4 us
  starting transfers between devices: 23.9 us -> 22 us
    all_to_all x2, waiting for transfers between devices: 11.8 us -> 16.6 us  [exchange(): lax.all_to_all(value, 'shard', 0, 0, axis_index_groups=[order], tiled=True)]
    all_to_all x2, starting transfers between devices: 10.8 us -> 9.37 us  [exchange(): lax.all_to_all(value, 'shard', 0, 0, axis_index_groups=[order], tiled=True)]
    ppermute x8, waiting for transfers between devices: 4.41 us -> 2.99 us  [swaps(): moved[step] = lax.ppermute(by_step[step], 'shard', pairs)]
where the time goes in v14:
time: 88.3 us; the launch traced here: 87.8 us
  Pallas kernels  41.3 us (47%)
  waiting for transfers between devices  22.4 us (25%)
  starting transfers between devices  22 us (25%)
  between operations  1.04 us (1%)
  local copies, waits for them, and re-layouts  1 us (1%)
    pallas_call x10, Pallas kernels, call(): pl.pallas_call(kernel, out_shape=[jax.ShapeDtypeStruct(s, d) for s, d in...  41.3 us
    all_to_all x2, waiting for transfers between devices, exchange(): lax.all_to_all(value, 'shard', 0, 0, axis_index_groups=[order], tiled=True)  16.6 us
    ppermute x8, starting transfers between devices, swaps(): moved[step] = lax.ppermute(by_step[step], 'shard', pairs)  12.3 us
    all_to_all x2, starting transfers between devices, exchange(): lax.all_to_all(value, 'shard', 0, 0, axis_index_groups=[order], tiled=True)  9.37 us
    ppermute x8, waiting for transfers between devices, swaps(): moved[step] = lax.ppermute(by_step[step], 'shard', pairs)  2.99 us
    ppermute x2, waiting for transfers between devices, swap_cores(): lax.ppermute(value, 'shard', [(i, i + 1 - 2 * (i % 2)) for i in range(dev...  2.79 us
  transfers between devices with their start and end apart: 12, of which 7 were waited for; matrix products, arithmetic and copies ran while one was open for 0% of the time, Pallas kernels for 29%

profile of v14, /device:TPU:1, one launch (start us, length us, event | category | flops | bytes accessed | tf_op | source)
XLA Modules:
  0.0 87.8 jit_solution(14157498886344864096)
XLA Ops:
  0.6 0.0 copy-start.2
  0.6 0.0 copy-start.4
  0.7 3.7 %shard_map.111 = (bf16[608,128]{1,0:T(8,128)(2,1)}, bf16[608,128]{1,0:T(8,128)(2,1)}, bf16[608,128]{1,0:T(8,128)(2,1)}, bf16[608,128]{1,0:T(8,128)(2,1)}, f32[1024,128]{1,0:T(8,128)}) custom-call(bf16[1024,128]{1,0:T(8,128)(2,1)} %refs_4_.1, s32[4,64]{1,0:T(4,128)} %refs_6_.5, s32[8,256]{1,0:T(8,128)} %refs_8_.1, bf16[256,256]{1,0:T(8,128)(2,1)} %refs_11_.1, ...), custom_call_target="tpu_custom_call" | custom-call | flops 1000000000 | bytes 4194304 | tf_op jit(solution)/shard_map/pallas_call | solution.py:449
  4.4 0.1 collective-permute-start
  4.5 4.5 %collective-permute-start.1 = (bf16[608,128]{1,0:T(8,128)(2,1)}, bf16[608,128]{1,0:T(8,128)(2,1)S(1)}, u32[]{:S(2)}, u32[]{:S(2)}) collective-permute-start(bf16[608,128]{1,0:T(8,128)(2,1)} %get-tuple-element.37), channel_id=1, source_target_pairs={{1,2},{2,1},{3,4},{4,3},{5,6},{6,5},{7,8},{8,7},{9,10},{10,9},{11,... | collective-permute-start | bytes 466952 | tf_op jit(solution)/shard_map/ppermute | solution.py:23
  9.0 1.3 %collective-permute-start.2 = (bf16[608,128]{1,0:T(8,128)(2,1)}, bf16[608,128]{1,0:T(8,128)(2,1)S(1)}, u32[]{:S(2)}, u32[]{:S(2)}) collective-permute-start(bf16[608,128]{1,0:T(8,128)(2,1)} %get-tuple-element.38), channel_id=1, source_target_pairs={{0,2},{1,3},{2,0},{3,1},{4,6},{5,7},{6,4},{7,5},{8,10},{9,11},{10,... | collective-permute-start | bytes 466952 | tf_op jit(solution)/shard_map/ppermute | solution.py:23
  10.2 0.0 copy-start
  10.2 0.0 copy-start.6
  10.2 0.8 collective-permute-start.3
  11.0 0.0 copy-done.2
  11.1 0.0 copy-done.4
  11.1 7.3 %shard_map.112.refs_8_ = bf16[1024,3328]{1,0:T(8,128)(2,1)S(1)} custom-call(bf16[1024,128]{1,0:T(8,128)(2,1)S(1)} %copy-done.2, s32[27,1024]{1,0:T(8,128)S(1)} %copy-done.4), custom_call_target="tpu_custom_call" | custom-call | flops 4000000000 | bytes 4194304 | tf_op jit(solution)/shard_map/pallas_call | solution.py:449
  18.4 0.0 copy-start.3
  18.4 0.0 copy-start.5
  18.4 0.0 copy-start.8
  18.4 0.0 collective-permute-done.refs_0_
  18.4 0.0 collective-permute-done.1.refs_1_
  18.4 1.3 %collective-permute-done.2.refs_2_ = bf16[608,128]{1,0:T(8,128)(2,1)S(1)} collective-permute-done((bf16[608,128]{1,0:T(8,128)(2,1)}, bf16[608,128]{1,0:T(8,128)(2,1)S(1)}, u32[]{:S(2)}, u32[]{:S(2)}) %collective-permute-start.2) | collective-permute-done | bytes 155680 | tf_op jit(solution)/shard_map/ppermute | solution.py:23
  19.8 0.0 collective-permute-done.3.refs_3_
  19.8 0.0 copy-done
  19.8 0.0 copy-done.6
  19.8 6.6 %shard_map.113 = (bf16[1024,128]{1,0:T(8,128)(2,1)S(1)}, f32[1024,128]{1,0:T(8,128)S(1)}, bf16[1024,3456]{1,0:T(8,128)(2,1)S(1)}, bf16[128,128]{1,0:T(8,128)(2,1)S(1)}) custom-call(bf16[608,128]{1,0:T(8,128)(2,1)S(1)} %collective-permute-done.refs_0_, bf16[608,128]{1,0:T(8,128)(2,1)S(1)} %collective-permute-done.1.refs_1_, ...), custom_call_target="tpu_custom_call" | custom-call | flops 12000000000 | bytes 4194304 | tf_op jit(solution)/shard_map/pallas_call | solution.py:449
  26.4 0.0 copy-done.3
  26.4 0.0 copy-done.5
  26.4 0.0 copy-done.8
  26.4 2.6 %shard_map.114 = (f32[1024,128]{1,0:T(8,128)S(1)}, bf16[1024,128]{1,0:T(8,128)(2,1)S(1)}, bf16[256,1024]{1,0:T(8,128)(2,1)S(1)}, bf16[5632,128]{1,0:T(8,128)(2,1)S(1)}, bf16[2816,128]{1,0:T(8,128)(2,1)S(1)}) custom-call(bf16[608,128]{1,0:T(8,128)(2,1)S(1)} %collective-permute-done.refs_0_, bf16[608,128]{1,0:T(8,128)(2,1)S(1)} %collective-permute-done.1.refs_1_, ...), custom_call_target="tpu_custom_call" | custom-call | flops 3000000000 | bytes 4194304 | tf_op jit(solution)/shard_map/pallas_call | solution.py:449
  29.0 0.0 copy-start.9
  29.0 0.1 collective-permute-start.4
  29.1 2.2 %collective-permute-done.4.other_ref = bf16[2816,128]{1,0:T(8,128)(2,1)S(1)} collective-permute-done((bf16[2816,128]{1,0:T(8,128)(2,1)S(1)}, bf16[2816,128]{1,0:T(8,128)(2,1)S(1)}, u32[]{:S(2)}, u32[]{:S(2)}) %collective-permute-start.4) | collective-permute-done | bytes 720928 | tf_op jit(solution)/shard_map/ppermute | solution.py:462
  31.3 1.1 %shard_map.115.after_ref = bf16[2816,128]{1,0:T(8,128)(2,1)} custom-call(bf16[5632,128]{1,0:T(8,128)(2,1)S(1)} %get-tuple-element.45.terms_ref, bf16[2816,128]{1,0:T(8,128)(2,1)S(1)} %collective-permute-done.4.other_ref), custom_call_target="tpu_custom_call" | custom-call | flops 1000000 | bytes 4194304 | tf_op jit(solution)/shard_map/pallas_call | solution.py:449
  32.3 0.0 copy-done.9
  32.3 6.9 %all-to-all-start = ((bf16[32,88,128]{2,1,0:T(8,128)(2,1)}), bf16[32,88,128]{2,1,0:T(8,128)(2,1)S(1)}, u32[]{:S(2)}, u32[]{:S(2)}) async-start(bf16[32,88,128]{2,1,0:T(8,128)(2,1)} %bitcast), calls=%async_computation | async-start | bytes 1441792 | tf_op jit(solution)/shard_map/all_to_all | solution.py:473
  39.3 0.0 copy-start.10
  39.3 0.9 %copy-done.10 = bf16[1024,128]{1,0:T(8,128)(2,1)S(1)} copy-done((bf16[1024,128]{1,0:T(8,128)(2,1)S(1)}, bf16[1024,128]{1,0:T(8,128)(2,1)}, u32[]{:S(2)}) %copy-start.10) | copy-done | bytes 262168
  40.2 14.9 %shard_map.116 = (f32[1024,128]{1,0:T(8,128)S(1)}, bf16[96,128]{1,0:T(8,128)(2,1)S(1)}, bf16[96,128]{1,0:T(8,128)(2,1)S(1)}, bf16[96,128]{1,0:T(8,128)(2,1)S(1)}, bf16[96,128]{1,0:T(8,128)(2,1)S(1)}) custom-call(bf16[1024,128]{1,0:T(8,128)(2,1)S(1)} %copy-done.10, s32[27,1024]{1,0:T(8,128)S(1)} %copy-done.4, bf16[27,128,128]{2,1,0:T(8,128)(2,1)S(1)} %copy-done, ...), custom_call_target="tpu_custom_call" | custom-call | flops 20000000000 | bytes 4194304 | tf_op jit(solution)/shard_map/pallas_call | solution.py:449
  55.1 0.0 copy-start.1
  55.2 0.0 copy-start.7
  55.2 4.7 %all-to-all-done = bf16[32,88,128]{2,1,0:T(8,128)(2,1)S(1)} async-done(((bf16[32,88,128]{2,1,0:T(8,128)(2,1)}), bf16[32,88,128]{2,1,0:T(8,128)(2,1)S(1)}, u32[]{:S(2)}, u32[]{:S(2)}) %all-to-all-start) | async-done | bytes 720928 | tf_op jit(solution)/shard_map/all_to_all | solution.py:473
  59.9 1.0 %shard_map.117 = bf16[2816,128]{1,0:T(8,128)(2,1)} custom-call(bf16[2816,128]{1,0:T(8,128)(2,1)S(1)} %bitcast.8, bf16[96,128]{1,0:T(8,128)(2,1)S(1)} %get-tuple-element.52.after_ref), custom_call_target="tpu_custom_call" | custom-call | flops 1000000 | bytes 4194304 | tf_op jit(solution)/shard_map/pallas_call | solution.py:449
  60.8 2.4 %all-to-all-start.1 = ((bf16[32,88,128]{2,1,0:T(8,128)(2,1)}), bf16[32,88,128]{2,1,0:T(8,128)(2,1)S(1)}, u32[]{:S(2)}, u32[]{:S(2)}) async-start(bf16[32,88,128]{2,1,0:T(8,128)(2,1)} %bitcast.2), calls=%async_computation.1 | async-start | bytes 1441792 | tf_op jit(solution)/shard_map/all_to_all | solution.py:473
  63.3 0.5 collective-permute-start.5
  63.7 3.3 %collective-permute-start.6 = (bf16[96,128]{1,0:T(8,128)(2,1)S(1)}, bf16[96,128]{1,0:T(8,128)(2,1)S(1)}, u32[]{:S(2)}, u32[]{:S(2)}) collective-permute-start(bf16[96,128]{1,0:T(8,128)(2,1)S(1)} %get-tuple-element.53), channel_id=1, source_target_pairs={{1,2},{2,1},{3,4},{4,3},{5,6},{6,5},{7,8},{8,7},{9,10},{10,9},{11,... | collective-permute-start | bytes 73736 | tf_op jit(solution)/shard_map/ppermute | solution.py:23
  67.0 1.3 %collective-permute-start.7 = (bf16[96,128]{1,0:T(8,128)(2,1)S(1)}, bf16[96,128]{1,0:T(8,128)(2,1)S(1)}, u32[]{:S(2)}, u32[]{:S(2)}) collective-permute-start(bf16[96,128]{1,0:T(8,128)(2,1)S(1)} %get-tuple-element.54), channel_id=1, source_target_pairs={{0,2},{1,3},{2,0},{3,1},{4,6},{5,7},{6,4},{7,5},{8,10},{9,11},{10,... | collective-permute-start | bytes 73736 | tf_op jit(solution)/shard_map/ppermute | solution.py:23
  68.3 0.7 collective-permute-start.8
  69.0 0.0 collective-permute-done.5.refs_0_
  69.0 0.3 collective-permute-done.6.refs_1_
  69.3 1.4 %collective-permute-done.7.refs_2_ = bf16[96,128]{1,0:T(8,128)(2,1)S(1)} collective-permute-done((bf16[96,128]{1,0:T(8,128)(2,1)S(1)}, bf16[96,128]{1,0:T(8,128)(2,1)S(1)}, u32[]{:S(2)}, u32[]{:S(2)}) %collective-permute-start.7) | collective-permute-done | bytes 24608 | tf_op jit(solution)/shard_map/ppermute | solution.py:23
  70.6 0.0 collective-permute-done.8.refs_3_
  70.6 0.0 copy-done.1
  70.6 0.0 copy-done.7
  70.6 1.5 %shard_map.118 = (f32[1024,128]{1,0:T(8,128)}, bf16[256,256]{1,0:T(8,128)(2,1)}) custom-call(bf16[96,128]{1,0:T(8,128)(2,1)S(1)} %collective-permute-done.5.refs_0_, bf16[96,128]{1,0:T(8,128)(2,1)S(1)} %collective-permute-done.6.refs_1_, bf16[96,128]{1,0:T(8,128)(2,1)S(1)} %collective-permute-done.7.refs_2_, ...), custom_call_target="tpu_custom_call" | custom-call | flops 1000000000 | bytes 4194304 | tf_op jit(solution)/shard_map/pallas_call | solution.py:449
  72.1 12.0 %all-to-all-done.1 = bf16[32,88,128]{2,1,0:T(8,128)(2,1)S(1)} async-done(((bf16[32,88,128]{2,1,0:T(8,128)(2,1)}), bf16[32,88,128]{2,1,0:T(8,128)(2,1)S(1)}, u32[]{:S(2)}, u32[]{:S(2)}) %all-to-all-start.1) | async-done | bytes 720928 | tf_op jit(solution)/shard_map/all_to_all | solution.py:473
  84.0 0.2 collective-permute-start.9
  84.2 1.4 %shard_map.119 = (f32[3456,128]{1,0:T(8,128)}, f32[1024,256]{1,0:T(8,128)}) custom-call(bf16[2816,128]{1,0:T(8,128)(2,1)S(1)} %bitcast.7), custom_call_target="tpu_custom_call" | custom-call | flops 1000000 | bytes 4194304 | tf_op jit(solution)/shard_map/pallas_call | solution.py:449
  85.6 0.6 collective-permute-done.9.refs_0_
  86.2 1.4 %shard_map.120 = (f32[3456,128]{1,0:T(8,128)}, f32[1024,256]{1,0:T(8,128)}) custom-call(bf16[2816,128]{1,0:T(8,128)(2,1)S(1)} %collective-permute-done.9.refs_0_, f32[3456,128]{1,0:T(8,128)} %get-tuple-element.64.refs_1_, f32[1024,256]{1,0:T(8,128)} %get-tuple-element.65.refs_2_), custom_call_target="tpu_custom_call", output_to_operand_aliasing={{0}: (1, {}), {1}: (2, {})} | custom-call | flops 1000000 | bytes 4194304 | tf_op jit(solution)/shard_map/pallas_call | solution.py:449
Async XLA Ops:
  0.6 10.4 %copy-start.2 = (bf16[1024,128]{1,0:T(8,128)(2,1)S(1)}, bf16[1024,128]{1,0:T(8,128)(2,1)}, u32[]{:S(2)}) copy-start(bf16[1024,128]{1,0:T(8,128)(2,1)} %refs_4_.1) | copy-start | bytes 786436
  0.6 10.4 %copy-start.4 = (s32[27,1024]{1,0:T(8,128)S(1)}, s32[27,1024]{1,0:T(8,128)}, u32[]{:S(2)}) copy-start(s32[27,1024]{1,0:T(8,128)} %map_ref.3) | copy-start | bytes 331780
  4.4 14.0 %collective-permute-start = (bf16[608,128]{1,0:T(8,128)(2,1)}, bf16[608,128]{1,0:T(8,128)(2,1)S(1)}, u32[]{:S(2)}, u32[]{:S(2)}) collective-permute-start(bf16[608,128]{1,0:T(8,128)(2,1)} %get-tuple-element.36), channel_id=1, source_target_pairs={{0,1},{1,0},{2,3},{3,2},{4,5},{5,4},{6,7},{7,6},{8,9},{9,8},{10,11... | collective-permute-start | bytes 466952 | tf_op jit(solution)/shard_map/ppermute | solution.py:23
  4.5 13.9 %collective-permute-start.1 = (bf16[608,128]{1,0:T(8,128)(2,1)}, bf16[608,128]{1,0:T(8,128)(2,1)S(1)}, u32[]{:S(2)}, u32[]{:S(2)}) collective-permute-start(bf16[608,128]{1,0:T(8,128)(2,1)} %get-tuple-element.37), channel_id=1, source_target_pairs={{1,2},{2,1},{3,4},{4,3},{5,6},{6,5},{7,8},{8,7},{9,10},{10,9},{11,... | collective-permute-start | bytes 466952 | tf_op jit(solution)/shard_map/ppermute | solution.py:23
  9.0 10.8 %collective-permute-start.2 = (bf16[608,128]{1,0:T(8,128)(2,1)}, bf16[608,128]{1,0:T(8,128)(2,1)S(1)}, u32[]{:S(2)}, u32[]{:S(2)}) collective-permute-start(bf16[608,128]{1,0:T(8,128)(2,1)} %get-tuple-element.38), channel_id=1, source_target_pairs={{0,2},{1,3},{2,0},{3,1},{4,6},{5,7},{6,4},{7,5},{8,10},{9,11},{10,... | collective-permute-start | bytes 466952 | tf_op jit(solution)/shard_map/ppermute | solution.py:23
  10.2 9.5 %copy-start = (bf16[27,128,128]{2,1,0:T(8,128)(2,1)S(1)}, bf16[27,128,128]{2,1,0:T(8,128)(2,1)}, u32[]{:S(2)}) copy-start(bf16[27,128,128]{2,1,0:T(8,128)(2,1)} %weight_ref.1) | copy-start | bytes 2654212
  10.2 9.5 %copy-start.6 = (s32[4,32]{1,0:T(4,128)S(1)}, s32[4,32]{1,0:T(4,128)}, u32[]{:S(2)}) copy-start(s32[4,32]{1,0:T(4,128)} %refs_6_.4) | copy-start | bytes 1540
  10.2 9.5 %collective-permute-start.3 = (bf16[608,128]{1,0:T(8,128)(2,1)}, bf16[608,128]{1,0:T(8,128)(2,1)S(1)}, u32[]{:S(2)}, u32[]{:S(2)}) collective-permute-start(bf16[608,128]{1,0:T(8,128)(2,1)} %get-tuple-element.39), channel_id=1, source_target_pairs={{2,4},{3,5},{4,2},{5,3},{6,8},{7,9},{8,6},{9,7},{10,12},{11,13},{1... | collective-permute-start | bytes 466952 | tf_op jit(solution)/shard_map/ppermute | solution.py:23
  18.4 8.0 %copy-start.3 = (bf16[256,256]{1,0:T(8,128)(2,1)S(1)}, bf16[256,256]{1,0:T(8,128)(2,1)}, u32[]{:S(2)}) copy-start(bf16[256,256]{1,0:T(8,128)(2,1)} %refs_11_.1) | copy-start | bytes 393220
  18.4 8.0 %copy-start.5 = (s32[8,256]{1,0:T(8,128)S(1)}, s32[8,256]{1,0:T(8,128)}, u32[]{:S(2)}) copy-start(s32[8,256]{1,0:T(8,128)} %refs_8_.1) | copy-start | bytes 24580
  18.4 8.0 %copy-start.8 = (f32[1024,128]{1,0:T(8,128)S(1)}, f32[1024,128]{1,0:T(8,128)}, u32[]{:S(2)}) copy-start(f32[1024,128]{1,0:T(8,128)} %get-tuple-element.42.refs_7_) | copy-start | bytes 1572868
  29.0 3.3 %copy-start.9 = (bf16[1024,128]{1,0:T(8,128)(2,1)}, bf16[1024,128]{1,0:T(8,128)(2,1)S(1)}, u32[]{:S(2)}) copy-start(bf16[1024,128]{1,0:T(8,128)(2,1)S(1)} %get-tuple-element.47.pgrad_ref) | copy-start | bytes 786436
  29.0 2.3 %collective-permute-start.4 = (bf16[2816,128]{1,0:T(8,128)(2,1)S(1)}, bf16[2816,128]{1,0:T(8,128)(2,1)S(1)}, u32[]{:S(2)}, u32[]{:S(2)}) collective-permute-start(bf16[2816,128]{1,0:T(8,128)(2,1)S(1)} %get-tuple-element.46), channel_id=1, source_target_pairs={{0,1},{1,0},{2,3},{3,2},{4,5},{5,4},{6,7},{7,6},{8,9},{9,8},{10,11... | collective-permute-start | bytes 2162696 | tf_op jit(solution)/shard_map/ppermute | solution.py:462
  32.3 27.6 %all-to-all-start = ((bf16[32,88,128]{2,1,0:T(8,128)(2,1)}), bf16[32,88,128]{2,1,0:T(8,128)(2,1)S(1)}, u32[]{:S(2)}, u32[]{:S(2)}) async-start(bf16[32,88,128]{2,1,0:T(8,128)(2,1)} %bitcast), calls=%async_computation | async-start | bytes 1441792 | tf_op jit(solution)/shard_map/all_to_all | solution.py:473
  39.3 1.0 %copy-start.10 = (bf16[1024,128]{1,0:T(8,128)(2,1)S(1)}, bf16[1024,128]{1,0:T(8,128)(2,1)}, u32[]{:S(2)}) copy-start(bf16[1024,128]{1,0:T(8,128)(2,1)} %copy-done.9) | copy-start | bytes 786436
  55.1 15.5 %copy-start.1 = (bf16[8,128,256]{2,1,0:T(8,128)(2,1)S(1)}, bf16[8,128,256]{2,1,0:T(8,128)(2,1)}, u32[]{:S(2)}) copy-start(bf16[8,128,256]{2,1,0:T(8,128)(2,1)} %refs_9_.1) | copy-start | bytes 1572868
  55.2 15.5 %copy-start.7 = (s32[4,64]{1,0:T(4,128)S(1)}, s32[4,64]{1,0:T(4,128)}, u32[]{:S(2)}) copy-start(s32[4,64]{1,0:T(4,128)} %refs_6_.5) | copy-start | bytes 3076
  60.8 23.2 %all-to-all-start.1 = ((bf16[32,88,128]{2,1,0:T(8,128)(2,1)}), bf16[32,88,128]{2,1,0:T(8,128)(2,1)S(1)}, u32[]{:S(2)}, u32[]{:S(2)}) async-start(bf16[32,88,128]{2,1,0:T(8,128)(2,1)} %bitcast.2), calls=%async_computation.1 | async-start | bytes 1441792 | tf_op jit(solution)/shard_map/all_to_all | solution.py:473
  63.3 5.7 %collective-permute-start.5 = (bf16[96,128]{1,0:T(8,128)(2,1)S(1)}, bf16[96,128]{1,0:T(8,128)(2,1)S(1)}, u32[]{:S(2)}, u32[]{:S(2)}) collective-permute-start(bf16[96,128]{1,0:T(8,128)(2,1)S(1)} %get-tuple-element.52.after_ref), channel_id=1, source_target_pairs={{0,1},{1,0},{2,3},{3,2},{4,5},{5,4},{6,7},{7,6},{8,9},{9,8},{10,11... | collective-permute-start | bytes 73736 | tf_op jit(solution)/shard_map/ppermute | solution.py:23
  63.7 5.5 %collective-permute-start.6 = (bf16[96,128]{1,0:T(8,128)(2,1)S(1)}, bf16[96,128]{1,0:T(8,128)(2,1)S(1)}, u32[]{:S(2)}, u32[]{:S(2)}) collective-permute-start(bf16[96,128]{1,0:T(8,128)(2,1)S(1)} %get-tuple-element.53), channel_id=1, source_target_pairs={{1,2},{2,1},{3,4},{4,3},{5,6},{6,5},{7,8},{8,7},{9,10},{10,9},{11,... | collective-permute-start | bytes 73736 | tf_op jit(solution)/shard_map/ppermute | solution.py:23
  67.0 3.6 %collective-permute-start.7 = (bf16[96,128]{1,0:T(8,128)(2,1)S(1)}, bf16[96,128]{1,0:T(8,128)(2,1)S(1)}, u32[]{:S(2)}, u32[]{:S(2)}) collective-permute-start(bf16[96,128]{1,0:T(8,128)(2,1)S(1)} %get-tuple-element.54), channel_id=1, source_target_pairs={{0,2},{1,3},{2,0},{3,1},{4,6},{5,7},{6,4},{7,5},{8,10},{9,11},{10,... | collective-permute-start | bytes 73736 | tf_op jit(solution)/shard_map/ppermute | solution.py:23
  68.3 2.3 %collective-permute-start.8 = (bf16[96,128]{1,0:T(8,128)(2,1)S(1)}, bf16[96,128]{1,0:T(8,128)(2,1)S(1)}, u32[]{:S(2)}, u32[]{:S(2)}) collective-permute-start(bf16[96,128]{1,0:T(8,128)(2,1)S(1)} %get-tuple-element.55), channel_id=1, source_target_pairs={{2,4},{3,5},{4,2},{5,3},{6,8},{7,9},{8,6},{9,7},{10,12},{11,13},{1... | collective-permute-start | bytes 73736 | tf_op jit(solution)/shard_map/ppermute | solution.py:23
  84.0 2.2 %collective-permute-start.9 = (bf16[2816,128]{1,0:T(8,128)(2,1)S(1)}, bf16[2816,128]{1,0:T(8,128)(2,1)S(1)}, u32[]{:S(2)}, u32[]{:S(2)}) collective-permute-start(bf16[2816,128]{1,0:T(8,128)(2,1)S(1)} %bitcast.6), channel_id=1, source_target_pairs={{0,1},{1,0},{2,3},{3,2},{4,5},{5,4},{6,7},{7,6},{8,9},{9,8},{10,11... | collective-permute-start | bytes 2162696 | tf_op jit(solution)/shard_map/ppermute | solution.py:462

commit v15 on v12

--- a/solution.py
+++ b/solution.py
@@ -126,7 +126,8 @@
 
 def head_kernel(features_hbm, halo_hbm, child_map_hbm, out_grad_hbm, down_hbm, *refs):
     sources = (features_hbm, halo_hbm, child_map_hbm, out_grad_hbm, down_hbm)
-    buffers, sems = refs[-len(sources) - 1 : -1], refs[-1]
+    buffers, sems = refs[-len(sources) - 2 : -2], refs[-2]
+    back_sems = refs[-1]
     features_ref, halo_ref, child_map_ref, out_grad_ref, down_ref = buffers
     copies = [
         pltpu.make_async_copy(source, buffer, sems.at[n])
@@ -134,14 +135,22 @@
     ]
     for copy in copies:
         copy.start()
-    outs = refs[: -len(sources) - 1]
-    sends, back_ref = outs[:-1], outs[-1]
     slots, cap = halo_ref.shape
+    send_hbms, back_hbm = refs[:slots], refs[slots]
+    sends, back_ref = refs[slots + 1 : 2 * slots + 1], refs[2 * slots + 1]
     voxels = features_ref.shape[0]
     octants = child_map_ref.shape[0]
     cap2 = sends[0].shape[0] - cap
     cap2 //= 1 + octants * out_grad_ref.shape[1] // LANES
-    table_rows = voxels + slots * cap2
+    written = []
+
+    def write(first, last):
+        for send, send_hbm in zip(sends, send_hbms):
+            place = pl.ds(first, last - first)
+            sem = sems.at[len(copies) + len(written)]
+            written.append(pltpu.make_async_copy(send.at[place], send_hbm.at[place], sem))
+            written[-1].start()
+
     copies[0].wait()
     copies[1].wait()
     listed = gather_lists(halo_ref, features_ref[...]).astype(BF16)
@@ -150,31 +159,45 @@
     for copy in copies[2:]:
         copy.wait()
     upstream = out_grad_ref[...]
-    codes = encode(child_map_ref[...]).astype(BF16)
-    choosers, parts = [], []
+    rows = child_map_ref[...]
+    codes = encode(jnp.where(rows >= voxels, rows - voxels, slots * cap2)).astype(BF16)
+    sums = []
     for o in range(octants):
-        part = matmul_rt(upstream, down_ref[o])
-        high = part.astype(BF16)
-        low = (part - high.astype(F32)).astype(BF16)
-        choosers.append(one_hot_columns(codes[o : o + 1, :], table_rows))
-        parts.append(jnp.concatenate([high, low], axis=1))
-    both = matmul(jnp.concatenate(choosers, axis=1), jnp.concatenate(parts, axis=0))
-    total = both[:, :LANES] + both[:, LANES:]
-    back_ref[...] = total[:voxels]
-    for send, block in zip(sends, to_steps(jnp.split(total[voxels:].astype(BF16), slots), True)):
-        send[cap : cap + cap2, :] = block
-    sums = [matmul(chooser[voxels:], upstream).astype(BF16) for chooser in choosers]
+        chooser = one_hot_columns(codes[o : o + 1, :], slots * cap2)
+        sums.append(matmul(chooser, upstream).astype(BF16))
     blocks = []
     for s in range(slots):
-        rows = slice(s * cap2, (s + 1) * cap2)
+        listed_rows = slice(s * cap2, (s + 1) * cap2)
         halves = [
-            sums[o][rows, start : start + LANES]
+            sums[o][listed_rows, start : start + LANES]
             for o in range(octants)
             for start in range(0, upstream.shape[1], LANES)
         ]
         blocks.append(jnp.concatenate(halves, axis=0))
     for send, block in zip(sends, to_steps(blocks, True)):
         send[cap + cap2 :, :] = block
+    write(cap + cap2, sends[0].shape[0])
+    codes = half_codes(rows, voxels, slots * cap2)
+    half = voxels // 2
+    choosers, sides = [], []
+    for o in range(octants):
+        part = matmul_rt(upstream, down_ref[o]).astype(BF16)
+        code = codes[o : o + 1, :].astype(BF16)
+        right = column(code) < jnp.zeros(part.shape, BF16)
+        none = jnp.zeros(part.shape, BF16)
+        pair = [jnp.where(right, none, part), jnp.where(right, part, none)]
+        sides.append(jnp.concatenate(pair, axis=1))
+        choosers.append(one_hot_columns(jnp.abs(code), half + slots * cap2 // 2))
+    both = matmul(jnp.concatenate(choosers, axis=1), jnp.concatenate(sides, axis=0))
+    back_ref[0:half, :] = both[0:half, :LANES]
+    back_ref[half:, :] = both[0:half, LANES:]
+    far = jnp.concatenate([both[half:, :LANES], both[half:, LANES:]], axis=0).astype(BF16)
+    for send, block in zip(sends, to_steps(jnp.split(far, slots), True)):
+        send[cap : cap + cap2, :] = block
+    write(0, cap + cap2)
+    written += write_pieces(back_ref, back_hbm, back_sems)
+    for copy in written:
+        copy.wait()
 
 
 def half_codes(row, voxels, received):
@@ -353,22 +376,49 @@
     return pl.multiple_of(core * rows, 16), pl.multiple_of((1 - core) * rows, 16)
 
 
-def pair_kernel(terms_ref, other_ref, out_ref):
-    rows = other_ref.shape[0]
-    mine = terms_ref[pl.ds(my_half(rows)[0], rows), :].astype(F32)
-    out_ref[...] = (mine + other_ref[...].astype(F32)).astype(BF16)
-
-
-def sum_kernel(devices, scale, parts_ref, after_ref, out_ref):
+def write_pieces(stage_ref, out_hbm, sems, first=0, last=None):
+    pieces = sems.shape[0]
+    rows = stage_ref.shape[0] // pieces
+    copies = []
+    for n in range(first, pieces if last is None else last):
+        place = pl.ds(n * rows, rows)
+        copies.append(pltpu.make_async_copy(stage_ref.at[place], out_hbm.at[place], sems.at[n]))
+        copies[-1].start()
+    return copies
+
+
+def pair_kernel(terms_ref, other_ref, out_hbm, stage_ref, sems):
+    pieces = sems.shape[0]
+    rows = stage_ref.shape[0] // pieces
+    first = my_half(stage_ref.shape[0])[0]
+    copies = []
+    for n in range(pieces):
+        place = pl.ds(pl.multiple_of(first + n * rows, 16), rows)
+        other = other_ref[n * rows : (n + 1) * rows, :].astype(F32)
+        value = terms_ref[place, :].astype(F32) + other
+        stage_ref[n * rows : (n + 1) * rows, :] = value.astype(BF16)
+        copies += write_pieces(stage_ref, out_hbm, sems, n, n + 1)
+    for copy in copies:
+        copy.wait()
+
+
+def sum_kernel(devices, scale, parts_ref, after_ref, out_hbm, stage_ref, sems):
     rows = parts_ref.shape[0] // devices
+    sums = []
     for core in range(2):
-        mine = range(core, devices, 2)
         total = jnp.zeros((rows, LANES), F32)
-        for d in mine:
+        for d in range(core, devices, 2):
             total = total + parts_ref[d * rows : (d + 1) * rows, :].astype(F32)
-        total = (total * scale).astype(BF16)
-        for d in mine:
-            out_ref[d * rows : (d + 1) * rows, :] = total
+        sums.append((total * scale).astype(BF16))
+    pieces = sems.shape[0]
+    copies = []
+    for d in range(devices):
+        stage_ref[d * rows : (d + 1) * rows, :] = sums[d % 2]
+        if (d + 1) % (devices // pieces) == 0:
+            piece = d // (devices // pieces)
+            copies += write_pieces(stage_ref, out_hbm, sems, piece, piece + 1)
+    for copy in copies:
+        copy.wait()
 
 
 def final_kernel(own, *refs):
@@ -480,14 +530,17 @@
         head_kernel,
         (features, halo_rows, child_map, out_grad, down_weight),
         [((cap + cap2 + sum_rows, channels), BF16)] * slots + [((voxels, channels), F32)],
-        scratch=[
+        scratch=[pltpu.VMEM((cap + cap2 + sum_rows, channels), BF16)] * slots
+        + [pltpu.VMEM((voxels, channels), F32)]
+        + [
             pltpu.VMEM(value.shape, value.dtype)
             for value in (features, halo_rows, child_map, out_grad, down_weight)
         ]
-        + [pltpu.SemaphoreType.DMA((5,))],
+        + [pltpu.SemaphoreType.DMA((5 + 2 * slots,)), pltpu.SemaphoreType.DMA((4,))],
         limit=60,
         flops=giga,
         in_hbm=range(5),
+        out_hbm=True,
     )
     back_h = first[-1]
     received = swaps(first[:-1], (2, 3, 1, 0))
@@ -539,7 +592,9 @@
         pair_kernel,
         (terms, swap_cores(leaving_terms, devices)),
         [((half_rows, LANES), BF16)],
+        scratch=[pltpu.VMEM((half_rows, LANES), BF16), pltpu.SemaphoreType.DMA((8,))],
         flops=10**6,
+        out_hbm=True,
     )
     parts = exchange(pair_terms)
     spread = call(
@@ -554,8 +609,10 @@
         functools.partial(sum_kernel, devices, scale),
         (parts, spread[1]),
         [((half_rows, LANES), BF16)],
+        scratch=[pltpu.VMEM((half_rows, LANES), BF16), pltpu.SemaphoreType.DMA((8,))],
         flops=10**6,
         in_hbm=(1,),
+        out_hbm=True,
     )
     summed, *returning = lax.optimization_barrier((summed, *spread[1:]))
     returned = swaps(returning, (0, 1, 2, 3))

time: 87.8 us -> 87.2 us (level)
  no operation moved by 1% of the time
where the time goes in v15:
time: 87.2 us; the launch traced here: 86 us
  Pallas kernels  41.2 us (47%)
  starting transfers between devices  23.9 us (27%)
  waiting for transfers between devices  18.9 us (22%)
  between operations  1.06 us (1%)
  local copies, waits for them, and re-layouts  1 us (1%)
    pallas_call x10, Pallas kernels, call(): pl.pallas_call(kernel, out_shape=[jax.ShapeDtypeStruct(s, d) for s, d in...  41.2 us
    ppermute x8, starting transfers between devices, swaps(): moved[step] = lax.ppermute(by_step[step], 'shard', pairs)  12.3 us
    all_to_all x2, waiting for transfers between devices, exchange(): return lax.all_to_all(value, 'shard', 0, 0, tiled=True)  11.8 us
    all_to_all x2, starting transfers between devices, exchange(): return lax.all_to_all(value, 'shard', 0, 0, tiled=True)  10.8 us
    ppermute x8, waiting for transfers between devices, swaps(): moved[step] = lax.ppermute(by_step[step], 'shard', pairs)  4.42 us
    ppermute x2, waiting for transfers between devices, swap_cores(): lax.ppermute(value, 'shard', [(i, i + 1 - 2 * (i % 2)) for i in range(dev...  2.62 us
  transfers between devices with their start and end apart: 12, of which 7 were waited for; matrix products, arithmetic and copies ran while one was open for 0% of the time, Pallas kernels for 29%

profile of v15, /device:TPU:1, one launch (start us, length us, event | category | flops | bytes accessed | tf_op | source)
XLA Modules:
  0.0 86.0 jit_solution(9004016175329873065)
XLA Ops:
  0.6 0.0 copy-start.2
  0.6 0.0 copy-start.4
  0.7 3.6 %shard_map.111 = (bf16[608,128]{1,0:T(8,128)(2,1)}, bf16[608,128]{1,0:T(8,128)(2,1)}, bf16[608,128]{1,0:T(8,128)(2,1)}, bf16[608,128]{1,0:T(8,128)(2,1)}, f32[1024,128]{1,0:T(8,128)}) custom-call(bf16[1024,128]{1,0:T(8,128)(2,1)} %refs_4_.1, s32[4,64]{1,0:T(4,128)} %refs_6_.5, s32[8,256]{1,0:T(8,128)} %refs_8_.1, bf16[256,256]{1,0:T(8,128)(2,1)} %refs_11_.1, ...), custom_call_target="tpu_custom_call" | custom-call | flops 1000000000 | bytes 4194304 | tf_op jit(solution)/shard_map/pallas_call | solution.py:491
  4.3 0.1 collective-permute-start
  4.4 4.5 %collective-permute-start.1 = (bf16[608,128]{1,0:T(8,128)(2,1)}, bf16[608,128]{1,0:T(8,128)(2,1)S(1)}, u32[]{:S(2)}, u32[]{:S(2)}) collective-permute-start(bf16[608,128]{1,0:T(8,128)(2,1)} %get-tuple-element.37), channel_id=1, source_target_pairs={{1,2},{2,1},{3,4},{4,3},{5,6},{6,5},{7,8},{8,7},{9,10},{10,9},{11,... | collective-permute-start | bytes 466952 | tf_op jit(solution)/shard_map/ppermute | solution.py:23
  8.9 1.3 %collective-permute-start.2 = (bf16[608,128]{1,0:T(8,128)(2,1)}, bf16[608,128]{1,0:T(8,128)(2,1)S(1)}, u32[]{:S(2)}, u32[]{:S(2)}) collective-permute-start(bf16[608,128]{1,0:T(8,128)(2,1)} %get-tuple-element.38), channel_id=1, source_target_pairs={{0,2},{1,3},{2,0},{3,1},{4,6},{5,7},{6,4},{7,5},{8,10},{9,11},{10,... | collective-permute-start | bytes 466952 | tf_op jit(solution)/shard_map/ppermute | solution.py:23
  10.1 0.0 copy-start
  10.1 0.0 copy-start.6
  10.1 0.8 collective-permute-start.3
  10.9 0.0 copy-done.2
  11.0 0.0 copy-done.4
  11.0 7.3 %shard_map.112.refs_8_ = bf16[1024,3328]{1,0:T(8,128)(2,1)S(1)} custom-call(bf16[1024,128]{1,0:T(8,128)(2,1)S(1)} %copy-done.2, s32[27,1024]{1,0:T(8,128)S(1)} %copy-done.4), custom_call_target="tpu_custom_call" | custom-call | flops 4000000000 | bytes 4194304 | tf_op jit(solution)/shard_map/pallas_call | solution.py:491
  18.3 0.0 copy-start.3
  18.3 0.0 copy-start.5
  18.3 0.0 copy-start.8
  18.3 0.0 collective-permute-done.refs_0_
  18.3 0.0 collective-permute-done.1.refs_1_
  18.3 1.3 %collective-permute-done.2.refs_2_ = bf16[608,128]{1,0:T(8,128)(2,1)S(1)} collective-permute-done((bf16[608,128]{1,0:T(8,128)(2,1)}, bf16[608,128]{1,0:T(8,128)(2,1)S(1)}, u32[]{:S(2)}, u32[]{:S(2)}) %collective-permute-start.2) | collective-permute-done | bytes 155680 | tf_op jit(solution)/shard_map/ppermute | solution.py:23
  19.7 0.0 collective-permute-done.3.refs_3_
  19.7 0.0 copy-done
  19.7 0.0 copy-done.6
  19.7 6.6 %shard_map.113 = (bf16[1024,128]{1,0:T(8,128)(2,1)S(1)}, f32[1024,128]{1,0:T(8,128)S(1)}, bf16[1024,3456]{1,0:T(8,128)(2,1)S(1)}, bf16[128,128]{1,0:T(8,128)(2,1)S(1)}) custom-call(bf16[608,128]{1,0:T(8,128)(2,1)S(1)} %collective-permute-done.refs_0_, bf16[608,128]{1,0:T(8,128)(2,1)S(1)} %collective-permute-done.1.refs_1_, ...), custom_call_target="tpu_custom_call" | custom-call | flops 12000000000 | bytes 4194304 | tf_op jit(solution)/shard_map/pallas_call | solution.py:491
  26.3 0.0 copy-done.3
  26.3 0.0 copy-done.5
  26.3 0.0 copy-done.8
  26.3 2.6 %shard_map.114 = (f32[1024,128]{1,0:T(8,128)S(1)}, bf16[1024,128]{1,0:T(8,128)(2,1)S(1)}, bf16[256,1024]{1,0:T(8,128)(2,1)S(1)}, bf16[5632,128]{1,0:T(8,128)(2,1)S(1)}, bf16[2816,128]{1,0:T(8,128)(2,1)S(1)}) custom-call(bf16[608,128]{1,0:T(8,128)(2,1)S(1)} %collective-permute-done.refs_0_, bf16[608,128]{1,0:T(8,128)(2,1)S(1)} %collective-permute-done.1.refs_1_, ...), custom_call_target="tpu_custom_call" | custom-call | flops 3000000000 | bytes 4194304 | tf_op jit(solution)/shard_map/pallas_call | solution.py:491
  28.9 0.0 copy-start.9
  28.9 0.1 collective-permute-start.4
  29.0 2.2 %collective-permute-done.4.other_ref = bf16[2816,128]{1,0:T(8,128)(2,1)S(1)} collective-permute-done((bf16[2816,128]{1,0:T(8,128)(2,1)S(1)}, bf16[2816,128]{1,0:T(8,128)(2,1)S(1)}, u32[]{:S(2)}, u32[]{:S(2)}) %collective-permute-start.4) | collective-permute-done | bytes 720928 | tf_op jit(solution)/shard_map/ppermute | solution.py:504
  31.2 0.9 %shard_map.115.after_ref = bf16[2816,128]{1,0:T(8,128)(2,1)} custom-call(bf16[5632,128]{1,0:T(8,128)(2,1)S(1)} %get-tuple-element.45.terms_ref, bf16[2816,128]{1,0:T(8,128)(2,1)S(1)} %collective-permute-done.4.other_ref), custom_call_target="tpu_custom_call" | custom-call | flops 1000000 | bytes 4194304 | tf_op jit(solution)/shard_map/pallas_call | solution.py:491
  32.1 0.0 copy-done.9
  32.1 6.9 %all-to-all-start = ((bf16[32,88,128]{2,1,0:T(8,128)(2,1)}), bf16[32,88,128]{2,1,0:T(8,128)(2,1)S(1)}, u32[]{:S(2)}, u32[]{:S(2)}) async-start(bf16[32,88,128]{2,1,0:T(8,128)(2,1)} %bitcast), calls=%async_computation | async-start | bytes 1441792 | tf_op jit(solution)/shard_map/all_to_all | solution.py:508
  39.1 0.0 copy-start.10
  39.1 0.9 %copy-done.10 = bf16[1024,128]{1,0:T(8,128)(2,1)S(1)} copy-done((bf16[1024,128]{1,0:T(8,128)(2,1)S(1)}, bf16[1024,128]{1,0:T(8,128)(2,1)}, u32[]{:S(2)}) %copy-start.10) | copy-done | bytes 262168
  40.0 14.9 %shard_map.116 = (f32[1024,128]{1,0:T(8,128)S(1)}, bf16[96,128]{1,0:T(8,128)(2,1)S(1)}, bf16[96,128]{1,0:T(8,128)(2,1)S(1)}, bf16[96,128]{1,0:T(8,128)(2,1)S(1)}, bf16[96,128]{1,0:T(8,128)(2,1)S(1)}) custom-call(bf16[1024,128]{1,0:T(8,128)(2,1)S(1)} %copy-done.10, s32[27,1024]{1,0:T(8,128)S(1)} %copy-done.4, bf16[27,128,128]{2,1,0:T(8,128)(2,1)S(1)} %copy-done, ...), custom_call_target="tpu_custom_call" | custom-call | flops 20000000000 | bytes 4194304 | tf_op jit(solution)/shard_map/pallas_call | solution.py:491
  55.0 0.0 copy-start.1
  55.0 0.0 copy-start.7
  55.0 3.0 %all-to-all-done = bf16[32,88,128]{2,1,0:T(8,128)(2,1)S(1)} async-done(((bf16[32,88,128]{2,1,0:T(8,128)(2,1)}), bf16[32,88,128]{2,1,0:T(8,128)(2,1)S(1)}, u32[]{:S(2)}, u32[]{:S(2)}) %all-to-all-start) | async-done | bytes 720928 | tf_op jit(solution)/shard_map/all_to_all | solution.py:508
  58.0 1.0 %shard_map.117 = bf16[2816,128]{1,0:T(8,128)(2,1)} custom-call(bf16[2816,128]{1,0:T(8,128)(2,1)S(1)} %bitcast.8, bf16[96,128]{1,0:T(8,128)(2,1)S(1)} %get-tuple-element.52.after_ref), custom_call_target="tpu_custom_call" | custom-call | flops 1000000 | bytes 4194304 | tf_op jit(solution)/shard_map/pallas_call | solution.py:491
  59.1 3.9 %all-to-all-start.1 = ((bf16[32,88,128]{2,1,0:T(8,128)(2,1)}), bf16[32,88,128]{2,1,0:T(8,128)(2,1)S(1)}, u32[]{:S(2)}, u32[]{:S(2)}) async-start(bf16[32,88,128]{2,1,0:T(8,128)(2,1)} %bitcast.2), calls=%async_computation.1 | async-start | bytes 1441792 | tf_op jit(solution)/shard_map/all_to_all | solution.py:508
  62.9 0.3 collective-permute-start.5
  63.3 3.4 %collective-permute-start.6 = (bf16[96,128]{1,0:T(8,128)(2,1)S(1)}, bf16[96,128]{1,0:T(8,128)(2,1)S(1)}, u32[]{:S(2)}, u32[]{:S(2)}) collective-permute-start(bf16[96,128]{1,0:T(8,128)(2,1)S(1)} %get-tuple-element.53), channel_id=1, source_target_pairs={{1,2},{2,1},{3,4},{4,3},{5,6},{6,5},{7,8},{8,7},{9,10},{10,9},{11,... | collective-permute-start | bytes 73736 | tf_op jit(solution)/shard_map/ppermute | solution.py:23
  66.7 1.2 %collective-permute-start.7 = (bf16[96,128]{1,0:T(8,128)(2,1)S(1)}, bf16[96,128]{1,0:T(8,128)(2,1)S(1)}, u32[]{:S(2)}, u32[]{:S(2)}) collective-permute-start(bf16[96,128]{1,0:T(8,128)(2,1)S(1)} %get-tuple-element.54), channel_id=1, source_target_pairs={{0,2},{1,3},{2,0},{3,1},{4,6},{5,7},{6,4},{7,5},{8,10},{9,11},{10,... | collective-permute-start | bytes 73736 | tf_op jit(solution)/shard_map/ppermute | solution.py:23
  67.9 0.7 collective-permute-start.8
  68.6 0.0 collective-permute-done.5.refs_0_
  68.6 0.1 collective-permute-done.6.refs_1_
  68.8 2.9 %collective-permute-done.7.refs_2_ = bf16[96,128]{1,0:T(8,128)(2,1)S(1)} collective-permute-done((bf16[96,128]{1,0:T(8,128)(2,1)S(1)}, bf16[96,128]{1,0:T(8,128)(2,1)S(1)}, u32[]{:S(2)}, u32[]{:S(2)}) %collective-permute-start.7) | collective-permute-done | bytes 24608 | tf_op jit(solution)/shard_map/ppermute | solution.py:23
  71.7 0.0 collective-permute-done.8.refs_3_
  71.7 0.0 copy-done.1
  71.7 0.0 copy-done.7
  71.7 1.5 %shard_map.118 = (f32[1024,128]{1,0:T(8,128)}, bf16[256,256]{1,0:T(8,128)(2,1)}) custom-call(bf16[96,128]{1,0:T(8,128)(2,1)S(1)} %collective-permute-done.5.refs_0_, bf16[96,128]{1,0:T(8,128)(2,1)S(1)} %collective-permute-done.6.refs_1_, bf16[96,128]{1,0:T(8,128)(2,1)S(1)} %collective-permute-done.7.refs_2_, ...), custom_call_target="tpu_custom_call" | custom-call | flops 1000000000 | bytes 4194304 | tf_op jit(solution)/shard_map/pallas_call | solution.py:491
  73.1 8.8 %all-to-all-done.1 = bf16[32,88,128]{2,1,0:T(8,128)(2,1)S(1)} async-done(((bf16[32,88,128]{2,1,0:T(8,128)(2,1)}), bf16[32,88,128]{2,1,0:T(8,128)(2,1)S(1)}, u32[]{:S(2)}, u32[]{:S(2)}) %all-to-all-start.1) | async-done | bytes 720928 | tf_op jit(solution)/shard_map/all_to_all | solution.py:508
  81.9 0.8 collective-permute-start.9
  82.7 1.4 %shard_map.119 = (f32[3456,128]{1,0:T(8,128)}, f32[1024,256]{1,0:T(8,128)}) custom-call(bf16[2816,128]{1,0:T(8,128)(2,1)S(1)} %bitcast.7), custom_call_target="tpu_custom_call" | custom-call | flops 1000000 | bytes 4194304 | tf_op jit(solution)/shard_map/pallas_call | solution.py:491
  84.1 0.4 collective-permute-done.9.refs_0_
  84.5 1.4 %shard_map.120 = (f32[3456,128]{1,0:T(8,128)}, f32[1024,256]{1,0:T(8,128)}) custom-call(bf16[2816,128]{1,0:T(8,128)(2,1)S(1)} %collective-permute-done.9.refs_0_, f32[3456,128]{1,0:T(8,128)} %get-tuple-element.64.refs_1_, f32[1024,256]{1,0:T(8,128)} %get-tuple-element.65.refs_2_), custom_call_target="tpu_custom_call", output_to_operand_aliasing={{0}: (1, {}), {1}: (2, {})} | custom-call | flops 1000000 | bytes 4194304 | tf_op jit(solution)/shard_map/pallas_call | solution.py:491
Async XLA Ops:
  0.6 10.3 %copy-start.2 = (bf16[1024,128]{1,0:T(8,128)(2,1)S(1)}, bf16[1024,128]{1,0:T(8,128)(2,1)}, u32[]{:S(2)}) copy-start(bf16[1024,128]{1,0:T(8,128)(2,1)} %refs_4_.1) | copy-start | bytes 786436
  0.6 10.3 %copy-start.4 = (s32[27,1024]{1,0:T(8,128)S(1)}, s32[27,1024]{1,0:T(8,128)}, u32[]{:S(2)}) copy-start(s32[27,1024]{1,0:T(8,128)} %map_ref.3) | copy-start | bytes 331780
  4.3 14.0 %collective-permute-start = (bf16[608,128]{1,0:T(8,128)(2,1)}, bf16[608,128]{1,0:T(8,128)(2,1)S(1)}, u32[]{:S(2)}, u32[]{:S(2)}) collective-permute-start(bf16[608,128]{1,0:T(8,128)(2,1)} %get-tuple-element.36), channel_id=1, source_target_pairs={{0,1},{1,0},{2,3},{3,2},{4,5},{5,4},{6,7},{7,6},{8,9},{9,8},{10,11... | collective-permute-start | bytes 466952 | tf_op jit(solution)/shard_map/ppermute | solution.py:23
  4.4 13.9 %collective-permute-start.1 = (bf16[608,128]{1,0:T(8,128)(2,1)}, bf16[608,128]{1,0:T(8,128)(2,1)S(1)}, u32[]{:S(2)}, u32[]{:S(2)}) collective-permute-start(bf16[608,128]{1,0:T(8,128)(2,1)} %get-tuple-element.37), channel_id=1, source_target_pairs={{1,2},{2,1},{3,4},{4,3},{5,6},{6,5},{7,8},{8,7},{9,10},{10,9},{11,... | collective-permute-start | bytes 466952 | tf_op jit(solution)/shard_map/ppermute | solution.py:23
  8.9 10.8 %collective-permute-start.2 = (bf16[608,128]{1,0:T(8,128)(2,1)}, bf16[608,128]{1,0:T(8,128)(2,1)S(1)}, u32[]{:S(2)}, u32[]{:S(2)}) collective-permute-start(bf16[608,128]{1,0:T(8,128)(2,1)} %get-tuple-element.38), channel_id=1, source_target_pairs={{0,2},{1,3},{2,0},{3,1},{4,6},{5,7},{6,4},{7,5},{8,10},{9,11},{10,... | collective-permute-start | bytes 466952 | tf_op jit(solution)/shard_map/ppermute | solution.py:23
  10.1 9.5 %copy-start = (bf16[27,128,128]{2,1,0:T(8,128)(2,1)S(1)}, bf16[27,128,128]{2,1,0:T(8,128)(2,1)}, u32[]{:S(2)}) copy-start(bf16[27,128,128]{2,1,0:T(8,128)(2,1)} %weight_ref.1) | copy-start | bytes 2654212
  10.1 9.5 %copy-start.6 = (s32[4,32]{1,0:T(4,128)S(1)}, s32[4,32]{1,0:T(4,128)}, u32[]{:S(2)}) copy-start(s32[4,32]{1,0:T(4,128)} %refs_6_.4) | copy-start | bytes 1540
  10.1 9.5 %collective-permute-start.3 = (bf16[608,128]{1,0:T(8,128)(2,1)}, bf16[608,128]{1,0:T(8,128)(2,1)S(1)}, u32[]{:S(2)}, u32[]{:S(2)}) collective-permute-start(bf16[608,128]{1,0:T(8,128)(2,1)} %get-tuple-element.39), channel_id=1, source_target_pairs={{2,4},{3,5},{4,2},{5,3},{6,8},{7,9},{8,6},{9,7},{10,12},{11,13},{1... | collective-permute-start | bytes 466952 | tf_op jit(solution)/shard_map/ppermute | solution.py:23
  18.3 8.0 %copy-start.3 = (bf16[256,256]{1,0:T(8,128)(2,1)S(1)}, bf16[256,256]{1,0:T(8,128)(2,1)}, u32[]{:S(2)}) copy-start(bf16[256,256]{1,0:T(8,128)(2,1)} %refs_11_.1) | copy-start | bytes 393220
  18.3 8.0 %copy-start.5 = (s32[8,256]{1,0:T(8,128)S(1)}, s32[8,256]{1,0:T(8,128)}, u32[]{:S(2)}) copy-start(s32[8,256]{1,0:T(8,128)} %refs_8_.1) | copy-start | bytes 24580
  18.3 8.0 %copy-start.8 = (f32[1024,128]{1,0:T(8,128)S(1)}, f32[1024,128]{1,0:T(8,128)}, u32[]{:S(2)}) copy-start(f32[1024,128]{1,0:T(8,128)} %get-tuple-element.42.refs_7_) | copy-start | bytes 1572868
  28.9 3.2 %copy-start.9 = (bf16[1024,128]{1,0:T(8,128)(2,1)}, bf16[1024,128]{1,0:T(8,128)(2,1)S(1)}, u32[]{:S(2)}) copy-start(bf16[1024,128]{1,0:T(8,128)(2,1)S(1)} %get-tuple-element.47.pgrad_ref) | copy-start | bytes 786436
  28.9 2.3 %collective-permute-start.4 = (bf16[2816,128]{1,0:T(8,128)(2,1)S(1)}, bf16[2816,128]{1,0:T(8,128)(2,1)S(1)}, u32[]{:S(2)}, u32[]{:S(2)}) collective-permute-start(bf16[2816,128]{1,0:T(8,128)(2,1)S(1)} %get-tuple-element.46), channel_id=1, source_target_pairs={{0,1},{1,0},{2,3},{3,2},{4,5},{5,4},{6,7},{7,6},{8,9},{9,8},{10,11... | collective-permute-start | bytes 2162696 | tf_op jit(solution)/shard_map/ppermute | solution.py:504
  32.1 25.9 %all-to-all-start = ((bf16[32,88,128]{2,1,0:T(8,128)(2,1)}), bf16[32,88,128]{2,1,0:T(8,128)(2,1)S(1)}, u32[]{:S(2)}, u32[]{:S(2)}) async-start(bf16[32,88,128]{2,1,0:T(8,128)(2,1)} %bitcast), calls=%async_computation | async-start | bytes 1441792 | tf_op jit(solution)/shard_map/all_to_all | solution.py:508
  39.1 1.0 %copy-start.10 = (bf16[1024,128]{1,0:T(8,128)(2,1)S(1)}, bf16[1024,128]{1,0:T(8,128)(2,1)}, u32[]{:S(2)}) copy-start(bf16[1024,128]{1,0:T(8,128)(2,1)} %copy-done.9) | copy-start | bytes 786436
  55.0 16.7 %copy-start.1 = (bf16[8,128,256]{2,1,0:T(8,128)(2,1)S(1)}, bf16[8,128,256]{2,1,0:T(8,128)(2,1)}, u32[]{:S(2)}) copy-start(bf16[8,128,256]{2,1,0:T(8,128)(2,1)} %refs_9_.1) | copy-start | bytes 1572868
  55.0 16.7 %copy-start.7 = (s32[4,64]{1,0:T(4,128)S(1)}, s32[4,64]{1,0:T(4,128)}, u32[]{:S(2)}) copy-start(s32[4,64]{1,0:T(4,128)} %refs_6_.5) | copy-start | bytes 3076
  59.1 22.8 %all-to-all-start.1 = ((bf16[32,88,128]{2,1,0:T(8,128)(2,1)}), bf16[32,88,128]{2,1,0:T(8,128)(2,1)S(1)}, u32[]{:S(2)}, u32[]{:S(2)}) async-start(bf16[32,88,128]{2,1,0:T(8,128)(2,1)} %bitcast.2), calls=%async_computation.1 | async-start | bytes 1441792 | tf_op jit(solution)/shard_map/all_to_all | solution.py:508
  62.9 5.7 %collective-permute-start.5 = (bf16[96,128]{1,0:T(8,128)(2,1)S(1)}, bf16[96,128]{1,0:T(8,128)(2,1)S(1)}, u32[]{:S(2)}, u32[]{:S(2)}) collective-permute-start(bf16[96,128]{1,0:T(8,128)(2,1)S(1)} %get-tuple-element.52.after_ref), channel_id=1, source_target_pairs={{0,1},{1,0},{2,3},{3,2},{4,5},{5,4},{6,7},{7,6},{8,9},{9,8},{10,11... | collective-permute-start | bytes 73736 | tf_op jit(solution)/shard_map/ppermute | solution.py:23
  63.3 5.5 %collective-permute-start.6 = (bf16[96,128]{1,0:T(8,128)(2,1)S(1)}, bf16[96,128]{1,0:T(8,128)(2,1)S(1)}, u32[]{:S(2)}, u32[]{:S(2)}) collective-permute-start(bf16[96,128]{1,0:T(8,128)(2,1)S(1)} %get-tuple-element.53), channel_id=1, source_target_pairs={{1,2},{2,1},{3,4},{4,3},{5,6},{6,5},{7,8},{8,7},{9,10},{10,9},{11,... | collective-permute-start | bytes 73736 | tf_op jit(solution)/shard_map/ppermute | solution.py:23
  66.7 5.0 %collective-permute-start.7 = (bf16[96,128]{1,0:T(8,128)(2,1)S(1)}, bf16[96,128]{1,0:T(8,128)(2,1)S(1)}, u32[]{:S(2)}, u32[]{:S(2)}) collective-permute-start(bf16[96,128]{1,0:T(8,128)(2,1)S(1)} %get-tuple-element.54), channel_id=1, source_target_pairs={{0,2},{1,3},{2,0},{3,1},{4,6},{5,7},{6,4},{7,5},{8,10},{9,11},{10,... | collective-permute-start | bytes 73736 | tf_op jit(solution)/shard_map/ppermute | solution.py:23
  67.9 3.7 %collective-permute-start.8 = (bf16[96,128]{1,0:T(8,128)(2,1)S(1)}, bf16[96,128]{1,0:T(8,128)(2,1)S(1)}, u32[]{:S(2)}, u32[]{:S(2)}) collective-permute-start(bf16[96,128]{1,0:T(8,128)(2,1)S(1)} %get-tuple-element.55), channel_id=1, source_target_pairs={{2,4},{3,5},{4,2},{5,3},{6,8},{7,9},{8,6},{9,7},{10,12},{11,13},{1... | collective-permute-start | bytes 73736 | tf_op jit(solution)/shard_map/ppermute | solution.py:23
  81.9 2.6 %collective-permute-start.9 = (bf16[2816,128]{1,0:T(8,128)(2,1)S(1)}, bf16[2816,128]{1,0:T(8,128)(2,1)S(1)}, u32[]{:S(2)}, u32[]{:S(2)}) collective-permute-start(bf16[2816,128]{1,0:T(8,128)(2,1)S(1)} %bitcast.6), channel_id=1, source_target_pairs={{0,1},{1,0},{2,3},{3,2},{4,5},{5,4},{6,7},{7,6},{8,9},{9,8},{10,11... | collective-permute-start | bytes 2162696 | tf_op jit(solution)/shard_map/ppermute | solution.py:504

commit v16 on v15

--- a/solution.py
+++ b/solution.py
@@ -212,8 +212,8 @@
     return code * jnp.where(outside, far_sign, near_sign)
 
 
-def offset_of(n, middle):
-    return n + jnp.where(n >= middle, 1, 0)
+def outer_offsets(kernel_count):
+    return [k for k in range(kernel_count) if k != kernel_count // 2]
 
 
 def code_column(map_ref, k, voxels, received):
@@ -224,25 +224,28 @@
     return jnp.where(col < jnp.zeros(col.shape, BF16), both[:, LANES:], both[:, :LANES])
 
 
-def local_kernel(received, features_ref, map_ref, early_ref, table_ref):
+def local_kernel(received, features_ref, map_ref, early_ref, col_ref, table_ref):
     voxels = features_ref.shape[0]
-    half = voxels // 2
+    kernel_count = map_ref.shape[0]
+    half, middle = voxels // 2, kernel_count // 2
     table_ref[:, 0:LANES] = features_ref[0:half, :]
     table_ref[:, LANES:] = features_ref[half:, :]
-    middle = map_ref.shape[0] // 2
-    for n in range(early_ref.shape[1] // LANES):
-        col = code_column(map_ref, offset_of(n, middle), voxels, received)
+    early_ref[:, middle * LANES : (middle + 1) * LANES] = features_ref[...]
+    for k in outer_offsets(kernel_count):
+        lanes = slice(k * LANES, (k + 1) * LANES)
+        col = code_column(map_ref, k, voxels, received)
+        col_ref[:, lanes] = col
         both = matmul(one_hot_rows(jnp.abs(col), half), table_ref[...]).astype(BF16)
-        early_ref[:, n * LANES : (n + 1) * LANES] = pick_side(col, both)
+        early_ref[:, lanes] = pick_side(col, both)
 
 
 def forward_kernel(slots, cap, *refs):
     received = refs[:slots]
-    features_ref, map_ref, weight_ref, child_ref, early_ref = refs[slots : slots + 5]
-    hidden_ref, pre_ref, stacked_ref, leaving_ref, halo_ref, kernel_ref = refs[slots + 5 :]
+    features_ref, weight_ref, child_ref, early_ref, col_ref = refs[slots : slots + 5]
+    hidden_ref, pre_ref, stacked_ref, leaving_ref, halo_ref = refs[slots + 5 :]
     voxels = features_ref.shape[0]
-    gathers = map_ref.shape[0] - 1
-    middle = gathers // 2
+    kernel_count = weight_ref.shape[0]
+    middle = kernel_count // 2
     half, half_halo = voxels // 2, slots * cap // 2
     features = features_ref[...]
     halo_ref[...] = jnp.zeros(halo_ref.shape, BF16)
@@ -252,22 +255,18 @@
         for n in range(2):
             row, lane = n * half_halo + place, 2 * n * LANES + side
             halo_ref[row : row + cap, lane : lane + LANES] = block
-    kernel_ref[0:middle] = weight_ref[0:middle]
-    kernel_ref[middle:gathers] = weight_ref[middle + 1 :]
-    kernel_ref[gathers] = weight_ref[middle]
-
-    for j in range(middle):
-        numbers = (2 * j, 2 * j + 1)
-        cols = [code_column(map_ref, offset_of(n, middle), voxels, slots * cap) for n in numbers]
+    outer = outer_offsets(kernel_count)
+    for first in range(0, len(outer), 2):
+        places = [slice(k * LANES, (k + 1) * LANES) for k in outer[first : first + 2]]
+        cols = [col_ref[:, lanes] for lanes in places]
         choosers = [one_hot_rows(jnp.abs(col), half_halo, half) for col in cols]
         far = matmul(jnp.concatenate(choosers, axis=1), halo_ref[...]).astype(BF16)
-        for n in numbers:
-            both = far[:, 2 * (n % 2) * LANES : 2 * (n % 2 + 1) * LANES]
-            lanes = slice(n * LANES, (n + 1) * LANES)
-            stacked_ref[:, lanes] = pick_side(cols[n % 2], both) + early_ref[:, lanes]
-
-    stacked_ref[:, gathers * LANES :] = features
-    pre = matmul(stacked_ref[...], kernel_ref[...].reshape(-1, LANES))
+        for n, lanes in enumerate(places):
+            both = far[:, 2 * n * LANES : 2 * (n + 1) * LANES]
+            stacked_ref[:, lanes] = pick_side(cols[n], both) + early_ref[:, lanes]
+    lanes = slice(middle * LANES, (middle + 1) * LANES)
+    stacked_ref[:, lanes] = early_ref[:, lanes]
+    pre = matmul(stacked_ref[...], weight_ref[...].reshape(-1, LANES))
     pre_ref[...] = pre
     hidden = (features.astype(F32) + pre * jax.nn.sigmoid(pre)).astype(BF16)
     hidden_ref[...] = hidden
@@ -281,7 +280,6 @@
     hgrad_ref, pgrad_ref, early_ref, terms_ref, send_ref = refs[slots + 8 :]
     cap2 = child_ref.shape[1]
     kernel_count = stacked_ref.shape[1] // LANES
-    middle = kernel_count // 2
     blocks = to_slots([r[cap : cap + cap2, :] for r in received], True)
     hgrad = add_lists(back_ref[...], child_ref, blocks)
     hgrad_ref[...] = hgrad
@@ -290,9 +288,8 @@
     pgrad = hgrad * (sig * (1.0 + pre * (1.0 - sig)))
     pgrad_ref[...] = pgrad.astype(BF16)
     terms = matmul(jnp.transpose(pgrad).astype(BF16), stacked_ref[...])
-    order = [k for k in range(kernel_count) if k != middle] + [middle]
-    for n, k in enumerate(order):
-        block = jnp.transpose(terms[:, n * LANES : (n + 1) * LANES])
+    for k in range(kernel_count):
+        block = jnp.transpose(terms[:, k * LANES : (k + 1) * LANES])
         terms_ref[k * LANES : (k + 1) * LANES, :] = block.astype(BF16)
     voxels = hidden_ref.shape[0]
     half = voxels // 2
@@ -544,26 +541,23 @@
     )
     back_h = first[-1]
     received = swaps(first[:-1], (2, 3, 1, 0))
-    (early,) = call(
+    early, cols = call(
         functools.partial(local_kernel, slots * cap),
         (features, neighbour_map),
-        [((voxels, conv_rows - channels), BF16)],
+        [((voxels, conv_rows), BF16)] * 2,
         scratch=[pltpu.VMEM((voxels // 2, 2 * channels), BF16)],
         flops=4 * giga,
     )
     hidden, pre_act, stacked, leaving = call(
         functools.partial(forward_kernel, slots, cap),
-        (*received, features, neighbour_map, conv_weight, child_rows, early),
+        (*received, features, conv_weight, child_rows, early, cols),
         [
             ((voxels, channels), BF16),
             ((voxels, channels), F32),
             ((voxels, conv_rows), BF16),
             ((slots * cap2, channels), BF16),
         ],
-        scratch=[
-            pltpu.VMEM((slots * cap, 4 * channels), BF16),
-            pltpu.VMEM(conv_weight.shape, BF16),
-        ],
+        scratch=[pltpu.VMEM((slots * cap, 4 * channels), BF16)],
         flops=12 * giga,
     )
     hidden_grad, pre_grad, early_h, terms, leaving_terms = call(

time: 87.2 us -> 96.7 us (1.11)
  the two profiles are of different devices: /device:TPU:1 before, /device:TPU:17 now
where the time goes in v16:
time: 96.7 us; the launch traced here: 96.2 us
  Pallas kernels  45.1 us (47%)
  starting transfers between devices  27.2 us (28%)
  waiting for transfers between devices  15.2 us (16%)
  local copies, waits for them, and re-layouts  7.54 us (8%)
  between operations  1.08 us (1%)
    pallas_call x10, Pallas kernels, call(): pl.pallas_call(kernel, out_shape=[jax.ShapeDtypeStruct(s, d) for s, d in...  45.1 us
    ppermute x8, starting transfers between devices, swaps(): moved[step] = lax.ppermute(by_step[step], 'shard', pairs)  16 us
    ppermute x8, waiting for transfers between devices, swaps(): moved[step] = lax.ppermute(by_step[step], 'shard', pairs)  11.6 us
    all_to_all x2, starting transfers between devices, exchange(): return lax.all_to_all(value, 'shard', 0, 0, tiled=True)  9.73 us
    unnamed x30, local copies, waits for them, and re-layouts  7.54 us
    ppermute x2, waiting for transfers between devices, swap_cores(): lax.ppermute(value, 'shard', [(i, i + 1 - 2 * (i % 2)) for i in range(dev...  2.26 us
  transfers between devices with their start and end apart: 12, of which 4 were waited for; matrix products, arithmetic and copies ran while one was open for 0% of the time, Pallas kernels for 26%

profile of v16, /device:TPU:17, one launch (start us, length us, event | category | flops | bytes accessed | tf_op | source)
XLA Modules:
  0.0 96.2 jit_solution(10182429590397245282)
XLA Ops:
  0.6 3.6 %shard_map.111 = (bf16[608,128]{1,0:T(8,128)(2,1)}, bf16[608,128]{1,0:T(8,128)(2,1)}, bf16[608,128]{1,0:T(8,128)(2,1)}, bf16[608,128]{1,0:T(8,128)(2,1)}, f32[1024,128]{1,0:T(8,128)}) custom-call(bf16[1024,128]{1,0:T(8,128)(2,1)} %refs_4_.1, s32[4,64]{1,0:T(4,128)} %refs_6_.5, s32[8,256]{1,0:T(8,128)} %refs_8_.1, bf16[256,256]{1,0:T(8,128)(2,1)} %refs_11_.1, ...), custom_call_target="tpu_custom_call" | custom-call | flops 1000000000 | bytes 4194304 | tf_op jit(solution)/shard_map/pallas_call | solution.py:488
  4.2 0.7 collective-permute-start
  4.9 3.0 %collective-permute-start.1 = (bf16[608,128]{1,0:T(8,128)(2,1)}, bf16[608,128]{1,0:T(8,128)(2,1)S(1)}, u32[]{:S(2)}, u32[]{:S(2)}) collective-permute-start(bf16[608,128]{1,0:T(8,128)(2,1)} %get-tuple-element.39), channel_id=1, source_target_pairs={{1,2},{2,1},{3,4},{4,3},{5,6},{6,5},{7,8},{8,7},{9,10},{10,9},{11,... | collective-permute-start | bytes 466952 | tf_op jit(solution)/shard_map/ppermute | solution.py:23
  8.0 1.3 %collective-permute-start.2 = (bf16[608,128]{1,0:T(8,128)(2,1)}, bf16[608,128]{1,0:T(8,128)(2,1)S(1)}, u32[]{:S(2)}, u32[]{:S(2)}) collective-permute-start(bf16[608,128]{1,0:T(8,128)(2,1)} %get-tuple-element.40), channel_id=1, source_target_pairs={{0,2},{1,3},{2,0},{3,1},{4,6},{5,7},{6,4},{7,5},{8,10},{9,11},{10,... | collective-permute-start | bytes 466952 | tf_op jit(solution)/shard_map/ppermute | solution.py:23
  9.2 0.0 copy-start
  9.2 3.1 %collective-permute-start.3 = (bf16[608,128]{1,0:T(8,128)(2,1)}, bf16[608,128]{1,0:T(8,128)(2,1)S(1)}, u32[]{:S(2)}, u32[]{:S(2)}) collective-permute-start(bf16[608,128]{1,0:T(8,128)(2,1)} %get-tuple-element.41), channel_id=1, source_target_pairs={{2,4},{3,5},{4,2},{5,3},{6,8},{7,9},{8,6},{9,7},{10,12},{11,13},{1... | collective-permute-start | bytes 466952 | tf_op jit(solution)/shard_map/ppermute | solution.py:23
  12.4 0.0 copy-start.2
  12.4 0.9 copy-done.2
  13.3 0.0 copy-start.4
  13.3 0.9 copy-done.4
  14.2 0.0 copy-start.7
  14.2 7.3 %shard_map.112 = (bf16[1024,3456]{1,0:T(8,128)(2,1)S(1)}, bf16[1024,3456]{1,0:T(8,128)(2,1)S(1)}) custom-call(bf16[1024,128]{1,0:T(8,128)(2,1)S(1)} %copy-done.2, s32[27,1024]{1,0:T(8,128)S(1)} %copy-done.4), custom_call_target="tpu_custom_call" | custom-call | flops 4000000000 | bytes 4194304 | tf_op jit(solution)/shard_map/pallas_call | solution.py:488
  21.6 0.0 copy-start.14
  21.6 2.9 %copy-done.14 = bf16[1024,3456]{1,0:T(8,128)(2,1)} copy-done((bf16[1024,3456]{1,0:T(8,128)(2,1)}, bf16[1024,3456]{1,0:T(8,128)(2,1)S(1)}, u32[]{:S(2)}) %copy-start.14) | copy-done | bytes 7077912
  24.5 0.0 collective-permute-done.refs_0_
  24.5 0.0 collective-permute-done.1.refs_1_
  24.5 0.0 collective-permute-done.2.refs_2_
  24.5 0.0 collective-permute-done.3.refs_3_
  24.5 0.0 copy-done
  24.5 0.0 copy-done.7
  24.5 0.0 copy-start.3
  24.5 0.0 copy-start.6
  24.5 0.0 copy-start.11
  24.5 10.5 %shard_map.113 = (bf16[1024,128]{1,0:T(8,128)(2,1)S(1)}, f32[1024,128]{1,0:T(8,128)S(1)}, bf16[1024,3456]{1,0:T(8,128)(2,1)S(1)}, bf16[128,128]{1,0:T(8,128)(2,1)S(1)}) custom-call(bf16[608,128]{1,0:T(8,128)(2,1)S(1)} %collective-permute-done.refs_0_, bf16[608,128]{1,0:T(8,128)(2,1)S(1)} %collective-permute-done.1.refs_1_, ...), custom_call_target="tpu_custom_call" | custom-call | flops 12000000000 | bytes 4194304 | tf_op jit(solution)/shard_map/pallas_call | solution.py:488
  35.0 0.0 copy-done.3
  35.0 0.0 copy-done.6
  35.1 0.0 copy-done.11
  35.1 0.0 copy-start.5
  35.1 2.6 %shard_map.114 = (f32[1024,128]{1,0:T(8,128)S(1)}, bf16[1024,128]{1,0:T(8,128)(2,1)S(1)}, bf16[256,1024]{1,0:T(8,128)(2,1)S(1)}, bf16[5632,128]{1,0:T(8,128)(2,1)S(1)}, bf16[2816,128]{1,0:T(8,128)(2,1)S(1)}) custom-call(bf16[608,128]{1,0:T(8,128)(2,1)S(1)} %collective-permute-done.refs_0_, bf16[608,128]{1,0:T(8,128)(2,1)S(1)} %collective-permute-done.1.refs_1_, ...), custom_call_target="tpu_custom_call" | custom-call | flops 3000000000 | bytes 4194304 | tf_op jit(solution)/shard_map/pallas_call | solution.py:488
  37.7 0.0 copy-start.12
  37.7 1.1 %collective-permute-start.4 = (bf16[2816,128]{1,0:T(8,128)(2,1)S(1)}, bf16[2816,128]{1,0:T(8,128)(2,1)S(1)}, u32[]{:S(2)}, u32[]{:S(2)}) collective-permute-start(bf16[2816,128]{1,0:T(8,128)(2,1)S(1)} %get-tuple-element.50), channel_id=1, source_target_pairs={{0,1},{1,0},{2,3},{3,2},{4,5},{5,4},{6,7},{7,6},{8,9},{9,8},{10,11... | collective-permute-start | bytes 2162696 | tf_op jit(solution)/shard_map/ppermute | solution.py:501
  38.8 1.8 %collective-permute-done.4.other_ref = bf16[2816,128]{1,0:T(8,128)(2,1)S(1)} collective-permute-done((bf16[2816,128]{1,0:T(8,128)(2,1)S(1)}, bf16[2816,128]{1,0:T(8,128)(2,1)S(1)}, u32[]{:S(2)}, u32[]{:S(2)}) %collective-permute-start.4) | collective-permute-done | bytes 720928 | tf_op jit(solution)/shard_map/ppermute | solution.py:501
  40.6 0.9 shard_map.115.after_ref
  41.6 0.0 copy-done.12
  41.6 5.0 %all-to-all-start = ((bf16[32,88,128]{2,1,0:T(8,128)(2,1)}), bf16[32,88,128]{2,1,0:T(8,128)(2,1)S(1)}, u32[]{:S(2)}, u32[]{:S(2)}) async-start(bf16[32,88,128]{2,1,0:T(8,128)(2,1)} %bitcast), calls=%async_computation | async-start | bytes 1441792 | tf_op jit(solution)/shard_map/all_to_all | solution.py:505
  46.6 0.0 copy-done.5
  46.6 0.0 copy-start.13
  46.6 0.9 copy-done.13
  47.6 0.0 copy-start.1
  47.6 0.0 copy-start.8
  47.6 14.9 %shard_map.116 = (f32[1024,128]{1,0:T(8,128)S(1)}, bf16[96,128]{1,0:T(8,128)(2,1)S(1)}, bf16[96,128]{1,0:T(8,128)(2,1)S(1)}, bf16[96,128]{1,0:T(8,128)(2,1)S(1)}, bf16[96,128]{1,0:T(8,128)(2,1)S(1)}) custom-call(bf16[1024,128]{1,0:T(8,128)(2,1)S(1)} %copy-done.13, s32[27,1024]{1,0:T(8,128)S(1)} %copy-done.5, bf16[27,128,128]{2,1,0:T(8,128)(2,1)S(1)} %copy-done, ...), custom_call_target="tpu_custom_call" | custom-call | flops 20000000000 | bytes 4194304 | tf_op jit(solution)/shard_map/pallas_call | solution.py:488
  62.5 0.0 copy-start.9
  62.5 0.8 copy-done.9
  63.3 1.4 %all-to-all-done = bf16[32,88,128]{2,1,0:T(8,128)(2,1)S(1)} async-done(((bf16[32,88,128]{2,1,0:T(8,128)(2,1)}), bf16[32,88,128]{2,1,0:T(8,128)(2,1)S(1)}, u32[]{:S(2)}, u32[]{:S(2)}) %all-to-all-start) | async-done | bytes 720928 | tf_op jit(solution)/shard_map/all_to_all | solution.py:505
  64.7 1.0 %shard_map.117 = bf16[2816,128]{1,0:T(8,128)(2,1)} custom-call(bf16[2816,128]{1,0:T(8,128)(2,1)S(1)} %bitcast.8, bf16[96,128]{1,0:T(8,128)(2,1)S(1)} %get-tuple-element.56.after_ref), custom_call_target="tpu_custom_call" | custom-call | flops 1000000 | bytes 4194304 | tf_op jit(solution)/shard_map/pallas_call | solution.py:488
  65.8 4.7 %all-to-all-start.1 = ((bf16[32,88,128]{2,1,0:T(8,128)(2,1)}), bf16[32,88,128]{2,1,0:T(8,128)(2,1)S(1)}, u32[]{:S(2)}, u32[]{:S(2)}) async-start(bf16[32,88,128]{2,1,0:T(8,128)(2,1)} %bitcast.2), calls=%async_computation.1 | async-start | bytes 1441792 | tf_op jit(solution)/shard_map/all_to_all | solution.py:505
  70.5 0.4 collective-permute-start.5
  70.9 3.1 %collective-permute-start.6 = (bf16[96,128]{1,0:T(8,128)(2,1)S(1)}, bf16[96,128]{1,0:T(8,128)(2,1)S(1)}, u32[]{:S(2)}, u32[]{:S(2)}) collective-permute-start(bf16[96,128]{1,0:T(8,128)(2,1)S(1)} %get-tuple-element.57), channel_id=1, source_target_pairs={{1,2},{2,1},{3,4},{4,3},{5,6},{6,5},{7,8},{8,7},{9,10},{10,9},{11,... | collective-permute-start | bytes 73736 | tf_op jit(solution)/shard_map/ppermute | solution.py:23
  74.0 1.3 %collective-permute-start.7 = (bf16[96,128]{1,0:T(8,128)(2,1)S(1)}, bf16[96,128]{1,0:T(8,128)(2,1)S(1)}, u32[]{:S(2)}, u32[]{:S(2)}) collective-permute-start(bf16[96,128]{1,0:T(8,128)(2,1)S(1)} %get-tuple-element.58), channel_id=1, source_target_pairs={{0,2},{1,3},{2,0},{3,1},{4,6},{5,7},{6,4},{7,5},{8,10},{9,11},{10,... | collective-permute-start | bytes 73736 | tf_op jit(solution)/shard_map/ppermute | solution.py:23
  75.3 3.1 %collective-permute-start.8 = (bf16[96,128]{1,0:T(8,128)(2,1)S(1)}, bf16[96,128]{1,0:T(8,128)(2,1)S(1)}, u32[]{:S(2)}, u32[]{:S(2)}) collective-permute-start(bf16[96,128]{1,0:T(8,128)(2,1)S(1)} %get-tuple-element.59), channel_id=1, source_target_pairs={{2,4},{3,5},{4,2},{5,3},{6,8},{7,9},{8,6},{9,7},{10,12},{11,13},{1... | collective-permute-start | bytes 73736 | tf_op jit(solution)/shard_map/ppermute | solution.py:23
  78.4 0.0 collective-permute-done.5.refs_0_
  78.4 0.0 collective-permute-done.6.refs_1_
  78.4 0.0 collective-permute-done.7.refs_2_
  78.4 11.5 %collective-permute-done.8.refs_3_ = bf16[96,128]{1,0:T(8,128)(2,1)S(1)} collective-permute-done((bf16[96,128]{1,0:T(8,128)(2,1)S(1)}, bf16[96,128]{1,0:T(8,128)(2,1)S(1)}, u32[]{:S(2)}, u32[]{:S(2)}) %collective-permute-start.8) | collective-permute-done | bytes 24608 | tf_op jit(solution)/shard_map/ppermute | solution.py:23
  89.9 0.0 copy-done.1
  89.9 0.0 copy-done.8
  89.9 0.0 copy-start.10
  89.9 1.0 %copy-done.10 = f32[1024,128]{1,0:T(8,128)S(1)} copy-done((f32[1024,128]{1,0:T(8,128)S(1)}, f32[1024,128]{1,0:T(8,128)}, u32[]{:S(2)}) %copy-start.10) | copy-done | bytes 524312
  91.0 1.5 %shard_map.118 = (f32[1024,128]{1,0:T(8,128)}, bf16[256,256]{1,0:T(8,128)(2,1)}) custom-call(bf16[96,128]{1,0:T(8,128)(2,1)S(1)} %collective-permute-done.5.refs_0_, bf16[96,128]{1,0:T(8,128)(2,1)S(1)} %collective-permute-done.6.refs_1_, bf16[96,128]{1,0:T(8,128)(2,1)S(1)} %collective-permute-done.7.refs_2_, ...), custom_call_target="tpu_custom_call" | custom-call | flops 1000000000 | bytes 4194304 | tf_op jit(solution)/shard_map/pallas_call | solution.py:488
  92.4 0.0 all-to-all-done.1
  92.4 0.4 collective-permute-start.9
  92.8 1.4 %shard_map.119 = (f32[3456,128]{1,0:T(8,128)}, f32[1024,256]{1,0:T(8,128)}) custom-call(bf16[2816,128]{1,0:T(8,128)(2,1)S(1)} %bitcast.7), custom_call_target="tpu_custom_call" | custom-call | flops 1000000 | bytes 4194304 | tf_op jit(solution)/shard_map/pallas_call | solution.py:488
  94.2 0.4 collective-permute-done.9.refs_0_
  94.6 1.4 %shard_map.120 = (f32[3456,128]{1,0:T(8,128)}, f32[1024,256]{1,0:T(8,128)}) custom-call(bf16[2816,128]{1,0:T(8,128)(2,1)S(1)} %collective-permute-done.9.refs_0_, f32[3456,128]{1,0:T(8,128)} %get-tuple-element.68.refs_1_, f32[1024,256]{1,0:T(8,128)} %get-tuple-element.69.refs_2_), custom_call_target="tpu_custom_call", output_to_operand_aliasing={{0}: (1, {}), {1}: (2, {})} | custom-call | flops 1000000 | bytes 4194304 | tf_op jit(solution)/shard_map/pallas_call | solution.py:488
Async XLA Ops:
  4.2 20.3 %collective-permute-start = (bf16[608,128]{1,0:T(8,128)(2,1)}, bf16[608,128]{1,0:T(8,128)(2,1)S(1)}, u32[]{:S(2)}, u32[]{:S(2)}) collective-permute-start(bf16[608,128]{1,0:T(8,128)(2,1)} %get-tuple-element.38), channel_id=1, source_target_pairs={{0,1},{1,0},{2,3},{3,2},{4,5},{5,4},{6,7},{7,6},{8,9},{9,8},{10,11... | collective-permute-start | bytes 466952 | tf_op jit(solution)/shard_map/ppermute | solution.py:23
  4.9 19.5 %collective-permute-start.1 = (bf16[608,128]{1,0:T(8,128)(2,1)}, bf16[608,128]{1,0:T(8,128)(2,1)S(1)}, u32[]{:S(2)}, u32[]{:S(2)}) collective-permute-start(bf16[608,128]{1,0:T(8,128)(2,1)} %get-tuple-element.39), channel_id=1, source_target_pairs={{1,2},{2,1},{3,4},{4,3},{5,6},{6,5},{7,8},{8,7},{9,10},{10,9},{11,... | collective-permute-start | bytes 466952 | tf_op jit(solution)/shard_map/ppermute | solution.py:23
  8.0 16.5 %collective-permute-start.2 = (bf16[608,128]{1,0:T(8,128)(2,1)}, bf16[608,128]{1,0:T(8,128)(2,1)S(1)}, u32[]{:S(2)}, u32[]{:S(2)}) collective-permute-start(bf16[608,128]{1,0:T(8,128)(2,1)} %get-tuple-element.40), channel_id=1, source_target_pairs={{0,2},{1,3},{2,0},{3,1},{4,6},{5,7},{6,4},{7,5},{8,10},{9,11},{10,... | collective-permute-start | bytes 466952 | tf_op jit(solution)/shard_map/ppermute | solution.py:23
  9.2 15.2 %copy-start = (bf16[27,128,128]{2,1,0:T(8,128)(2,1)S(1)}, bf16[27,128,128]{2,1,0:T(8,128)(2,1)}, u32[]{:S(2)}) copy-start(bf16[27,128,128]{2,1,0:T(8,128)(2,1)} %weight_ref.1) | copy-start | bytes 2654212
  9.2 15.2 %collective-permute-start.3 = (bf16[608,128]{1,0:T(8,128)(2,1)}, bf16[608,128]{1,0:T(8,128)(2,1)S(1)}, u32[]{:S(2)}, u32[]{:S(2)}) collective-permute-start(bf16[608,128]{1,0:T(8,128)(2,1)} %get-tuple-element.41), channel_id=1, source_target_pairs={{2,4},{3,5},{4,2},{5,3},{6,8},{7,9},{8,6},{9,7},{10,12},{11,13},{1... | collective-permute-start | bytes 466952 | tf_op jit(solution)/shard_map/ppermute | solution.py:23
  12.4 1.0 copy-start.2
  13.3 0.9 copy-start.4
  14.2 10.3 %copy-start.7 = (s32[4,32]{1,0:T(4,128)S(1)}, s32[4,32]{1,0:T(4,128)}, u32[]{:S(2)}) copy-start(s32[4,32]{1,0:T(4,128)} %refs_6_.4) | copy-start | bytes 1540
  21.6 2.9 %copy-start.14 = (bf16[1024,3456]{1,0:T(8,128)(2,1)}, bf16[1024,3456]{1,0:T(8,128)(2,1)S(1)}, u32[]{:S(2)}) copy-start(bf16[1024,3456]{1,0:T(8,128)(2,1)S(1)} %get-tuple-element.43.refs_8_) | copy-start | bytes 21233668
  24.5 10.5 %copy-start.3 = (bf16[256,256]{1,0:T(8,128)(2,1)S(1)}, bf16[256,256]{1,0:T(8,128)(2,1)}, u32[]{:S(2)}) copy-start(bf16[256,256]{1,0:T(8,128)(2,1)} %refs_11_.1) | copy-start | bytes 393220
  24.5 10.5 %copy-start.6 = (s32[8,256]{1,0:T(8,128)S(1)}, s32[8,256]{1,0:T(8,128)}, u32[]{:S(2)}) copy-start(s32[8,256]{1,0:T(8,128)} %refs_8_.1) | copy-start | bytes 24580
  24.5 10.5 %copy-start.11 = (f32[1024,128]{1,0:T(8,128)S(1)}, f32[1024,128]{1,0:T(8,128)}, u32[]{:S(2)}) copy-start(f32[1024,128]{1,0:T(8,128)} %get-tuple-element.46.refs_7_) | copy-start | bytes 1572868
  35.1 11.5 %copy-start.5 = (s32[27,1024]{1,0:T(8,128)S(1)}, s32[27,1024]{1,0:T(8,128)}, u32[]{:S(2)}) copy-start(s32[27,1024]{1,0:T(8,128)} %map_ref.3) | copy-start | bytes 331780
  37.7 3.9 %copy-start.12 = (bf16[1024,128]{1,0:T(8,128)(2,1)}, bf16[1024,128]{1,0:T(8,128)(2,1)S(1)}, u32[]{:S(2)}) copy-start(bf16[1024,128]{1,0:T(8,128)(2,1)S(1)} %get-tuple-element.51.pgrad_ref) | copy-start | bytes 786436
  37.7 2.9 %collective-permute-start.4 = (bf16[2816,128]{1,0:T(8,128)(2,1)S(1)}, bf16[2816,128]{1,0:T(8,128)(2,1)S(1)}, u32[]{:S(2)}, u32[]{:S(2)}) collective-permute-start(bf16[2816,128]{1,0:T(8,128)(2,1)S(1)} %get-tuple-element.50), channel_id=1, source_target_pairs={{0,1},{1,0},{2,3},{3,2},{4,5},{5,4},{6,7},{7,6},{8,9},{9,8},{10,11... | collective-permute-start | bytes 2162696 | tf_op jit(solution)/shard_map/ppermute | solution.py:501
  41.6 23.2 %all-to-all-start = ((bf16[32,88,128]{2,1,0:T(8,128)(2,1)}), bf16[32,88,128]{2,1,0:T(8,128)(2,1)S(1)}, u32[]{:S(2)}, u32[]{:S(2)}) async-start(bf16[32,88,128]{2,1,0:T(8,128)(2,1)} %bitcast), calls=%async_computation | async-start | bytes 1441792 | tf_op jit(solution)/shard_map/all_to_all | solution.py:505
  46.6 1.0 copy-start.13
  47.6 42.4 %copy-start.1 = (bf16[8,128,256]{2,1,0:T(8,128)(2,1)S(1)}, bf16[8,128,256]{2,1,0:T(8,128)(2,1)}, u32[]{:S(2)}) copy-start(bf16[8,128,256]{2,1,0:T(8,128)(2,1)} %refs_9_.1) | copy-start | bytes 1572868
  47.6 42.4 %copy-start.8 = (s32[4,64]{1,0:T(4,128)S(1)}, s32[4,64]{1,0:T(4,128)}, u32[]{:S(2)}) copy-start(s32[4,64]{1,0:T(4,128)} %refs_6_.5) | copy-start | bytes 3076
  62.5 0.8 copy-start.9
  65.8 26.7 %all-to-all-start.1 = ((bf16[32,88,128]{2,1,0:T(8,128)(2,1)}), bf16[32,88,128]{2,1,0:T(8,128)(2,1)S(1)}, u32[]{:S(2)}, u32[]{:S(2)}) async-start(bf16[32,88,128]{2,1,0:T(8,128)(2,1)} %bitcast.2), calls=%async_computation.1 | async-start | bytes 1441792 | tf_op jit(solution)/shard_map/all_to_all | solution.py:505
  70.5 7.9 %collective-permute-start.5 = (bf16[96,128]{1,0:T(8,128)(2,1)S(1)}, bf16[96,128]{1,0:T(8,128)(2,1)S(1)}, u32[]{:S(2)}, u32[]{:S(2)}) collective-permute-start(bf16[96,128]{1,0:T(8,128)(2,1)S(1)} %get-tuple-element.56.after_ref), channel_id=1, source_target_pairs={{0,1},{1,0},{2,3},{3,2},{4,5},{5,4},{6,7},{7,6},{8,9},{9,8},{10,11... | collective-permute-start | bytes 73736 | tf_op jit(solution)/shard_map/ppermute | solution.py:23
  70.9 7.5 %collective-permute-start.6 = (bf16[96,128]{1,0:T(8,128)(2,1)S(1)}, bf16[96,128]{1,0:T(8,128)(2,1)S(1)}, u32[]{:S(2)}, u32[]{:S(2)}) collective-permute-start(bf16[96,128]{1,0:T(8,128)(2,1)S(1)} %get-tuple-element.57), channel_id=1, source_target_pairs={{1,2},{2,1},{3,4},{4,3},{5,6},{6,5},{7,8},{8,7},{9,10},{10,9},{11,... | collective-permute-start | bytes 73736 | tf_op jit(solution)/shard_map/ppermute | solution.py:23
  74.0 4.4 %collective-permute-start.7 = (bf16[96,128]{1,0:T(8,128)(2,1)S(1)}, bf16[96,128]{1,0:T(8,128)(2,1)S(1)}, u32[]{:S(2)}, u32[]{:S(2)}) collective-permute-start(bf16[96,128]{1,0:T(8,128)(2,1)S(1)} %get-tuple-element.58), channel_id=1, source_target_pairs={{0,2},{1,3},{2,0},{3,1},{4,6},{5,7},{6,4},{7,5},{8,10},{9,11},{10,... | collective-permute-start | bytes 73736 | tf_op jit(solution)/shard_map/ppermute | solution.py:23
  75.3 14.6 %collective-permute-start.8 = (bf16[96,128]{1,0:T(8,128)(2,1)S(1)}, bf16[96,128]{1,0:T(8,128)(2,1)S(1)}, u32[]{:S(2)}, u32[]{:S(2)}) collective-permute-start(bf16[96,128]{1,0:T(8,128)(2,1)S(1)} %get-tuple-element.59), channel_id=1, source_target_pairs={{2,4},{3,5},{4,2},{5,3},{6,8},{7,9},{8,6},{9,7},{10,12},{11,13},{1... | collective-permute-start | bytes 73736 | tf_op jit(solution)/shard_map/ppermute | solution.py:23
  89.9 1.0 %copy-start.10 = (f32[1024,128]{1,0:T(8,128)S(1)}, f32[1024,128]{1,0:T(8,128)}, u32[]{:S(2)}) copy-start(f32[1024,128]{1,0:T(8,128)} %copy-done.9) | copy-start | bytes 1572868
  92.4 2.2 %collective-permute-start.9 = (bf16[2816,128]{1,0:T(8,128)(2,1)S(1)}, bf16[2816,128]{1,0:T(8,128)(2,1)S(1)}, u32[]{:S(2)}, u32[]{:S(2)}) collective-permute-start(bf16[2816,128]{1,0:T(8,128)(2,1)S(1)} %bitcast.6), channel_id=1, source_target_pairs={{0,1},{1,0},{2,3},{3,2},{4,5},{5,4},{6,7},{7,6},{8,9},{9,8},{10,11... | collective-permute-start | bytes 2162696 | tf_op jit(solution)/shard_map/ppermute | solution.py:501

commit v17 on v15

--- a/solution.py
+++ b/solution.py
@@ -240,6 +240,7 @@
     received = refs[:slots]
     features_ref, map_ref, weight_ref, child_ref, early_ref = refs[slots : slots + 5]
     hidden_ref, pre_ref, stacked_ref, leaving_ref, halo_ref, kernel_ref = refs[slots + 5 :]
+    done = 0
     voxels = features_ref.shape[0]
     gathers = map_ref.shape[0] - 1
     middle = gathers // 2
@@ -265,10 +266,17 @@
             both = far[:, 2 * (n % 2) * LANES : 2 * (n % 2 + 1) * LANES]
             lanes = slice(n * LANES, (n + 1) * LANES)
             stacked_ref[:, lanes] = pick_side(cols[n % 2], both) + early_ref[:, lanes]
-
-    stacked_ref[:, gathers * LANES :] = features
-    pre = matmul(stacked_ref[...], kernel_ref[...].reshape(-1, LANES))
-    pre_ref[...] = pre
+        last = 2 * j + 2
+        if last == gathers:
+            stacked_ref[:, gathers * LANES :] = features
+            last = gathers + 1
+        if last - done > 2:
+            columns = stacked_ref[:, done * LANES : last * LANES]
+            term = matmul(columns, kernel_ref[done:last].reshape(-1, LANES))
+            pre_ref[...] = term if done == 0 else pre_ref[...] + term
+            done = last
+
+    pre = pre_ref[...]
     hidden = (features.astype(F32) + pre * jax.nn.sigmoid(pre)).astype(BF16)
     hidden_ref[...] = hidden
     leaving_ref[...] = gather_lists(child_ref, hidden).astype(BF16)

time: 87.2 us -> 87.1 us (level)
  no operation moved by 1% of the time
where the time goes in v17:
time: 87.1 us; the launch traced here: 86 us
  Pallas kernels  41.1 us (47%)
  starting transfers between devices  23.9 us (27%)
  waiting for transfers between devices  18.9 us (22%)
  between operations  1.06 us (1%)
  local copies, waits for them, and re-layouts  1 us (1%)
    pallas_call x10, Pallas kernels, call(): pl.pallas_call(kernel, out_shape=[jax.ShapeDtypeStruct(s, d) for s, d in...  41.1 us
    ppermute x8, starting transfers between devices, swaps(): moved[step] = lax.ppermute(by_step[step], 'shard', pairs)  12.3 us
    all_to_all x2, waiting for transfers between devices, exchange(): return lax.all_to_all(value, 'shard', 0, 0, tiled=True)  11.8 us
    all_to_all x2, starting transfers between devices, exchange(): return lax.all_to_all(value, 'shard', 0, 0, tiled=True)  10.8 us
    ppermute x8, waiting for transfers between devices, swaps(): moved[step] = lax.ppermute(by_step[step], 'shard', pairs)  4.42 us
    ppermute x2, waiting for transfers between devices, swap_cores(): lax.ppermute(value, 'shard', [(i, i + 1 - 2 * (i % 2)) for i in range(dev...  2.62 us
  transfers between devices with their start and end apart: 12, of which 7 were waited for; matrix products, arithmetic and copies ran while one was open for 0% of the time, Pallas kernels for 29%

profile of v17, /device:TPU:1, one launch (start us, length us, event | category | flops | bytes accessed | tf_op | source)
XLA Modules:
  0.0 86.0 jit_solution(12626404596362020674)
XLA Ops:
  0.6 0.0 copy-start.2
  0.6 0.0 copy-start.4
  0.7 3.6 %shard_map.111 = (bf16[608,128]{1,0:T(8,128)(2,1)}, bf16[608,128]{1,0:T(8,128)(2,1)}, bf16[608,128]{1,0:T(8,128)(2,1)}, bf16[608,128]{1,0:T(8,128)(2,1)}, f32[1024,128]{1,0:T(8,128)}) custom-call(bf16[1024,128]{1,0:T(8,128)(2,1)} %refs_4_.1, s32[4,64]{1,0:T(4,128)} %refs_6_.5, s32[8,256]{1,0:T(8,128)} %refs_8_.1, bf16[256,256]{1,0:T(8,128)(2,1)} %refs_11_.1, ...), custom_call_target="tpu_custom_call" | custom-call | flops 1000000000 | bytes 4194304 | tf_op jit(solution)/shard_map/pallas_call | solution.py:499
  4.3 0.1 collective-permute-start
  4.4 4.5 %collective-permute-start.1 = (bf16[608,128]{1,0:T(8,128)(2,1)}, bf16[608,128]{1,0:T(8,128)(2,1)S(1)}, u32[]{:S(2)}, u32[]{:S(2)}) collective-permute-start(bf16[608,128]{1,0:T(8,128)(2,1)} %get-tuple-element.37), channel_id=1, source_target_pairs={{1,2},{2,1},{3,4},{4,3},{5,6},{6,5},{7,8},{8,7},{9,10},{10,9},{11,... | collective-permute-start | bytes 466952 | tf_op jit(solution)/shard_map/ppermute | solution.py:23
  8.9 1.3 %collective-permute-start.2 = (bf16[608,128]{1,0:T(8,128)(2,1)}, bf16[608,128]{1,0:T(8,128)(2,1)S(1)}, u32[]{:S(2)}, u32[]{:S(2)}) collective-permute-start(bf16[608,128]{1,0:T(8,128)(2,1)} %get-tuple-element.38), channel_id=1, source_target_pairs={{0,2},{1,3},{2,0},{3,1},{4,6},{5,7},{6,4},{7,5},{8,10},{9,11},{10,... | collective-permute-start | bytes 466952 | tf_op jit(solution)/shard_map/ppermute | solution.py:23
  10.1 0.0 copy-start
  10.1 0.0 copy-start.6
  10.1 0.8 collective-permute-start.3
  10.9 0.0 copy-done.2
  11.0 0.0 copy-done.4
  11.0 7.3 %shard_map.112.refs_8_ = bf16[1024,3328]{1,0:T(8,128)(2,1)S(1)} custom-call(bf16[1024,128]{1,0:T(8,128)(2,1)S(1)} %copy-done.2, s32[27,1024]{1,0:T(8,128)S(1)} %copy-done.4), custom_call_target="tpu_custom_call" | custom-call | flops 4000000000 | bytes 4194304 | tf_op jit(solution)/shard_map/pallas_call | solution.py:499
  18.3 0.0 copy-start.3
  18.3 0.0 copy-start.5
  18.3 0.0 copy-start.8
  18.3 0.0 collective-permute-done.refs_0_
  18.3 0.0 collective-permute-done.1.refs_1_
  18.3 1.3 %collective-permute-done.2.refs_2_ = bf16[608,128]{1,0:T(8,128)(2,1)S(1)} collective-permute-done((bf16[608,128]{1,0:T(8,128)(2,1)}, bf16[608,128]{1,0:T(8,128)(2,1)S(1)}, u32[]{:S(2)}, u32[]{:S(2)}) %collective-permute-start.2) | collective-permute-done | bytes 155680 | tf_op jit(solution)/shard_map/ppermute | solution.py:23
  19.7 0.0 collective-permute-done.3.refs_3_
  19.7 0.0 copy-done
  19.7 0.0 copy-done.6
  19.7 6.5 %shard_map.113 = (bf16[1024,128]{1,0:T(8,128)(2,1)S(1)}, f32[1024,128]{1,0:T(8,128)S(1)}, bf16[1024,3456]{1,0:T(8,128)(2,1)S(1)}, bf16[128,128]{1,0:T(8,128)(2,1)S(1)}) custom-call(bf16[608,128]{1,0:T(8,128)(2,1)S(1)} %collective-permute-done.refs_0_, bf16[608,128]{1,0:T(8,128)(2,1)S(1)} %collective-permute-done.1.refs_1_, ...), custom_call_target="tpu_custom_call" | custom-call | flops 12000000000 | bytes 4194304 | tf_op jit(solution)/shard_map/pallas_call | solution.py:499
  26.2 0.0 copy-done.3
  26.2 0.0 copy-done.5
  26.2 0.0 copy-done.8
  26.2 2.6 %shard_map.114 = (f32[1024,128]{1,0:T(8,128)S(1)}, bf16[1024,128]{1,0:T(8,128)(2,1)S(1)}, bf16[256,1024]{1,0:T(8,128)(2,1)S(1)}, bf16[5632,128]{1,0:T(8,128)(2,1)S(1)}, bf16[2816,128]{1,0:T(8,128)(2,1)S(1)}) custom-call(bf16[608,128]{1,0:T(8,128)(2,1)S(1)} %collective-permute-done.refs_0_, bf16[608,128]{1,0:T(8,128)(2,1)S(1)} %collective-permute-done.1.refs_1_, ...), custom_call_target="tpu_custom_call" | custom-call | flops 3000000000 | bytes 4194304 | tf_op jit(solution)/shard_map/pallas_call | solution.py:499
  28.8 0.0 copy-start.9
  28.9 0.1 collective-permute-start.4
  28.9 2.2 %collective-permute-done.4.other_ref = bf16[2816,128]{1,0:T(8,128)(2,1)S(1)} collective-permute-done((bf16[2816,128]{1,0:T(8,128)(2,1)S(1)}, bf16[2816,128]{1,0:T(8,128)(2,1)S(1)}, u32[]{:S(2)}, u32[]{:S(2)}) %collective-permute-start.4) | collective-permute-done | bytes 720928 | tf_op jit(solution)/shard_map/ppermute | solution.py:512
  31.1 0.9 %shard_map.115.after_ref = bf16[2816,128]{1,0:T(8,128)(2,1)} custom-call(bf16[5632,128]{1,0:T(8,128)(2,1)S(1)} %get-tuple-element.45.terms_ref, bf16[2816,128]{1,0:T(8,128)(2,1)S(1)} %collective-permute-done.4.other_ref), custom_call_target="tpu_custom_call" | custom-call | flops 1000000 | bytes 4194304 | tf_op jit(solution)/shard_map/pallas_call | solution.py:499
  32.1 0.0 copy-done.9
  32.1 6.9 %all-to-all-start = ((bf16[32,88,128]{2,1,0:T(8,128)(2,1)}), bf16[32,88,128]{2,1,0:T(8,128)(2,1)S(1)}, u32[]{:S(2)}, u32[]{:S(2)}) async-start(bf16[32,88,128]{2,1,0:T(8,128)(2,1)} %bitcast), calls=%async_computation | async-start | bytes 1441792 | tf_op jit(solution)/shard_map/all_to_all | solution.py:516
  39.0 0.0 copy-start.10
  39.0 0.9 %copy-done.10 = bf16[1024,128]{1,0:T(8,128)(2,1)S(1)} copy-done((bf16[1024,128]{1,0:T(8,128)(2,1)S(1)}, bf16[1024,128]{1,0:T(8,128)(2,1)}, u32[]{:S(2)}) %copy-start.10) | copy-done | bytes 262168
  40.0 14.9 %shard_map.116 = (f32[1024,128]{1,0:T(8,128)S(1)}, bf16[96,128]{1,0:T(8,128)(2,1)S(1)}, bf16[96,128]{1,0:T(8,128)(2,1)S(1)}, bf16[96,128]{1,0:T(8,128)(2,1)S(1)}, bf16[96,128]{1,0:T(8,128)(2,1)S(1)}) custom-call(bf16[1024,128]{1,0:T(8,128)(2,1)S(1)} %copy-done.10, s32[27,1024]{1,0:T(8,128)S(1)} %copy-done.4, bf16[27,128,128]{2,1,0:T(8,128)(2,1)S(1)} %copy-done, ...), custom_call_target="tpu_custom_call" | custom-call | flops 20000000000 | bytes 4194304 | tf_op jit(solution)/shard_map/pallas_call | solution.py:499
  54.9 0.0 copy-start.1
  54.9 0.0 copy-start.7
  54.9 3.0 %all-to-all-done = bf16[32,88,128]{2,1,0:T(8,128)(2,1)S(1)} async-done(((bf16[32,88,128]{2,1,0:T(8,128)(2,1)}), bf16[32,88,128]{2,1,0:T(8,128)(2,1)S(1)}, u32[]{:S(2)}, u32[]{:S(2)}) %all-to-all-start) | async-done | bytes 720928 | tf_op jit(solution)/shard_map/all_to_all | solution.py:516
  58.0 1.0 %shard_map.117 = bf16[2816,128]{1,0:T(8,128)(2,1)} custom-call(bf16[2816,128]{1,0:T(8,128)(2,1)S(1)} %bitcast.8, bf16[96,128]{1,0:T(8,128)(2,1)S(1)} %get-tuple-element.52.after_ref), custom_call_target="tpu_custom_call" | custom-call | flops 1000000 | bytes 4194304 | tf_op jit(solution)/shard_map/pallas_call | solution.py:499
  59.0 3.9 %all-to-all-start.1 = ((bf16[32,88,128]{2,1,0:T(8,128)(2,1)}), bf16[32,88,128]{2,1,0:T(8,128)(2,1)S(1)}, u32[]{:S(2)}, u32[]{:S(2)}) async-start(bf16[32,88,128]{2,1,0:T(8,128)(2,1)} %bitcast.2), calls=%async_computation.1 | async-start | bytes 1441792 | tf_op jit(solution)/shard_map/all_to_all | solution.py:516
  62.9 0.3 collective-permute-start.5
  63.2 3.4 %collective-permute-start.6 = (bf16[96,128]{1,0:T(8,128)(2,1)S(1)}, bf16[96,128]{1,0:T(8,128)(2,1)S(1)}, u32[]{:S(2)}, u32[]{:S(2)}) collective-permute-start(bf16[96,128]{1,0:T(8,128)(2,1)S(1)} %get-tuple-element.53), channel_id=1, source_target_pairs={{1,2},{2,1},{3,4},{4,3},{5,6},{6,5},{7,8},{8,7},{9,10},{10,9},{11,... | collective-permute-start | bytes 73736 | tf_op jit(solution)/shard_map/ppermute | solution.py:23
  66.6 1.2 %collective-permute-start.7 = (bf16[96,128]{1,0:T(8,128)(2,1)S(1)}, bf16[96,128]{1,0:T(8,128)(2,1)S(1)}, u32[]{:S(2)}, u32[]{:S(2)}) collective-permute-start(bf16[96,128]{1,0:T(8,128)(2,1)S(1)} %get-tuple-element.54), channel_id=1, source_target_pairs={{0,2},{1,3},{2,0},{3,1},{4,6},{5,7},{6,4},{7,5},{8,10},{9,11},{10,... | collective-permute-start | bytes 73736 | tf_op jit(solution)/shard_map/ppermute | solution.py:23
  67.9 0.7 collective-permute-start.8
  68.5 0.0 collective-permute-done.5.refs_0_
  68.6 0.1 collective-permute-done.6.refs_1_
  68.7 2.9 %collective-permute-done.7.refs_2_ = bf16[96,128]{1,0:T(8,128)(2,1)S(1)} collective-permute-done((bf16[96,128]{1,0:T(8,128)(2,1)S(1)}, bf16[96,128]{1,0:T(8,128)(2,1)S(1)}, u32[]{:S(2)}, u32[]{:S(2)}) %collective-permute-start.7) | collective-permute-done | bytes 24608 | tf_op jit(solution)/shard_map/ppermute | solution.py:23
  71.6 0.0 collective-permute-done.8.refs_3_
  71.6 0.0 copy-done.1
  71.6 0.0 copy-done.7
  71.6 1.5 %shard_map.118 = (f32[1024,128]{1,0:T(8,128)}, bf16[256,256]{1,0:T(8,128)(2,1)}) custom-call(bf16[96,128]{1,0:T(8,128)(2,1)S(1)} %collective-permute-done.5.refs_0_, bf16[96,128]{1,0:T(8,128)(2,1)S(1)} %collective-permute-done.6.refs_1_, bf16[96,128]{1,0:T(8,128)(2,1)S(1)} %collective-permute-done.7.refs_2_, ...), custom_call_target="tpu_custom_call" | custom-call | flops 1000000000 | bytes 4194304 | tf_op jit(solution)/shard_map/pallas_call | solution.py:499
  73.1 8.8 %all-to-all-done.1 = bf16[32,88,128]{2,1,0:T(8,128)(2,1)S(1)} async-done(((bf16[32,88,128]{2,1,0:T(8,128)(2,1)}), bf16[32,88,128]{2,1,0:T(8,128)(2,1)S(1)}, u32[]{:S(2)}, u32[]{:S(2)}) %all-to-all-start.1) | async-done | bytes 720928 | tf_op jit(solution)/shard_map/all_to_all | solution.py:516
  81.8 0.8 collective-permute-start.9
  82.6 1.4 %shard_map.119 = (f32[3456,128]{1,0:T(8,128)}, f32[1024,256]{1,0:T(8,128)}) custom-call(bf16[2816,128]{1,0:T(8,128)(2,1)S(1)} %bitcast.7), custom_call_target="tpu_custom_call" | custom-call | flops 1000000 | bytes 4194304 | tf_op jit(solution)/shard_map/pallas_call | solution.py:499
  84.0 0.4 collective-permute-done.9.refs_0_
  84.4 1.4 %shard_map.120 = (f32[3456,128]{1,0:T(8,128)}, f32[1024,256]{1,0:T(8,128)}) custom-call(bf16[2816,128]{1,0:T(8,128)(2,1)S(1)} %collective-permute-done.9.refs_0_, f32[3456,128]{1,0:T(8,128)} %get-tuple-element.64.refs_1_, f32[1024,256]{1,0:T(8,128)} %get-tuple-element.65.refs_2_), custom_call_target="tpu_custom_call", output_to_operand_aliasing={{0}: (1, {}), {1}: (2, {})} | custom-call | flops 1000000 | bytes 4194304 | tf_op jit(solution)/shard_map/pallas_call | solution.py:499
Async XLA Ops:
  0.6 10.3 %copy-start.2 = (bf16[1024,128]{1,0:T(8,128)(2,1)S(1)}, bf16[1024,128]{1,0:T(8,128)(2,1)}, u32[]{:S(2)}) copy-start(bf16[1024,128]{1,0:T(8,128)(2,1)} %refs_4_.1) | copy-start | bytes 786436
  0.6 10.3 %copy-start.4 = (s32[27,1024]{1,0:T(8,128)S(1)}, s32[27,1024]{1,0:T(8,128)}, u32[]{:S(2)}) copy-start(s32[27,1024]{1,0:T(8,128)} %map_ref.3) | copy-start | bytes 331780
  4.3 14.0 %collective-permute-start = (bf16[608,128]{1,0:T(8,128)(2,1)}, bf16[608,128]{1,0:T(8,128)(2,1)S(1)}, u32[]{:S(2)}, u32[]{:S(2)}) collective-permute-start(bf16[608,128]{1,0:T(8,128)(2,1)} %get-tuple-element.36), channel_id=1, source_target_pairs={{0,1},{1,0},{2,3},{3,2},{4,5},{5,4},{6,7},{7,6},{8,9},{9,8},{10,11... | collective-permute-start | bytes 466952 | tf_op jit(solution)/shard_map/ppermute | solution.py:23
  4.4 13.9 %collective-permute-start.1 = (bf16[608,128]{1,0:T(8,128)(2,1)}, bf16[608,128]{1,0:T(8,128)(2,1)S(1)}, u32[]{:S(2)}, u32[]{:S(2)}) collective-permute-start(bf16[608,128]{1,0:T(8,128)(2,1)} %get-tuple-element.37), channel_id=1, source_target_pairs={{1,2},{2,1},{3,4},{4,3},{5,6},{6,5},{7,8},{8,7},{9,10},{10,9},{11,... | collective-permute-start | bytes 466952 | tf_op jit(solution)/shard_map/ppermute | solution.py:23
  8.9 10.8 %collective-permute-start.2 = (bf16[608,128]{1,0:T(8,128)(2,1)}, bf16[608,128]{1,0:T(8,128)(2,1)S(1)}, u32[]{:S(2)}, u32[]{:S(2)}) collective-permute-start(bf16[608,128]{1,0:T(8,128)(2,1)} %get-tuple-element.38), channel_id=1, source_target_pairs={{0,2},{1,3},{2,0},{3,1},{4,6},{5,7},{6,4},{7,5},{8,10},{9,11},{10,... | collective-permute-start | bytes 466952 | tf_op jit(solution)/shard_map/ppermute | solution.py:23
  10.1 9.5 %copy-start = (bf16[27,128,128]{2,1,0:T(8,128)(2,1)S(1)}, bf16[27,128,128]{2,1,0:T(8,128)(2,1)}, u32[]{:S(2)}) copy-start(bf16[27,128,128]{2,1,0:T(8,128)(2,1)} %weight_ref.1) | copy-start | bytes 2654212
  10.1 9.5 %copy-start.6 = (s32[4,32]{1,0:T(4,128)S(1)}, s32[4,32]{1,0:T(4,128)}, u32[]{:S(2)}) copy-start(s32[4,32]{1,0:T(4,128)} %refs_6_.4) | copy-start | bytes 1540
  10.1 9.5 %collective-permute-start.3 = (bf16[608,128]{1,0:T(8,128)(2,1)}, bf16[608,128]{1,0:T(8,128)(2,1)S(1)}, u32[]{:S(2)}, u32[]{:S(2)}) collective-permute-start(bf16[608,128]{1,0:T(8,128)(2,1)} %get-tuple-element.39), channel_id=1, source_target_pairs={{2,4},{3,5},{4,2},{5,3},{6,8},{7,9},{8,6},{9,7},{10,12},{11,13},{1... | collective-permute-start | bytes 466952 | tf_op jit(solution)/shard_map/ppermute | solution.py:23
  18.3 7.9 %copy-start.3 = (bf16[256,256]{1,0:T(8,128)(2,1)S(1)}, bf16[256,256]{1,0:T(8,128)(2,1)}, u32[]{:S(2)}) copy-start(bf16[256,256]{1,0:T(8,128)(2,1)} %refs_11_.1) | copy-start | bytes 393220
  18.3 7.9 %copy-start.5 = (s32[8,256]{1,0:T(8,128)S(1)}, s32[8,256]{1,0:T(8,128)}, u32[]{:S(2)}) copy-start(s32[8,256]{1,0:T(8,128)} %refs_8_.1) | copy-start | bytes 24580
  18.3 7.9 %copy-start.8 = (f32[1024,128]{1,0:T(8,128)S(1)}, f32[1024,128]{1,0:T(8,128)}, u32[]{:S(2)}) copy-start(f32[1024,128]{1,0:T(8,128)} %get-tuple-element.42.refs_7_) | copy-start | bytes 1572868
  28.8 3.2 %copy-start.9 = (bf16[1024,128]{1,0:T(8,128)(2,1)}, bf16[1024,128]{1,0:T(8,128)(2,1)S(1)}, u32[]{:S(2)}) copy-start(bf16[1024,128]{1,0:T(8,128)(2,1)S(1)} %get-tuple-element.47.pgrad_ref) | copy-start | bytes 786436
  28.9 2.3 %collective-permute-start.4 = (bf16[2816,128]{1,0:T(8,128)(2,1)S(1)}, bf16[2816,128]{1,0:T(8,128)(2,1)S(1)}, u32[]{:S(2)}, u32[]{:S(2)}) collective-permute-start(bf16[2816,128]{1,0:T(8,128)(2,1)S(1)} %get-tuple-element.46), channel_id=1, source_target_pairs={{0,1},{1,0},{2,3},{3,2},{4,5},{5,4},{6,7},{7,6},{8,9},{9,8},{10,11... | collective-permute-start | bytes 2162696 | tf_op jit(solution)/shard_map/ppermute | solution.py:512
  32.1 25.9 %all-to-all-start = ((bf16[32,88,128]{2,1,0:T(8,128)(2,1)}), bf16[32,88,128]{2,1,0:T(8,128)(2,1)S(1)}, u32[]{:S(2)}, u32[]{:S(2)}) async-start(bf16[32,88,128]{2,1,0:T(8,128)(2,1)} %bitcast), calls=%async_computation | async-start | bytes 1441792 | tf_op jit(solution)/shard_map/all_to_all | solution.py:516
  39.0 1.0 %copy-start.10 = (bf16[1024,128]{1,0:T(8,128)(2,1)S(1)}, bf16[1024,128]{1,0:T(8,128)(2,1)}, u32[]{:S(2)}) copy-start(bf16[1024,128]{1,0:T(8,128)(2,1)} %copy-done.9) | copy-start | bytes 786436
  54.9 16.7 %copy-start.1 = (bf16[8,128,256]{2,1,0:T(8,128)(2,1)S(1)}, bf16[8,128,256]{2,1,0:T(8,128)(2,1)}, u32[]{:S(2)}) copy-start(bf16[8,128,256]{2,1,0:T(8,128)(2,1)} %refs_9_.1) | copy-start | bytes 1572868
  54.9 16.7 %copy-start.7 = (s32[4,64]{1,0:T(4,128)S(1)}, s32[4,64]{1,0:T(4,128)}, u32[]{:S(2)}) copy-start(s32[4,64]{1,0:T(4,128)} %refs_6_.5) | copy-start | bytes 3076
  59.0 22.8 %all-to-all-start.1 = ((bf16[32,88,128]{2,1,0:T(8,128)(2,1)}), bf16[32,88,128]{2,1,0:T(8,128)(2,1)S(1)}, u32[]{:S(2)}, u32[]{:S(2)}) async-start(bf16[32,88,128]{2,1,0:T(8,128)(2,1)} %bitcast.2), calls=%async_computation.1 | async-start | bytes 1441792 | tf_op jit(solution)/shard_map/all_to_all | solution.py:516
  62.9 5.7 %collective-permute-start.5 = (bf16[96,128]{1,0:T(8,128)(2,1)S(1)}, bf16[96,128]{1,0:T(8,128)(2,1)S(1)}, u32[]{:S(2)}, u32[]{:S(2)}) collective-permute-start(bf16[96,128]{1,0:T(8,128)(2,1)S(1)} %get-tuple-element.52.after_ref), channel_id=1, source_target_pairs={{0,1},{1,0},{2,3},{3,2},{4,5},{5,4},{6,7},{7,6},{8,9},{9,8},{10,11... | collective-permute-start | bytes 73736 | tf_op jit(solution)/shard_map/ppermute | solution.py:23
  63.2 5.5 %collective-permute-start.6 = (bf16[96,128]{1,0:T(8,128)(2,1)S(1)}, bf16[96,128]{1,0:T(8,128)(2,1)S(1)}, u32[]{:S(2)}, u32[]{:S(2)}) collective-permute-start(bf16[96,128]{1,0:T(8,128)(2,1)S(1)} %get-tuple-element.53), channel_id=1, source_target_pairs={{1,2},{2,1},{3,4},{4,3},{5,6},{6,5},{7,8},{8,7},{9,10},{10,9},{11,... | collective-permute-start | bytes 73736 | tf_op jit(solution)/shard_map/ppermute | solution.py:23
  66.6 5.0 %collective-permute-start.7 = (bf16[96,128]{1,0:T(8,128)(2,1)S(1)}, bf16[96,128]{1,0:T(8,128)(2,1)S(1)}, u32[]{:S(2)}, u32[]{:S(2)}) collective-permute-start(bf16[96,128]{1,0:T(8,128)(2,1)S(1)} %get-tuple-element.54), channel_id=1, source_target_pairs={{0,2},{1,3},{2,0},{3,1},{4,6},{5,7},{6,4},{7,5},{8,10},{9,11},{10,... | collective-permute-start | bytes 73736 | tf_op jit(solution)/shard_map/ppermute | solution.py:23
  67.9 3.7 %collective-permute-start.8 = (bf16[96,128]{1,0:T(8,128)(2,1)S(1)}, bf16[96,128]{1,0:T(8,128)(2,1)S(1)}, u32[]{:S(2)}, u32[]{:S(2)}) collective-permute-start(bf16[96,128]{1,0:T(8,128)(2,1)S(1)} %get-tuple-element.55), channel_id=1, source_target_pairs={{2,4},{3,5},{4,2},{5,3},{6,8},{7,9},{8,6},{9,7},{10,12},{11,13},{1... | collective-permute-start | bytes 73736 | tf_op jit(solution)/shard_map/ppermute | solution.py:23
  81.8 2.6 %collective-permute-start.9 = (bf16[2816,128]{1,0:T(8,128)(2,1)S(1)}, bf16[2816,128]{1,0:T(8,128)(2,1)S(1)}, u32[]{:S(2)}, u32[]{:S(2)}) collective-permute-start(bf16[2816,128]{1,0:T(8,128)(2,1)S(1)} %bitcast.6), channel_id=1, source_target_pairs={{0,1},{1,0},{2,3},{3,2},{4,5},{5,4},{6,7},{7,6},{8,9},{9,8},{10,11... | collective-permute-start | bytes 2162696 | tf_op jit(solution)/shard_map/ppermute | solution.py:512

commit v18 on v17

--- a/solution.py
+++ b/solution.py
@@ -239,33 +239,25 @@
 def forward_kernel(slots, cap, *refs):
     received = refs[:slots]
     features_ref, map_ref, weight_ref, child_ref, early_ref = refs[slots : slots + 5]
-    hidden_ref, pre_ref, stacked_ref, leaving_ref, halo_ref, kernel_ref = refs[slots + 5 :]
+    hidden_ref, pre_ref, stacked_ref, leaving_ref, kernel_ref = refs[slots + 5 :]
     done = 0
     voxels = features_ref.shape[0]
     gathers = map_ref.shape[0] - 1
     middle = gathers // 2
-    half, half_halo = voxels // 2, slots * cap // 2
     features = features_ref[...]
-    halo_ref[...] = jnp.zeros(halo_ref.shape, BF16)
-    for s, block in enumerate(to_slots([r[0:cap, :] for r in received], False)):
-        place = (s % (slots // 2)) * cap
-        side = (s // (slots // 2)) * LANES
-        for n in range(2):
-            row, lane = n * half_halo + place, 2 * n * LANES + side
-            halo_ref[row : row + cap, lane : lane + LANES] = block
+    halo = jnp.concatenate(to_slots([r[0:cap, :] for r in received], False), axis=0)
     kernel_ref[0:middle] = weight_ref[0:middle]
     kernel_ref[middle:gathers] = weight_ref[middle + 1 :]
     kernel_ref[gathers] = weight_ref[middle]
 
     for j in range(middle):
         numbers = (2 * j, 2 * j + 1)
-        cols = [code_column(map_ref, offset_of(n, middle), voxels, slots * cap) for n in numbers]
-        choosers = [one_hot_rows(jnp.abs(col), half_halo, half) for col in cols]
-        far = matmul(jnp.concatenate(choosers, axis=1), halo_ref[...]).astype(BF16)
         for n in numbers:
-            both = far[:, 2 * (n % 2) * LANES : 2 * (n % 2 + 1) * LANES]
+            rows = map_ref[pl.ds(offset_of(n, middle), 1), :]
+            codes = encode(jnp.where(rows >= voxels, rows - voxels, slots * cap)).astype(BF16)
+            far = matmul(one_hot_rows(column(codes), slots * cap), halo).astype(BF16)
             lanes = slice(n * LANES, (n + 1) * LANES)
-            stacked_ref[:, lanes] = pick_side(cols[n % 2], both) + early_ref[:, lanes]
+            stacked_ref[:, lanes] = far + early_ref[:, lanes]
         last = 2 * j + 2
         if last == gathers:
             stacked_ref[:, gathers * LANES :] = features
@@ -568,10 +560,7 @@
             ((voxels, conv_rows), BF16),
             ((slots * cap2, channels), BF16),
         ],
-        scratch=[
-            pltpu.VMEM((slots * cap, 4 * channels), BF16),
-            pltpu.VMEM(conv_weight.shape, BF16),
-        ],
+        scratch=[pltpu.VMEM(conv_weight.shape, BF16)],
         flops=12 * giga,
     )
     hidden_grad, pre_grad, early_h, terms, leaving_terms = call(

time: 87.1 us -> 86.9 us (level)
  no operation moved by 1% of the time
where the time goes in v18:
time: 86.9 us; the launch traced here: 85.8 us
  Pallas kernels  40.9 us (47%)
  starting transfers between devices  23.9 us (28%)
  waiting for transfers between devices  18.9 us (22%)
  between operations  1.06 us (1%)
  local copies, waits for them, and re-layouts  1 us (1%)
    pallas_call x10, Pallas kernels, call(): pl.pallas_call(kernel, out_shape=[jax.ShapeDtypeStruct(s, d) for s, d in...  40.9 us
    ppermute x8, starting transfers between devices, swaps(): moved[step] = lax.ppermute(by_step[step], 'shard', pairs)  12.3 us
    all_to_all x2, waiting for transfers between devices, exchange(): return lax.all_to_all(value, 'shard', 0, 0, tiled=True)  11.8 us
    all_to_all x2, starting transfers between devices, exchange(): return lax.all_to_all(value, 'shard', 0, 0, tiled=True)  10.8 us
    ppermute x8, waiting for transfers between devices, swaps(): moved[step] = lax.ppermute(by_step[step], 'shard', pairs)  4.42 us
    ppermute x2, waiting for transfers between devices, swap_cores(): lax.ppermute(value, 'shard', [(i, i + 1 - 2 * (i % 2)) for i in range(dev...  2.62 us
  transfers between devices with their start and end apart: 12, of which 7 were waited for; matrix products, arithmetic and copies ran while one was open for 0% of the time, Pallas kernels for 29%

profile of v18, /device:TPU:1, one launch (start us, length us, event | category | flops | bytes accessed | tf_op | source)
XLA Modules:
  0.0 85.8 jit_solution(6736590658246689770)
XLA Ops:
  0.6 0.0 copy-start.2
  0.6 0.0 copy-start.4
  0.7 3.6 %shard_map.111 = (bf16[608,128]{1,0:T(8,128)(2,1)}, bf16[608,128]{1,0:T(8,128)(2,1)}, bf16[608,128]{1,0:T(8,128)(2,1)}, bf16[608,128]{1,0:T(8,128)(2,1)}, f32[1024,128]{1,0:T(8,128)}) custom-call(bf16[1024,128]{1,0:T(8,128)(2,1)} %refs_4_.1, s32[4,64]{1,0:T(4,128)} %refs_6_.5, s32[8,256]{1,0:T(8,128)} %refs_8_.1, bf16[256,256]{1,0:T(8,128)(2,1)} %refs_11_.1, ...), custom_call_target="tpu_custom_call" | custom-call | flops 1000000000 | bytes 4194304 | tf_op jit(solution)/shard_map/pallas_call | solution.py:491
  4.3 0.1 collective-permute-start
  4.4 4.5 %collective-permute-start.1 = (bf16[608,128]{1,0:T(8,128)(2,1)}, bf16[608,128]{1,0:T(8,128)(2,1)S(1)}, u32[]{:S(2)}, u32[]{:S(2)}) collective-permute-start(bf16[608,128]{1,0:T(8,128)(2,1)} %get-tuple-element.37), channel_id=1, source_target_pairs={{1,2},{2,1},{3,4},{4,3},{5,6},{6,5},{7,8},{8,7},{9,10},{10,9},{11,... | collective-permute-start | bytes 466952 | tf_op jit(solution)/shard_map/ppermute | solution.py:23
  8.9 1.3 %collective-permute-start.2 = (bf16[608,128]{1,0:T(8,128)(2,1)}, bf16[608,128]{1,0:T(8,128)(2,1)S(1)}, u32[]{:S(2)}, u32[]{:S(2)}) collective-permute-start(bf16[608,128]{1,0:T(8,128)(2,1)} %get-tuple-element.38), channel_id=1, source_target_pairs={{0,2},{1,3},{2,0},{3,1},{4,6},{5,7},{6,4},{7,5},{8,10},{9,11},{10,... | collective-permute-start | bytes 466952 | tf_op jit(solution)/shard_map/ppermute | solution.py:23
  10.1 0.0 copy-start
  10.1 0.0 copy-start.6
  10.1 0.8 collective-permute-start.3
  10.9 0.0 copy-done.2
  11.0 0.0 copy-done.4
  11.0 7.3 %shard_map.112.refs_8_ = bf16[1024,3328]{1,0:T(8,128)(2,1)S(1)} custom-call(bf16[1024,128]{1,0:T(8,128)(2,1)S(1)} %copy-done.2, s32[27,1024]{1,0:T(8,128)S(1)} %copy-done.4), custom_call_target="tpu_custom_call" | custom-call | flops 4000000000 | bytes 4194304 | tf_op jit(solution)/shard_map/pallas_call | solution.py:491
  18.3 0.0 copy-start.3
  18.3 0.0 copy-start.5
  18.3 0.0 copy-start.8
  18.3 0.0 collective-permute-done.refs_0_
  18.3 0.0 collective-permute-done.1.refs_1_
  18.3 1.3 %collective-permute-done.2.refs_2_ = bf16[608,128]{1,0:T(8,128)(2,1)S(1)} collective-permute-done((bf16[608,128]{1,0:T(8,128)(2,1)}, bf16[608,128]{1,0:T(8,128)(2,1)S(1)}, u32[]{:S(2)}, u32[]{:S(2)}) %collective-permute-start.2) | collective-permute-done | bytes 155680 | tf_op jit(solution)/shard_map/ppermute | solution.py:23
  19.7 0.0 collective-permute-done.3.refs_3_
  19.7 0.0 copy-done
  19.7 0.0 copy-done.6
  19.7 6.3 %shard_map.113 = (bf16[1024,128]{1,0:T(8,128)(2,1)S(1)}, f32[1024,128]{1,0:T(8,128)S(1)}, bf16[1024,3456]{1,0:T(8,128)(2,1)S(1)}, bf16[128,128]{1,0:T(8,128)(2,1)S(1)}) custom-call(bf16[608,128]{1,0:T(8,128)(2,1)S(1)} %collective-permute-done.refs_0_, bf16[608,128]{1,0:T(8,128)(2,1)S(1)} %collective-permute-done.1.refs_1_, ...), custom_call_target="tpu_custom_call" | custom-call | flops 12000000000 | bytes 4194304 | tf_op jit(solution)/shard_map/pallas_call | solution.py:491
  26.0 0.0 copy-done.3
  26.0 0.0 copy-done.5
  26.0 0.0 copy-done.8
  26.0 2.6 %shard_map.114 = (f32[1024,128]{1,0:T(8,128)S(1)}, bf16[1024,128]{1,0:T(8,128)(2,1)S(1)}, bf16[256,1024]{1,0:T(8,128)(2,1)S(1)}, bf16[5632,128]{1,0:T(8,128)(2,1)S(1)}, bf16[2816,128]{1,0:T(8,128)(2,1)S(1)}) custom-call(bf16[608,128]{1,0:T(8,128)(2,1)S(1)} %collective-permute-done.refs_0_, bf16[608,128]{1,0:T(8,128)(2,1)S(1)} %collective-permute-done.1.refs_1_, ...), custom_call_target="tpu_custom_call" | custom-call | flops 3000000000 | bytes 4194304 | tf_op jit(solution)/shard_map/pallas_call | solution.py:491
  28.6 0.0 copy-start.9
  28.6 0.1 collective-permute-start.4
  28.7 2.2 %collective-permute-done.4.other_ref = bf16[2816,128]{1,0:T(8,128)(2,1)S(1)} collective-permute-done((bf16[2816,128]{1,0:T(8,128)(2,1)S(1)}, bf16[2816,128]{1,0:T(8,128)(2,1)S(1)}, u32[]{:S(2)}, u32[]{:S(2)}) %collective-permute-start.4) | collective-permute-done | bytes 720928 | tf_op jit(solution)/shard_map/ppermute | solution.py:504
  30.9 0.9 %shard_map.115.after_ref = bf16[2816,128]{1,0:T(8,128)(2,1)} custom-call(bf16[5632,128]{1,0:T(8,128)(2,1)S(1)} %get-tuple-element.45.terms_ref, bf16[2816,128]{1,0:T(8,128)(2,1)S(1)} %collective-permute-done.4.other_ref), custom_call_target="tpu_custom_call" | custom-call | flops 1000000 | bytes 4194304 | tf_op jit(solution)/shard_map/pallas_call | solution.py:491
  31.8 0.0 copy-done.9
  31.8 6.9 %all-to-all-start = ((bf16[32,88,128]{2,1,0:T(8,128)(2,1)}), bf16[32,88,128]{2,1,0:T(8,128)(2,1)S(1)}, u32[]{:S(2)}, u32[]{:S(2)}) async-start(bf16[32,88,128]{2,1,0:T(8,128)(2,1)} %bitcast), calls=%async_computation | async-start | bytes 1441792 | tf_op jit(solution)/shard_map/all_to_all | solution.py:508
  38.8 0.0 copy-start.10
  38.8 0.9 %copy-done.10 = bf16[1024,128]{1,0:T(8,128)(2,1)S(1)} copy-done((bf16[1024,128]{1,0:T(8,128)(2,1)S(1)}, bf16[1024,128]{1,0:T(8,128)(2,1)}, u32[]{:S(2)}) %copy-start.10) | copy-done | bytes 262168
  39.7 14.9 %shard_map.116 = (f32[1024,128]{1,0:T(8,128)S(1)}, bf16[96,128]{1,0:T(8,128)(2,1)S(1)}, bf16[96,128]{1,0:T(8,128)(2,1)S(1)}, bf16[96,128]{1,0:T(8,128)(2,1)S(1)}, bf16[96,128]{1,0:T(8,128)(2,1)S(1)}) custom-call(bf16[1024,128]{1,0:T(8,128)(2,1)S(1)} %copy-done.10, s32[27,1024]{1,0:T(8,128)S(1)} %copy-done.4, bf16[27,128,128]{2,1,0:T(8,128)(2,1)S(1)} %copy-done, ...), custom_call_target="tpu_custom_call" | custom-call | flops 20000000000 | bytes 4194304 | tf_op jit(solution)/shard_map/pallas_call | solution.py:491
  54.7 0.0 copy-start.1
  54.7 0.0 copy-start.7
  54.7 3.1 %all-to-all-done = bf16[32,88,128]{2,1,0:T(8,128)(2,1)S(1)} async-done(((bf16[32,88,128]{2,1,0:T(8,128)(2,1)}), bf16[32,88,128]{2,1,0:T(8,128)(2,1)S(1)}, u32[]{:S(2)}, u32[]{:S(2)}) %all-to-all-start) | async-done | bytes 720928 | tf_op jit(solution)/shard_map/all_to_all | solution.py:508
  57.7 1.0 %shard_map.117 = bf16[2816,128]{1,0:T(8,128)(2,1)} custom-call(bf16[2816,128]{1,0:T(8,128)(2,1)S(1)} %bitcast.8, bf16[96,128]{1,0:T(8,128)(2,1)S(1)} %get-tuple-element.52.after_ref), custom_call_target="tpu_custom_call" | custom-call | flops 1000000 | bytes 4194304 | tf_op jit(solution)/shard_map/pallas_call | solution.py:491
  58.8 3.9 %all-to-all-start.1 = ((bf16[32,88,128]{2,1,0:T(8,128)(2,1)}), bf16[32,88,128]{2,1,0:T(8,128)(2,1)S(1)}, u32[]{:S(2)}, u32[]{:S(2)}) async-start(bf16[32,88,128]{2,1,0:T(8,128)(2,1)} %bitcast.2), calls=%async_computation.1 | async-start | bytes 1441792 | tf_op jit(solution)/shard_map/all_to_all | solution.py:508
  62.6 0.3 collective-permute-start.5
  63.0 3.4 %collective-permute-start.6 = (bf16[96,128]{1,0:T(8,128)(2,1)S(1)}, bf16[96,128]{1,0:T(8,128)(2,1)S(1)}, u32[]{:S(2)}, u32[]{:S(2)}) collective-permute-start(bf16[96,128]{1,0:T(8,128)(2,1)S(1)} %get-tuple-element.53), channel_id=1, source_target_pairs={{1,2},{2,1},{3,4},{4,3},{5,6},{6,5},{7,8},{8,7},{9,10},{10,9},{11,... | collective-permute-start | bytes 73736 | tf_op jit(solution)/shard_map/ppermute | solution.py:23
  66.4 1.2 %collective-permute-start.7 = (bf16[96,128]{1,0:T(8,128)(2,1)S(1)}, bf16[96,128]{1,0:T(8,128)(2,1)S(1)}, u32[]{:S(2)}, u32[]{:S(2)}) collective-permute-start(bf16[96,128]{1,0:T(8,128)(2,1)S(1)} %get-tuple-element.54), channel_id=1, source_target_pairs={{0,2},{1,3},{2,0},{3,1},{4,6},{5,7},{6,4},{7,5},{8,10},{9,11},{10,... | collective-permute-start | bytes 73736 | tf_op jit(solution)/shard_map/ppermute | solution.py:23
  67.6 0.7 collective-permute-start.8
  68.3 0.0 collective-permute-done.5.refs_0_
  68.3 0.1 collective-permute-done.6.refs_1_
  68.5 2.9 %collective-permute-done.7.refs_2_ = bf16[96,128]{1,0:T(8,128)(2,1)S(1)} collective-permute-done((bf16[96,128]{1,0:T(8,128)(2,1)S(1)}, bf16[96,128]{1,0:T(8,128)(2,1)S(1)}, u32[]{:S(2)}, u32[]{:S(2)}) %collective-permute-start.7) | collective-permute-done | bytes 24608 | tf_op jit(solution)/shard_map/ppermute | solution.py:23
  71.4 0.0 collective-permute-done.8.refs_3_
  71.4 0.0 copy-done.1
  71.4 0.0 copy-done.7
  71.4 1.5 %shard_map.118 = (f32[1024,128]{1,0:T(8,128)}, bf16[256,256]{1,0:T(8,128)(2,1)}) custom-call(bf16[96,128]{1,0:T(8,128)(2,1)S(1)} %collective-permute-done.5.refs_0_, bf16[96,128]{1,0:T(8,128)(2,1)S(1)} %collective-permute-done.6.refs_1_, bf16[96,128]{1,0:T(8,128)(2,1)S(1)} %collective-permute-done.7.refs_2_, ...), custom_call_target="tpu_custom_call" | custom-call | flops 1000000000 | bytes 4194304 | tf_op jit(solution)/shard_map/pallas_call | solution.py:491
  72.8 8.8 %all-to-all-done.1 = bf16[32,88,128]{2,1,0:T(8,128)(2,1)S(1)} async-done(((bf16[32,88,128]{2,1,0:T(8,128)(2,1)}), bf16[32,88,128]{2,1,0:T(8,128)(2,1)S(1)}, u32[]{:S(2)}, u32[]{:S(2)}) %all-to-all-start.1) | async-done | bytes 720928 | tf_op jit(solution)/shard_map/all_to_all | solution.py:508
  81.6 0.8 collective-permute-start.9
  82.4 1.4 %shard_map.119 = (f32[3456,128]{1,0:T(8,128)}, f32[1024,256]{1,0:T(8,128)}) custom-call(bf16[2816,128]{1,0:T(8,128)(2,1)S(1)} %bitcast.7), custom_call_target="tpu_custom_call" | custom-call | flops 1000000 | bytes 4194304 | tf_op jit(solution)/shard_map/pallas_call | solution.py:491
  83.8 0.4 collective-permute-done.9.refs_0_
  84.2 1.4 %shard_map.120 = (f32[3456,128]{1,0:T(8,128)}, f32[1024,256]{1,0:T(8,128)}) custom-call(bf16[2816,128]{1,0:T(8,128)(2,1)S(1)} %collective-permute-done.9.refs_0_, f32[3456,128]{1,0:T(8,128)} %get-tuple-element.64.refs_1_, f32[1024,256]{1,0:T(8,128)} %get-tuple-element.65.refs_2_), custom_call_target="tpu_custom_call", output_to_operand_aliasing={{0}: (1, {}), {1}: (2, {})} | custom-call | flops 1000000 | bytes 4194304 | tf_op jit(solution)/shard_map/pallas_call | solution.py:491
Async XLA Ops:
  0.6 10.3 %copy-start.2 = (bf16[1024,128]{1,0:T(8,128)(2,1)S(1)}, bf16[1024,128]{1,0:T(8,128)(2,1)}, u32[]{:S(2)}) copy-start(bf16[1024,128]{1,0:T(8,128)(2,1)} %refs_4_.1) | copy-start | bytes 786436
  0.6 10.3 %copy-start.4 = (s32[27,1024]{1,0:T(8,128)S(1)}, s32[27,1024]{1,0:T(8,128)}, u32[]{:S(2)}) copy-start(s32[27,1024]{1,0:T(8,128)} %map_ref.3) | copy-start | bytes 331780
  4.3 14.0 %collective-permute-start = (bf16[608,128]{1,0:T(8,128)(2,1)}, bf16[608,128]{1,0:T(8,128)(2,1)S(1)}, u32[]{:S(2)}, u32[]{:S(2)}) collective-permute-start(bf16[608,128]{1,0:T(8,128)(2,1)} %get-tuple-element.36), channel_id=1, source_target_pairs={{0,1},{1,0},{2,3},{3,2},{4,5},{5,4},{6,7},{7,6},{8,9},{9,8},{10,11... | collective-permute-start | bytes 466952 | tf_op jit(solution)/shard_map/ppermute | solution.py:23
  4.4 13.9 %collective-permute-start.1 = (bf16[608,128]{1,0:T(8,128)(2,1)}, bf16[608,128]{1,0:T(8,128)(2,1)S(1)}, u32[]{:S(2)}, u32[]{:S(2)}) collective-permute-start(bf16[608,128]{1,0:T(8,128)(2,1)} %get-tuple-element.37), channel_id=1, source_target_pairs={{1,2},{2,1},{3,4},{4,3},{5,6},{6,5},{7,8},{8,7},{9,10},{10,9},{11,... | collective-permute-start | bytes 466952 | tf_op jit(solution)/shard_map/ppermute | solution.py:23
  8.9 10.8 %collective-permute-start.2 = (bf16[608,128]{1,0:T(8,128)(2,1)}, bf16[608,128]{1,0:T(8,128)(2,1)S(1)}, u32[]{:S(2)}, u32[]{:S(2)}) collective-permute-start(bf16[608,128]{1,0:T(8,128)(2,1)} %get-tuple-element.38), channel_id=1, source_target_pairs={{0,2},{1,3},{2,0},{3,1},{4,6},{5,7},{6,4},{7,5},{8,10},{9,11},{10,... | collective-permute-start | bytes 466952 | tf_op jit(solution)/shard_map/ppermute | solution.py:23
  10.1 9.5 %copy-start = (bf16[27,128,128]{2,1,0:T(8,128)(2,1)S(1)}, bf16[27,128,128]{2,1,0:T(8,128)(2,1)}, u32[]{:S(2)}) copy-start(bf16[27,128,128]{2,1,0:T(8,128)(2,1)} %weight_ref.1) | copy-start | bytes 2654212
  10.1 9.5 %copy-start.6 = (s32[4,32]{1,0:T(4,128)S(1)}, s32[4,32]{1,0:T(4,128)}, u32[]{:S(2)}) copy-start(s32[4,32]{1,0:T(4,128)} %refs_6_.4) | copy-start | bytes 1540
  10.1 9.5 %collective-permute-start.3 = (bf16[608,128]{1,0:T(8,128)(2,1)}, bf16[608,128]{1,0:T(8,128)(2,1)S(1)}, u32[]{:S(2)}, u32[]{:S(2)}) collective-permute-start(bf16[608,128]{1,0:T(8,128)(2,1)} %get-tuple-element.39), channel_id=1, source_target_pairs={{2,4},{3,5},{4,2},{5,3},{6,8},{7,9},{8,6},{9,7},{10,12},{11,13},{1... | collective-permute-start | bytes 466952 | tf_op jit(solution)/shard_map/ppermute | solution.py:23
  18.3 7.7 %copy-start.3 = (bf16[256,256]{1,0:T(8,128)(2,1)S(1)}, bf16[256,256]{1,0:T(8,128)(2,1)}, u32[]{:S(2)}) copy-start(bf16[256,256]{1,0:T(8,128)(2,1)} %refs_11_.1) | copy-start | bytes 393220
  18.3 7.7 %copy-start.5 = (s32[8,256]{1,0:T(8,128)S(1)}, s32[8,256]{1,0:T(8,128)}, u32[]{:S(2)}) copy-start(s32[8,256]{1,0:T(8,128)} %refs_8_.1) | copy-start | bytes 24580
  18.3 7.7 %copy-start.8 = (f32[1024,128]{1,0:T(8,128)S(1)}, f32[1024,128]{1,0:T(8,128)}, u32[]{:S(2)}) copy-start(f32[1024,128]{1,0:T(8,128)} %get-tuple-element.42.refs_7_) | copy-start | bytes 1572868
  28.6 3.2 %copy-start.9 = (bf16[1024,128]{1,0:T(8,128)(2,1)}, bf16[1024,128]{1,0:T(8,128)(2,1)S(1)}, u32[]{:S(2)}) copy-start(bf16[1024,128]{1,0:T(8,128)(2,1)S(1)} %get-tuple-element.47.pgrad_ref) | copy-start | bytes 786436
  28.6 2.3 %collective-permute-start.4 = (bf16[2816,128]{1,0:T(8,128)(2,1)S(1)}, bf16[2816,128]{1,0:T(8,128)(2,1)S(1)}, u32[]{:S(2)}, u32[]{:S(2)}) collective-permute-start(bf16[2816,128]{1,0:T(8,128)(2,1)S(1)} %get-tuple-element.46), channel_id=1, source_target_pairs={{0,1},{1,0},{2,3},{3,2},{4,5},{5,4},{6,7},{7,6},{8,9},{9,8},{10,11... | collective-permute-start | bytes 2162696 | tf_op jit(solution)/shard_map/ppermute | solution.py:504
  31.8 25.9 %all-to-all-start = ((bf16[32,88,128]{2,1,0:T(8,128)(2,1)}), bf16[32,88,128]{2,1,0:T(8,128)(2,1)S(1)}, u32[]{:S(2)}, u32[]{:S(2)}) async-start(bf16[32,88,128]{2,1,0:T(8,128)(2,1)} %bitcast), calls=%async_computation | async-start | bytes 1441792 | tf_op jit(solution)/shard_map/all_to_all | solution.py:508
  38.8 1.0 %copy-start.10 = (bf16[1024,128]{1,0:T(8,128)(2,1)S(1)}, bf16[1024,128]{1,0:T(8,128)(2,1)}, u32[]{:S(2)}) copy-start(bf16[1024,128]{1,0:T(8,128)(2,1)} %copy-done.9) | copy-start | bytes 786436
  54.7 16.7 %copy-start.1 = (bf16[8,128,256]{2,1,0:T(8,128)(2,1)S(1)}, bf16[8,128,256]{2,1,0:T(8,128)(2,1)}, u32[]{:S(2)}) copy-start(bf16[8,128,256]{2,1,0:T(8,128)(2,1)} %refs_9_.1) | copy-start | bytes 1572868
  54.7 16.7 %copy-start.7 = (s32[4,64]{1,0:T(4,128)S(1)}, s32[4,64]{1,0:T(4,128)}, u32[]{:S(2)}) copy-start(s32[4,64]{1,0:T(4,128)} %refs_6_.5) | copy-start | bytes 3076
  58.8 22.8 %all-to-all-start.1 = ((bf16[32,88,128]{2,1,0:T(8,128)(2,1)}), bf16[32,88,128]{2,1,0:T(8,128)(2,1)S(1)}, u32[]{:S(2)}, u32[]{:S(2)}) async-start(bf16[32,88,128]{2,1,0:T(8,128)(2,1)} %bitcast.2), calls=%async_computation.1 | async-start | bytes 1441792 | tf_op jit(solution)/shard_map/all_to_all | solution.py:508
  62.6 5.7 %collective-permute-start.5 = (bf16[96,128]{1,0:T(8,128)(2,1)S(1)}, bf16[96,128]{1,0:T(8,128)(2,1)S(1)}, u32[]{:S(2)}, u32[]{:S(2)}) collective-permute-start(bf16[96,128]{1,0:T(8,128)(2,1)S(1)} %get-tuple-element.52.after_ref), channel_id=1, source_target_pairs={{0,1},{1,0},{2,3},{3,2},{4,5},{5,4},{6,7},{7,6},{8,9},{9,8},{10,11... | collective-permute-start | bytes 73736 | tf_op jit(solution)/shard_map/ppermute | solution.py:23
  63.0 5.5 %collective-permute-start.6 = (bf16[96,128]{1,0:T(8,128)(2,1)S(1)}, bf16[96,128]{1,0:T(8,128)(2,1)S(1)}, u32[]{:S(2)}, u32[]{:S(2)}) collective-permute-start(bf16[96,128]{1,0:T(8,128)(2,1)S(1)} %get-tuple-element.53), channel_id=1, source_target_pairs={{1,2},{2,1},{3,4},{4,3},{5,6},{6,5},{7,8},{8,7},{9,10},{10,9},{11,... | collective-permute-start | bytes 73736 | tf_op jit(solution)/shard_map/ppermute | solution.py:23
  66.4 5.0 %collective-permute-start.7 = (bf16[96,128]{1,0:T(8,128)(2,1)S(1)}, bf16[96,128]{1,0:T(8,128)(2,1)S(1)}, u32[]{:S(2)}, u32[]{:S(2)}) collective-permute-start(bf16[96,128]{1,0:T(8,128)(2,1)S(1)} %get-tuple-element.54), channel_id=1, source_target_pairs={{0,2},{1,3},{2,0},{3,1},{4,6},{5,7},{6,4},{7,5},{8,10},{9,11},{10,... | collective-permute-start | bytes 73736 | tf_op jit(solution)/shard_map/ppermute | solution.py:23
  67.6 3.7 %collective-permute-start.8 = (bf16[96,128]{1,0:T(8,128)(2,1)S(1)}, bf16[96,128]{1,0:T(8,128)(2,1)S(1)}, u32[]{:S(2)}, u32[]{:S(2)}) collective-permute-start(bf16[96,128]{1,0:T(8,128)(2,1)S(1)} %get-tuple-element.55), channel_id=1, source_target_pairs={{2,4},{3,5},{4,2},{5,3},{6,8},{7,9},{8,6},{9,7},{10,12},{11,13},{1... | collective-permute-start | bytes 73736 | tf_op jit(solution)/shard_map/ppermute | solution.py:23
  81.6 2.6 %collective-permute-start.9 = (bf16[2816,128]{1,0:T(8,128)(2,1)S(1)}, bf16[2816,128]{1,0:T(8,128)(2,1)S(1)}, u32[]{:S(2)}, u32[]{:S(2)}) collective-permute-start(bf16[2816,128]{1,0:T(8,128)(2,1)S(1)} %bitcast.6), channel_id=1, source_target_pairs={{0,1},{1,0},{2,3},{3,2},{4,5},{5,4},{6,7},{7,6},{8,9},{9,8},{10,11... | collective-permute-start | bytes 2162696 | tf_op jit(solution)/shard_map/ppermute | solution.py:504

commit v19 on v18

--- a/solution.py
+++ b/solution.py
@@ -94,6 +94,11 @@
 def pick_rows(col, table):
     both = matmul(one_hot_rows(jnp.abs(col), table.shape[0]), table).astype(BF16)
     return jnp.where(col < jnp.zeros(col.shape, BF16), both[:, LANES:], both[:, :LANES])
+
+
+def turn(value):
+    blocks = [jnp.transpose(value[n : n + LANES, :]) for n in range(0, value.shape[0], LANES)]
+    return jnp.concatenate(blocks, axis=1)
 
 
 def list_row(lists, first, per_row):
@@ -287,13 +292,13 @@
     hgrad_ref[...] = hgrad
     pre = pre_ref[...]
     sig = jax.nn.sigmoid(pre)
-    pgrad = hgrad * (sig * (1.0 + pre * (1.0 - sig)))
-    pgrad_ref[...] = pgrad.astype(BF16)
-    terms = matmul(jnp.transpose(pgrad).astype(BF16), stacked_ref[...])
+    pgrad = (hgrad * (sig * (1.0 + pre * (1.0 - sig)))).astype(BF16)
+    pgrad_ref[...] = pgrad
+    terms = matmul(turn(pgrad), stacked_ref[...]).astype(BF16)
     order = [k for k in range(kernel_count) if k != middle] + [middle]
     for n, k in enumerate(order):
         block = jnp.transpose(terms[:, n * LANES : (n + 1) * LANES])
-        terms_ref[k * LANES : (k + 1) * LANES, :] = block.astype(BF16)
+        terms_ref[k * LANES : (k + 1) * LANES, :] = block
     voxels = hidden_ref.shape[0]
     half = voxels // 2
     hidden = hidden_ref[...]
@@ -314,7 +319,7 @@
     for n in range(octants * across):
         rows = slice(n * cap2, (n + 1) * cap2)
         sums.append(jnp.concatenate([block[rows, :] for block in blocks], axis=0))
-    leaving_t = jnp.transpose(leaving_ref[...].astype(F32)).astype(BF16)
+    leaving_t = turn(leaving_ref[...])
     far = matmul(leaving_t, jnp.concatenate(sums, axis=1))
     row = kernel_count * LANES
     for n in range(octants * across):
@@ -427,7 +432,7 @@
     rows = block_ref.shape[0]
     conv_rows = conv_hbm.shape[0]
     core = lax.rem(lax.axis_index("shard"), 2)
-    piece = 4 * LANES
+    piece = 2 * LANES
     assert rows <= conv_rows <= 2 * rows and rows % LANES == 0
 
     def write(half):

time: 86.9 us -> 86.8 us (level)
  no operation moved by 1% of the time
where the time goes in v19:
time: 86.8 us; the launch traced here: 85.7 us
  Pallas kernels  40.9 us (47%)
  starting transfers between devices  23.9 us (28%)
  waiting for transfers between devices  18.9 us (22%)
  between operations  1.06 us (1%)
  local copies, waits for them, and re-layouts  1 us (1%)
    pallas_call x10, Pallas kernels, call(): pl.pallas_call(kernel, out_shape=[jax.ShapeDtypeStruct(s, d) for s, d in...  40.9 us
    ppermute x8, starting transfers between devices, swaps(): moved[step] = lax.ppermute(by_step[step], 'shard', pairs)  12.3 us
    all_to_all x2, waiting for transfers between devices, exchange(): return lax.all_to_all(value, 'shard', 0, 0, tiled=True)  11.8 us
    all_to_all x2, starting transfers between devices, exchange(): return lax.all_to_all(value, 'shard', 0, 0, tiled=True)  10.8 us
    ppermute x8, waiting for transfers between devices, swaps(): moved[step] = lax.ppermute(by_step[step], 'shard', pairs)  4.42 us
    ppermute x2, waiting for transfers between devices, swap_cores(): lax.ppermute(value, 'shard', [(i, i + 1 - 2 * (i % 2)) for i in range(dev...  2.63 us
  transfers between devices with their start and end apart: 12, of which 7 were waited for; matrix products, arithmetic and copies ran while one was open for 0% of the time, Pallas kernels for 29%

profile of v19, /device:TPU:1, one launch (start us, length us, event | category | flops | bytes accessed | tf_op | source)
XLA Modules:
  0.0 85.7 jit_solution(5859807549102107440)
XLA Ops:
  0.6 0.0 copy-start.2
  0.6 0.0 copy-start.4
  0.7 3.6 %shard_map.111 = (bf16[608,128]{1,0:T(8,128)(2,1)}, bf16[608,128]{1,0:T(8,128)(2,1)}, bf16[608,128]{1,0:T(8,128)(2,1)}, bf16[608,128]{1,0:T(8,128)(2,1)}, f32[1024,128]{1,0:T(8,128)}) custom-call(bf16[1024,128]{1,0:T(8,128)(2,1)} %refs_4_.1, s32[4,64]{1,0:T(4,128)} %refs_6_.5, s32[8,256]{1,0:T(8,128)} %refs_8_.1, bf16[256,256]{1,0:T(8,128)(2,1)} %refs_11_.1, ...), custom_call_target="tpu_custom_call" | custom-call | flops 1000000000 | bytes 4194304 | tf_op jit(solution)/shard_map/pallas_call | solution.py:496
  4.3 0.1 collective-permute-start
  4.4 4.5 %collective-permute-start.1 = (bf16[608,128]{1,0:T(8,128)(2,1)}, bf16[608,128]{1,0:T(8,128)(2,1)S(1)}, u32[]{:S(2)}, u32[]{:S(2)}) collective-permute-start(bf16[608,128]{1,0:T(8,128)(2,1)} %get-tuple-element.37), channel_id=1, source_target_pairs={{1,2},{2,1},{3,4},{4,3},{5,6},{6,5},{7,8},{8,7},{9,10},{10,9},{11,... | collective-permute-start | bytes 466952 | tf_op jit(solution)/shard_map/ppermute | solution.py:23
  8.9 1.3 %collective-permute-start.2 = (bf16[608,128]{1,0:T(8,128)(2,1)}, bf16[608,128]{1,0:T(8,128)(2,1)S(1)}, u32[]{:S(2)}, u32[]{:S(2)}) collective-permute-start(bf16[608,128]{1,0:T(8,128)(2,1)} %get-tuple-element.38), channel_id=1, source_target_pairs={{0,2},{1,3},{2,0},{3,1},{4,6},{5,7},{6,4},{7,5},{8,10},{9,11},{10,... | collective-permute-start | bytes 466952 | tf_op jit(solution)/shard_map/ppermute | solution.py:23
  10.1 0.0 copy-start
  10.1 0.0 copy-start.6
  10.1 0.8 collective-permute-start.3
  10.9 0.0 copy-done.2
  11.0 0.0 copy-done.4
  11.0 7.3 %shard_map.112.refs_8_ = bf16[1024,3328]{1,0:T(8,128)(2,1)S(1)} custom-call(bf16[1024,128]{1,0:T(8,128)(2,1)S(1)} %copy-done.2, s32[27,1024]{1,0:T(8,128)S(1)} %copy-done.4), custom_call_target="tpu_custom_call" | custom-call | flops 4000000000 | bytes 4194304 | tf_op jit(solution)/shard_map/pallas_call | solution.py:496
  18.3 0.0 copy-start.3
  18.3 0.0 copy-start.5
  18.3 0.0 copy-start.8
  18.3 0.0 collective-permute-done.refs_0_
  18.3 0.0 collective-permute-done.1.refs_1_
  18.3 1.3 %collective-permute-done.2.refs_2_ = bf16[608,128]{1,0:T(8,128)(2,1)S(1)} collective-permute-done((bf16[608,128]{1,0:T(8,128)(2,1)}, bf16[608,128]{1,0:T(8,128)(2,1)S(1)}, u32[]{:S(2)}, u32[]{:S(2)}) %collective-permute-start.2) | collective-permute-done | bytes 155680 | tf_op jit(solution)/shard_map/ppermute | solution.py:23
  19.7 0.0 collective-permute-done.3.refs_3_
  19.7 0.0 copy-done
  19.7 0.0 copy-done.6
  19.7 6.3 %shard_map.113 = (bf16[1024,128]{1,0:T(8,128)(2,1)S(1)}, f32[1024,128]{1,0:T(8,128)S(1)}, bf16[1024,3456]{1,0:T(8,128)(2,1)S(1)}, bf16[128,128]{1,0:T(8,128)(2,1)S(1)}) custom-call(bf16[608,128]{1,0:T(8,128)(2,1)S(1)} %collective-permute-done.refs_0_, bf16[608,128]{1,0:T(8,128)(2,1)S(1)} %collective-permute-done.1.refs_1_, ...), custom_call_target="tpu_custom_call" | custom-call | flops 12000000000 | bytes 4194304 | tf_op jit(solution)/shard_map/pallas_call | solution.py:496
  26.0 0.0 copy-done.3
  26.0 0.0 copy-done.5
  26.0 0.0 copy-done.8
  26.0 2.6 %shard_map.114 = (f32[1024,128]{1,0:T(8,128)S(1)}, bf16[1024,128]{1,0:T(8,128)(2,1)S(1)}, bf16[256,1024]{1,0:T(8,128)(2,1)S(1)}, bf16[5632,128]{1,0:T(8,128)(2,1)S(1)}, bf16[2816,128]{1,0:T(8,128)(2,1)S(1)}) custom-call(bf16[608,128]{1,0:T(8,128)(2,1)S(1)} %collective-permute-done.refs_0_, bf16[608,128]{1,0:T(8,128)(2,1)S(1)} %collective-permute-done.1.refs_1_, ...), custom_call_target="tpu_custom_call" | custom-call | flops 3000000000 | bytes 4194304 | tf_op jit(solution)/shard_map/pallas_call | solution.py:496
  28.6 0.0 copy-start.9
  28.6 0.1 collective-permute-start.4
  28.7 2.2 %collective-permute-done.4.other_ref = bf16[2816,128]{1,0:T(8,128)(2,1)S(1)} collective-permute-done((bf16[2816,128]{1,0:T(8,128)(2,1)S(1)}, bf16[2816,128]{1,0:T(8,128)(2,1)S(1)}, u32[]{:S(2)}, u32[]{:S(2)}) %collective-permute-start.4) | collective-permute-done | bytes 720928 | tf_op jit(solution)/shard_map/ppermute | solution.py:509
  30.9 0.9 %shard_map.115.after_ref = bf16[2816,128]{1,0:T(8,128)(2,1)} custom-call(bf16[5632,128]{1,0:T(8,128)(2,1)S(1)} %get-tuple-element.45.terms_ref, bf16[2816,128]{1,0:T(8,128)(2,1)S(1)} %collective-permute-done.4.other_ref), custom_call_target="tpu_custom_call" | custom-call | flops 1000000 | bytes 4194304 | tf_op jit(solution)/shard_map/pallas_call | solution.py:496
  31.8 0.0 copy-done.9
  31.8 6.9 %all-to-all-start = ((bf16[32,88,128]{2,1,0:T(8,128)(2,1)}), bf16[32,88,128]{2,1,0:T(8,128)(2,1)S(1)}, u32[]{:S(2)}, u32[]{:S(2)}) async-start(bf16[32,88,128]{2,1,0:T(8,128)(2,1)} %bitcast), calls=%async_computation | async-start | bytes 1441792 | tf_op jit(solution)/shard_map/all_to_all | solution.py:513
  38.8 0.0 copy-start.10
  38.8 0.9 %copy-done.10 = bf16[1024,128]{1,0:T(8,128)(2,1)S(1)} copy-done((bf16[1024,128]{1,0:T(8,128)(2,1)S(1)}, bf16[1024,128]{1,0:T(8,128)(2,1)}, u32[]{:S(2)}) %copy-start.10) | copy-done | bytes 262168
  39.7 14.9 %shard_map.116 = (f32[1024,128]{1,0:T(8,128)S(1)}, bf16[96,128]{1,0:T(8,128)(2,1)S(1)}, bf16[96,128]{1,0:T(8,128)(2,1)S(1)}, bf16[96,128]{1,0:T(8,128)(2,1)S(1)}, bf16[96,128]{1,0:T(8,128)(2,1)S(1)}) custom-call(bf16[1024,128]{1,0:T(8,128)(2,1)S(1)} %copy-done.10, s32[27,1024]{1,0:T(8,128)S(1)} %copy-done.4, bf16[27,128,128]{2,1,0:T(8,128)(2,1)S(1)} %copy-done, ...), custom_call_target="tpu_custom_call" | custom-call | flops 20000000000 | bytes 4194304 | tf_op jit(solution)/shard_map/pallas_call | solution.py:496
  54.6 0.0 copy-start.1
  54.7 0.0 copy-start.7
  54.7 3.1 %all-to-all-done = bf16[32,88,128]{2,1,0:T(8,128)(2,1)S(1)} async-done(((bf16[32,88,128]{2,1,0:T(8,128)(2,1)}), bf16[32,88,128]{2,1,0:T(8,128)(2,1)S(1)}, u32[]{:S(2)}, u32[]{:S(2)}) %all-to-all-start) | async-done | bytes 720928 | tf_op jit(solution)/shard_map/all_to_all | solution.py:513
  57.7 1.0 %shard_map.117 = bf16[2816,128]{1,0:T(8,128)(2,1)} custom-call(bf16[2816,128]{1,0:T(8,128)(2,1)S(1)} %bitcast.8, bf16[96,128]{1,0:T(8,128)(2,1)S(1)} %get-tuple-element.52.after_ref), custom_call_target="tpu_custom_call" | custom-call | flops 1000000 | bytes 4194304 | tf_op jit(solution)/shard_map/pallas_call | solution.py:496
  58.7 3.9 %all-to-all-start.1 = ((bf16[32,88,128]{2,1,0:T(8,128)(2,1)}), bf16[32,88,128]{2,1,0:T(8,128)(2,1)S(1)}, u32[]{:S(2)}, u32[]{:S(2)}) async-start(bf16[32,88,128]{2,1,0:T(8,128)(2,1)} %bitcast.2), calls=%async_computation.1 | async-start | bytes 1441792 | tf_op jit(solution)/shard_map/all_to_all | solution.py:513
  62.6 0.3 collective-permute-start.5
  63.0 3.4 %collective-permute-start.6 = (bf16[96,128]{1,0:T(8,128)(2,1)S(1)}, bf16[96,128]{1,0:T(8,128)(2,1)S(1)}, u32[]{:S(2)}, u32[]{:S(2)}) collective-permute-start(bf16[96,128]{1,0:T(8,128)(2,1)S(1)} %get-tuple-element.53), channel_id=1, source_target_pairs={{1,2},{2,1},{3,4},{4,3},{5,6},{6,5},{7,8},{8,7},{9,10},{10,9},{11,... | collective-permute-start | bytes 73736 | tf_op jit(solution)/shard_map/ppermute | solution.py:23
  66.4 1.2 %collective-permute-start.7 = (bf16[96,128]{1,0:T(8,128)(2,1)S(1)}, bf16[96,128]{1,0:T(8,128)(2,1)S(1)}, u32[]{:S(2)}, u32[]{:S(2)}) collective-permute-start(bf16[96,128]{1,0:T(8,128)(2,1)S(1)} %get-tuple-element.54), channel_id=1, source_target_pairs={{0,2},{1,3},{2,0},{3,1},{4,6},{5,7},{6,4},{7,5},{8,10},{9,11},{10,... | collective-permute-start | bytes 73736 | tf_op jit(solution)/shard_map/ppermute | solution.py:23
  67.6 0.7 collective-permute-start.8
  68.3 0.0 collective-permute-done.5.refs_0_
  68.3 0.1 collective-permute-done.6.refs_1_
  68.4 2.9 %collective-permute-done.7.refs_2_ = bf16[96,128]{1,0:T(8,128)(2,1)S(1)} collective-permute-done((bf16[96,128]{1,0:T(8,128)(2,1)S(1)}, bf16[96,128]{1,0:T(8,128)(2,1)S(1)}, u32[]{:S(2)}, u32[]{:S(2)}) %collective-permute-start.7) | collective-permute-done | bytes 24608 | tf_op jit(solution)/shard_map/ppermute | solution.py:23
  71.4 0.0 collective-permute-done.8.refs_3_
  71.4 0.0 copy-done.1
  71.4 0.0 copy-done.7
  71.4 1.5 %shard_map.118 = (f32[1024,128]{1,0:T(8,128)}, bf16[256,256]{1,0:T(8,128)(2,1)}) custom-call(bf16[96,128]{1,0:T(8,128)(2,1)S(1)} %collective-permute-done.5.refs_0_, bf16[96,128]{1,0:T(8,128)(2,1)S(1)} %collective-permute-done.6.refs_1_, bf16[96,128]{1,0:T(8,128)(2,1)S(1)} %collective-permute-done.7.refs_2_, ...), custom_call_target="tpu_custom_call" | custom-call | flops 1000000000 | bytes 4194304 | tf_op jit(solution)/shard_map/pallas_call | solution.py:496
  72.8 8.8 %all-to-all-done.1 = bf16[32,88,128]{2,1,0:T(8,128)(2,1)S(1)} async-done(((bf16[32,88,128]{2,1,0:T(8,128)(2,1)}), bf16[32,88,128]{2,1,0:T(8,128)(2,1)S(1)}, u32[]{:S(2)}, u32[]{:S(2)}) %all-to-all-start.1) | async-done | bytes 720928 | tf_op jit(solution)/shard_map/all_to_all | solution.py:513
  81.6 0.8 collective-permute-start.9
  82.4 1.4 %shard_map.119 = (f32[3456,128]{1,0:T(8,128)}, f32[1024,256]{1,0:T(8,128)}) custom-call(bf16[2816,128]{1,0:T(8,128)(2,1)S(1)} %bitcast.7), custom_call_target="tpu_custom_call" | custom-call | flops 1000000 | bytes 4194304 | tf_op jit(solution)/shard_map/pallas_call | solution.py:496
  83.7 0.5 collective-permute-done.9.refs_0_
  84.2 1.4 %shard_map.120 = (f32[3456,128]{1,0:T(8,128)}, f32[1024,256]{1,0:T(8,128)}) custom-call(bf16[2816,128]{1,0:T(8,128)(2,1)S(1)} %collective-permute-done.9.refs_0_, f32[3456,128]{1,0:T(8,128)} %get-tuple-element.64.refs_1_, f32[1024,256]{1,0:T(8,128)} %get-tuple-element.65.refs_2_), custom_call_target="tpu_custom_call", output_to_operand_aliasing={{0}: (1, {}), {1}: (2, {})} | custom-call | flops 1000000 | bytes 4194304 | tf_op jit(solution)/shard_map/pallas_call | solution.py:496
Async XLA Ops:
  0.6 10.3 %copy-start.2 = (bf16[1024,128]{1,0:T(8,128)(2,1)S(1)}, bf16[1024,128]{1,0:T(8,128)(2,1)}, u32[]{:S(2)}) copy-start(bf16[1024,128]{1,0:T(8,128)(2,1)} %refs_4_.1) | copy-start | bytes 786436
  0.6 10.3 %copy-start.4 = (s32[27,1024]{1,0:T(8,128)S(1)}, s32[27,1024]{1,0:T(8,128)}, u32[]{:S(2)}) copy-start(s32[27,1024]{1,0:T(8,128)} %map_ref.3) | copy-start | bytes 331780
  4.3 14.0 %collective-permute-start = (bf16[608,128]{1,0:T(8,128)(2,1)}, bf16[608,128]{1,0:T(8,128)(2,1)S(1)}, u32[]{:S(2)}, u32[]{:S(2)}) collective-permute-start(bf16[608,128]{1,0:T(8,128)(2,1)} %get-tuple-element.36), channel_id=1, source_target_pairs={{0,1},{1,0},{2,3},{3,2},{4,5},{5,4},{6,7},{7,6},{8,9},{9,8},{10,11... | collective-permute-start | bytes 466952 | tf_op jit(solution)/shard_map/ppermute | solution.py:23
  4.4 13.9 %collective-permute-start.1 = (bf16[608,128]{1,0:T(8,128)(2,1)}, bf16[608,128]{1,0:T(8,128)(2,1)S(1)}, u32[]{:S(2)}, u32[]{:S(2)}) collective-permute-start(bf16[608,128]{1,0:T(8,128)(2,1)} %get-tuple-element.37), channel_id=1, source_target_pairs={{1,2},{2,1},{3,4},{4,3},{5,6},{6,5},{7,8},{8,7},{9,10},{10,9},{11,... | collective-permute-start | bytes 466952 | tf_op jit(solution)/shard_map/ppermute | solution.py:23
  8.9 10.8 %collective-permute-start.2 = (bf16[608,128]{1,0:T(8,128)(2,1)}, bf16[608,128]{1,0:T(8,128)(2,1)S(1)}, u32[]{:S(2)}, u32[]{:S(2)}) collective-permute-start(bf16[608,128]{1,0:T(8,128)(2,1)} %get-tuple-element.38), channel_id=1, source_target_pairs={{0,2},{1,3},{2,0},{3,1},{4,6},{5,7},{6,4},{7,5},{8,10},{9,11},{10,... | collective-permute-start | bytes 466952 | tf_op jit(solution)/shard_map/ppermute | solution.py:23
  10.1 9.5 %copy-start = (bf16[27,128,128]{2,1,0:T(8,128)(2,1)S(1)}, bf16[27,128,128]{2,1,0:T(8,128)(2,1)}, u32[]{:S(2)}) copy-start(bf16[27,128,128]{2,1,0:T(8,128)(2,1)} %weight_ref.1) | copy-start | bytes 2654212
  10.1 9.5 %copy-start.6 = (s32[4,32]{1,0:T(4,128)S(1)}, s32[4,32]{1,0:T(4,128)}, u32[]{:S(2)}) copy-start(s32[4,32]{1,0:T(4,128)} %refs_6_.4) | copy-start | bytes 1540
  10.1 9.5 %collective-permute-start.3 = (bf16[608,128]{1,0:T(8,128)(2,1)}, bf16[608,128]{1,0:T(8,128)(2,1)S(1)}, u32[]{:S(2)}, u32[]{:S(2)}) collective-permute-start(bf16[608,128]{1,0:T(8,128)(2,1)} %get-tuple-element.39), channel_id=1, source_target_pairs={{2,4},{3,5},{4,2},{5,3},{6,8},{7,9},{8,6},{9,7},{10,12},{11,13},{1... | collective-permute-start | bytes 466952 | tf_op jit(solution)/shard_map/ppermute | solution.py:23
  18.3 7.7 %copy-start.3 = (bf16[256,256]{1,0:T(8,128)(2,1)S(1)}, bf16[256,256]{1,0:T(8,128)(2,1)}, u32[]{:S(2)}) copy-start(bf16[256,256]{1,0:T(8,128)(2,1)} %refs_11_.1) | copy-start | bytes 393220
  18.3 7.7 %copy-start.5 = (s32[8,256]{1,0:T(8,128)S(1)}, s32[8,256]{1,0:T(8,128)}, u32[]{:S(2)}) copy-start(s32[8,256]{1,0:T(8,128)} %refs_8_.1) | copy-start | bytes 24580
  18.3 7.7 %copy-start.8 = (f32[1024,128]{1,0:T(8,128)S(1)}, f32[1024,128]{1,0:T(8,128)}, u32[]{:S(2)}) copy-start(f32[1024,128]{1,0:T(8,128)} %get-tuple-element.42.refs_7_) | copy-start | bytes 1572868
  28.6 3.2 %copy-start.9 = (bf16[1024,128]{1,0:T(8,128)(2,1)}, bf16[1024,128]{1,0:T(8,128)(2,1)S(1)}, u32[]{:S(2)}) copy-start(bf16[1024,128]{1,0:T(8,128)(2,1)S(1)} %get-tuple-element.47.pgrad_ref) | copy-start | bytes 786436
  28.6 2.3 %collective-permute-start.4 = (bf16[2816,128]{1,0:T(8,128)(2,1)S(1)}, bf16[2816,128]{1,0:T(8,128)(2,1)S(1)}, u32[]{:S(2)}, u32[]{:S(2)}) collective-permute-start(bf16[2816,128]{1,0:T(8,128)(2,1)S(1)} %get-tuple-element.46), channel_id=1, source_target_pairs={{0,1},{1,0},{2,3},{3,2},{4,5},{5,4},{6,7},{7,6},{8,9},{9,8},{10,11... | collective-permute-start | bytes 2162696 | tf_op jit(solution)/shard_map/ppermute | solution.py:509
  31.8 25.9 %all-to-all-start = ((bf16[32,88,128]{2,1,0:T(8,128)(2,1)}), bf16[32,88,128]{2,1,0:T(8,128)(2,1)S(1)}, u32[]{:S(2)}, u32[]{:S(2)}) async-start(bf16[32,88,128]{2,1,0:T(8,128)(2,1)} %bitcast), calls=%async_computation | async-start | bytes 1441792 | tf_op jit(solution)/shard_map/all_to_all | solution.py:513
  38.8 1.0 %copy-start.10 = (bf16[1024,128]{1,0:T(8,128)(2,1)S(1)}, bf16[1024,128]{1,0:T(8,128)(2,1)}, u32[]{:S(2)}) copy-start(bf16[1024,128]{1,0:T(8,128)(2,1)} %copy-done.9) | copy-start | bytes 786436
  54.6 16.7 %copy-start.1 = (bf16[8,128,256]{2,1,0:T(8,128)(2,1)S(1)}, bf16[8,128,256]{2,1,0:T(8,128)(2,1)}, u32[]{:S(2)}) copy-start(bf16[8,128,256]{2,1,0:T(8,128)(2,1)} %refs_9_.1) | copy-start | bytes 1572868
  54.7 16.7 %copy-start.7 = (s32[4,64]{1,0:T(4,128)S(1)}, s32[4,64]{1,0:T(4,128)}, u32[]{:S(2)}) copy-start(s32[4,64]{1,0:T(4,128)} %refs_6_.5) | copy-start | bytes 3076
  58.7 22.8 %all-to-all-start.1 = ((bf16[32,88,128]{2,1,0:T(8,128)(2,1)}), bf16[32,88,128]{2,1,0:T(8,128)(2,1)S(1)}, u32[]{:S(2)}, u32[]{:S(2)}) async-start(bf16[32,88,128]{2,1,0:T(8,128)(2,1)} %bitcast.2), calls=%async_computation.1 | async-start | bytes 1441792 | tf_op jit(solution)/shard_map/all_to_all | solution.py:513
  62.6 5.7 %collective-permute-start.5 = (bf16[96,128]{1,0:T(8,128)(2,1)S(1)}, bf16[96,128]{1,0:T(8,128)(2,1)S(1)}, u32[]{:S(2)}, u32[]{:S(2)}) collective-permute-start(bf16[96,128]{1,0:T(8,128)(2,1)S(1)} %get-tuple-element.52.after_ref), channel_id=1, source_target_pairs={{0,1},{1,0},{2,3},{3,2},{4,5},{5,4},{6,7},{7,6},{8,9},{9,8},{10,11... | collective-permute-start | bytes 73736 | tf_op jit(solution)/shard_map/ppermute | solution.py:23
  63.0 5.5 %collective-permute-start.6 = (bf16[96,128]{1,0:T(8,128)(2,1)S(1)}, bf16[96,128]{1,0:T(8,128)(2,1)S(1)}, u32[]{:S(2)}, u32[]{:S(2)}) collective-permute-start(bf16[96,128]{1,0:T(8,128)(2,1)S(1)} %get-tuple-element.53), channel_id=1, source_target_pairs={{1,2},{2,1},{3,4},{4,3},{5,6},{6,5},{7,8},{8,7},{9,10},{10,9},{11,... | collective-permute-start | bytes 73736 | tf_op jit(solution)/shard_map/ppermute | solution.py:23
  66.4 5.0 %collective-permute-start.7 = (bf16[96,128]{1,0:T(8,128)(2,1)S(1)}, bf16[96,128]{1,0:T(8,128)(2,1)S(1)}, u32[]{:S(2)}, u32[]{:S(2)}) collective-permute-start(bf16[96,128]{1,0:T(8,128)(2,1)S(1)} %get-tuple-element.54), channel_id=1, source_target_pairs={{0,2},{1,3},{2,0},{3,1},{4,6},{5,7},{6,4},{7,5},{8,10},{9,11},{10,... | collective-permute-start | bytes 73736 | tf_op jit(solution)/shard_map/ppermute | solution.py:23
  67.6 3.7 %collective-permute-start.8 = (bf16[96,128]{1,0:T(8,128)(2,1)S(1)}, bf16[96,128]{1,0:T(8,128)(2,1)S(1)}, u32[]{:S(2)}, u32[]{:S(2)}) collective-permute-start(bf16[96,128]{1,0:T(8,128)(2,1)S(1)} %get-tuple-element.55), channel_id=1, source_target_pairs={{2,4},{3,5},{4,2},{5,3},{6,8},{7,9},{8,6},{9,7},{10,12},{11,13},{1... | collective-permute-start | bytes 73736 | tf_op jit(solution)/shard_map/ppermute | solution.py:23
  81.6 2.6 %collective-permute-start.9 = (bf16[2816,128]{1,0:T(8,128)(2,1)S(1)}, bf16[2816,128]{1,0:T(8,128)(2,1)S(1)}, u32[]{:S(2)}, u32[]{:S(2)}) collective-permute-start(bf16[2816,128]{1,0:T(8,128)(2,1)S(1)} %bitcast.6), channel_id=1, source_target_pairs={{0,1},{1,0},{2,3},{3,2},{4,5},{5,4},{6,7},{7,6},{8,9},{9,8},{10,11... | collective-permute-start | bytes 2162696 | tf_op jit(solution)/shard_map/ppermute | solution.py:509
